TPU v7x, 32 devices: a whole 2x2x4 slice. The times are simulated.
32 devices in a mesh: batch: 16 (over z, y, x), stream: 2 (over core).
Axes of the slice: x: 2, y: 2, z: 4, core: 2. Of those that a mesh axis runs over, the one named last changes fastest.
Arguments:
- tokens: bfloat16 [16384, 1024], P('batch'), may hold values from -6 to 6
- cotangent: bfloat16 [16384, 1024], P('batch'), may hold values from -6 to 6
- branch_weight: bfloat16 [2, 2, 4096, 1024], P('stream')
- branch_bias: bfloat16 [2, 2, 4096], P('stream'), may hold values from -1.1953125 to 1.1953125
- up_weight: bfloat16 [2, 4096, 1024], replicated, may hold values from -0.1875 to 0.1875
- down_bias: bfloat16 [2, 1024], replicated, may hold values from -3 to 3
- norm_gain: bfloat16 [2, 1024], replicated, may hold values from 0.5 to 1.5
- norm_bias: bfloat16 [2, 1024], replicated, may hold values from -2 to 2
- freq_seeds: int32 [2, 16, 64], replicated, may hold values from 1 to 63
- doc_starts: int32 [16, 4], P('batch'), may hold values from 0 to 1023, as said below
Outputs:
- result: float32 [16384, 1024], P('batch')
- input_grad: float32 [16384, 1024], P('batch')
- branch_weight_grad: float32 [2, 2, 4096, 1024], P('stream', None, 'batch')
- branch_bias_grad: float32 [2, 2, 4096], P('stream', None, 'batch')
- up_weight_grad: float32 [2, 4096, 1024], P(None, ('batch', 'stream'))
- down_bias_grad: float32 [2, 1024], P(None, 'batch')
- norm_gain_grad: float32 [2, 1024], P(None, 'batch')
- norm_bias_grad: float32 [2, 1024], P(None, 'batch')
Inputs may be any that keep to these rules, and one draw needn't show every extreme that they name: `doc_starts`: row s lists the first positions of the 4 documents of sequence s, strictly increasing, the first being 0.
All inputs are finite; a program needn't handle non-finite values.
Results may differ from a plain program's by a relative error of at most 0.038.
Values sent between devices are 32-bit elements; how exact they have to be, the bound alone decides.
A program may use at most 384 MiB of HBM per device.

v0:
```python
import math

import jax
import jax.numpy as jnp
from jax import lax
from jax.sharding import PartitionSpec as P

HEADS = 16
DH = 64
ROT = 16
FEAT = 64
LAYERS = 2


EPSILON = 1e-05
HIGH = lax.Precision.HIGHEST


def layer_norm(values, scale_gain, offset):
    average = jnp.mean(values, -1, keepdims=True)
    centered = values - average
    variance = jnp.mean(centered * centered, -1, keepdims=True)
    return centered * lax.rsqrt(variance + EPSILON) * scale_gain + offset


def normal_quantile(prob):
    nearer = jnp.minimum(prob, 1.0 - prob)
    radius = jnp.sqrt(-2.0 * jnp.log(nearer))
    upper = 2.515517 + 0.802853 * radius + 0.010328 * radius * radius
    lower = (
        1.0 + 1.432788 * radius + 0.189269 * radius * radius + 0.001308 * radius * radius * radius
    )
    magnitude = radius - upper / lower
    return jnp.where(prob > 0.5, magnitude, -magnitude)


def cosine_table(head_size):
    samples = jnp.arange(head_size, dtype=jnp.float32)
    freqs = samples[:, None]
    angles = math.pi * (samples[None, :] + 0.5) * freqs / head_size
    cosine_rows = jnp.cos(angles) * math.sqrt(2.0 / head_size)
    return jnp.where(freqs == 0.0, cosine_rows * math.sqrt(0.5), cosine_rows)


def feature_tables(seeds):
    indices = jnp.arange(FEAT, dtype=jnp.int32)
    lattice = indices[None, :, None] * seeds[:, None, :] % FEAT
    frequency = normal_quantile((lattice.astype(jnp.float32) + 0.5) / FEAT)
    cosine_rows = cosine_table(DH)
    project = jnp.einsum("kn,hmk->hnm", cosine_rows, frequency, precision=HIGH) * DH ** (-0.25)
    weights = FEAT * jax.nn.softmax(-0.5 / DH * jnp.sum(frequency * frequency, -1), axis=-1)
    return (project, weights)


def rotary_tables(length):
    position = jnp.arange(length, dtype=jnp.float32)
    inverse = 10000.0 ** (-jnp.arange(0, ROT, 2, dtype=jnp.float32) / ROT)
    angles = position[:, None] * inverse[None, :]
    angles = jnp.concatenate([angles, angles], axis=1)
    return (jnp.cos(angles), jnp.sin(angles))


def rotate(head_values, cosine_rows, sine_rows):
    turned_part = head_values[..., :ROT]
    halfway = ROT // 2
    swapped = jnp.concatenate([-turned_part[..., halfway:], turned_part[..., :halfway]], axis=-1)
    rotated = turned_part * cosine_rows[:, None, :] + swapped * sine_rows[:, None, :]
    return jnp.concatenate([rotated, head_values[..., ROT:]], axis=-1)


def feature_maps(queries, keys_in, cosine_rows, sine_rows, project, weights):
    length = queries.shape[0]
    query_heads = queries.reshape(length, HEADS, DH)
    key_heads = keys_in.reshape(length, HEADS, DH)
    query_z = jnp.einsum(
        "thd,hdm->thm", rotate(query_heads, cosine_rows, sine_rows), project, precision=HIGH
    )
    key_z = jnp.einsum(
        "thd,hdm->thm", rotate(key_heads, cosine_rows, sine_rows), project, precision=HIGH
    )
    key_z = key_z - 0.5 / math.sqrt(DH) * jnp.sum(key_heads * key_heads, -1, keepdims=True)
    return (jnp.exp(query_z), weights[None, :, :] * jnp.exp(key_z))


def contract_rows(left, right):
    return lax.dot_general(
        left, right, (((0,), (0,)), ((), ())), preferred_element_type=jnp.float32
    )


def contract_cols(left, right):
    return lax.dot_general(
        left, right, (((1,), (1,)), ((), ())), preferred_element_type=jnp.float32
    )


def attend_forward(
    hidden_low, weights_block, bias_block, project, weights, cosine_rows, sine_rows, allowed
):
    length, model_width = hidden_low.shape
    projected = contract_cols(hidden_low, weights_block[: 3 * model_width]) + bias_block[
        : 3 * model_width
    ].astype(jnp.float32)
    query_feat, key_feat = feature_maps(
        projected[:, :model_width],
        projected[:, model_width : 2 * model_width],
        cosine_rows,
        sine_rows,
        project,
        weights,
    )
    query_low = query_feat.astype(jnp.bfloat16)
    key_low = key_feat.astype(jnp.bfloat16)
    value_low = projected[:, 2 * model_width :].astype(jnp.bfloat16).reshape(length, HEADS, DH)
    block_rows = min(512, length)
    pieces = []
    for first_row in range(0, length, block_rows):
        finish = first_row + block_rows
        scores = jnp.einsum(
            "qhm,khm->hqk",
            query_low[first_row:finish],
            key_low[:finish],
            preferred_element_type=jnp.float32,
        )
        scores = jnp.where(allowed[None, first_row:finish, :finish], scores, 0.0)
        totals = jnp.sum(scores, -1)
        numerator = jnp.einsum(
            "hqk,khd->qhd",
            scores.astype(jnp.bfloat16),
            value_low[:finish],
            preferred_element_type=jnp.float32,
        )
        pieces.append(numerator / jnp.transpose(totals)[:, :, None])
    mixed_heads = jnp.concatenate(pieces, axis=0).reshape(length, model_width)
    branch = jnp.dot(
        mixed_heads.astype(jnp.bfloat16),
        weights_block[3 * model_width :],
        preferred_element_type=jnp.float32,
    )
    branch = branch + bias_block[3 * model_width :].astype(jnp.float32)
    kept_state = jnp.concatenate([projected, mixed_heads], axis=1)
    return (branch, kept_state)


def mlp_forward(hidden_low, weights_block, bias_block, up_block, down_block):
    hidden_units = contract_cols(hidden_low, up_block) + bias_block.astype(jnp.float32)
    active_low = jax.nn.gelu(hidden_units, approximate=False).astype(jnp.bfloat16)
    branch = jnp.dot(
        active_low, weights_block, preferred_element_type=jnp.float32
    ) + down_block.astype(jnp.float32)
    return (branch, hidden_units)


def attend_backward(
    grad_low,
    hidden_low,
    kept_state,
    weights_block,
    project,
    weights,
    cosine_rows,
    sine_rows,
    allowed,
):
    length, model_width = hidden_low.shape
    projected = kept_state[:, : 3 * model_width]
    mixed_flat = kept_state[:, 3 * model_width :]
    grad_out_weight = contract_rows(mixed_flat.astype(jnp.bfloat16), grad_low)
    grad_out_bias = jnp.sum(grad_low.astype(jnp.float32), 0)
    grad_mixed = contract_cols(grad_low, weights_block[3 * model_width :])
    grad_mixed = grad_mixed.astype(jnp.bfloat16).astype(jnp.float32).reshape(length, HEADS, DH)
    mixed_heads = mixed_flat.reshape(length, HEADS, DH)

    def features_only(queries, keys_in):
        return feature_maps(queries, keys_in, cosine_rows, sine_rows, project, weights)

    (query_feat, key_feat), feature_back = jax.vjp(
        features_only, projected[:, :model_width], projected[:, model_width : 2 * model_width]
    )
    query_low = query_feat.astype(jnp.bfloat16)
    key_low = key_feat.astype(jnp.bfloat16)
    value_low = projected[:, 2 * model_width :].astype(jnp.bfloat16).reshape(length, HEADS, DH)
    grad_value = jnp.zeros((length, HEADS, DH), jnp.float32)
    grad_key_feat = jnp.zeros(key_feat.shape, jnp.float32)
    query_parts = []
    block_rows = min(512, length)
    for first_row in range(0, length, block_rows):
        finish = first_row + block_rows
        visible = allowed[None, first_row:finish, :finish]
        scores = jnp.einsum(
            "qhm,khm->hqk",
            query_low[first_row:finish],
            key_low[:finish],
            preferred_element_type=jnp.float32,
        )
        scores = jnp.where(visible, scores, 0.0)
        totals = jnp.transpose(jnp.sum(scores, -1))
        grad_block = grad_mixed[first_row:finish]
        grad_numer = (grad_block / totals[:, :, None]).astype(jnp.bfloat16)
        grad_totals = -jnp.sum(grad_block * mixed_heads[first_row:finish], -1) / totals
        grad_scores = jnp.einsum(
            "qhd,khd->hqk", grad_numer, value_low[:finish], preferred_element_type=jnp.float32
        )
        grad_scores = grad_scores + jnp.transpose(grad_totals)[:, :, None]
        grad_scores = jnp.where(
            visible, grad_scores.astype(jnp.bfloat16), jnp.zeros((), jnp.bfloat16)
        )
        grad_value = grad_value.at[:finish].add(
            jnp.einsum(
                "hqk,qhd->khd",
                scores.astype(jnp.bfloat16),
                grad_numer,
                preferred_element_type=jnp.float32,
            )
        )
        query_parts.append(
            jnp.einsum(
                "hqk,khm->qhm", grad_scores, key_low[:finish], preferred_element_type=jnp.float32
            )
        )
        grad_key_feat = grad_key_feat.at[:finish].add(
            jnp.einsum(
                "hqk,qhm->khm",
                grad_scores,
                query_low[first_row:finish],
                preferred_element_type=jnp.float32,
            )
        )
    grad_query, grad_key = feature_back((jnp.concatenate(query_parts, axis=0), grad_key_feat))
    grad_projected = jnp.concatenate(
        [grad_query, grad_key, grad_value.reshape(length, model_width)], axis=1
    ).astype(jnp.bfloat16)
    grad_in_weight = contract_rows(grad_projected, hidden_low)
    grad_in_bias = jnp.sum(grad_projected.astype(jnp.float32), 0)
    grad_hidden = jnp.dot(
        grad_projected, weights_block[: 3 * model_width], preferred_element_type=jnp.float32
    )
    grad_block_weight = jnp.concatenate([grad_in_weight, grad_out_weight], axis=0)
    grad_block_bias = jnp.concatenate([grad_in_bias, grad_out_bias], axis=0)
    grad_up_zero = jnp.zeros((4 * model_width, model_width), jnp.float32)
    return (grad_hidden, grad_block_weight, grad_block_bias, grad_up_zero)


def mlp_backward(grad_low, hidden_low, kept_state, weights_block, up_block):
    active, gelu_back = jax.vjp(
        lambda unit_values: jax.nn.gelu(unit_values, approximate=False), kept_state
    )
    grad_down = contract_rows(active.astype(jnp.bfloat16), grad_low)
    grad_active = contract_cols(grad_low, weights_block)
    grad_units = gelu_back(grad_active)[0].astype(jnp.bfloat16)
    grad_up_bias = jnp.sum(grad_units.astype(jnp.float32), 0)
    grad_up = contract_rows(grad_units, hidden_low)
    grad_hidden = jnp.dot(grad_units, up_block, preferred_element_type=jnp.float32)
    return (grad_hidden, grad_down, grad_up_bias, grad_up)


def shards(
    tokens,
    cotangent,
    branch_weight,
    branch_bias,
    up_weight,
    down_bias,
    norm_gain,
    norm_bias,
    freq_seeds,
    doc_starts,
):
    stream_index = lax.axis_index("stream")
    is_attention = stream_index == 0
    length = tokens.shape[0]
    position = jnp.arange(length, dtype=jnp.int32)
    doc_ids = jnp.sum((doc_starts[0][None, :] <= position[:, None]).astype(jnp.int32), axis=1)
    allowed = (doc_ids[:, None] == doc_ids[None, :]) & (position[None, :] <= position[:, None])
    cosine_rows, sine_rows = rotary_tables(length)
    tables = [feature_tables(freq_seeds[layer_idx]) for layer_idx in range(LAYERS)]
    residual = tokens.astype(jnp.float32)
    layer_inputs = []
    hidden_lows = []
    kept_states = []
    for layer_idx in range(LAYERS):
        weights_block = branch_weight[0, layer_idx]
        bias_block = branch_bias[0, layer_idx]
        project, weights = tables[layer_idx]
        layer_inputs.append(residual)
        hidden_low = layer_norm(
            residual,
            norm_gain[layer_idx].astype(jnp.float32),
            norm_bias[layer_idx].astype(jnp.float32),
        ).astype(jnp.bfloat16)
        own_branch, kept_state = lax.cond(
            is_attention,
            lambda: attend_forward(
                hidden_low,
                weights_block,
                bias_block,
                project,
                weights,
                cosine_rows,
                sine_rows,
                allowed,
            ),
            lambda: mlp_forward(
                hidden_low, weights_block, bias_block, up_weight[layer_idx], down_bias[layer_idx]
            ),
        )
        residual = residual + lax.psum(own_branch, "stream")
        hidden_lows.append(hidden_low)
        kept_states.append(kept_state)
    grad_residual = cotangent.astype(jnp.float32)
    weight_shares = [None] * LAYERS
    bias_shares = [None] * LAYERS
    gain_shares = [None] * LAYERS
    offset_shares = [None] * LAYERS
    down_shares = [None] * LAYERS
    up_shares = [None] * LAYERS
    for layer_idx in reversed(range(LAYERS)):
        weights_block = branch_weight[0, layer_idx]
        project, weights = tables[layer_idx]
        grad_low = grad_residual.astype(jnp.bfloat16)
        hidden_low = hidden_lows[layer_idx]
        kept_state = kept_states[layer_idx]
        grad_part, grad_block_weight, grad_block_bias, grad_up = lax.cond(
            is_attention,
            lambda: attend_backward(
                grad_low,
                hidden_low,
                kept_state,
                weights_block,
                project,
                weights,
                cosine_rows,
                sine_rows,
                allowed,
            ),
            lambda: mlp_backward(
                grad_low, hidden_low, kept_state, weights_block, up_weight[layer_idx]
            ),
        )
        grad_hidden = lax.psum(grad_part, "stream")

        def normed(values, scale_gain, offset):
            return layer_norm(values, scale_gain, offset)

        _, norm_back = jax.vjp(
            normed,
            layer_inputs[layer_idx],
            norm_gain[layer_idx].astype(jnp.float32),
            norm_bias[layer_idx].astype(jnp.float32),
        )
        grad_input, grad_gain, grad_offset = norm_back(grad_hidden)
        grad_down_bias = jnp.sum(grad_low.astype(jnp.float32), 0)
        shares = (
            lax.psum_scatter(grad_block_weight, "batch", scatter_dimension=0, tiled=True),
            lax.psum_scatter(grad_block_bias, "batch", scatter_dimension=0, tiled=True),
            lax.psum_scatter(grad_gain, "batch", scatter_dimension=0, tiled=True),
            lax.psum_scatter(grad_offset, "batch", scatter_dimension=0, tiled=True),
            lax.psum_scatter(grad_down_bias, "batch", scatter_dimension=0, tiled=True),
        )
        weight_shares[layer_idx] = shares[0]
        bias_shares[layer_idx] = shares[1]
        gain_shares[layer_idx] = shares[2]
        offset_shares[layer_idx] = shares[3]
        down_shares[layer_idx] = shares[4]
        up_shares[layer_idx] = lax.psum_scatter(
            grad_up, ("batch", "stream"), scatter_dimension=0, tiled=True
        )
        grad_residual = grad_residual + grad_input
    return (
        residual,
        grad_residual,
        jnp.stack(weight_shares)[None],
        jnp.stack(bias_shares)[None],
        jnp.stack(up_shares),
        jnp.stack(down_shares),
        jnp.stack(gain_shares),
        jnp.stack(offset_shares),
    )


def solution(mesh):
    placed = (
        P("batch", None),
        P("batch", None),
        P("stream", None, None, None),
        P("stream", None, None),
        P(),
        P(),
        P(),
        P(),
        P(),
        P("batch", None),
    )
    return jax.shard_map(
        shards,
        mesh=mesh,
        in_specs=placed,
        out_specs=(
            P("batch", None),
            P("batch", None),
            P("stream", None, "batch", None),
            P("stream", None, "batch"),
            P(None, ("batch", "stream"), None),
            P(None, "batch"),
            P(None, "batch"),
            P(None, "batch"),
        ),
        check_vma=False,
    )
```

profile of v0, /device:TPU:0, one launch (start us, length us, event | category | flops | bytes accessed | tf_op | source)
XLA Modules:
  0.0 1944.5 jit_solution(3924097634155393616)
XLA Ops:
  20.0 12.1 slice_bitcast_fusion
  35.8 122.9 %conditional.4 = (f32[1024,4096]{1,0:T(8,128)}, f32[1024,1024]{1,0:T(8,128)S(1)}, f32[1024,1024]{1,0:T(8,128)}) conditional(s32[]{:T(128)} %convert_element_type.208, (bf16[2,4096,1024]{2,1,0:T(8,128)(2,1)}, bf16[1024,1024]{1,0:T(8,128)(2,1)}, bf16[4096]{0:T(1024)(128)(2,1)S(1)}, bf16[4096,1024]{1,0:T(8,128)(2,1)}, ...), branch_computations={%region_6.7_spmd, %region_7.11_spmd} | conditional | flops 17456697344 | bytes 317763776 | solution.py:291
  47.1 12.1 fusion.443
  118.1 12.3 bitcast_divide_fusion
  146.5 11.8 pad_maximum_fusion
  167.7 27.6 %all-reduce.34.cloned.1.call-done = f32[1024,1024]{1,0:T(8,128)} async-done(((f32[1024,1024]{1,0:T(8,128)}), f32[1024,1024]{1,0:T(8,128)}) %all-reduce.34.cloned.1.call-update) | async-done | bytes 4194320 | tf_op jit(solution)/shard_map/psum | solution.py:307
  202.1 134.0 %conditional.5 = (f32[1024,4096]{1,0:T(8,128)}, f32[1024,1024]{1,0:T(8,128)S(1)}, f32[1024,1024]{1,0:T(8,128)}) conditional(s32[]{:T(128)} %convert_element_type.208, (bf16[2,4096,1024]{2,1,0:T(8,128)(2,1)}, bf16[1024,1024]{1,0:T(8,128)(2,1)}, bf16[4096]{0:T(1024)(128)(2,1)S(1)}, bf16[4096,1024]{1,0:T(8,128)(2,1)}, ...), branch_computations={%region_17.18_spmd, %region_18.22_spmd} | conditional | flops 17456697344 | bytes 316715264 | solution.py:291
  216.0 12.3 fusion.445
  295.2 12.9 bitcast_divide_fusion.2
  324.1 11.8 pad_maximum_fusion.2
  338.1 219.4 %conditional.6 = (f32[1024,1024]{1,0:T(8,128)}, f32[4096,1024]{1,0:T(8,128)}, f32[4096]{0:T(1024)S(1)}, f32[4096,1024]{1,0:T(8,128)}) conditional(s32[]{:T(128)} %convert_element_type.208, (f32[1024,4096]{1,0:T(8,128)}, bf16[1024,1024]{1,0:T(8,128)(2,1)S(1)}, bf16[4096,1024]{1,0:T(8,128)(2,1)}, bf16[2,4096,1024]{2,1,0:T(8,128)(2,1)}, ...), branch_computations={%region_23.25_spmd, %region_25.34_spmd} | conditional | flops 34682695680 | bytes 801518080 | solution.py:323
  360.0 17.5 copy.150
  485.4 13.0 convolution_bitcast_fusion
  564.4 22.8 %all-reduce.36.cloned.1.call-done = f32[1024,1024]{1,0:T(8,128)} async-done(((f32[1024,1024]{1,0:T(8,128)}), f32[1024,1024]{1,0:T(8,128)}) %all-reduce.36.cloned.1.call-update) | async-done | bytes 4194320 | tf_op jit(solution)/shard_map/psum | solution.py:340
  597.1 213.5 %conditional.7 = (f32[1024,1024]{1,0:T(8,128)}, f32[4096,1024]{1,0:T(8,128)}, f32[4096]{0:T(1024)S(1)}, f32[4096,1024]{1,0:T(8,128)}) conditional(s32[]{:T(128)} %convert_element_type.208, (f32[1024,4096]{1,0:T(8,128)}, bf16[1024,1024]{1,0:T(8,128)(2,1)S(1)}, bf16[4096,1024]{1,0:T(8,128)(2,1)}, bf16[2,4096,1024]{2,1,0:T(8,128)(2,1)}, ...), branch_computations={%region_37.39_spmd, %region_39.0_spmd} | conditional | flops 34682695680 | bytes 812003840 | solution.py:323
  615.6 17.5 copy.152
  705.0 11.8 fusion.297
  739.3 11.6 convolution_bitcast_fusion.1
  815.1 35.9 %all-reduce.38.cloned.1.call-done = (f32[1024,1024]{1,0:T(8,128)}, f32[1024,1024]{1,0:T(8,128)}) async-done(((f32[1024,1024]{1,0:T(8,128)}, f32[1024,1024]{1,0:T(8,128)}), (f32[1024,1024]{1,0:T(8,128)}, f32[1024,1024]{1,0:T(8,128)})) %all-reduce.38.cloned.1.call-update) | async-done | bytes 8388624 | tf_op jit(solution)/shard_map/psum | solution.py:307
  865.0 82.1 %all-reduce.28 = (f32[4096]{0:T(1024)S(1)}, f32[4096]{0:T(1024)S(1)}, f32[1024]{0:T(1024)S(1)}, f32[1024]{0:T(1024)S(1)}, f32[1024]{0:T(1024)S(1)}, /*index=5*/f...) all-reduce(f32[4096]{0:T(1024)S(1)} %copy-done.97, ...), channel_id=5, replica_groups=mesh['batch'=16,'stream'=2] {'batch'}, use_global_device_ids=true, to_apply=%region_54.55.clone | all-reduce | flops 14336 | bytes 114688
  949.8 253.5 %reduce-scatter.7.cloned.1.call-done = f32[256,1024]{1,0:T(8,128)} async-done(((f32[4096,1024]{1,0:T(8,128)}), f32[256,1024]{1,0:T(8,128)}) %reduce-scatter.7.cloned.1.call-update) | async-done | bytes 1048592 | tf_op jit(solution)/shard_map/reduce_scatter | solution.py:354
  1203.3 354.2 %reduce-scatter.5.cloned.1.call-done = f32[256,1024]{1,0:T(8,128)} async-done(((f32[4096,1024]{1,0:T(8,128)}), f32[256,1024]{1,0:T(8,128)}) %reduce-scatter.5.cloned.1.call-update) | async-done | bytes 1048592 | tf_op jit(solution)/shard_map/reduce_scatter | solution.py:354
  1560.6 187.6 %reduce-scatter.11.cloned.1.call-done = f32[128,1024]{1,0:T(8,128)} async-done(((f32[4096,1024]{1,0:T(8,128)}), f32[128,1024]{1,0:T(8,128)}) %reduce-scatter.11.cloned.1.call-update) | async-done | bytes 524304 | tf_op jit(solution)/shard_map/reduce_scatter | solution.py:365
  1748.2 186.9 %reduce-scatter.9.cloned.1.call-done = f32[128,1024]{1,0:T(8,128)} async-done(((f32[4096,1024]{1,0:T(8,128)}), f32[128,1024]{1,0:T(8,128)}) %reduce-scatter.9.cloned.1.call-update) | async-done | bytes 524304 | tf_op jit(solution)/shard_map/reduce_scatter | solution.py:365
  (445 shorter events, 590.0 us)
Async XLA Ops:
  7.2 188.1 %all-reduce.34.cloned.1.call-start = ((), (), s32[]{:S(2)}) async-start(), calls=%async_computation.4 | async-start | bytes 8388608 | tf_op jit(solution)/shard_map/psum | solution.py:307
  7.2 24.8 %copy-start.102 = (pred[64]{0:T(512)(128)(4,1)}, pred[64]{0:T(512)(128)(4,1)S(1)}, u32[]{:S(2)}) copy-start(pred[64]{0:T(512)(128)(4,1)S(1)} %iota_compare_fusion.2) | copy-start | bytes 196
  7.3 24.8 %copy-start.104 = (f32[64]{0:T(128)}, f32[64]{0:T(128)S(1)}, u32[]{:S(2)}) copy-start(f32[64]{0:T(128)S(1)} %add_multiply_fusion) | copy-start | bytes 772
  10.0 23.6 %copy-start.71 = (f32[1024]{0:T(1024)}, f32[1024]{0:T(1024)S(1)}, u32[]{:S(2)}) copy-start(f32[1024]{0:T(1024)S(1)} %broadcast_multiply_fusion.5) | copy-start | bytes 12292
  12.3 21.3 %copy-start.82 = (f32[1024]{0:T(1024)}, f32[1024]{0:T(1024)S(1)}, u32[]{:S(2)}) copy-start(f32[1024]{0:T(1024)S(1)} %fusion.403) | copy-start | bytes 12292
  13.7 19.9 %copy-start.75 = (f32[1,1024]{1,0:T(1,128)}, f32[1,1024]{1,0:T(1,128)S(1)}, u32[]{:S(2)}) copy-start(f32[1,1024]{1,0:T(1,128)S(1)} %get-tuple-element.544) | copy-start | bytes 12292
  163.9 31.3 %copy-start.5 = (bf16[1024,1024]{1,0:T(8,128)(2,1)S(1)}, bf16[1024,1024]{1,0:T(8,128)(2,1)}, u32[]{:S(2)}) copy-start(bf16[1024,1024]{1,0:T(8,128)(2,1)} %param.42) | copy-start | bytes 6291460
  164.0 423.3 %all-reduce.36.cloned.1.call-start = ((), (), s32[]{:S(2)}) async-start(), calls=%async_computation.5 | async-start | bytes 8388608 | tf_op jit(solution)/shard_map/psum | solution.py:340
  167.7 32.3 %copy-start.80 = (f32[1,1024]{1,0:T(1,128)S(1)}, f32[1,1024]{1,0:T(1,128)}, u32[]{:S(2)}) copy-start(f32[1,1024]{1,0:T(1,128)} %get-tuple-element.543) | copy-start | bytes 12292
  167.7 32.3 %copy-start.93 = (f32[1,1024]{1,0:T(1,128)S(1)}, f32[1,1024]{1,0:T(1,128)}, u32[]{:S(2)}) copy-start(f32[1,1024]{1,0:T(1,128)} %get-tuple-element.545) | copy-start | bytes 12292
  202.0 134.1 %copy-start.18 = (bf16[1024,1024]{1,0:T(8,128)(2,1)S(1)}, bf16[1024,1024]{1,0:T(8,128)(2,1)}, u32[]{:S(2)}) copy-start(bf16[1024,1024]{1,0:T(8,128)(2,1)} %param.43) | copy-start | bytes 6291460
  408.2 34.2 %copy-start.39 = (bf16[1024,16,64]{0,2,1:T(8,128)(2,1)}, bf16[1024,16,64]{0,2,1:T(8,128)(2,1)S(1)}, u32[]{:S(2)}) copy-start(bf16[1024,16,64]{0,2,1:T(8,128)(2,1)S(1)} %get-tuple-element.493) | copy-start | bytes 6291460 | tf_op jit(solution)/shard_map/cond
  413.6 28.8 %copy-start.41 = (bf16[1024,16,64]{0,2,1:T(8,128)(2,1)}, bf16[1024,16,64]{0,2,1:T(8,128)(2,1)S(1)}, u32[]{:S(2)}) copy-start(bf16[1024,16,64]{0,2,1:T(8,128)(2,1)S(1)} %get-tuple-element.491) | copy-start | bytes 6291460 | tf_op jit(solution)/shard_map/cond
  557.5 293.4 %all-reduce.38.cloned.1.call-start = ((), (), s32[]{:S(2)}) async-start(), calls=%async_computation.10 | async-start | bytes 16777216 | tf_op jit(solution)/shard_map/psum | solution.py:307
  557.5 29.7 %copy-start.74 = (f32[1024]{0:T(1024)S(1)}, f32[1024]{0:T(1024)}, u32[]{:S(2)}) copy-start(f32[1024]{0:T(1024)} %copy-done.73) | copy-start | bytes 12292
  557.5 29.7 %copy-start.79 = (f32[1024]{0:T(1024)S(1)}, f32[1024]{0:T(1024)}, u32[]{:S(2)}) copy-start(f32[1024]{0:T(1024)} %copy-done.78) | copy-start | bytes 12292
  557.6 29.7 %copy-start.81 = (f32[1,1024]{1,0:T(1,128)S(1)}, f32[1,1024]{1,0:T(1,128)}, u32[]{:S(2)}) copy-start(f32[1,1024]{1,0:T(1,128)} %get-tuple-element.543) | copy-start | bytes 12292
  564.4 28.1 %copy-start.89 = (f32[1024]{0:T(1024)S(1)}, f32[1024]{0:T(1024)}, u32[]{:S(2)}) copy-start(f32[1024]{0:T(1024)} %copy-done.88) | copy-start | bytes 12292
  662.8 33.8 %copy-start.40 = (bf16[1024,16,64]{0,2,1:T(8,128)(2,1)}, bf16[1024,16,64]{0,2,1:T(8,128)(2,1)S(1)}, u32[]{:S(2)}) copy-start(bf16[1024,16,64]{0,2,1:T(8,128)(2,1)S(1)} %get-tuple-element.525) | copy-start | bytes 6291460 | tf_op jit(solution)/shard_map/cond
  668.1 28.4 %copy-start.43 = (bf16[1024,16,64]{0,2,1:T(8,128)(2,1)}, bf16[1024,16,64]{0,2,1:T(8,128)(2,1)S(1)}, u32[]{:S(2)}) copy-start(bf16[1024,16,64]{0,2,1:T(8,128)(2,1)S(1)} %get-tuple-element.523) | copy-start | bytes 6291460 | tf_op jit(solution)/shard_map/cond
  810.7 392.7 %reduce-scatter.7.cloned.1.call-start = ((), (), s32[]{:S(2)}) async-start(), calls=%async_computation.7 | async-start | bytes 17825792 | tf_op jit(solution)/shard_map/reduce_scatter | solution.py:354
  811.2 746.2 %reduce-scatter.5.cloned.1.call-start = ((), (), s32[]{:S(2)}) async-start(), calls=%async_computation.6 | async-start | bytes 17825792 | tf_op jit(solution)/shard_map/reduce_scatter | solution.py:354
  811.8 936.4 %reduce-scatter.11.cloned.1.call-start = ((), (), s32[]{:S(2)}) async-start(), calls=%async_computation.9 | async-start | bytes 17301504 | tf_op jit(solution)/shard_map/reduce_scatter | solution.py:365
  812.4 1122.7 %reduce-scatter.9.cloned.1.call-start = ((), (), s32[]{:S(2)}) async-start(), calls=%async_computation.8 | async-start | bytes 17301504 | tf_op jit(solution)/shard_map/reduce_scatter | solution.py:365
  (96 other events, 542.7 us)
Sparse Core Ops, SparseCore 0:
  164.1 31.1 all-reduce.33
  557.6 29.5 all-reduce.35
  810.8 40.0 all-reduce.37
  853.1 350.2 reduce-scatter.6
  1205.5 351.9 reduce-scatter.4
  1559.6 188.5 reduce-scatter.10
  1750.5 184.5 reduce-scatter.8
where the time goes:
time: 1950 us; the launch traced here: 1940 us
  waiting for transfers between devices  1070 us (55%)
  matrix products  380 us (19%)
  local copies, waits for them, and re-layouts  209 us (11%)
  other arithmetic  155 us (8%)
  blocking collectives  82.1 us (4%)
  loops' own time  30.8 us (2%)
    reduce_scatter x2, waiting for transfers between devices, shards(): lax.psum_scatter(grad_block_weight, 'batch', scatter_dimension=0, tiled=T...  608 us
    reduce_scatter x2, waiting for transfers between devices, shards(): lax.psum_scatter(grad_up, ('batch', 'stream'), scatter_dimension=0, tiled...  375 us
    unnamed x1, blocking collectives  82.1 us
    psum x2, waiting for transfers between devices, shards(): residual = residual + lax.psum(own_branch, 'stream')  63.4 us
    another operation x4, local copies, waits for them, and re-layouts  51 us
  transfers between devices with their start and end apart: 7, of which 7 were waited for; matrix products, arithmetic and copies ran while one was open for 2% of the time, Pallas kernels for 0%

commit v1 on v0

v1 whole, which is shorter than its diff:
```python
import functools
import math

import jax
import jax.numpy as jnp
import numpy as np
from jax import lax
from jax.experimental import pallas as pl
from jax.experimental.pallas import tpu as pltpu
from jax.sharding import PartitionSpec as P

HEADS = 16
DH = 64
ROT = 16
FEAT = 64
LAYERS = 2
EPSILON = 1e-05
HIGH = lax.Precision.HIGHEST
F32 = jnp.float32
BF16 = jnp.bfloat16
WIDE = 256
PAIR = 128
QUADS = HEADS * DH // WIDE
PAIRS = HEADS * DH // PAIR
ROWS = 256
VMEM_LIMIT = 56 * 1024 * 1024


def params():
    return pltpu.CompilerParams(vmem_limit_bytes=VMEM_LIMIT)


def whole(shape):
    zeros = (0,) * len(shape)
    return pl.BlockSpec(shape, lambda *_: zeros, pipeline_mode=pl.Buffered(1))


def dot_nn(left, right):
    return lax.dot_general(left, right, (((1,), (0,)), ((), ())), preferred_element_type=F32)


def dot_nt(left, right):
    return lax.dot_general(left, right, (((1,), (1,)), ((), ())), preferred_element_type=F32)


def split(values):
    upper = values.astype(BF16)
    return upper, (values - upper.astype(F32)).astype(BF16)


def lane_index(rows, lanes):
    return lax.broadcasted_iota(jnp.int32, (rows, lanes), 1)


def row_index(rows, lanes):
    return lax.broadcasted_iota(jnp.int32, (rows, lanes), 0)


def cosine_block():
    samples = np.arange(DH, dtype=np.float64)
    angles = math.pi * (samples[None, :] + 0.5) * samples[:, None] / DH
    table = np.cos(angles) * math.sqrt(2.0 / DH)
    table[0] *= math.sqrt(0.5)
    return np.kron(np.eye(WIDE // DH), table.T * DH ** (-0.25)).astype(np.float32)


def rotary_rows(length):
    position = np.arange(length, dtype=np.float32)
    inverse = (10000.0 ** (-np.arange(0, ROT, 2, dtype=np.float32) / ROT)).astype(np.float32)
    angles = position[:, None] * inverse[None, :]
    cosine, sine = np.cos(angles), np.sin(angles)
    rest = DH - ROT
    cosine_head = np.concatenate([cosine, cosine, np.ones((length, rest))], 1)
    sine_head = np.concatenate([-sine, sine, np.zeros((length, rest))], 1)
    repeat = PAIR // DH
    return (
        np.tile(cosine_head, (1, repeat)).astype(np.float32),
        np.tile(sine_head, (1, repeat)).astype(np.float32),
    )


def tables_kernel(seeds_ref, cosine_ref, upper_ref, lower_ref, weight_ref):
    feature = lane_index(WIDE, WIDE)
    lattice = (feature % FEAT) * seeds_ref[0] % FEAT
    prob = (lattice.astype(F32) + 0.5) / FEAT
    radius = jnp.sqrt(-2.0 * jnp.log(jnp.minimum(prob, 1.0 - prob)))
    above = 2.515517 + 0.802853 * radius + 0.010328 * radius * radius
    below = (
        1.0 + 1.432788 * radius + 0.189269 * radius * radius + 0.001308 * radius * radius * radius
    )
    magnitude = radius - above / below
    same_head = row_index(WIDE, WIDE) // DH == feature // FEAT
    omega = jnp.where(same_head, jnp.where(prob > 0.5, magnitude, -magnitude), 0.0)
    project = jnp.dot(cosine_ref[...], omega, precision=HIGH, preferred_element_type=F32)
    upper_ref[0, 0], lower_ref[0, 0] = split(project)
    grown = jnp.exp(-0.5 / DH * jnp.sum(omega * omega, axis=0, keepdims=True))
    total = jnp.dot(
        jnp.broadcast_to(grown, (8, WIDE)),
        same_head.astype(F32),
        precision=HIGH,
        preferred_element_type=F32,
    )
    weight_ref[0, 0] = FEAT * grown / total[:1]


def feature_tables(seeds):
    return pl.pallas_call(
        tables_kernel,
        grid=(LAYERS, QUADS),
        in_specs=[
            pl.BlockSpec((1, WIDE, 1), lambda l, g: (l, g, 0)),
            whole((WIDE, WIDE)),
        ],
        out_specs=[
            pl.BlockSpec((1, 1, WIDE, WIDE), lambda l, g: (l, g, 0, 0)),
            pl.BlockSpec((1, 1, WIDE, WIDE), lambda l, g: (l, g, 0, 0)),
            pl.BlockSpec((1, 1, 1, WIDE), lambda l, g: (l, g, 0, 0)),
        ],
        out_shape=[
            jax.ShapeDtypeStruct((LAYERS, QUADS, WIDE, WIDE), BF16),
            jax.ShapeDtypeStruct((LAYERS, QUADS, WIDE, WIDE), BF16),
            jax.ShapeDtypeStruct((LAYERS, QUADS, 1, WIDE), F32),
        ],
        compiler_params=params(),
        name="feature_tables",
    )(seeds.reshape(LAYERS, HEADS * DH, 1), jnp.asarray(cosine_block()))


def turn(values, cosine, sine):
    lanes = values.shape[1]
    half = ROT // 2
    lane = lane_index(*values.shape) % DH
    swapped = jnp.where(
        lane < half, pltpu.roll(values, lanes - half, 1), pltpu.roll(values, half, 1)
    )
    return values * cosine + swapped * sine


def turn_back(values, cosine, sine):
    lanes = values.shape[1]
    half = ROT // 2
    lane = lane_index(*values.shape) % DH
    turned = values * sine
    swapped = jnp.where(
        lane < half, pltpu.roll(turned, lanes - half, 1), pltpu.roll(turned, half, 1)
    )
    return values * cosine + jnp.where(lane < ROT, swapped, 0.0)


def normalized(x_ref_rows, gain, offset):
    average = jnp.mean(x_ref_rows, -1, keepdims=True)
    centered = x_ref_rows - average
    variance = jnp.mean(centered * centered, -1, keepdims=True)
    return centered * lax.rsqrt(variance + EPSILON) * gain + offset


def start_layer(stream, x_ref, h_ref, gain_ref, offset_ref):
    length = h_ref.shape[0]
    step = min(128, length)

    @pl.loop(0, length // step)
    def _(index):
        rows = pl.ds(pl.multiple_of(index * step, step), step)
        values = stream[0][rows].astype(F32)
        if len(stream) > 1:
            values = values + (stream[1][rows] + stream[2][rows])
            x_ref[rows] = values
        h_ref[rows] = normalized(
            values, gain_ref[...].astype(F32), offset_ref[...].astype(F32)
        ).astype(BF16)


def gelu_parts(units):
    grown = jnp.exp(-0.5 * units * units)
    inverse = 1.0 / (1.0 + (0.3275911 * math.sqrt(0.5)) * jnp.abs(units))
    series = 0.5 * 1.061405429
    for factor in (-1.453152027, 1.421413741, -0.284496736, 0.254829592):
        series = series * inverse + 0.5 * factor
    tail = series * inverse * grown
    below = jnp.where(units >= 0.0, 1.0 - tail, tail)
    return below, grown * (1.0 / math.sqrt(2.0 * math.pi))


FF_BLOCK = 512


def mlp_forward_kernel(count, *refs):
    stream, refs = refs[:count], refs[count:]
    gain_ref, offset_ref, up_ref, bias_ref, down_ref, down_bias_ref = refs[:6]
    refs = refs[6:]
    x_ref = None
    if count > 1:
        x_ref, refs = refs[0], refs[1:]
    part_ref, h_ref, act_ref, slope_ref = refs
    step = pl.program_id(0)

    @pl.when(step == 0)
    def _():
        start_layer(stream, x_ref, h_ref, gain_ref, offset_ref)
        part_ref[...] = jnp.broadcast_to(down_bias_ref[...].astype(F32), part_ref.shape)

    for first in range(0, h_ref.shape[0], ROWS):
        rows = slice(first, first + ROWS)
        units = dot_nt(h_ref[rows], up_ref[0]) + bias_ref[0]
        below, density = gelu_parts(units)
        active = (units * below).astype(BF16)
        act_ref[0, rows] = active
        slope_ref[0, rows] = (below + units * density).astype(BF16)
        part_ref[rows] += dot_nn(active, down_ref[0, 0])


def plane_block(length, lanes):
    per_plane = 1024 // lanes
    return pl.BlockSpec((1, length, lanes), lambda j: (j // per_plane, 0, j % per_plane))


def mlp_forward(layer, stream, gain, offset, up, biases, down_weight, down_bias):
    length, width = stream[0].shape
    hidden = up.shape[1]
    blocks = hidden // FF_BLOCK
    state = jax.ShapeDtypeStruct((4, length, width), BF16)
    full = jax.ShapeDtypeStruct((length, width), F32)
    out_shape = [full, jax.ShapeDtypeStruct((length, width), BF16), state, state]
    out_specs = [whole((length, width)), whole((length, width))]
    out_specs += [plane_block(length, FF_BLOCK)] * 2
    if len(stream) > 1:
        out_shape, out_specs = [full] + out_shape, [whole((length, width))] + out_specs
    return pl.pallas_call(
        functools.partial(mlp_forward_kernel, len(stream)),
        grid=(blocks,),
        in_specs=[whole((length, width))] * len(stream)
        + [
            whole((1, width)),
            whole((1, width)),
            pl.BlockSpec((1, FF_BLOCK, width), lambda j: (layer, j, 0)),
            pl.BlockSpec((1, 1, FF_BLOCK), lambda j: (j, 0, 0)),
            pl.BlockSpec((1, 1, FF_BLOCK, width), lambda j: (0, layer, j, 0)),
            whole((1, width)),
        ],
        out_specs=out_specs,
        out_shape=out_shape,
        compiler_params=params(),
        name="mlp_forward",
    )(*stream, gain, offset, up, biases.reshape(blocks, 1, FF_BLOCK), down_weight, down_bias)


def mlp_backward_kernel(
    grad_ref, h_ref, act_ref, slope_ref, down_ref, up_ref,
    part_ref, weight_ref, near_ref, far_ref, bias_ref, grad_t, h_t,
):
    step = pl.program_id(0)

    @pl.when(step == 0)
    def _():
        grad_t[...] = grad_ref[...].T
        h_t[...] = h_ref[...].T
        part_ref[...] = jnp.zeros_like(part_ref)

    length = h_ref.shape[0]
    bias = jnp.zeros((1, FF_BLOCK), F32)
    pieces = []
    for first in range(0, length, ROWS):
        rows = slice(first, first + ROWS)
        grad_act = dot_nt(grad_ref[rows], down_ref[0, 0])
        grad_unit = (grad_act * slope_ref[0, rows].astype(F32)).astype(BF16)
        bias += jnp.sum(grad_unit.astype(F32), axis=0, keepdims=True)
        pieces.append(grad_unit)
        part_ref[rows] += dot_nn(grad_unit, up_ref[0])
    bias_ref[0] = bias
    units = jnp.concatenate(pieces, axis=0)
    half = near_ref.shape[2]
    for first in range(0, h_t.shape[0], ROWS):
        rows = slice(first, first + ROWS)
        for block in range(FF_BLOCK // WIDE):
            lanes = slice(block * WIDE, (block + 1) * WIDE)
            weight_ref[block, rows] = dot_nn(grad_t[rows], act_ref[0, :, lanes])
            up_grad = dot_nn(h_t[rows], units[:, lanes])
            near_ref[block, rows] = up_grad[:, :half]
            far_ref[block, rows] = up_grad[:, half:]


def mlp_backward(layer, grad, h, act, slope, down_weight, up):
    length, width = h.shape
    hidden = up.shape[1]
    blocks = hidden // FF_BLOCK
    per = FF_BLOCK // WIDE
    halves = jax.ShapeDtypeStruct((hidden // WIDE, width, WIDE // 2), F32)
    return pl.pallas_call(
        mlp_backward_kernel,
        grid=(blocks,),
        in_specs=[
            whole((length, width)),
            whole((length, width)),
            plane_block(length, FF_BLOCK),
            plane_block(length, FF_BLOCK),
            pl.BlockSpec((1, 1, FF_BLOCK, width), lambda j: (0, layer, j, 0)),
            pl.BlockSpec((1, FF_BLOCK, width), lambda j: (layer, j, 0)),
        ],
        out_specs=[
            whole((length, width)),
            pl.BlockSpec((per, width, WIDE), lambda j: (j, 0, 0)),
            pl.BlockSpec((per, width, WIDE // 2), lambda j: (j, 0, 0)),
            pl.BlockSpec((per, width, WIDE // 2), lambda j: (j, 0, 0)),
            pl.BlockSpec((1, 1, FF_BLOCK), lambda j: (j, 0, 0)),
        ],
        out_shape=[
            jax.ShapeDtypeStruct((length, width), F32),
            jax.ShapeDtypeStruct((hidden // WIDE, width, WIDE), F32),
            halves,
            halves,
            jax.ShapeDtypeStruct((blocks, 1, FF_BLOCK), F32),
        ],
        scratch_shapes=[pltpu.VMEM((width, length), BF16), pltpu.VMEM((width, length), BF16)],
        compiler_params=params(),
        name="mlp_backward",
    )(grad, h, act, slope, down_weight, up)


def head_sums(values, ones):
    upper, lower = split(values)
    return dot_nn(upper, ones) + dot_nn(lower, ones)


def same_head_ones():
    same = row_index(WIDE, WIDE) // DH == lane_index(WIDE, WIDE) // DH
    return jnp.where(same, 1.0, 0.0).astype(BF16)


def project_kernel(count, *refs):
    stream, refs = refs[:count], refs[count:]
    gain_ref, offset_ref, weight_ref, bias_ref = refs[:4]
    upper_ref, lower_ref, scale_ref, cosine_ref, sine_ref = refs[4:9]
    refs = refs[9:]
    x_ref = None
    if count > 1:
        x_ref, refs = refs[0], refs[1:]
    h_ref, state_ref, keys = refs
    step = pl.program_id(0)
    kind, group = step // QUADS, step % QUADS
    length = h_ref.shape[0]

    @pl.when(step == 0)
    def _():
        start_layer(stream, x_ref, h_ref, gain_ref, offset_ref)

    def features(values, rows):
        cosine = jnp.concatenate([cosine_ref[rows]] * (WIDE // PAIR), axis=1)
        sine = jnp.concatenate([sine_ref[rows]] * (WIDE // PAIR), axis=1)
        upper, lower = split(turn(values, cosine, sine))
        table_up, table_low = upper_ref[0, 0], lower_ref[0, 0]
        return dot_nn(upper, table_up) + (dot_nn(lower, table_up) + dot_nn(upper, table_low))

    @pl.when(kind == 0)
    def _():
        for first in range(0, length, ROWS):
            rows = slice(first, first + ROWS)
            values = dot_nt(h_ref[rows], weight_ref[0, 0]) + bias_ref[0]
            state_ref[0, rows] = jnp.exp(features(values, rows)).astype(BF16)

    @pl.when(kind == 1)
    def _():
        ones = same_head_ones()
        for first in range(0, length, ROWS):
            rows = slice(first, first + ROWS)
            values = dot_nt(h_ref[rows], weight_ref[0, 0]) + bias_ref[0]
            keys[group, rows] = values.astype(BF16)
            squares = head_sums(values * values, ones)
            logs = features(values, rows) - (0.5 / math.sqrt(DH)) * squares
            state_ref[0, rows] = (scale_ref[0, 0] * jnp.exp(logs)).astype(BF16)

    @pl.when(kind == 2)
    def _():
        state_ref[0] = keys[group]

    @pl.when(kind == 3)
    def _():
        for first in range(0, length, ROWS):
            rows = slice(first, first + ROWS)
            values = dot_nt(h_ref[rows], weight_ref[0, 0]) + bias_ref[0]
            state_ref[0, rows] = values.astype(BF16)


def project_forward(layer, stream, gain, offset, weight, biases, tables, rotary):
    length, width = stream[0].shape
    full = jax.ShapeDtypeStruct((length, width), F32)
    state = jax.ShapeDtypeStruct((4, length, width), BF16)
    out_shape = [jax.ShapeDtypeStruct((length, width), BF16), state]
    out_specs = [whole((length, width)), plane_block(length, WIDE)]
    if len(stream) > 1:
        out_shape, out_specs = [full] + out_shape, [whole((length, width))] + out_specs

    def source(j):
        return jnp.where(j < 2 * QUADS, j, jnp.maximum(j - QUADS, 2 * QUADS - 1))

    def table(j):
        return jnp.where(j < 2 * QUADS, j % QUADS, QUADS - 1)

    return pl.pallas_call(
        functools.partial(project_kernel, len(stream)),
        grid=(4 * QUADS,),
        in_specs=[whole((length, width))] * len(stream)
        + [
            whole((1, width)),
            whole((1, width)),
            pl.BlockSpec((1, 1, WIDE, width), lambda j: (0, layer, source(j), 0)),
            pl.BlockSpec((1, 1, WIDE), lambda j: (source(j), 0, 0)),
            pl.BlockSpec((1, 1, WIDE, WIDE), lambda j: (layer, table(j), 0, 0)),
            pl.BlockSpec((1, 1, WIDE, WIDE), lambda j: (layer, table(j), 0, 0)),
            pl.BlockSpec((1, 1, 1, WIDE), lambda j: (layer, table(j), 0, 0)),
            whole((length, PAIR)),
            whole((length, PAIR)),
        ],
        out_specs=out_specs,
        out_shape=out_shape,
        scratch_shapes=[pltpu.VMEM((QUADS, length, WIDE), BF16)],
        compiler_params=params(),
        name="project_forward",
    )(*stream, gain, offset, weight, biases.reshape(-1, 1, WIDE), *tables, *rotary)


def write_mask(starts_ref, mask_ref, flipped):
    length = mask_ref.shape[0]
    keys = lane_index(1, length)
    documents = sum((starts_ref[0, i] <= keys).astype(jnp.int32) for i in range(starts_ref.shape[1]))
    for first in range(0, length, ROWS):
        own = row_index(ROWS, 1) + first
        document = sum(
            (starts_ref[0, i] <= own).astype(jnp.int32) for i in range(starts_ref.shape[1])
        )
        order = (own <= keys) if flipped else (keys <= own)
        seen = (document == documents) & order
        mask_ref[first : first + ROWS] = jnp.where(seen, 1.0, 0.0).astype(BF16)


def attend_kernel(starts_ref, state_ref, out_ref, mask_ref):
    @pl.when(pl.program_id(0) == 0)
    def _():
        write_mask(starts_ref, mask_ref, False)

    length = mask_ref.shape[0]
    zero = jnp.zeros((), BF16)
    one = jnp.ones((), BF16)
    for first in range(0, length, ROWS):
        rows = slice(first, first + ROWS)
        finish = first + ROWS
        left = lane_index(finish, PAIR) < DH
        seen = mask_ref[rows, :finish] > zero
        sums = []
        for own in (left, ~left):
            keys = jnp.where(own, state_ref[1, :finish], zero)
            scores = dot_nt(state_ref[0, rows], keys).astype(BF16)
            scores = jnp.where(seen, scores, zero)
            sums.append(dot_nn(scores, jnp.where(own, state_ref[3, :finish], one)))
        left = lane_index(ROWS, PAIR) < DH
        numer = jnp.where(left, sums[0], sums[1])
        denom = jnp.where(left, pltpu.roll(sums[0], DH, 1), pltpu.roll(sums[1], DH, 1))
        inverse = 1.0 / denom
        out_ref[0, rows] = (numer * inverse).astype(BF16)
        out_ref[1, rows], out_ref[2, rows] = split(inverse)


def attend_forward(starts, state):
    _, length, width = state.shape
    block = pl.BlockSpec((4, length, PAIR), lambda p: (0, 0, p))
    return pl.pallas_call(
        attend_kernel,
        grid=(PAIRS,),
        in_specs=[pl.BlockSpec(memory_space=pltpu.SMEM), block],
        out_specs=block,
        out_shape=jax.ShapeDtypeStruct(state.shape, BF16),
        scratch_shapes=[pltpu.VMEM((length, length), BF16)],
        compiler_params=params(),
        name="attend_forward",
    )(starts, state)


def mix_kernel(mixed_ref, weight_ref, bias_ref, part_ref):
    part_ref[...] = dot_nn(mixed_ref[0], weight_ref[0, 0]) + bias_ref[0]


def mix_forward(layer, mixed, weight, biases):
    _, length, width = mixed.shape
    return pl.pallas_call(
        mix_kernel,
        grid=(QUADS,),
        in_specs=[
            pl.BlockSpec((1, length, width), lambda j: (0, 0, 0), pipeline_mode=pl.Buffered(1)),
            pl.BlockSpec((1, 1, width, WIDE), lambda j: (0, layer, 3, j)),
            pl.BlockSpec((1, 1, WIDE), lambda j: (3 * QUADS + j, 0, 0)),
        ],
        out_specs=pl.BlockSpec((length, WIDE), lambda j: (0, j)),
        out_shape=jax.ShapeDtypeStruct((length, width), F32),
        compiler_params=params(),
        name="mix_forward",
    )(mixed, weight, biases.reshape(-1, 1, WIDE))


def mix_backward_kernel(grad_ref, weight_ref, mixed_ref, out_ref):
    row, lane = row_index(WIDE, WIDE), lane_index(WIDE, WIDE)
    partner = (row // PAIR == lane // PAIR) & (row // DH != lane // DH)
    ones = jnp.where(partner, 1.0, 0.0).astype(BF16)
    length = grad_ref.shape[0]
    for first in range(0, length, ROWS):
        rows = slice(first, first + ROWS)
        grad = dot_nt(grad_ref[rows], weight_ref[0, 0]).astype(BF16).astype(F32)
        inverse = mixed_ref[1, rows].astype(F32) + mixed_ref[2, rows].astype(F32)
        scaled = grad * inverse
        upper, lower = split(-head_sums(scaled * mixed_ref[0, rows].astype(F32), ones))
        numer = scaled.astype(BF16)
        lane = lane_index(ROWS, WIDE)
        spare = jnp.where(
            lane % DH == 0, upper, jnp.where(lane % DH == 1, lower, jnp.zeros((), BF16))
        )
        left = lane % PAIR < DH
        out_ref[0, rows] = jnp.where(left, numer, spare)
        out_ref[1, rows] = jnp.where(left, spare, numer)


def mix_backward(layer, grad, weight, mixed):
    _, length, width = mixed.shape
    return pl.pallas_call(
        mix_backward_kernel,
        grid=(QUADS,),
        in_specs=[
            whole((length, width)),
            pl.BlockSpec((1, 1, WIDE, width), lambda j: (0, layer, 3 * QUADS + j, 0)),
            pl.BlockSpec((4, length, WIDE), lambda j: (0, 0, j)),
        ],
        out_specs=pl.BlockSpec((2, length, WIDE), lambda j: (0, 0, j)),
        out_shape=jax.ShapeDtypeStruct((2, length, width), BF16),
        compiler_params=params(),
        name="mix_backward",
    )(grad, weight, mixed)


def attend_backward_kernel(starts_ref, state_ref, numer_ref, out_ref, mask_ref, query_t):
    @pl.when(pl.program_id(0) == 0)
    def _():
        write_mask(starts_ref, mask_ref, True)

    length = mask_ref.shape[0]
    zero = jnp.zeros((), BF16)
    one = jnp.ones((), BF16)
    query_t[...] = jnp.zeros_like(query_t)
    for first in range(0, length, ROWS):
        rows = slice(first, first + ROWS)
        seen = mask_ref[rows, first:] > zero
        lane = lane_index(ROWS, PAIR)
        left = lane < DH
        spare = jnp.where(lane % DH < 2, one, zero)
        keys, values = state_ref[1, rows], state_ref[3, rows]
        queries = state_ref[0, first:]
        numer = jnp.where(lane_index(length - first, PAIR) < DH, numer_ref[0, first:], numer_ref[1, first:])
        grads = []
        for head, own in enumerate((left, ~left)):
            own_keys = jnp.where(own, keys, zero)
            scores = dot_nt(own_keys, queries).astype(BF16)
            scores = jnp.where(seen, scores, zero)
            grad_value = dot_nn(scores, numer)
            grad_scores = dot_nt(jnp.where(own, values, spare), numer_ref[head, first:]).astype(BF16)
            grad_scores = jnp.where(seen, grad_scores, zero)
            grad_key = dot_nn(grad_scores, queries)
            query_t[head, :, first:] += dot_nn(own_keys.T[head * DH : (head + 1) * DH], grad_scores)
            grads.append((grad_value, grad_key))
        out_ref[2, rows] = jnp.where(left, grads[0][0], grads[1][0]).astype(BF16)
        grad_key = jnp.where(left, grads[0][1], grads[1][1])
        out_ref[1, rows] = (grad_key * keys.astype(F32)).astype(BF16)
    for first in range(0, length, ROWS):
        rows = slice(first, first + ROWS)
        grad_query = jnp.concatenate([query_t[0, :, rows], query_t[1, :, rows]], axis=0).T
        out_ref[0, rows] = (grad_query * state_ref[0, rows].astype(F32)).astype(BF16)


def attend_backward(starts, state, numer):
    _, length, width = state.shape
    return pl.pallas_call(
        attend_backward_kernel,
        grid=(PAIRS,),
        in_specs=[
            pl.BlockSpec(memory_space=pltpu.SMEM),
            pl.BlockSpec((4, length, PAIR), lambda p: (0, 0, p)),
            pl.BlockSpec((2, length, PAIR), lambda p: (0, 0, p)),
        ],
        out_specs=pl.BlockSpec((3, length, PAIR), lambda p: (0, 0, p)),
        out_shape=jax.ShapeDtypeStruct((3, length, width), BF16),
        scratch_shapes=[
            pltpu.VMEM((length, length), BF16),
            pltpu.VMEM((2, DH, length), F32),
        ],
        compiler_params=params(),
        name="attend_backward",
    )(starts, state, numer)


def project_backward_kernel(
    grad_ref, h_ref, mixed_ref, feat_ref, keys_ref, table_ref, cosine_ref, sine_ref, weight_ref,
    part_ref, out_ref, bias_ref, grad_t, h_t, flow,
):
    step = pl.program_id(0)
    kind, length = step // QUADS, h_ref.shape[0]

    @pl.when(step == 0)
    def _():
        grad_t[...] = grad_ref[...].T
        h_t[...] = h_ref[...].T
        part_ref[...] = jnp.zeros_like(part_ref)

    def project_back(rows):
        cosine = jnp.concatenate([cosine_ref[rows]] * (WIDE // PAIR), axis=1)
        sine = jnp.concatenate([sine_ref[rows]] * (WIDE // PAIR), axis=1)
        return turn_back(dot_nt(feat_ref[0, rows], table_ref[0, 0]), cosine, sine)

    @pl.when(kind == 0)
    def _():
        flow[...] = mixed_ref[0]
        bias_ref[0] = jnp.sum(feat_ref[0, :1].astype(F32), axis=0, keepdims=True)

    @pl.when(kind == 1)
    def _():
        for first in range(0, length, ROWS):
            rows = slice(first, first + ROWS)
            flow[rows] = project_back(rows).astype(BF16)

    @pl.when(kind == 2)
    def _():
        ones = same_head_ones()
        for first in range(0, length, ROWS):
            rows = slice(first, first + ROWS)
            shrink = dot_nn(feat_ref[0, rows], ones) * (1.0 / math.sqrt(DH))
            flow[rows] = (project_back(rows) - keys_ref[0, rows].astype(F32) * shrink).astype(BF16)

    @pl.when(kind == 3)
    def _():
        flow[...] = feat_ref[0]

    @pl.when(kind > 0)
    def _():
        bias = jnp.zeros((1, WIDE), F32)
        for first in range(0, length, ROWS):
            rows = slice(first, first + ROWS)
            bias += jnp.sum(flow[rows].astype(F32), axis=0, keepdims=True)
            part_ref[rows] += dot_nn(flow[rows], weight_ref[0, 0])
            out_ref[0, rows] = dot_nn(h_t[rows], flow[...])
        bias_ref[0] = bias

    @pl.when(kind == 0)
    def _():
        for first in range(0, length, ROWS):
            rows = slice(first, first + ROWS)
            out_ref[0, rows] = dot_nn(grad_t[rows], flow[...])


def project_backward(layer, grad, h, mixed, feats, state, tables, rotary, weight):
    _, length, width = state.shape
    blocks = 4 * QUADS

    def at(j):
        return jnp.maximum(j - QUADS, 0)

    def target(j):
        return jnp.where(j < QUADS, 3 * QUADS + j, j - QUADS)

    return pl.pallas_call(
        project_backward_kernel,
        grid=(blocks,),
        in_specs=[
            whole((length, width)),
            whole((length, width)),
            pl.BlockSpec((1, length, WIDE), lambda j: (0, 0, jnp.minimum(j, QUADS - 1))),
            pl.BlockSpec((1, length, WIDE), lambda j: (at(j) // QUADS, 0, at(j) % QUADS)),
            pl.BlockSpec(
                (1, length, WIDE), lambda j: (2, 0, jnp.clip(j - 2 * QUADS, 0, QUADS - 1))
            ),
            pl.BlockSpec((1, 1, WIDE, WIDE), lambda j: (layer, at(j) % QUADS, 0, 0)),
            whole((length, PAIR)),
            whole((length, PAIR)),
            pl.BlockSpec((1, 1, WIDE, width), lambda j: (0, layer, at(j), 0)),
        ],
        out_specs=[
            whole((length, width)),
            pl.BlockSpec((1, width, WIDE), lambda j: (target(j), 0, 0)),
            pl.BlockSpec((1, 1, WIDE), lambda j: (target(j), 0, 0)),
        ],
        out_shape=[
            jax.ShapeDtypeStruct((length, width), F32),
            jax.ShapeDtypeStruct((blocks, width, WIDE), F32),
            jax.ShapeDtypeStruct((blocks, 1, WIDE), F32),
        ],
        scratch_shapes=[
            pltpu.VMEM((width, length), BF16),
            pltpu.VMEM((width, length), BF16),
            pltpu.VMEM((length, WIDE), BF16),
        ],
        compiler_params=params(),
        name="project_backward",
    )(grad, h, mixed, feats, state, tables[0], *rotary, weight)


def norm_backward_kernel(x_ref, own_ref, other_ref, grad_ref, gain_ref, out_ref, sums_ref):
    @pl.when(pl.program_id(0) == 0)
    def _():
        sums_ref[...] = jnp.zeros_like(sums_ref)

    values = x_ref[...].astype(F32)
    average = jnp.mean(values, -1, keepdims=True)
    centered = values - average
    variance = jnp.mean(centered * centered, -1, keepdims=True)
    inverse = lax.rsqrt(variance + EPSILON)
    unit = centered * inverse
    incoming = own_ref[...] + other_ref[...]
    grad_unit = incoming * gain_ref[...].astype(F32)
    first = jnp.mean(grad_unit, -1, keepdims=True)
    second = jnp.mean(grad_unit * unit, -1, keepdims=True)
    grad = grad_ref[...].astype(F32)
    out = grad + inverse * (grad_unit - first - unit * second)
    out_ref[...] = out.astype(out_ref.dtype)
    sums_ref[0:1] += jnp.sum(incoming * unit, axis=0, keepdims=True)
    sums_ref[1:2] += jnp.sum(incoming, axis=0, keepdims=True)
    sums_ref[2:3] += jnp.sum(grad, axis=0, keepdims=True)


def norm_backward(x, own, other, grad, gain, kind):
    length, width = own.shape
    block = pl.BlockSpec((ROWS, width), lambda i: (i, 0))
    return pl.pallas_call(
        norm_backward_kernel,
        grid=(length // ROWS,),
        in_specs=[block, block, block, block, whole((1, width))],
        out_specs=[block, whole((8, width))],
        out_shape=[
            jax.ShapeDtypeStruct((length, width), kind),
            jax.ShapeDtypeStruct((8, width), F32),
        ],
        compiler_params=params(),
        name="norm_backward",
    )(x, own, other, grad, gain)


def shards(
    tokens, cotangent, branch_weight, branch_bias, up_weight, down_bias,
    norm_gain, norm_bias, freq_seeds, doc_starts,
):
    is_attention = lax.axis_index("stream") == 0
    length, width = tokens.shape
    rotary = tuple(jnp.asarray(table) for table in rotary_rows(length))
    biases = branch_bias[0].astype(F32)
    tables = lax.cond(
        is_attention,
        lambda: tuple(feature_tables(freq_seeds)),
        lambda: (
            jnp.zeros((LAYERS, QUADS, WIDE, WIDE), BF16),
            jnp.zeros((LAYERS, QUADS, WIDE, WIDE), BF16),
            jnp.zeros((LAYERS, QUADS, 1, WIDE), F32),
        ),
    )
    swap = [(0, 1), (1, 0)]

    def attention(layer, stream):
        gain, offset = norm_gain[layer : layer + 1], norm_bias[layer : layer + 1]
        *x, h, state = project_forward(
            layer, stream, gain, offset, branch_weight, biases[layer], tables, rotary
        )
        mixed = attend_forward(doc_starts, state)
        part = mix_forward(layer, mixed, branch_weight, biases[layer])
        return tuple(x) + (part, h, state, mixed)

    def feed_forward(layer, stream):
        gain, offset = norm_gain[layer : layer + 1], norm_bias[layer : layer + 1]
        return tuple(
            mlp_forward(
                layer, stream, gain, offset, up_weight, biases[layer], branch_weight,
                down_bias[layer : layer + 1],
            )
        )

    stream = (tokens,)
    inputs, kept = [], []
    for layer in range(LAYERS):
        *x, part, h, state, mixed = lax.cond(
            is_attention,
            functools.partial(attention, layer, stream),
            functools.partial(feed_forward, layer, stream),
        )
        inputs.append(x[0] if x else tokens)
        kept.append((h, state, mixed))
        stream = (inputs[-1], part, lax.ppermute(part, "stream", swap))
    result = stream[0] + (stream[1] + stream[2])

    def attention_back(layer, grad):
        h, state, mixed = kept[layer]
        numer = mix_backward(layer, grad, branch_weight, mixed)
        feats = attend_backward(doc_starts, state, numer)
        part, weight, bias = project_backward(
            layer, grad, h, mixed, feats, state, tables, rotary, branch_weight
        )
        blank = jnp.zeros((weight.shape[0], width, WIDE // 2), F32)
        return part, weight, blank, blank, bias.reshape(-1, WIDE)

    def feed_forward_back(layer, grad):
        h, act, slope = kept[layer]
        part, weight, near, far, bias = mlp_backward(
            layer, grad, h, act, slope, branch_weight, up_weight
        )
        return part, weight, near, far, bias.reshape(-1, WIDE)

    grad = cotangent
    shares = [None] * LAYERS
    for layer in reversed(range(LAYERS)):
        part, weight, near, far, bias = lax.cond(
            is_attention,
            functools.partial(attention_back, layer, grad),
            functools.partial(feed_forward_back, layer, grad),
        )
        other = lax.ppermute(part, "stream", swap)
        kind = BF16 if layer else F32
        new_grad, sums = norm_backward(
            inputs[layer], part, other, grad, norm_gain[layer : layer + 1], kind
        )
        bias = jnp.where(
            is_attention & (jnp.arange(bias.shape[0])[:, None] >= 3 * QUADS),
            jnp.tile(sums[2].reshape(QUADS, WIDE), (bias.shape[0] // QUADS, 1)),
            bias,
        )
        scatter = functools.partial(
            lax.psum_scatter, axis_name="batch", scatter_dimension=0, tiled=True
        )
        if weight.shape[0] == lax.axis_size("batch"):
            near = lax.ppermute(near, "stream", [(1, 0)])
            up = jnp.where(is_attention, near, far)
            weight = rows_of(scatter(weight))
            up = rows_of(scatter(up))
        else:
            weight = scatter(rows_of(weight))
            up = rows_of(jnp.concatenate([near, far], axis=2))
            up = lax.psum_scatter(up, ("batch", "stream"), scatter_dimension=0, tiled=True)
        shares[layer] = (
            weight,
            scatter(bias.reshape(-1)),
            up,
            scatter(sums[2]),
            scatter(sums[0]),
            scatter(sums[1]),
        )
        grad = new_grad
    weight, bias, up, down, gain, offset = [list(group) for group in zip(*shares)]
    return (
        result,
        grad,
        jnp.stack(weight)[None],
        jnp.stack(bias)[None],
        jnp.stack(up),
        jnp.stack(down),
        jnp.stack(gain),
        jnp.stack(offset),
    )


def rows_of(blocks):
    return jnp.transpose(blocks, (0, 2, 1)).reshape(-1, blocks.shape[1])


def solution(mesh):
    placed = (
        P("batch", None),
        P("batch", None),
        P("stream", None, None, None),
        P("stream", None, None),
        P(),
        P(),
        P(),
        P(),
        P(),
        P("batch", None),
    )
    return jax.shard_map(
        shards,
        mesh=mesh,
        in_specs=placed,
        out_specs=(
            P("batch", None),
            P("batch", None),
            P("stream", None, "batch", None),
            P("stream", None, "batch"),
            P(None, ("batch", "stream"), None),
            P(None, "batch"),
            P(None, "batch"),
            P(None, "batch"),
        ),
        check_vma=False,
    )
```

time: 1950 us -> 1360 us (0.70)
  matrix products: 380 us -> 0 us
  Pallas kernels: 0 us -> 293 us
  waiting for transfers between devices: 1070 us -> 816 us
  other arithmetic: 155 us -> 36.4 us
  local copies, waits for them, and re-layouts: 209 us -> 101 us
  loops' own time: 30.8 us -> 1.21 us
    dot_general x54 -> x0, matrix products: 380 us -> none  [the longest x4 38.3 us: attend_backward(): jnp.einsum('hqk,qhd->khd', scores.astype(jnp.bfloat16), grad_numer, prefe...]
    pallas_call x0 -> x15, Pallas kernels: none -> 293 us  [the longest x2 67.6 us: project_backward(): pl.pallas_call(project_backward_kernel, grid=(blocks,), in_specs=[whole((...]
    reduce_scatter x4, waiting for transfers between devices: 982 us -> 788 us  [the longest x2 703 us: shards(): weight = rows_of(scatter(weight))]
    slice x46 -> x6, local copies, waits for them, and re-layouts: 97.2 us -> 5.5 us  [the longest x2 2.75 us: attention(): gain, offset = (norm_gain[layer:layer + 1], norm_bias[layer:layer + 1])]
    psum x3 -> x0, waiting for transfers between devices: 86.3 us -> none  [the longest x2 63.4 us: shards(): residual = residual + lax.psum(own_branch, 'stream')]
    reduce_sum x25 -> x0, other arithmetic: 51.4 us -> none  [the longest x4 11.8 us: feature_maps(): jnp.sum(key_heads * key_heads, -1, keepdims=True)]
    cond x110 -> x24, local copies, waits for them, and re-layouts: 24.1 us -> 73.8 us  [the longest x6 72.4 us: shards(): lax.cond(is_attention, functools.partial(attention_back, layer, grad), fu...]
    concatenate x8 -> x0, other arithmetic: 42.3 us -> none  [the longest x2 23.6 us: attend_forward(): kept_state = jnp.concatenate([projected, mixed_heads], axis=1)]
  transfers between devices with their start and end apart: 7 -> 10, of which waited for: 7 -> 8; matrix products, arithmetic and copies ran while one was open for 2% -> 7% of each run, Pallas kernels for 0% -> 7%
where the time goes in v1:
time: 1360 us; the launch traced here: 1350 us
  waiting for transfers between devices  816 us (60%)
  Pallas kernels  293 us (22%)
  local copies, waits for them, and re-layouts  101 us (7%)
  blocking collectives  79.5 us (6%)
  other arithmetic  36.4 us (3%)
  between operations  15.4 us (1%)
    reduce_scatter x2, waiting for transfers between devices, shards(): weight = rows_of(scatter(weight))  703 us
    reduce_scatter x2, waiting for transfers between devices, shards(): up = rows_of(scatter(up))  84.8 us
    unnamed x1, blocking collectives  79.5 us
    cond x6, local copies, waits for them, and re-layouts, shards(): lax.cond(is_attention, functools.partial(attention_back, layer, grad), fu...  72.4 us
    pallas_call x2, Pallas kernels, project_backward(): pl.pallas_call(project_backward_kernel, grid=(blocks,), in_specs=[whole((...  67.6 us
    pallas_call x2, Pallas kernels, attend_backward(): pl.pallas_call(attend_backward_kernel, grid=(PAIRS,), in_specs=[pl.BlockS...  66.6 us
    pallas_call x2, Pallas kernels, project_forward(): pl.pallas_call(functools.partial(project_kernel, len(stream)), grid=(4 *...  61.6 us
    pallas_call x2, Pallas kernels, attend_forward(): pl.pallas_call(attend_kernel, grid=(PAIRS,), in_specs=[pl.BlockSpec(memor...  38.2 us
  transfers between devices with their start and end apart: 10, of which 8 were waited for; matrix products, arithmetic and copies ran while one was open for 7% of the time, Pallas kernels for 7%

profile of v1, /device:TPU:0, one launch (start us, length us, event | category | flops | bytes accessed | tf_op | source)
XLA Modules:
  0.0 1346.4 jit_solution(8672134050465945471)
XLA Ops:
  8.0 11.2 conditional.5
  20.1 55.7 %conditional.6 = ((f32[1024,1024]{1,0:T(8,128)}, bf16[1024,1024]{1,0:T(8,128)(2,1)}, bf16[4,1024,1024]{2,1,0:T(8,128)(2,1)}, bf16[4,1024,1024]{2,1,0:T(8,128)(2,1)})) conditional(s32[]{:T(128)} %convert_element_type.13, (bf16[2,1024]{1,0:T(2,128)(2,1)}, bf16[2,1024]{1,0:T(2,128)(2,1)}, f32[2,4096]{1,0:T(2,128)S(1)}, bf16[2,1024]{1,0:T(2,128)(2,1)}, ...), branch_computations={%region_2.0_spmd, %region_3.0_spmd} | conditional | bytes 32900 | solution.py:779
  20.9 29.4 %project_forward.2 = (bf16[1024,1024]{1,0:T(8,128)(2,1)}, bf16[4,1024,1024]{2,1,0:T(8,128)(2,1)}) custom-call(bf16[1024,1024]{1,0:T(8,128)(2,1)} %get-tuple-element.154.refs_0_, bf16[1,1024]{1,0:T(2,128)(2,1)} %bitcast.62, bf16[1,1024]{1,0:T(2,128)(2,1)} %bitcast.70, bf16[1,2,4096,1024]{3,2,1,0:T(8,128)(2,1)} %get-tuple-element.157.refs_3_.weight_ref, ...), custom_call_target="tpu_custom_call" | custom-call | tf_op jit(solution)/shard_map/cond/branch_1_fun/project_forward/pallas_call | solution.py:398
  50.4 19.1 %attend_forward.2.mixed_ref = bf16[4,1024,1024]{2,1,0:T(8,128)(2,1)} custom-call(s32[1,4]{1,0:T(1,128)S(1)} %copy-done.12, bf16[4,1024,1024]{2,1,0:T(8,128)(2,1)} %get-tuple-element.339.state_ref), custom_call_target="tpu_custom_call" | custom-call | tf_op jit(solution)/shard_map/cond/branch_1_fun/attend_forward/pallas_call | solution.py:465
  83.2 61.5 %conditional.7 = ((f32[1024,1024]{1,0:T(8,128)}, f32[1024,1024]{1,0:T(8,128)}, bf16[1024,1024]{1,0:T(8,128)(2,1)}, bf16[4,1024,1024]{2,1,0:T(8,128)(2,1)}, bf16[4,1024,1024]{2,1,0:T(8,128)(2,1)})) conditional(s32[]{:T(128)} %convert_element_type.13, (bf16[2,1024]{1,0:T(2,128)(2,1)}, bf16[2,1024]{1,0:T(2,128)(2,1)}, f32[2,4096]{1,0:T(2,128)S(1)}, ...), branch_computations={%region_4.0_spmd, %region_5.0_spmd} | conditional | bytes 45064 | solution.py:779
  87.0 32.2 %project_forward.3 = (f32[1024,1024]{1,0:T(8,128)}, bf16[1024,1024]{1,0:T(8,128)(2,1)}, bf16[4,1024,1024]{2,1,0:T(8,128)(2,1)}) custom-call(bf16[1024,1024]{1,0:T(8,128)(2,1)} %get-tuple-element.175.refs_0_, f32[1024,1024]{1,0:T(8,128)} %get-tuple-element.176.refs_1_, f32[1024,1024]{1,0:T(8,128)S(1)} %get-tuple-element.177.refs_2_, ...), custom_call_target="tpu_custom_call" | custom-call | tf_op jit(solution)/shard_map/cond/branch_1_fun/project_forward/pallas_call | solution.py:398
  119.1 19.1 %attend_forward.3.mixed_ref = bf16[4,1024,1024]{2,1,0:T(8,128)(2,1)} custom-call(s32[1,4]{1,0:T(1,128)S(1)} %copy-done.13, bf16[4,1024,1024]{2,1,0:T(8,128)(2,1)} %get-tuple-element.349.state_ref), custom_call_target="tpu_custom_call" | custom-call | tf_op jit(solution)/shard_map/cond/branch_1_fun/attend_forward/pallas_call | solution.py:465
  144.7 86.6 %conditional.8 = (f32[1024,1024]{1,0:T(8,128)}, f32[16,1024,256]{2,1,0:T(8,128)}, f32[16,1024,128]{2,1,0:T(8,128)}, f32[16,1024,128]{2,1,0:T(8,128)}, f32[16,256]{1,0:T(8,128)S(1)}) conditional(s32[]{:T(128)} %convert_element_type.13, (bf16[1024,1024]{1,0:T(8,128)(2,1)S(1)}, bf16[1024,1024]{1,0:T(8,128)(2,1)}, bf16[4,1024,1024]{2,1,0:T(8,128)(2,1)}, ...), branch_computations={%region_6.0_spmd, %region_7.0_spmd} | conditional | bytes 29393120 | solution.py:809
  144.9 10.7 mix_backward.2.numer_ref
  155.6 33.3 %attend_backward.2.feat_ref = bf16[3,1024,1024]{2,1,0:T(8,128)(2,1)} custom-call(s32[1,4]{1,0:T(1,128)S(1)} %copy-done.14, bf16[4,1024,1024]{2,1,0:T(8,128)(2,1)} %get-tuple-element.206.state_ref.keys_ref, bf16[2,1024,1024]{2,1,0:T(8,128)(2,1)} %mix_backward.2.numer_ref), custom_call_target="tpu_custom_call" | custom-call | tf_op jit(solution)/shard_map/cond/branch_1_fun/attend_backward/pallas_call | solution.py:576
  188.9 33.4 %project_backward.2 = (f32[1024,1024]{1,0:T(8,128)}, f32[16,1024,256]{2,1,0:T(8,128)}, f32[16,1,256]{2,1,0:T(1,128)}) custom-call(bf16[1024,1024]{1,0:T(8,128)(2,1)S(1)} %get-tuple-element.202.grad_ref, bf16[1024,1024]{1,0:T(8,128)(2,1)S(1)} %copy-done.7, bf16[4,1024,1024]{2,1,0:T(8,128)(2,1)} %get-tuple-element.204.mixed_ref, ...), custom_call_target="tpu_custom_call" | custom-call | tf_op jit(solution)/shard_map/cond/branch_1_fun/project_backward/pallas_call | solution.py:663
  255.9 9.6 broadcast_select_fusion
  281.6 88.4 %conditional.9 = (f32[1024,1024]{1,0:T(8,128)}, f32[16,1024,256]{2,1,0:T(8,128)}, f32[16,1024,128]{2,1,0:T(8,128)}, f32[16,1024,128]{2,1,0:T(8,128)}, f32[16,256]{1,0:T(8,128)S(1)}) conditional(s32[]{:T(128)} %convert_element_type.13, (bf16[1024,1024]{1,0:T(8,128)(2,1)}, bf16[1024,1024]{1,0:T(8,128)(2,1)S(1)}, bf16[4,1024,1024]{2,1,0:T(8,128)(2,1)}, ...), branch_computations={%region_8.9_spmd, %region_9.10_spmd} | conditional | bytes 21004392 | solution.py:809
  282.1 11.4 mix_backward.3.numer_ref
  293.5 33.3 %attend_backward.3.feat_ref = bf16[3,1024,1024]{2,1,0:T(8,128)(2,1)} custom-call(s32[1,4]{1,0:T(1,128)S(1)} %get-tuple-element.228.starts_ref, bf16[4,1024,1024]{2,1,0:T(8,128)(2,1)} %get-tuple-element.229.state_ref.keys_ref, bf16[2,1024,1024]{2,1,0:T(8,128)(2,1)} %mix_backward.3.numer_ref), custom_call_target="tpu_custom_call" | custom-call | tf_op jit(solution)/shard_map/cond/branch_1_fun/attend_backward/pallas_call | solution.py:576
  326.8 34.2 %project_backward.3 = (f32[1024,1024]{1,0:T(8,128)}, f32[16,1024,256]{2,1,0:T(8,128)}, f32[16,1,256]{2,1,0:T(1,128)}) custom-call(bf16[1024,1024]{1,0:T(8,128)(2,1)} %get-tuple-element.225.grad_ref, bf16[1024,1024]{1,0:T(8,128)(2,1)S(1)} %get-tuple-element.226.h_ref, bf16[4,1024,1024]{2,1,0:T(8,128)(2,1)} %get-tuple-element.227.mixed_ref, ...), custom_call_target="tpu_custom_call" | custom-call | tf_op jit(solution)/shard_map/cond/branch_1_fun/project_backward/pallas_call | solution.py:663
  380.7 9.3 copy.42
  394.6 9.7 broadcast_select_fusion.1
  404.4 17.6 %copy.40 = f32[16,1024,256]{1,2,0:T(8,128)} copy(f32[16,1024,256]{2,1,0:T(8,128)} %get-tuple-element.288) | data formatting | bytes 33554432 | tf_op jit(solution)/shard_map/cond | solution.py:809
  422.1 17.7 %copy.39 = f32[16,1024,256]{1,2,0:T(8,128)} copy(f32[16,1024,256]{2,1,0:T(8,128)} %get-tuple-element.287) | data formatting | bytes 33554432 | tf_op jit(solution)/shard_map/cond | solution.py:809
  464.3 79.5 %all-reduce.8 = (f32[4096]{0:T(1024)S(1)}, f32[4096]{0:T(1024)S(1)}, f32[1024]{0:T(1024)S(1)}, f32[1024]{0:T(1024)S(1)}, f32[1024]{0:T(1024)S(1)}, /*index=5*/f3...) all-reduce(f32[4096]{0:T(1024)S(1)} %bitcast.66, ...), channel_id=5, replica_groups=mesh['batch'=16,'stream'=2] {'batch'}, use_global_device_ids=true, to_apply=%region_13.14.clone | all-reduce | flops 14336 | bytes 114688
  546.7 84.8 %reduce-scatter.9.cloned.1.call-done = f32[1,1024,128]{1,2,0:T(8,128)} async-done(((f32[16,1024,128]{1,2,0:T(8,128)}), f32[1,1024,128]{1,2,0:T(8,128)}) %reduce-scatter.9.cloned.1.call-update) | async-done | bytes 524304 | tf_op jit(solution)/shard_map/reduce_scatter | solution.py:831
  633.8 348.6 %reduce-scatter.7.cloned.1.call-done = f32[1,1024,256]{1,2,0:T(8,128)} async-done(((f32[16,1024,256]{1,2,0:T(8,128)}), f32[1,1024,256]{1,2,0:T(8,128)}) %reduce-scatter.7.cloned.1.call-update) | async-done | bytes 1048592 | tf_op jit(solution)/shard_map/reduce_scatter | solution.py:830
  982.3 354.2 %reduce-scatter.5.cloned.1.call-done = f32[1,1024,256]{1,2,0:T(8,128)} async-done(((f32[16,1024,256]{1,2,0:T(8,128)}), f32[1,1024,256]{1,2,0:T(8,128)}) %reduce-scatter.5.cloned.1.call-update) | async-done | bytes 1048592 | tf_op jit(solution)/shard_map/reduce_scatter | solution.py:830
  (101 shorter events, 142.7 us)
Async XLA Ops:
  7.2 539.5 %reduce-scatter.11.cloned.1.call-start = ((), (), s32[]{:S(2)}) async-start(), calls=%async_computation.7 | async-start | bytes 8912896 | tf_op jit(solution)/shard_map/reduce_scatter | solution.py:831
  19.2 1.0 copy-start.2
  20.9 29.4 %copy-start.12 = (s32[1,4]{1,0:T(1,128)S(1)}, s32[1,4]{1,0:T(1,128)}, u32[]{:S(2)}) copy-start(s32[1,4]{1,0:T(1,128)} %get-tuple-element.153.starts_ref) | copy-start | bytes 52 | tf_op jit(solution)/shard_map/cond
  75.8 7.4 collective-permute-start
  83.2 61.5 %copy-start.1 = (bf16[1024,1024]{1,0:T(8,128)(2,1)S(1)}, bf16[1024,1024]{1,0:T(8,128)(2,1)}, u32[]{:S(2)}) copy-start(bf16[1024,1024]{1,0:T(8,128)(2,1)} %grad_ref.1) | copy-start | bytes 6291460
  87.0 32.2 %copy-start.13 = (s32[1,4]{1,0:T(1,128)S(1)}, s32[1,4]{1,0:T(1,128)}, u32[]{:S(2)}) copy-start(s32[1,4]{1,0:T(1,128)} %get-tuple-element.188.starts_ref) | copy-start | bytes 52 | tf_op jit(solution)/shard_map/cond
  144.9 10.7 copy-start.14
  155.6 33.3 %copy-start.3 = (f32[1024,128]{1,0:T(8,128)S(1)}, f32[1024,128]{1,0:T(8,128)}, u32[]{:S(2)}) copy-start(f32[1024,128]{1,0:T(8,128)} %get-tuple-element.210.sine_ref) | copy-start | bytes 1572868 | tf_op jit(solution)/shard_map/cond
  155.6 33.3 %copy-start.5 = (f32[1024,128]{1,0:T(8,128)S(1)}, f32[1024,128]{1,0:T(8,128)}, u32[]{:S(2)}) copy-start(f32[1024,128]{1,0:T(8,128)} %get-tuple-element.209.cosine_ref) | copy-start | bytes 1572868 | tf_op jit(solution)/shard_map/cond
  155.6 33.3 %copy-start.7 = (bf16[1024,1024]{1,0:T(8,128)(2,1)S(1)}, bf16[1024,1024]{1,0:T(8,128)(2,1)}, u32[]{:S(2)}) copy-start(bf16[1024,1024]{1,0:T(8,128)(2,1)} %get-tuple-element.203.h_ref) | copy-start | bytes 6291460 | tf_op jit(solution)/shard_map/cond
  240.5 15.4 %collective-permute-start.5 = (f32[16,1024,128]{1,2,0:T(8,128)}, f32[16,1024,128]{1,2,0:T(8,128)}, u32[]{:S(2)}, u32[]{:S(2)}) collective-permute-start(f32[16,1024,128]{1,2,0:T(8,128)} %copy.43), channel_id=1, source_target_pairs={{1,0},{3,2},{5,4},{7,6},{9,8},{11,10},{13,12},{15,14},{17,16},{19,... | collective-permute-start | bytes 25165832 | tf_op jit(solution)/shard_map/ppermute | solution.py:828
  265.5 16.1 %copy-start.11 = (s32[1,4]{1,0:T(1,128)S(1)}, s32[1,4]{1,0:T(1,128)}, u32[]{:S(2)}) copy-start(s32[1,4]{1,0:T(1,128)} %param.32) | copy-start | bytes 52
  265.5 366.0 %reduce-scatter.9.cloned.1.call-start = ((), (), s32[]{:S(2)}) async-start(), calls=%async_computation.6 | async-start | bytes 8912896 | tf_op jit(solution)/shard_map/reduce_scatter | solution.py:831
  265.6 16.1 %copy-start.8 = (bf16[1024,1024]{1,0:T(8,128)(2,1)S(1)}, bf16[1024,1024]{1,0:T(8,128)(2,1)}, u32[]{:S(2)}) copy-start(bf16[1024,1024]{1,0:T(8,128)(2,1)} %get-tuple-element.282) | copy-start | bytes 6291460
  265.6 7.6 collective-permute-start.2
  293.5 33.3 %copy-start.4 = (f32[1024,128]{1,0:T(8,128)S(1)}, f32[1024,128]{1,0:T(8,128)}, u32[]{:S(2)}) copy-start(f32[1024,128]{1,0:T(8,128)} %get-tuple-element.233.sine_ref) | copy-start | bytes 1572868 | tf_op jit(solution)/shard_map/cond
  293.5 33.3 %copy-start.6 = (f32[1024,128]{1,0:T(8,128)S(1)}, f32[1024,128]{1,0:T(8,128)}, u32[]{:S(2)}) copy-start(f32[1024,128]{1,0:T(8,128)} %get-tuple-element.232.cosine_ref) | copy-start | bytes 1572868 | tf_op jit(solution)/shard_map/cond
  379.2 15.4 %collective-permute-start.4 = (f32[16,1024,128]{1,2,0:T(8,128)}, f32[16,1024,128]{1,2,0:T(8,128)}, u32[]{:S(2)}, u32[]{:S(2)}) collective-permute-start(f32[16,1024,128]{1,2,0:T(8,128)} %copy.41), channel_id=1, source_target_pairs={{1,0},{3,2},{5,4},{7,6},{9,8},{11,10},{13,12},{15,14},{17,16},{19,... | collective-permute-start | bytes 25165832 | tf_op jit(solution)/shard_map/ppermute | solution.py:828
  404.3 578.0 %reduce-scatter.7.cloned.1.call-start = ((), (), s32[]{:S(2)}) async-start(), calls=%async_computation.5 | async-start | bytes 17825792 | tf_op jit(solution)/shard_map/reduce_scatter | solution.py:830
  422.0 914.5 %reduce-scatter.5.cloned.1.call-start = ((), (), s32[]{:S(2)}) async-start(), calls=%async_computation.4 | async-start | bytes 17825792 | tf_op jit(solution)/shard_map/reduce_scatter | solution.py:830
  439.8 7.6 collective-permute-start.1
  440.1 15.9 %collective-permute-start.3 = (f32[1024,1024]{1,0:T(8,128)}, f32[1024,1024]{1,0:T(8,128)}, u32[]{:S(2)}, u32[]{:S(2)}) collective-permute-start(f32[1024,1024]{1,0:T(8,128)} %get-tuple-element.285.own_ref), channel_id=1, source_target_pairs={{0,1},{1,0},{2,3},{3,2},{4,5},{5,4},{6,7},{7,6},{8,9},{9,8},{10,11... | collective-permute-start | bytes 12582920 | tf_op jit(solution)/shard_map/ppermute | solution.py:814
  442.3 13.7 %copy-start = (bf16[1024,1024]{1,0:T(8,128)(2,1)S(1)}, bf16[1024,1024]{1,0:T(8,128)(2,1)}, u32[]{:S(2)}) copy-start(bf16[1024,1024]{1,0:T(8,128)(2,1)} %x_ref.1) | copy-start | bytes 6291460
  442.3 13.7 %copy-start.9 = (f32[1024,1024]{1,0:T(8,128)S(1)}, f32[1024,1024]{1,0:T(8,128)}, u32[]{:S(2)}) copy-start(f32[1024,1024]{1,0:T(8,128)} %get-tuple-element.285.own_ref) | copy-start | bytes 12582916
  (2 other events, 1.3 us)
Sparse Core Ops, SparseCore 0:
  265.6 180.5 reduce-scatter.10
  448.5 182.9 reduce-scatter.8
  633.8 348.5 reduce-scatter.6
  984.5 351.9 reduce-scatter.4

commit v2 on v1

--- a/solution.py
+++ b/solution.py
@@ -268,15 +268,17 @@
         part_ref[rows] += dot_nn(grad_unit, up_ref[0])
     bias_ref[0] = bias
     units = jnp.concatenate(pieces, axis=0)
-    half = near_ref.shape[2]
+    folded, half = near_ref.shape[1], near_ref.shape[2] // 2
     for first in range(0, h_t.shape[0], ROWS):
         rows = slice(first, first + ROWS)
         for block in range(FF_BLOCK // WIDE):
             lanes = slice(block * WIDE, (block + 1) * WIDE)
             weight_ref[block, rows] = dot_nn(grad_t[rows], act_ref[0, :, lanes])
             up_grad = dot_nn(h_t[rows], units[:, lanes])
-            near_ref[block, rows] = up_grad[:, :half]
-            far_ref[block, rows] = up_grad[:, half:]
+            side = 0 if first < folded else half
+            place = slice(first % folded, first % folded + ROWS)
+            near_ref[block, place, side : side + half] = up_grad[:, :half]
+            far_ref[block, place, side : side + half] = up_grad[:, half:]
 
 
 def mlp_backward(layer, grad, h, act, slope, down_weight, up):
@@ -284,7 +286,7 @@
     hidden = up.shape[1]
     blocks = hidden // FF_BLOCK
     per = FF_BLOCK // WIDE
-    halves = jax.ShapeDtypeStruct((hidden // WIDE, width, WIDE // 2), F32)
+    halves = jax.ShapeDtypeStruct((hidden // WIDE, width // 2, WIDE), F32)
     return pl.pallas_call(
         mlp_backward_kernel,
         grid=(blocks,),
@@ -299,8 +301,8 @@
         out_specs=[
             whole((length, width)),
             pl.BlockSpec((per, width, WIDE), lambda j: (j, 0, 0)),
-            pl.BlockSpec((per, width, WIDE // 2), lambda j: (j, 0, 0)),
-            pl.BlockSpec((per, width, WIDE // 2), lambda j: (j, 0, 0)),
+            pl.BlockSpec((per, width // 2, WIDE), lambda j: (j, 0, 0)),
+            pl.BlockSpec((per, width // 2, WIDE), lambda j: (j, 0, 0)),
             pl.BlockSpec((1, 1, FF_BLOCK), lambda j: (j, 0, 0)),
         ],
         out_shape=[
@@ -594,8 +596,9 @@
 
 def project_backward_kernel(
     grad_ref, h_ref, mixed_ref, feat_ref, keys_ref, table_ref, cosine_ref, sine_ref, weight_ref,
-    part_ref, out_ref, bias_ref, grad_t, h_t, flow,
+    part_ref, out_ref, bias_ref, near_ref, far_ref, grad_t, h_t, flow,
 ):
+    del near_ref, far_ref
     step = pl.program_id(0)
     kind, length = step // QUADS, h_ref.shape[0]
 
@@ -680,11 +683,15 @@
             whole((length, width)),
             pl.BlockSpec((1, width, WIDE), lambda j: (target(j), 0, 0)),
             pl.BlockSpec((1, 1, WIDE), lambda j: (target(j), 0, 0)),
+            pl.BlockSpec(memory_space=pl.ANY),
+            pl.BlockSpec(memory_space=pl.ANY),
         ],
         out_shape=[
             jax.ShapeDtypeStruct((length, width), F32),
             jax.ShapeDtypeStruct((blocks, width, WIDE), F32),
             jax.ShapeDtypeStruct((blocks, 1, WIDE), F32),
+            jax.ShapeDtypeStruct((blocks, width // 2, WIDE), F32),
+            jax.ShapeDtypeStruct((blocks, width // 2, WIDE), F32),
         ],
         scratch_shapes=[
             pltpu.VMEM((width, length), BF16),
@@ -734,6 +741,231 @@
         compiler_params=params(),
         name="norm_backward",
     )(x, own, other, grad, gain)
+
+
+MESH = pl.DeviceIdType.MESH
+UNIT = 8
+SLOTS = 4
+LAG = 1
+ORDERS = ((0, 1, 2, 3), (1, 0, 2, 3), (0, 2, 3, 1), (1, 2, 3, 0), (0, 2, 3, 1), (1, 2, 3, 0))
+
+
+def bit_of(index, bit):
+    return (index // (1 << bit)) % 2
+
+
+def flip(index, bit):
+    return index + (1 << bit) * (1 - 2 * bit_of(index, bit))
+
+
+def scatter_kernel(bits, rows, layers, *refs):
+    sources, refs = refs[: 3 * layers], refs[3 * layers :]
+    small_ref, weight_out, up_out, small_out = refs[:4]
+    held, refs = refs[4:], None
+    flows, stages = len(ORDERS), bits
+    weight_sum, up_sum = held[:2]
+    small_held = held[2 : 2 + stages]
+    held = held[2 + stages :]
+    held, sems = held[: flows * (stages + 1)], held[flows * (stages + 1) :]
+    load_sem, send_sem, recv_sem, credit, small_send, small_recv = sems
+    held = [held[f * (stages + 1) : (f + 1) * (stages + 1)] for f in range(flows)]
+    me, core = lax.axis_index("batch"), lax.axis_index("stream")
+    weight_units, up_units = rows[0] // UNIT, rows[1] // UNIT
+    per_layer = weight_units + up_units
+    total = per_layer * layers // flows
+
+    barrier = pltpu.get_barrier_semaphore()
+    for bit in range(bits):
+        pl.semaphore_signal(
+            barrier, inc=1, device_id={"batch": flip(me, bit)}, device_id_type=MESH
+        )
+    pl.semaphore_wait(barrier, bits)
+
+    def view(order, stage, mine):
+        left = sorted(set(range(bits)) - set(order[:stage]), reverse=True)
+        pick = bit_of(me, order[stage])
+        pick = pick if mine else 1 - pick
+        return tuple(pick if bit == order[stage] else slice(None) for bit in left)
+
+    def remote(flow, stage, slot, source):
+        return pltpu.make_async_remote_copy(
+            src_ref=source,
+            dst_ref=held[flow][stage + 1].at[slot],
+            send_sem=send_sem.at[flow, stage, slot],
+            recv_sem=recv_sem.at[flow, stage, slot],
+            device_id={"batch": flip(me, ORDERS[flow][stage])},
+            device_id_type=MESH,
+        )
+
+    def sent_from(flow, stage, slot):
+        if stage == 0:
+            return held[flow][0].at[slot]
+        return held[flow][stage].at[(slot,) + view(ORDERS[flow], stage, False)]
+
+    def load(flow, slot, source):
+        return pltpu.make_async_copy(source, held[flow][0].at[slot], load_sem.at[flow, slot])
+
+    def return_credit(flow, stage, unit):
+        @pl.when(unit + SLOTS < total)
+        def _():
+            pl.semaphore_signal(
+                credit.at[flow, stage],
+                inc=1,
+                device_id={"batch": flip(me, ORDERS[flow][stage])},
+                device_id_type=MESH,
+            )
+
+    def take_credit(flow, stage, unit):
+        @pl.when(unit >= SLOTS)
+        def _():
+            pl.semaphore_wait(credit.at[flow, stage], 1)
+
+    def places(place, act):
+        for layer in range(layers):
+            base = layer * per_layer
+            middle = base + weight_units
+            pl.when((place >= base) & (place < middle))(
+                functools.partial(act, layer, False, (place - base) * UNIT)
+            )
+            pl.when((place >= middle) & (place < base + per_layer))(
+                functools.partial(act, layer, True, (place - middle) * UNIT)
+            )
+
+    def begin(flow, unit):
+        slot = lax.rem(unit, SLOTS)
+        take_credit(flow, 0, unit)
+
+        def start(source, row):
+            at = (pl.ds(pl.multiple_of(row, UNIT), UNIT),)
+            remote(flow, 0, slot, source.at[view(ORDERS[flow], 0, False) + at]).start()
+            load(flow, slot, source.at[view(ORDERS[flow], 0, True) + at]).start()
+
+        def act(layer, is_up, row):
+            if not is_up:
+                start(sources[3 * layer], row)
+            else:
+                for side in range(2):
+                    pl.when(core == side)(
+                        functools.partial(start, sources[3 * layer + 1 + side], row)
+                    )
+
+        places(unit * flows + flow, act)
+
+    def advance(flow, stage, unit):
+        slot = lax.rem(unit, SLOTS)
+        order, buffer = ORDERS[flow], held[flow][stage]
+        copy = remote(flow, stage - 1, slot, sent_from(flow, stage - 1, slot))
+        copy.wait_recv()
+        if stage == 1:
+            kept = (slice(None),) * (bits - 1) + (pl.ds(0, UNIT),)
+            kept = tuple(view(order, 0, True)) + kept[bits - 1 :]
+            load(flow, slot, sources[0].at[kept]).wait()
+            mine = held[flow][0][slot]
+        else:
+            mine = held[flow][stage - 1][(slot,) + view(order, stage - 1, True)]
+        value = buffer[slot] + mine
+        if stage < stages:
+            buffer[slot] = value
+            take_credit(flow, stage, unit)
+            remote(flow, stage, slot, sent_from(flow, stage, slot)).start()
+        else:
+
+            def act(layer, is_up, row):
+                target = up_sum if is_up else weight_sum
+                target[layer, pl.ds(pl.multiple_of(row, UNIT), UNIT)] = value
+
+            places(unit * flows + flow, act)
+        copy.wait_send()
+        if stage >= 2:
+            return_credit(flow, stage - 2, unit)
+        if stage == stages:
+            return_credit(flow, stage - 1, unit)
+
+    def small_copy(stage):
+        source = small_ref if stage == 0 else small_held[stage - 1]
+        return pltpu.make_async_remote_copy(
+            src_ref=source.at[view(ORDERS[0], stage, False)],
+            dst_ref=small_held[stage],
+            send_sem=small_send.at[stage],
+            recv_sem=small_recv.at[stage],
+            device_id={"batch": flip(me, ORDERS[0][stage])},
+            device_id_type=MESH,
+        )
+
+    def small_step(stage):
+        if stage > 0:
+            small_copy(stage - 1).wait()
+            source = small_ref if stage == 1 else small_held[stage - 2]
+            sums = small_held[stage - 1][...] + source[view(ORDERS[0], stage - 1, True)]
+            if stage == stages:
+                small_out[...] = sums
+            else:
+                small_held[stage - 1][...] = sums
+        if stage < stages:
+            small_copy(stage).start()
+
+    def step(index, carry):
+        for flow in range(flows):
+            pl.when(index < total)(functools.partial(begin, flow, index))
+        for flow in range(flows):
+            for stage in range(1, stages + 1):
+                unit = index - LAG * stage
+                pl.when((unit >= 0) & (unit < total))(
+                    functools.partial(advance, flow, stage, unit)
+                )
+        for stage in range(stages + 1):
+            pl.when(index == stages + 2 * stage)(functools.partial(small_step, stage))
+        return carry
+
+    lax.fori_loop(0, total + LAG * stages, step, 0)
+    half = WIDE // 2
+    for layer in range(layers):
+        weight_out[layers - 1 - layer] = weight_sum[layer].T
+        folded = up_sum.shape[1]
+        up_out[layers - 1 - layer, :, :folded] = up_sum[layer, :, :half].T
+        up_out[layers - 1 - layer, :, folded:] = up_sum[layer, :, half:].T
+
+
+def reduce_scatter(grads, small):
+    layers = len(grads) // 3
+    count, width = grads[0].shape[:2]
+    folded = grads[1].shape[1]
+    bits = count.bit_length() - 1
+    small = jnp.pad(small, ((0, 0), (0, -small.shape[1] % 1024)))
+    small = small.reshape((2,) * bits + (-1, 128))
+    scratch = [pltpu.VMEM((layers, width, WIDE), F32), pltpu.VMEM((layers, folded, WIDE), F32)]
+    scratch += [
+        pltpu.VMEM((2,) * (bits - 1 - stage) + small.shape[-2:], F32) for stage in range(bits)
+    ]
+    for _ in ORDERS:
+        for stage in range(bits + 1):
+            lead = (SLOTS,) + (2,) * (bits - 1 - max(stage - 1, 0))
+            scratch.append(pltpu.VMEM(lead + (UNIT, WIDE), F32))
+    scratch += [
+        pltpu.SemaphoreType.DMA((len(ORDERS), SLOTS)),
+        pltpu.SemaphoreType.DMA((len(ORDERS), bits, SLOTS)),
+        pltpu.SemaphoreType.DMA((len(ORDERS), bits, SLOTS)),
+        pltpu.SemaphoreType.REGULAR((len(ORDERS), bits)),
+        pltpu.SemaphoreType.DMA((bits,)),
+        pltpu.SemaphoreType.DMA((bits,)),
+    ]
+    weight, up, small = pl.pallas_call(
+        functools.partial(scatter_kernel, bits, (width, folded), layers),
+        in_specs=[pl.BlockSpec(memory_space=pl.ANY)] * len(grads)
+        + [pl.BlockSpec(memory_space=pltpu.VMEM)],
+        out_specs=[pl.BlockSpec(memory_space=pltpu.VMEM)] * 3,
+        out_shape=[
+            jax.ShapeDtypeStruct((layers, WIDE, width), F32),
+            jax.ShapeDtypeStruct((layers, WIDE // 2, width), F32),
+            jax.ShapeDtypeStruct(small.shape[-2:], F32),
+        ],
+        scratch_shapes=scratch,
+        compiler_params=pltpu.CompilerParams(
+            collective_id=0, has_side_effects=True, vmem_limit_bytes=VMEM_LIMIT
+        ),
+        name="reduce_scatter",
+    )(*[array.reshape((2,) * bits + array.shape[1:]) for array in grads], small)
+    return weight, up, small.reshape(-1)
 
 
 def shards(
@@ -790,11 +1022,10 @@
         h, state, mixed = kept[layer]
         numer = mix_backward(layer, grad, branch_weight, mixed)
         feats = attend_backward(doc_starts, state, numer)
-        part, weight, bias = project_backward(
+        part, weight, bias, near, far = project_backward(
             layer, grad, h, mixed, feats, state, tables, rotary, branch_weight
         )
-        blank = jnp.zeros((weight.shape[0], width, WIDE // 2), F32)
-        return part, weight, blank, blank, bias.reshape(-1, WIDE)
+        return part, weight, near, far, bias.reshape(-1, WIDE)
 
     def feed_forward_back(layer, grad):
         h, act, slope = kept[layer]
@@ -804,7 +1035,9 @@
         return part, weight, near, far, bias.reshape(-1, WIDE)
 
     grad = cotangent
-    shares = [None] * LAYERS
+    count = lax.axis_size("batch")
+    blocked = count == branch_weight.shape[2] // WIDE
+    grads, vectors = [], []
     for layer in reversed(range(LAYERS)):
         part, weight, near, far, bias = lax.cond(
             is_attention,
@@ -812,6 +1045,8 @@
             functools.partial(feed_forward_back, layer, grad),
         )
         other = lax.ppermute(part, "stream", swap)
+        if blocked:
+            near = lax.ppermute(near, "stream", [(1, 0)])
         kind = BF16 if layer else F32
         new_grad, sums = norm_backward(
             inputs[layer], part, other, grad, norm_gain[layer : layer + 1], kind
@@ -821,38 +1056,50 @@
             jnp.tile(sums[2].reshape(QUADS, WIDE), (bias.shape[0] // QUADS, 1)),
             bias,
         )
-        scatter = functools.partial(
-            lax.psum_scatter, axis_name="batch", scatter_dimension=0, tiled=True
-        )
-        if weight.shape[0] == lax.axis_size("batch"):
-            near = lax.ppermute(near, "stream", [(1, 0)])
-            up = jnp.where(is_attention, near, far)
-            weight = rows_of(scatter(weight))
-            up = rows_of(scatter(up))
-        else:
-            weight = scatter(rows_of(weight))
-            up = rows_of(jnp.concatenate([near, far], axis=2))
-            up = lax.psum_scatter(up, ("batch", "stream"), scatter_dimension=0, tiled=True)
-        shares[layer] = (
-            weight,
-            scatter(bias.reshape(-1)),
-            up,
-            scatter(sums[2]),
-            scatter(sums[0]),
-            scatter(sums[1]),
-        )
+        vectors = [bias.reshape(count, -1), sums[:3].reshape(3, count, -1)] + vectors
+        grads += [weight, near, far]
         grad = new_grad
-    weight, bias, up, down, gain, offset = [list(group) for group in zip(*shares)]
+    small = jnp.concatenate(
+        [part.reshape(count, -1) for part in vectors[0::2]]
+        + [jnp.moveaxis(part, 0, 1).reshape(count, -1) for part in vectors[1::2]],
+        axis=1,
+    )
+    if blocked:
+        weight, up, small = reduce_scatter(grads, small)
+    else:
+        weight, up, small = scatter_rows(grads, small)
+    each = branch_weight.shape[2] // count
+    bias, sums = small[: LAYERS * each], small[LAYERS * each :]
+    sums = sums[: LAYERS * 3 * (width // count)].reshape(LAYERS, 3, -1)
     return (
         result,
         grad,
-        jnp.stack(weight)[None],
-        jnp.stack(bias)[None],
-        jnp.stack(up),
-        jnp.stack(down),
-        jnp.stack(gain),
-        jnp.stack(offset),
+        weight[None],
+        bias.reshape(1, LAYERS, -1),
+        up,
+        sums[:, 2],
+        sums[:, 0],
+        sums[:, 1],
     )
+
+
+def scatter_rows(grads, small):
+    scatter = functools.partial(
+        lax.psum_scatter, axis_name="batch", scatter_dimension=0, tiled=True
+    )
+    weights, ups = [], []
+    for weight, near, far in zip(grads[0::3], grads[1::3], grads[2::3]):
+        half = near.shape[2] // 2
+        whole_up = [
+            jnp.concatenate([side[..., :half], side[..., half:]], axis=1) for side in (near, far)
+        ]
+        whole_up = rows_of(jnp.concatenate(whole_up, axis=2))
+        whole_up = jnp.where(lax.axis_index("stream") == 1, whole_up, 0.0)
+        weights.append(scatter(rows_of(weight)))
+        ups.append(
+            lax.psum_scatter(whole_up, ("batch", "stream"), scatter_dimension=0, tiled=True)
+        )
+    return jnp.stack(weights[::-1]), jnp.stack(ups[::-1]), scatter(small)[0]
 
 
 def rows_of(blocks):

time: 1360 us -> 729 us (0.54)
  waiting for transfers between devices: 816 us -> 28 us
  Pallas kernels: 293 us -> 655 us
  local copies, waits for them, and re-layouts: 101 us -> 20 us
  blocking collectives: 79.5 us -> 0 us
  other arithmetic: 36.4 us -> 9.66 us
  between operations: 15.4 us -> 1.25 us
    reduce_scatter x4 -> x0, waiting for transfers between devices: 788 us -> none  [the longest x2 703 us: shards(): weight = rows_of(scatter(weight))]
    pallas_call x0 -> x1, Pallas kernels: none -> 361 us  [reduce_scatter(): pl.pallas_call(functools.partial(scatter_kernel, bits, (width, folded), l...]
    unnamed x1 -> x0, blocking collectives: 79.5 us -> none
    cond x24 -> x16, local copies, waits for them, and re-layouts: 73.8 us -> 2.77 us  [the longest x6 72.4 us: shards(): lax.cond(is_attention, functools.partial(attention_back, layer, grad), fu...]
    select_n x2 -> x1, other arithmetic: 19.2 us -> 0.08 us  [shards(): jnp.where(is_attention & (jnp.arange(bias.shape[0])[:, None] >= 3 * QUADS...]
    another operation x10 -> x0, local copies, waits for them, and re-layouts: 17 us -> none
  transfers between devices with their start and end apart: 10 -> 6, of which waited for: 8 -> 3; matrix products, arithmetic and copies ran while one was open for 7% -> 2% of each run, Pallas kernels for 7% -> 13%
where the time goes in v2:
time: 729 us; the launch traced here: 722 us
  Pallas kernels  655 us (90%)
  waiting for transfers between devices  28 us (4%)
  local copies, waits for them, and re-layouts  20 us (3%)
  other arithmetic  9.66 us (1%)
  starting transfers between devices  7.31 us (1%)
    pallas_call x1, Pallas kernels, reduce_scatter(): pl.pallas_call(functools.partial(scatter_kernel, bits, (width, folded), l...  361 us
    pallas_call x2, Pallas kernels, project_backward(): pl.pallas_call(project_backward_kernel, grid=(blocks,), in_specs=[whole((...  68.3 us
    pallas_call x2, Pallas kernels, attend_backward(): pl.pallas_call(attend_backward_kernel, grid=(PAIRS,), in_specs=[pl.BlockS...  66.6 us
    pallas_call x2, Pallas kernels, project_forward(): pl.pallas_call(functools.partial(project_kernel, len(stream)), grid=(4 *...  60.5 us
    pallas_call x2, Pallas kernels, attend_forward(): pl.pallas_call(attend_kernel, grid=(PAIRS,), in_specs=[pl.BlockSpec(memor...  38.3 us
    pallas_call x2, Pallas kernels, mix_backward(): pl.pallas_call(mix_backward_kernel, grid=(QUADS,), in_specs=[whole((lengt...  22.7 us
    ppermute x2, waiting for transfers between devices, shards(): stream = (inputs[-1], part, lax.ppermute(part, 'stream', swap))  22.5 us
    pallas_call x2, Pallas kernels, norm_backward(): pl.pallas_call(norm_backward_kernel, grid=(length // ROWS,), in_specs=[bl...  15.6 us
  transfers between devices with their start and end apart: 6, of which 3 were waited for; matrix products, arithmetic and copies ran while one was open for 2% of the time, Pallas kernels for 13%

profile of v2, /device:TPU:0, one launch (start us, length us, event | category | flops | bytes accessed | tf_op | source)
XLA Modules:
  0.0 722.4 jit_solution(5184389867923690897)
XLA Ops:
  1.6 11.9 %conditional.5 = ((bf16[2,4,256,256]{3,2,1,0:T(8,128)(2,1)S(1)}, bf16[2,4,256,256]{3,2,1,0:T(8,128)(2,1)}, f32[2,4,1,256]{3,2,1,0:T(1,128)S(1)})) conditional(s32[]{:T(128)} %convert_element_type.15, () %tuple.46, (s32[2,16,64]{2,1,0:T(8,128)}) %tuple.57), branch_computations={%region_0.0_spmd, %region_1.0_spmd.clone} | conditional | bytes 2105384 | solution.py:979
  4.3 9.2 %feature_tables.1 = (bf16[2,4,256,256]{3,2,1,0:T(8,128)(2,1)S(1)}, bf16[2,4,256,256]{3,2,1,0:T(8,128)(2,1)}, f32[2,4,1,256]{3,2,1,0:T(1,128)S(1)}) custom-call(s32[2,1024,1]{2,1,0:T(8,128)} %reshape.108.seeds_ref, f32[256,256]{1,0:T(8,128)} %constant.22.clone.2.cosine_ref), custom_call_target="tpu_custom_call" | custom-call | tf_op jit(solution)/shard_map/cond/branch_1_fun/feature_tables/pallas_call | solution.py:107
  13.5 55.3 %conditional.6 = ((f32[1024,1024]{1,0:T(8,128)}, bf16[1024,1024]{1,0:T(8,128)(2,1)}, bf16[4,1024,1024]{2,1,0:T(8,128)(2,1)}, bf16[4,1024,1024]{2,1,0:T(8,128)(2,1)})) conditional(s32[]{:T(128)} %convert_element_type.15, (bf16[2,1024]{1,0:T(2,128)(2,1)S(1)}, bf16[2,1024]{1,0:T(2,128)(2,1)S(1)}, f32[2,4096]{1,0:T(2,128)S(1)}, ...), branch_computations={%region_2.0_spmd, %region_3.0_spmd} | conditional | bytes 32808 | solution.py:1011
  14.4 29.0 %project_forward.2 = (bf16[1024,1024]{1,0:T(8,128)(2,1)}, bf16[4,1024,1024]{2,1,0:T(8,128)(2,1)}) custom-call(bf16[1024,1024]{1,0:T(8,128)(2,1)S(1)} %get-tuple-element.154.refs_0_, bf16[1,1024]{1,0:T(2,128)(2,1)S(1)} %bitcast.49, bf16[1,1024]{1,0:T(2,128)(2,1)S(1)} %bitcast.57, bf16[1,2,4096,1024]{3,2,1,0:T(8,128)(2,1)} %get-tuple-element.157.refs_3_.weight_ref, ...), custom_call_target="tpu_custom_call" | custom-call | tf_op jit(solution)/shard_map/cond/branch_1_fun/project_forward/pallas_call | solution.py:400
  43.3 19.1 %attend_forward.2.mixed_ref = bf16[4,1024,1024]{2,1,0:T(8,128)(2,1)} custom-call(s32[1,4]{1,0:T(1,128)S(1)} %get-tuple-element.153.starts_ref, bf16[4,1024,1024]{2,1,0:T(8,128)(2,1)} %get-tuple-element.334.state_ref), custom_call_target="tpu_custom_call" | custom-call | tf_op jit(solution)/shard_map/cond/branch_1_fun/attend_forward/pallas_call | solution.py:467
  62.5 6.4 mix_forward.2
  68.9 7.4 %collective-permute-done = f32[1024,1024]{1,0:T(8,128)S(1)} collective-permute-done((f32[1024,1024]{1,0:T(8,128)}, f32[1024,1024]{1,0:T(8,128)S(1)}, u32[]{:S(2)}, u32[]{:S(2)}) %collective-permute-start) | collective-permute-done | bytes 4194336 | tf_op jit(solution)/shard_map/ppermute | solution.py:1018
  76.2 59.4 %conditional.7 = ((f32[1024,1024]{1,0:T(8,128)}, f32[1024,1024]{1,0:T(8,128)}, bf16[1024,1024]{1,0:T(8,128)(2,1)}, bf16[4,1024,1024]{2,1,0:T(8,128)(2,1)}, bf16[4,1024,1024]{2,1,0:T(8,128)(2,1)})) conditional(s32[]{:T(128)} %convert_element_type.15, (bf16[2,1024]{1,0:T(2,128)(2,1)S(1)}, bf16[2,1024]{1,0:T(2,128)(2,1)S(1)}, f32[2,4096]{1,0:T(2,128)S(1)}, ...), branch_computations={%region_4.0_spmd, %region_5.0_spmd} | conditional | bytes 45064 | solution.py:1011
  78.4 31.6 %project_forward.3 = (f32[1024,1024]{1,0:T(8,128)}, bf16[1024,1024]{1,0:T(8,128)(2,1)}, bf16[4,1024,1024]{2,1,0:T(8,128)(2,1)}) custom-call(bf16[1024,1024]{1,0:T(8,128)(2,1)S(1)} %get-tuple-element.175.refs_0_, f32[1024,1024]{1,0:T(8,128)} %get-tuple-element.176.refs_1_, f32[1024,1024]{1,0:T(8,128)S(1)} %get-tuple-element.177.refs_2_, ...), custom_call_target="tpu_custom_call" | custom-call | tf_op jit(solution)/shard_map/cond/branch_1_fun/project_forward/pallas_call | solution.py:400
  110.0 19.2 %attend_forward.3.mixed_ref = bf16[4,1024,1024]{2,1,0:T(8,128)(2,1)} custom-call(s32[1,4]{1,0:T(1,128)S(1)} %get-tuple-element.188.starts_ref, bf16[4,1024,1024]{2,1,0:T(8,128)(2,1)} %get-tuple-element.344.state_ref), custom_call_target="tpu_custom_call" | custom-call | tf_op jit(solution)/shard_map/cond/branch_1_fun/attend_forward/pallas_call | solution.py:467
  129.2 6.5 mix_forward.3
  135.7 79.8 %conditional.8 = (f32[1024,1024]{1,0:T(8,128)}, f32[16,1024,256]{2,1,0:T(8,128)}, f32[16,512,256]{2,1,0:T(8,128)}, f32[16,512,256]{2,1,0:T(8,128)}, f32[16,256]{1,0:T(8,128)S(1)}) conditional(s32[]{:T(128)} %convert_element_type.15, (bf16[1024,1024]{1,0:T(8,128)(2,1)}, bf16[1024,1024]{1,0:T(8,128)(2,1)}, bf16[4,1024,1024]{2,1,0:T(8,128)(2,1)}, ...), branch_computations={%region_6.0_spmd, %region_7.0_spmd} | conditional | bytes 12615804 | solution.py:1042
  135.8 11.4 %mix_backward.2.numer_ref = bf16[2,1024,1024]{2,1,0:T(8,128)(2,1)} custom-call(bf16[1024,1024]{1,0:T(8,128)(2,1)} %get-tuple-element.202.grad_ref, bf16[1,2,4096,1024]{3,2,1,0:T(8,128)(2,1)} %get-tuple-element.207.weight_ref, bf16[4,1024,1024]{2,1,0:T(8,128)(2,1)} %get-tuple-element.204.mixed_ref), custom_call_target="tpu_custom_call" | custom-call | tf_op jit(solution)/shard_map/cond/branch_1_fun/mix_backward/pallas_call | solution.py:523
  147.2 33.3 %attend_backward.2.feat_ref = bf16[3,1024,1024]{2,1,0:T(8,128)(2,1)} custom-call(s32[1,4]{1,0:T(1,128)S(1)} %get-tuple-element.205.starts_ref, bf16[4,1024,1024]{2,1,0:T(8,128)(2,1)} %get-tuple-element.206.state_ref.keys_ref, bf16[2,1024,1024]{2,1,0:T(8,128)(2,1)} %mix_backward.2.numer_ref), custom_call_target="tpu_custom_call" | custom-call | tf_op jit(solution)/shard_map/cond/branch_1_fun/attend_backward/pallas_call | solution.py:578
  180.5 34.2 %project_backward.2 = (f32[1024,1024]{1,0:T(8,128)}, f32[16,1024,256]{2,1,0:T(8,128)}, f32[16,1,256]{2,1,0:T(1,128)}, f32[16,512,256]{2,1,0:T(8,128)}, f32[16,512,256]{2,1,0:T(8,128)}) custom-call(bf16[1024,1024]{1,0:T(8,128)(2,1)S(1)} %copy-done.1, bf16[1024,1024]{1,0:T(8,128)(2,1)} %get-tuple-element.203.h_ref, ...), custom_call_target="tpu_custom_call" | custom-call | tf_op jit(solution)/shard_map/cond/branch_1_fun/project_backward/pallas_call | solution.py:666
  224.8 8.7 %norm_backward.2 = (bf16[1024,1024]{1,0:T(8,128)(2,1)}, f32[8,1024]{1,0:T(8,128)}) custom-call(f32[1024,1024]{1,0:T(8,128)} %get-tuple-element.282.x_ref, f32[1024,1024]{1,0:T(8,128)} %get-tuple-element.287.own_ref, f32[1024,1024]{1,0:T(8,128)} %copy-done.10, bf16[1024,1024]{1,0:T(8,128)(2,1)} %grad_ref.1, bf16[1,1024]{1,0:T(2,128)(2,1)} %get-tuple-element.317.gain_ref), custom_call_target="tpu_custom_call" | custom-call | tf_op jit(solution)/shard_map/norm_backward/pallas_call | solution.py:732
  233.5 81.1 %conditional.9 = (f32[1024,1024]{1,0:T(8,128)}, f32[16,1024,256]{2,1,0:T(8,128)}, f32[16,512,256]{2,1,0:T(8,128)}, f32[16,512,256]{2,1,0:T(8,128)}, f32[16,256]{1,0:T(8,128)S(1)}) conditional(s32[]{:T(128)} %convert_element_type.15, (bf16[1024,1024]{1,0:T(8,128)(2,1)}, bf16[1024,1024]{1,0:T(8,128)(2,1)S(1)}, bf16[4,1024,1024]{2,1,0:T(8,128)(2,1)}, ...), branch_computations={%region_8.9_spmd, %region_9.10_spmd} | conditional | bytes 21004440 | solution.py:1042
  235.0 11.3 %mix_backward.3.numer_ref = bf16[2,1024,1024]{2,1,0:T(8,128)(2,1)} custom-call(bf16[1024,1024]{1,0:T(8,128)(2,1)} %get-tuple-element.227.grad_ref, bf16[1,2,4096,1024]{3,2,1,0:T(8,128)(2,1)} %get-tuple-element.232.weight_ref, bf16[4,1024,1024]{2,1,0:T(8,128)(2,1)} %get-tuple-element.229.mixed_ref), custom_call_target="tpu_custom_call" | custom-call | tf_op jit(solution)/shard_map/cond/branch_1_fun/mix_backward/pallas_call | solution.py:523
  246.4 33.3 %attend_backward.3.feat_ref = bf16[3,1024,1024]{2,1,0:T(8,128)(2,1)} custom-call(s32[1,4]{1,0:T(1,128)S(1)} %get-tuple-element.230.starts_ref, bf16[4,1024,1024]{2,1,0:T(8,128)(2,1)} %get-tuple-element.231.state_ref.keys_ref, bf16[2,1024,1024]{2,1,0:T(8,128)(2,1)} %mix_backward.3.numer_ref), custom_call_target="tpu_custom_call" | custom-call | tf_op jit(solution)/shard_map/cond/branch_1_fun/attend_backward/pallas_call | solution.py:578
  279.7 34.2 %project_backward.3 = (f32[1024,1024]{1,0:T(8,128)}, f32[16,1024,256]{2,1,0:T(8,128)}, f32[16,1,256]{2,1,0:T(1,128)}, f32[16,512,256]{2,1,0:T(8,128)}, f32[16,512,256]{2,1,0:T(8,128)}) custom-call(bf16[1024,1024]{1,0:T(8,128)(2,1)} %get-tuple-element.227.grad_ref, bf16[1024,1024]{1,0:T(8,128)(2,1)S(1)} %copy-done.8, ...), custom_call_target="tpu_custom_call" | custom-call | tf_op jit(solution)/shard_map/cond/branch_1_fun/project_backward/pallas_call | solution.py:666
  320.8 15.1 %collective-permute-done.1 = f32[1024,1024]{1,0:T(8,128)} collective-permute-done((f32[1024,1024]{1,0:T(8,128)}, f32[1024,1024]{1,0:T(8,128)}, u32[]{:S(2)}, u32[]{:S(2)}) %collective-permute-start.1) | collective-permute-done | bytes 4194336 | tf_op jit(solution)/shard_map/ppermute | solution.py:1018
  336.0 8.6 %add_add_fusion = f32[1024,1024]{1,0:T(8,128)} fusion(f32[1024,1024]{1,0:T(8,128)} %get-tuple-element.282.x_ref, f32[1024,1024]{1,0:T(8,128)} %get-tuple-element.283, f32[1024,1024]{1,0:T(8,128)} %collective-permute-done.1), kind=kLoop, calls=%fused_computation.2 | loop fusion | flops 2097152 | bytes 16777216 | tf_op jit(solution)/shard_map/add | solution.py:1019
  344.6 6.9 norm_backward.3
  354.1 361.0 %reduce_scatter.1 = (f32[2,256,1024]{2,1,0:T(8,128)}, f32[2,128,1024]{2,1,0:T(8,128)}, f32[8,128]{1,0:T(8,128)}) custom-call(f32[2,2,2,2,1024,256]{5,4,3,2,1,0:T(8,128)} %bitcast.38, f32[2,2,2,2,512,256]{5,4,3,2,1,0:T(8,128)} %bitcast.7.refs_1_, f32[2,2,2,2,512,256]{5,4,3,2,1,0:T(8,128)} %bitcast.40, f32[2,2,2,2,1024,256]{5,4,3,2,1,0:T(8,128)} %bitcast.39, ...), custom_call_target="tpu_custom_call" | custom-call | tf_op jit(solution)/shard_map/reduce_scatter/pallas_call | solution.py:952
  (79 shorter events, 33.8 us)
Async XLA Ops:
  0.6 12.9 %copy-start.12 = (bf16[2,1024]{1,0:T(2,128)(2,1)S(1)}, bf16[2,1024]{1,0:T(2,128)(2,1)}, u32[]{:S(2)}) copy-start(bf16[2,1024]{1,0:T(2,128)(2,1)} %param.29) | copy-start | bytes 12292
  0.6 12.8 %copy-start.13 = (bf16[2,1024]{1,0:T(2,128)(2,1)S(1)}, bf16[2,1024]{1,0:T(2,128)(2,1)}, u32[]{:S(2)}) copy-start(bf16[2,1024]{1,0:T(2,128)(2,1)} %param.30) | copy-start | bytes 12292
  0.7 12.8 %copy-start.14 = (bf16[2,1024]{1,0:T(2,128)(2,1)S(1)}, bf16[2,1024]{1,0:T(2,128)(2,1)}, u32[]{:S(2)}) copy-start(bf16[2,1024]{1,0:T(2,128)(2,1)} %param.28) | copy-start | bytes 12292
  0.7 12.8 %copy-start = (bf16[1024,1024]{1,0:T(8,128)(2,1)S(1)}, bf16[1024,1024]{1,0:T(8,128)(2,1)}, u32[]{:S(2)}) copy-start(bf16[1024,1024]{1,0:T(8,128)(2,1)} %x_ref.1) | copy-start | bytes 6291460
  0.7 12.8 %copy-start.16 = (s32[1,4]{1,0:T(1,128)S(1)}, s32[1,4]{1,0:T(1,128)}, u32[]{:S(2)}) copy-start(s32[1,4]{1,0:T(1,128)} %param.32) | copy-start | bytes 52
  68.9 7.4 %collective-permute-start = (f32[1024,1024]{1,0:T(8,128)}, f32[1024,1024]{1,0:T(8,128)S(1)}, u32[]{:S(2)}, u32[]{:S(2)}) collective-permute-start(f32[1024,1024]{1,0:T(8,128)} %get-tuple-element.281), channel_id=1, source_target_pairs={{0,1},{1,0},{2,3},{3,2},{4,5},{5,4},{6,7},{7,6},{8,9},{9,8},{10,11... | collective-permute-start | bytes 12582920 | tf_op jit(solution)/shard_map/ppermute | solution.py:1018
  147.2 33.3 %copy-start.1 = (bf16[1024,1024]{1,0:T(8,128)(2,1)S(1)}, bf16[1024,1024]{1,0:T(8,128)(2,1)}, u32[]{:S(2)}) copy-start(bf16[1024,1024]{1,0:T(8,128)(2,1)} %get-tuple-element.202.grad_ref) | copy-start | bytes 6291460 | tf_op jit(solution)/shard_map/cond
  147.2 33.3 %copy-start.2 = (f32[1024,128]{1,0:T(8,128)S(1)}, f32[1024,128]{1,0:T(8,128)}, u32[]{:S(2)}) copy-start(f32[1024,128]{1,0:T(8,128)} %get-tuple-element.209.cosine_ref) | copy-start | bytes 1572868 | tf_op jit(solution)/shard_map/cond
  147.2 33.3 %copy-start.4 = (f32[1024,128]{1,0:T(8,128)S(1)}, f32[1024,128]{1,0:T(8,128)}, u32[]{:S(2)}) copy-start(f32[1024,128]{1,0:T(8,128)} %get-tuple-element.210.sine_ref) | copy-start | bytes 1572868 | tf_op jit(solution)/shard_map/cond
  215.4 7.4 %collective-permute-start.2 = (f32[1024,1024]{1,0:T(8,128)}, f32[1024,1024]{1,0:T(8,128)S(1)}, u32[]{:S(2)}, u32[]{:S(2)}) collective-permute-start(f32[1024,1024]{1,0:T(8,128)} %get-tuple-element.287.own_ref), channel_id=1, source_target_pairs={{0,1},{1,0},{2,3},{3,2},{4,5},{5,4},{6,7},{7,6},{8,9},{9,8},{10,11... | collective-permute-start | bytes 12582920 | tf_op jit(solution)/shard_map/ppermute | solution.py:1047
  216.0 138.1 %collective-permute-start.4 = (f32[16,512,256]{2,1,0:T(8,128)}, f32[16,512,256]{2,1,0:T(8,128)}, u32[]{:S(2)}, u32[]{:S(2)}) collective-permute-start(f32[16,512,256]{2,1,0:T(8,128)} %get-tuple-element.295), channel_id=1, source_target_pairs={{1,0},{3,2},{5,4},{7,6},{9,8},{11,10},{13,12},{15,14},{17,16},{19,... | collective-permute-start | bytes 25165832 | tf_op jit(solution)/shard_map/ppermute | solution.py:1049
  222.8 2.0 copy-start.10
  224.8 8.7 %copy-start.6 = (bf16[1024,1024]{1,0:T(8,128)(2,1)S(1)}, bf16[1024,1024]{1,0:T(8,128)(2,1)}, u32[]{:S(2)}) copy-start(bf16[1024,1024]{1,0:T(8,128)(2,1)} %get-tuple-element.289) | copy-start | bytes 6291460
  233.5 87.2 %copy-start.15 = (f32[8,1024]{1,0:T(8,128)S(1)}, f32[8,1024]{1,0:T(8,128)}, u32[]{:S(2)}) copy-start(f32[8,1024]{1,0:T(8,128)} %get-tuple-element.302) | copy-start | bytes 98308
  233.7 1.3 copy-start.7
  246.4 33.3 %copy-start.3 = (f32[1024,128]{1,0:T(8,128)S(1)}, f32[1024,128]{1,0:T(8,128)}, u32[]{:S(2)}) copy-start(f32[1024,128]{1,0:T(8,128)} %get-tuple-element.234.cosine_ref) | copy-start | bytes 1572868 | tf_op jit(solution)/shard_map/cond
  246.4 33.3 %copy-start.5 = (f32[1024,128]{1,0:T(8,128)S(1)}, f32[1024,128]{1,0:T(8,128)}, u32[]{:S(2)}) copy-start(f32[1024,128]{1,0:T(8,128)} %get-tuple-element.235.sine_ref) | copy-start | bytes 1572868 | tf_op jit(solution)/shard_map/cond
  246.4 33.3 %copy-start.8 = (bf16[1024,1024]{1,0:T(8,128)(2,1)S(1)}, bf16[1024,1024]{1,0:T(8,128)(2,1)}, u32[]{:S(2)}) copy-start(bf16[1024,1024]{1,0:T(8,128)(2,1)} %copy-done.7) | copy-start | bytes 6291460 | tf_op jit(solution)/shard_map/cond
  314.6 39.5 %collective-permute-start.5 = (f32[16,512,256]{2,1,0:T(8,128)}, f32[16,512,256]{2,1,0:T(8,128)}, u32[]{:S(2)}, u32[]{:S(2)}) collective-permute-start(f32[16,512,256]{2,1,0:T(8,128)} %get-tuple-element.298), channel_id=1, source_target_pairs={{1,0},{3,2},{5,4},{7,6},{9,8},{11,10},{13,12},{15,14},{17,16},{19,... | collective-permute-start | bytes 25165832 | tf_op jit(solution)/shard_map/ppermute | solution.py:1049
  316.1 19.8 %collective-permute-start.1 = (f32[1024,1024]{1,0:T(8,128)}, f32[1024,1024]{1,0:T(8,128)}, u32[]{:S(2)}, u32[]{:S(2)}) collective-permute-start(f32[1024,1024]{1,0:T(8,128)} %get-tuple-element.283), channel_id=1, source_target_pairs={{0,1},{1,0},{2,3},{3,2},{4,5},{5,4},{6,7},{7,6},{8,9},{9,8},{10,11... | collective-permute-start | bytes 12582920 | tf_op jit(solution)/shard_map/ppermute | solution.py:1018
  320.6 24.1 %collective-permute-start.3 = (f32[1024,1024]{1,0:T(8,128)}, f32[1024,1024]{1,0:T(8,128)}, u32[]{:S(2)}, u32[]{:S(2)}) collective-permute-start(f32[1024,1024]{1,0:T(8,128)} %get-tuple-element.292.own_ref), channel_id=1, source_target_pairs={{0,1},{1,0},{2,3},{3,2},{4,5},{5,4},{6,7},{7,6},{8,9},{9,8},{10,11... | collective-permute-start | bytes 12582920 | tf_op jit(solution)/shard_map/ppermute | solution.py:1047
  320.8 23.8 %copy-start.9 = (f32[1024,1024]{1,0:T(8,128)S(1)}, f32[1024,1024]{1,0:T(8,128)}, u32[]{:S(2)}) copy-start(f32[1024,1024]{1,0:T(8,128)} %get-tuple-element.292.own_ref) | copy-start | bytes 12582916
  715.1 5.9 copy-start.11

commit v3 on v2

--- a/solution.py
+++ b/solution.py
@@ -1,5 +1,6 @@
 import functools
 import math
+from typing import NamedTuple
 
 import jax
 import jax.numpy as jnp
@@ -747,7 +748,57 @@
 UNIT = 8
 SLOTS = 4
 LAG = 1
-ORDERS = ((0, 1, 2, 3), (1, 0, 2, 3), (0, 2, 3, 1), (1, 2, 3, 0), (0, 2, 3, 1), (1, 2, 3, 0))
+
+
+class Flow(NamedTuple):
+    order: tuple
+    layer: int
+    begun: int
+    start: int
+    segments: tuple
+
+
+def first_rows(rows):
+    cuts = (0, rows * 11 // 32, rows * 22 // 32, rows)
+    return tuple(zip(cuts[:-1], cuts[1:]))
+
+
+def begun_flows(rows, layer):
+    orders = (((0, 1, 2, 3),) * 2, ((1, 0, 2, 3),) * 2, ((2, 0, 1, 3), (2, 1, 0, 3)))
+    flows = []
+    for way in range(3):
+        for part in range(2):
+            segments = []
+            for is_up in range(2):
+                first, finish = first_rows(rows[is_up])[way]
+                half = (finish - first) // 2
+                base = first_rows(rows[0])[way]
+                base = base[1] - base[0] if is_up else 0
+                segments.append(
+                    (bool(is_up), first + part * half, half // UNIT, base + part * half)
+                )
+            flows.append(Flow(orders[way][part], layer, way, 0, tuple(segments)))
+    return flows
+
+
+def fresh_flows(rows, layer, start):
+    orders = ((0, 1, 2, 3), (1, 0, 2, 3)) + ((0, 2, 3, 1), (1, 2, 3, 0)) * 2
+    count = len(orders)
+    flows, at = [], [0, 0]
+    for index, order in enumerate(orders):
+        segments = []
+        for is_up in range(2):
+            units = rows[is_up] // UNIT
+            place = index if is_up == 0 else count - 1 - index
+            share = units // count + (place < units % count)
+            segments.append((bool(is_up), at[is_up] * UNIT, share, 0))
+            at[is_up] += share
+        flows.append(Flow(order, layer, -1, start, tuple(segments)))
+    return flows
+
+
+def units_of(flow):
+    return sum(segment[2] for segment in flow.segments)
 
 
 def bit_of(index, bit):
@@ -758,21 +809,19 @@
     return index + (1 << bit) * (1 - 2 * bit_of(index, bit))
 
 
-def scatter_kernel(bits, rows, layers, *refs):
+def scatter_kernel(bits, flows, layers, *refs):
     sources, refs = refs[: 3 * layers], refs[3 * layers :]
+    halves, refs = refs[:3], refs[3:]
     small_ref, weight_out, up_out, small_out = refs[:4]
-    held, refs = refs[4:], None
-    flows, stages = len(ORDERS), bits
-    weight_sum, up_sum = held[:2]
-    small_held = held[2 : 2 + stages]
-    held = held[2 + stages :]
-    held, sems = held[: flows * (stages + 1)], held[flows * (stages + 1) :]
+    stages = bits
+    weight_sum, up_sum = refs[4:6]
+    small_held = refs[6 : 6 + stages]
+    held = refs[6 + stages :]
+    held, sems = held[: len(flows) * (stages + 1)], held[len(flows) * (stages + 1) :]
     load_sem, send_sem, recv_sem, credit, small_send, small_recv = sems
-    held = [held[f * (stages + 1) : (f + 1) * (stages + 1)] for f in range(flows)]
+    held = [held[f * (stages + 1) : (f + 1) * (stages + 1)] for f in range(len(flows))]
     me, core = lax.axis_index("batch"), lax.axis_index("stream")
-    weight_units, up_units = rows[0] // UNIT, rows[1] // UNIT
-    per_layer = weight_units + up_units
-    total = per_layer * layers // flows
+    totals = [units_of(flow) for flow in flows]
 
     barrier = pltpu.get_barrier_semaphore()
     for bit in range(bits):
@@ -793,25 +842,33 @@
             dst_ref=held[flow][stage + 1].at[slot],
             send_sem=send_sem.at[flow, stage, slot],
             recv_sem=recv_sem.at[flow, stage, slot],
-            device_id={"batch": flip(me, ORDERS[flow][stage])},
+            device_id={"batch": flip(me, flows[flow].order[stage])},
             device_id_type=MESH,
         )
 
     def sent_from(flow, stage, slot):
         if stage == 0:
             return held[flow][0].at[slot]
-        return held[flow][stage].at[(slot,) + view(ORDERS[flow], stage, False)]
+        return held[flow][stage].at[(slot,) + view(flows[flow].order, stage, False)]
 
     def load(flow, slot, source):
         return pltpu.make_async_copy(source, held[flow][0].at[slot], load_sem.at[flow, slot])
 
+    def load_half(flow, slot, source):
+        return pltpu.make_async_copy(
+            source, held[flow][1].at[slot], recv_sem.at[flow, 0, slot]
+        )
+
     def return_credit(flow, stage, unit):
-        @pl.when(unit + SLOTS < total)
+        if stage == 0 and flows[flow].begun >= 0:
+            return
+
+        @pl.when(unit + SLOTS < totals[flow])
         def _():
             pl.semaphore_signal(
                 credit.at[flow, stage],
                 inc=1,
-                device_id={"batch": flip(me, ORDERS[flow][stage])},
+                device_id={"batch": flip(me, flows[flow].order[stage])},
                 device_id_type=MESH,
             )
 
@@ -820,27 +877,32 @@
         def _():
             pl.semaphore_wait(credit.at[flow, stage], 1)
 
-    def places(place, act):
-        for layer in range(layers):
-            base = layer * per_layer
-            middle = base + weight_units
-            pl.when((place >= base) & (place < middle))(
-                functools.partial(act, layer, False, (place - base) * UNIT)
+    def places(flow, unit, act):
+        base = 0
+        for is_up, row, units, half_row in flows[flow].segments:
+            offset = (unit - base) * UNIT
+            pl.when((unit >= base) & (unit < base + units))(
+                functools.partial(act, is_up, row + offset, half_row + offset)
             )
-            pl.when((place >= middle) & (place < base + per_layer))(
-                functools.partial(act, layer, True, (place - middle) * UNIT)
-            )
+            base += units
 
     def begin(flow, unit):
         slot = lax.rem(unit, SLOTS)
-        take_credit(flow, 0, unit)
+        order, layer, begun = flows[flow][:3]
+        if begun < 0:
+            take_credit(flow, 0, unit)
 
         def start(source, row):
             at = (pl.ds(pl.multiple_of(row, UNIT), UNIT),)
-            remote(flow, 0, slot, source.at[view(ORDERS[flow], 0, False) + at]).start()
-            load(flow, slot, source.at[view(ORDERS[flow], 0, True) + at]).start()
-
-        def act(layer, is_up, row):
+            load(flow, slot, source.at[view(order, 0, True) + at]).start()
+            if begun < 0:
+                remote(flow, 0, slot, source.at[view(order, 0, False) + at]).start()
+
+        def act(is_up, row, half_row):
+            if begun >= 0:
+                at = (slice(None),) * (bits - 1)
+                at += (pl.ds(pl.multiple_of(half_row, UNIT), UNIT),)
+                load_half(flow, slot, halves[begun].at[at]).start()
             if not is_up:
                 start(sources[3 * layer], row)
             else:
@@ -849,17 +911,19 @@
                         functools.partial(start, sources[3 * layer + 1 + side], row)
                     )
 
-        places(unit * flows + flow, act)
+        places(flow, unit, act)
 
     def advance(flow, stage, unit):
         slot = lax.rem(unit, SLOTS)
-        order, buffer = ORDERS[flow], held[flow][stage]
+        order, layer, begun = flows[flow][:3]
+        buffer = held[flow][stage]
         copy = remote(flow, stage - 1, slot, sent_from(flow, stage - 1, slot))
-        copy.wait_recv()
+        if stage == 1 and begun >= 0:
+            load_half(flow, slot, held[flow][0].at[slot]).wait()
+        else:
+            copy.wait_recv()
         if stage == 1:
-            kept = (slice(None),) * (bits - 1) + (pl.ds(0, UNIT),)
-            kept = tuple(view(order, 0, True)) + kept[bits - 1 :]
-            load(flow, slot, sources[0].at[kept]).wait()
+            load(flow, slot, held[flow][1].at[slot]).wait()
             mine = held[flow][0][slot]
         else:
             mine = held[flow][stage - 1][(slot,) + view(order, stage - 1, True)]
@@ -870,25 +934,28 @@
             remote(flow, stage, slot, sent_from(flow, stage, slot)).start()
         else:
 
-            def act(layer, is_up, row):
+            def act(is_up, row, half_row):
                 target = up_sum if is_up else weight_sum
                 target[layer, pl.ds(pl.multiple_of(row, UNIT), UNIT)] = value
 
-            places(unit * flows + flow, act)
-        copy.wait_send()
+            places(flow, unit, act)
+        if stage > 1 or begun < 0:
+            copy.wait_send()
         if stage >= 2:
             return_credit(flow, stage - 2, unit)
         if stage == stages:
             return_credit(flow, stage - 1, unit)
 
+    small_order = tuple(range(bits))
+
     def small_copy(stage):
         source = small_ref if stage == 0 else small_held[stage - 1]
         return pltpu.make_async_remote_copy(
-            src_ref=source.at[view(ORDERS[0], stage, False)],
+            src_ref=source.at[view(small_order, stage, False)],
             dst_ref=small_held[stage],
             send_sem=small_send.at[stage],
             recv_sem=small_recv.at[stage],
-            device_id={"batch": flip(me, ORDERS[0][stage])},
+            device_id={"batch": flip(me, small_order[stage])},
             device_id_type=MESH,
         )
 
@@ -896,7 +963,7 @@
         if stage > 0:
             small_copy(stage - 1).wait()
             source = small_ref if stage == 1 else small_held[stage - 2]
-            sums = small_held[stage - 1][...] + source[view(ORDERS[0], stage - 1, True)]
+            sums = small_held[stage - 1][...] + source[view(small_order, stage - 1, True)]
             if stage == stages:
                 small_out[...] = sums
             else:
@@ -905,19 +972,23 @@
             small_copy(stage).start()
 
     def step(index, carry):
-        for flow in range(flows):
-            pl.when(index < total)(functools.partial(begin, flow, index))
-        for flow in range(flows):
+        for place, flow in enumerate(flows):
+            unit = index - flow.start
+            pl.when((unit >= 0) & (unit < totals[place]))(
+                functools.partial(begin, place, unit)
+            )
+        for place, flow in enumerate(flows):
             for stage in range(1, stages + 1):
-                unit = index - LAG * stage
-                pl.when((unit >= 0) & (unit < total))(
-                    functools.partial(advance, flow, stage, unit)
+                unit = index - flow.start - LAG * stage
+                pl.when((unit >= 0) & (unit < totals[place]))(
+                    functools.partial(advance, place, stage, unit)
                 )
         for stage in range(stages + 1):
             pl.when(index == stages + 2 * stage)(functools.partial(small_step, stage))
         return carry
 
-    lax.fori_loop(0, total + LAG * stages, step, 0)
+    last = max(flow.start + total for flow, total in zip(flows, totals))
+    lax.fori_loop(0, last + LAG * stages, step, 0)
     half = WIDE // 2
     for layer in range(layers):
         weight_out[layers - 1 - layer] = weight_sum[layer].T
@@ -926,32 +997,103 @@
         up_out[layers - 1 - layer, :, folded:] = up_sum[layer, :, half:].T
 
 
-def reduce_scatter(grads, small):
+def pack_halves(weight, near, far):
+    count, width, lanes = weight.shape
+    bits = count.bit_length() - 1
+    rows = (width, near.shape[1])
+    ranges = [first_rows(length) for length in rows]
+
+    def kernel(weight_ref, near_ref, far_ref, *refs):
+        outs, sems = refs[:3], refs[3]
+        me, core = lax.axis_index("batch"), lax.axis_index("stream")
+
+        def copies(source, is_up):
+            for bit in range(3):
+                first, finish = ranges[is_up][bit]
+                base = ranges[0][bit][1] - ranges[0][bit][0] if is_up else 0
+                at = [slice(None)] * bits + [pl.ds(first, finish - first)]
+                at[bits - 1 - bit] = 1 - bit_of(me, bit)
+                to = (slice(None),) * (bits - 1) + (pl.ds(base, finish - first),)
+                yield pltpu.make_async_copy(
+                    source.at[tuple(at)], outs[bit].at[to], sems.at[is_up, bit]
+                )
+
+        def start(source, is_up):
+            for copy in copies(source, is_up):
+                copy.start()
+
+        start(weight_ref, 0)
+        for side, source in enumerate((near_ref, far_ref)):
+            pl.when(core == side)(functools.partial(start, source, 1))
+        for copy in list(copies(weight_ref, 0)) + list(copies(near_ref, 1)):
+            copy.wait()
+
+    shapes = [
+        (2,) * (bits - 1) + (sum(r[bit][1] - r[bit][0] for r in ranges), lanes) for bit in range(3)
+    ]
+    return pl.pallas_call(
+        kernel,
+        in_specs=[pl.BlockSpec(memory_space=pltpu.HBM)] * 3,
+        out_specs=[pl.BlockSpec(memory_space=pltpu.HBM)] * 3,
+        out_shape=[jax.ShapeDtypeStruct(shape, F32) for shape in shapes],
+        scratch_shapes=[pltpu.SemaphoreType.DMA((2, 3))],
+        name="pack_halves",
+    )(*[array.reshape((2,) * bits + array.shape[1:]) for array in (weight, near, far)])
+
+
+def send_halves(weight, near, far):
+    count = weight.shape[0]
+    received = []
+    for bit, part in enumerate(pack_halves(weight, near, far)):
+        pairs = [(source, flip(source, bit)) for source in range(count)]
+        received.append(lax.ppermute(part, "batch", pairs))
+    return received
+
+
+def after(first, others):
+    def kernel(*refs):
+        del refs
+
+    return pl.pallas_call(
+        kernel,
+        in_specs=[pl.BlockSpec(memory_space=pltpu.HBM)] * (1 + len(others)),
+        out_specs=pl.BlockSpec(memory_space=pltpu.HBM),
+        out_shape=jax.ShapeDtypeStruct(first.shape, first.dtype),
+        input_output_aliases={0: 0},
+        name="after",
+    )(first, *others)
+
+
+def reduce_scatter(grads, halves, small):
     layers = len(grads) // 3
     count, width = grads[0].shape[:2]
     folded = grads[1].shape[1]
     bits = count.bit_length() - 1
     small = jnp.pad(small, ((0, 0), (0, -small.shape[1] % 1024)))
     small = small.reshape((2,) * bits + (-1, 128))
+    flows = begun_flows((width, folded), 0)
+    for layer in range(1, layers):
+        start = max(flow.start + units_of(flow) for flow in flows)
+        flows = flows + fresh_flows((width, folded), layer, start)
     scratch = [pltpu.VMEM((layers, width, WIDE), F32), pltpu.VMEM((layers, folded, WIDE), F32)]
     scratch += [
         pltpu.VMEM((2,) * (bits - 1 - stage) + small.shape[-2:], F32) for stage in range(bits)
     ]
-    for _ in ORDERS:
+    for _ in flows:
         for stage in range(bits + 1):
             lead = (SLOTS,) + (2,) * (bits - 1 - max(stage - 1, 0))
             scratch.append(pltpu.VMEM(lead + (UNIT, WIDE), F32))
     scratch += [
-        pltpu.SemaphoreType.DMA((len(ORDERS), SLOTS)),
-        pltpu.SemaphoreType.DMA((len(ORDERS), bits, SLOTS)),
-        pltpu.SemaphoreType.DMA((len(ORDERS), bits, SLOTS)),
-        pltpu.SemaphoreType.REGULAR((len(ORDERS), bits)),
+        pltpu.SemaphoreType.DMA((len(flows), SLOTS)),
+        pltpu.SemaphoreType.DMA((len(flows), bits, SLOTS)),
+        pltpu.SemaphoreType.DMA((len(flows), bits, SLOTS)),
+        pltpu.SemaphoreType.REGULAR((len(flows), bits)),
         pltpu.SemaphoreType.DMA((bits,)),
         pltpu.SemaphoreType.DMA((bits,)),
     ]
     weight, up, small = pl.pallas_call(
-        functools.partial(scatter_kernel, bits, (width, folded), layers),
-        in_specs=[pl.BlockSpec(memory_space=pl.ANY)] * len(grads)
+        functools.partial(scatter_kernel, bits, flows, layers),
+        in_specs=[pl.BlockSpec(memory_space=pltpu.HBM)] * (len(grads) + len(halves))
         + [pl.BlockSpec(memory_space=pltpu.VMEM)],
         out_specs=[pl.BlockSpec(memory_space=pltpu.VMEM)] * 3,
         out_shape=[
@@ -964,7 +1106,7 @@
             collective_id=0, has_side_effects=True, vmem_limit_bytes=VMEM_LIMIT
         ),
         name="reduce_scatter",
-    )(*[array.reshape((2,) * bits + array.shape[1:]) for array in grads], small)
+    )(*[array.reshape((2,) * bits + array.shape[1:]) for array in grads], *halves, small)
     return weight, up, small.reshape(-1)
 
 
@@ -1044,9 +1186,13 @@
             functools.partial(attention_back, layer, grad),
             functools.partial(feed_forward_back, layer, grad),
         )
+        if blocked and layer < LAYERS - 1:
+            part = after(part, halves)
         other = lax.ppermute(part, "stream", swap)
         if blocked:
             near = lax.ppermute(near, "stream", [(1, 0)])
+            if layer == LAYERS - 1:
+                halves = send_halves(weight, near, far)
         kind = BF16 if layer else F32
         new_grad, sums = norm_backward(
             inputs[layer], part, other, grad, norm_gain[layer : layer + 1], kind
@@ -1065,7 +1211,7 @@
         axis=1,
     )
     if blocked:
-        weight, up, small = reduce_scatter(grads, small)
+        weight, up, small = reduce_scatter(grads, halves, small)
     else:
         weight, up, small = scatter_rows(grads, small)
     each = branch_weight.shape[2] // count

time: 729 us -> 1050 us (1.44)
  Pallas kernels: 655 us -> 965 us
  starting transfers between devices: 7.31 us -> 17.9 us
    pallas_call x1 -> x3, Pallas kernels: 361 us -> 671 us  [the longest x1 382 us: pack_halves(): pl.pallas_call(kernel, in_specs=[pl.BlockSpec(memory_space=pltpu.HBM)] *...]
  transfers between devices with their start and end apart: 6 -> 9, of which waited for: 3 -> 3; matrix products, arithmetic and copies ran while one was open for 2% -> 1% of each run, Pallas kernels for 13% -> 46%
where the time goes in v3:
time: 1050 us; the launch traced here: 1040 us
  Pallas kernels  965 us (92%)
  waiting for transfers between devices  31.5 us (3%)
  local copies, waits for them, and re-layouts  18.6 us (2%)
  starting transfers between devices  17.9 us (2%)
    pallas_call x1, Pallas kernels, pack_halves(): pl.pallas_call(kernel, in_specs=[pl.BlockSpec(memory_space=pltpu.HBM)] *...  382 us
    pallas_call x1, Pallas kernels, reduce_scatter(): pl.pallas_call(functools.partial(scatter_kernel, bits, flows, layers), in...  288 us
    pallas_call x2, Pallas kernels, project_backward(): pl.pallas_call(project_backward_kernel, grid=(blocks,), in_specs=[whole((...  68.3 us
    pallas_call x2, Pallas kernels, attend_backward(): pl.pallas_call(attend_backward_kernel, grid=(PAIRS,), in_specs=[pl.BlockS...  66.6 us
    pallas_call x2, Pallas kernels, project_forward(): pl.pallas_call(functools.partial(project_kernel, len(stream)), grid=(4 *...  60.5 us
    pallas_call x2, Pallas kernels, attend_forward(): pl.pallas_call(attend_kernel, grid=(PAIRS,), in_specs=[pl.BlockSpec(memor...  38.3 us
    pallas_call x2, Pallas kernels, mix_backward(): pl.pallas_call(mix_backward_kernel, grid=(QUADS,), in_specs=[whole((lengt...  22.7 us
    ppermute x2, waiting for transfers between devices, shards(): stream = (inputs[-1], part, lax.ppermute(part, 'stream', swap))  21.8 us
  transfers between devices with their start and end apart: 9, of which 3 were waited for; matrix products, arithmetic and copies ran while one was open for 1% of the time, Pallas kernels for 46%

profile of v3, /device:TPU:0, one launch (start us, length us, event | category | flops | bytes accessed | tf_op | source)
XLA Modules:
  0.0 1044.6 jit_solution(7235331837148740736)
XLA Ops:
  1.6 11.9 %conditional.5 = ((bf16[2,4,256,256]{3,2,1,0:T(8,128)(2,1)S(1)}, bf16[2,4,256,256]{3,2,1,0:T(8,128)(2,1)}, f32[2,4,1,256]{3,2,1,0:T(1,128)S(1)})) conditional(s32[]{:T(128)} %convert_element_type.15, () %tuple.46, (s32[2,16,64]{2,1,0:T(8,128)}) %tuple.57), branch_computations={%region_0.0_spmd, %region_1.0_spmd.clone} | conditional | bytes 2105384 | solution.py:1121
  4.3 9.2 feature_tables.1
  13.5 55.3 %conditional.6 = ((f32[1024,1024]{1,0:T(8,128)}, bf16[1024,1024]{1,0:T(8,128)(2,1)}, bf16[4,1024,1024]{2,1,0:T(8,128)(2,1)}, bf16[4,1024,1024]{2,1,0:T(8,128)(2,1)})) conditional(s32[]{:T(128)} %convert_element_type.15, (bf16[2,1024]{1,0:T(2,128)(2,1)S(1)}, bf16[2,1024]{1,0:T(2,128)(2,1)S(1)}, f32[2,4096]{1,0:T(2,128)S(1)}, ...), branch_computations={%region_2.0_spmd, %region_3.0_spmd} | conditional | bytes 32808 | solution.py:1153
  14.4 28.9 %project_forward.2 = (bf16[1024,1024]{1,0:T(8,128)(2,1)}, bf16[4,1024,1024]{2,1,0:T(8,128)(2,1)}) custom-call(bf16[1024,1024]{1,0:T(8,128)(2,1)S(1)} %get-tuple-element.154.refs_0_, bf16[1,1024]{1,0:T(2,128)(2,1)S(1)} %bitcast.51, bf16[1,1024]{1,0:T(2,128)(2,1)S(1)} %bitcast.59, bf16[1,2,4096,1024]{3,2,1,0:T(8,128)(2,1)} %get-tuple-element.157.refs_3_.weight_ref, ...), custom_call_target="tpu_custom_call" | custom-call | tf_op jit(solution)/shard_map/cond/branch_1_fun/project_forward/pallas_call | solution.py:401
  43.3 19.1 %attend_forward.2.mixed_ref = bf16[4,1024,1024]{2,1,0:T(8,128)(2,1)} custom-call(s32[1,4]{1,0:T(1,128)S(1)} %get-tuple-element.153.starts_ref, bf16[4,1024,1024]{2,1,0:T(8,128)(2,1)} %get-tuple-element.340.state_ref), custom_call_target="tpu_custom_call" | custom-call | tf_op jit(solution)/shard_map/cond/branch_1_fun/attend_forward/pallas_call | solution.py:468
  68.8 7.4 collective-permute-done
  76.2 59.3 %conditional.7 = ((f32[1024,1024]{1,0:T(8,128)}, f32[1024,1024]{1,0:T(8,128)}, bf16[1024,1024]{1,0:T(8,128)(2,1)}, bf16[4,1024,1024]{2,1,0:T(8,128)(2,1)}, bf16[4,1024,1024]{2,1,0:T(8,128)(2,1)})) conditional(s32[]{:T(128)} %convert_element_type.15, (bf16[2,1024]{1,0:T(2,128)(2,1)S(1)}, bf16[2,1024]{1,0:T(2,128)(2,1)S(1)}, f32[2,4096]{1,0:T(2,128)S(1)}, ...), branch_computations={%region_4.0_spmd, %region_5.0_spmd} | conditional | bytes 45064 | solution.py:1153
  78.4 31.5 %project_forward.3 = (f32[1024,1024]{1,0:T(8,128)}, bf16[1024,1024]{1,0:T(8,128)(2,1)}, bf16[4,1024,1024]{2,1,0:T(8,128)(2,1)}) custom-call(bf16[1024,1024]{1,0:T(8,128)(2,1)S(1)} %get-tuple-element.175.refs_0_, f32[1024,1024]{1,0:T(8,128)} %get-tuple-element.176.refs_1_, f32[1024,1024]{1,0:T(8,128)S(1)} %get-tuple-element.177.refs_2_, ...), custom_call_target="tpu_custom_call" | custom-call | tf_op jit(solution)/shard_map/cond/branch_1_fun/project_forward/pallas_call | solution.py:401
  109.9 19.1 %attend_forward.3.mixed_ref = bf16[4,1024,1024]{2,1,0:T(8,128)(2,1)} custom-call(s32[1,4]{1,0:T(1,128)S(1)} %get-tuple-element.188.starts_ref, bf16[4,1024,1024]{2,1,0:T(8,128)(2,1)} %get-tuple-element.350.state_ref), custom_call_target="tpu_custom_call" | custom-call | tf_op jit(solution)/shard_map/cond/branch_1_fun/attend_forward/pallas_call | solution.py:468
  135.4 79.7 %conditional.8 = (f32[1024,1024]{1,0:T(8,128)}, f32[16,1024,256]{2,1,0:T(8,128)}, f32[16,512,256]{2,1,0:T(8,128)}, f32[16,512,256]{2,1,0:T(8,128)}, f32[16,256]{1,0:T(8,128)S(1)}) conditional(s32[]{:T(128)} %convert_element_type.15, (bf16[1024,1024]{1,0:T(8,128)(2,1)}, bf16[1024,1024]{1,0:T(8,128)(2,1)}, bf16[4,1024,1024]{2,1,0:T(8,128)(2,1)}, ...), branch_computations={%region_6.0_spmd, %region_7.0_spmd} | conditional | bytes 12615804 | solution.py:1184
  135.6 11.4 %mix_backward.2.numer_ref = bf16[2,1024,1024]{2,1,0:T(8,128)(2,1)} custom-call(bf16[1024,1024]{1,0:T(8,128)(2,1)} %get-tuple-element.202.grad_ref, bf16[1,2,4096,1024]{3,2,1,0:T(8,128)(2,1)} %get-tuple-element.207.weight_ref, bf16[4,1024,1024]{2,1,0:T(8,128)(2,1)} %get-tuple-element.204.mixed_ref), custom_call_target="tpu_custom_call" | custom-call | tf_op jit(solution)/shard_map/cond/branch_1_fun/mix_backward/pallas_call | solution.py:524
  147.0 33.3 %attend_backward.2.feat_ref = bf16[3,1024,1024]{2,1,0:T(8,128)(2,1)} custom-call(s32[1,4]{1,0:T(1,128)S(1)} %get-tuple-element.205.starts_ref, bf16[4,1024,1024]{2,1,0:T(8,128)(2,1)} %get-tuple-element.206.state_ref.keys_ref, bf16[2,1024,1024]{2,1,0:T(8,128)(2,1)} %mix_backward.2.numer_ref), custom_call_target="tpu_custom_call" | custom-call | tf_op jit(solution)/shard_map/cond/branch_1_fun/attend_backward/pallas_call | solution.py:579
  180.3 34.2 %project_backward.2 = (f32[1024,1024]{1,0:T(8,128)}, f32[16,1024,256]{2,1,0:T(8,128)}, f32[16,1,256]{2,1,0:T(1,128)}, f32[16,512,256]{2,1,0:T(8,128)}, f32[16,512,256]{2,1,0:T(8,128)}) custom-call(bf16[1024,1024]{1,0:T(8,128)(2,1)S(1)} %copy-done.1, bf16[1024,1024]{1,0:T(8,128)(2,1)} %get-tuple-element.203.h_ref, ...), custom_call_target="tpu_custom_call" | custom-call | tf_op jit(solution)/shard_map/cond/branch_1_fun/project_backward/pallas_call | solution.py:667
  220.9 9.7 collective-permute-done.3
  230.6 382.3 %pack_halves.1 = (f32[2,2,2,528,256]{4,3,2,1,0:T(8,128)}, f32[2,2,2,528,256]{4,3,2,1,0:T(8,128)}, f32[2,2,2,480,256]{4,3,2,1,0:T(8,128)}) custom-call(f32[2,2,2,2,1024,256]{5,4,3,2,1,0:T(8,128)} %bitcast.38, f32[2,2,2,2,512,256]{5,4,3,2,1,0:T(8,128)} %bitcast.7.near_ref.refs_1_, f32[2,2,2,2,512,256]{5,4,3,2,1,0:T(8,128)} %bitcast.40), custom_call_target="tpu_custom_call" | custom-call | tf_op jit(solution)/shard_map/pack_halves/pallas_call | solution.py:1034
  619.6 8.7 norm_backward.2
  628.3 81.1 %conditional.9 = (f32[1024,1024]{1,0:T(8,128)}, f32[16,1024,256]{2,1,0:T(8,128)}, f32[16,512,256]{2,1,0:T(8,128)}, f32[16,512,256]{2,1,0:T(8,128)}, f32[16,256]{1,0:T(8,128)S(1)}) conditional(s32[]{:T(128)} %convert_element_type.15, (bf16[1024,1024]{1,0:T(8,128)(2,1)}, bf16[1024,1024]{1,0:T(8,128)(2,1)S(1)}, bf16[4,1024,1024]{2,1,0:T(8,128)(2,1)}, ...), branch_computations={%region_8.9_spmd, %region_9.10_spmd} | conditional | bytes 21004440 | solution.py:1184
  629.8 11.3 %mix_backward.3.numer_ref = bf16[2,1024,1024]{2,1,0:T(8,128)(2,1)} custom-call(bf16[1024,1024]{1,0:T(8,128)(2,1)} %get-tuple-element.227.grad_ref, bf16[1,2,4096,1024]{3,2,1,0:T(8,128)(2,1)} %get-tuple-element.232.weight_ref, bf16[4,1024,1024]{2,1,0:T(8,128)(2,1)} %get-tuple-element.229.mixed_ref), custom_call_target="tpu_custom_call" | custom-call | tf_op jit(solution)/shard_map/cond/branch_1_fun/mix_backward/pallas_call | solution.py:524
  641.2 33.3 %attend_backward.3.feat_ref = bf16[3,1024,1024]{2,1,0:T(8,128)(2,1)} custom-call(s32[1,4]{1,0:T(1,128)S(1)} %get-tuple-element.230.starts_ref, bf16[4,1024,1024]{2,1,0:T(8,128)(2,1)} %get-tuple-element.231.state_ref.keys_ref, bf16[2,1024,1024]{2,1,0:T(8,128)(2,1)} %mix_backward.3.numer_ref), custom_call_target="tpu_custom_call" | custom-call | tf_op jit(solution)/shard_map/cond/branch_1_fun/attend_backward/pallas_call | solution.py:579
  674.5 34.2 %project_backward.3 = (f32[1024,1024]{1,0:T(8,128)}, f32[16,1024,256]{2,1,0:T(8,128)}, f32[16,1,256]{2,1,0:T(1,128)}, f32[16,512,256]{2,1,0:T(8,128)}, f32[16,512,256]{2,1,0:T(8,128)}) custom-call(bf16[1024,1024]{1,0:T(8,128)(2,1)} %get-tuple-element.227.grad_ref, bf16[1024,1024]{1,0:T(8,128)(2,1)S(1)} %copy-done.9, ...), custom_call_target="tpu_custom_call" | custom-call | tf_op jit(solution)/shard_map/cond/branch_1_fun/project_backward/pallas_call | solution.py:667
  716.4 14.4 %collective-permute-done.1 = f32[1024,1024]{1,0:T(8,128)} collective-permute-done((f32[1024,1024]{1,0:T(8,128)}, f32[1024,1024]{1,0:T(8,128)}, u32[]{:S(2)}, u32[]{:S(2)}) %collective-permute-start.1) | collective-permute-done | bytes 4194336 | tf_op jit(solution)/shard_map/ppermute | solution.py:1160
  730.8 8.6 add_add_fusion
  739.4 6.9 norm_backward.3
  749.0 288.3 %reduce_scatter.1 = (f32[2,256,1024]{2,1,0:T(8,128)}, f32[2,128,1024]{2,1,0:T(8,128)}, f32[8,128]{1,0:T(8,128)}) custom-call(f32[2,2,2,2,1024,256]{5,4,3,2,1,0:T(8,128)} %bitcast.39, f32[2,2,2,2,512,256]{5,4,3,2,1,0:T(8,128)} %bitcast.7.near_ref.refs_1_, f32[2,2,2,2,512,256]{5,4,3,2,1,0:T(8,128)} %bitcast.41, f32[2,2,2,2,1024,256]{5,4,3,2,1,0:T(8,128)} %bitcast.42, ...), custom_call_target="tpu_custom_call" | custom-call | tf_op jit(solution)/shard_map/reduce_scatter/pallas_call | solution.py:1094
  (85 shorter events, 50.3 us)
Async XLA Ops:
  0.6 12.9 %copy-start.11 = (bf16[2,1024]{1,0:T(2,128)(2,1)S(1)}, bf16[2,1024]{1,0:T(2,128)(2,1)}, u32[]{:S(2)}) copy-start(bf16[2,1024]{1,0:T(2,128)(2,1)} %param.29) | copy-start | bytes 12292
  0.6 12.8 %copy-start.12 = (bf16[2,1024]{1,0:T(2,128)(2,1)S(1)}, bf16[2,1024]{1,0:T(2,128)(2,1)}, u32[]{:S(2)}) copy-start(bf16[2,1024]{1,0:T(2,128)(2,1)} %param.30) | copy-start | bytes 12292
  0.7 12.8 %copy-start.13 = (bf16[2,1024]{1,0:T(2,128)(2,1)S(1)}, bf16[2,1024]{1,0:T(2,128)(2,1)}, u32[]{:S(2)}) copy-start(bf16[2,1024]{1,0:T(2,128)(2,1)} %param.28) | copy-start | bytes 12292
  0.7 12.8 %copy-start = (bf16[1024,1024]{1,0:T(8,128)(2,1)S(1)}, bf16[1024,1024]{1,0:T(8,128)(2,1)}, u32[]{:S(2)}) copy-start(bf16[1024,1024]{1,0:T(8,128)(2,1)} %x_ref.1) | copy-start | bytes 6291460
  0.7 12.8 %copy-start.15 = (s32[1,4]{1,0:T(1,128)S(1)}, s32[1,4]{1,0:T(1,128)}, u32[]{:S(2)}) copy-start(s32[1,4]{1,0:T(1,128)} %param.32) | copy-start | bytes 52
  68.8 7.4 collective-permute-start
  147.0 33.3 %copy-start.1 = (bf16[1024,1024]{1,0:T(8,128)(2,1)S(1)}, bf16[1024,1024]{1,0:T(8,128)(2,1)}, u32[]{:S(2)}) copy-start(bf16[1024,1024]{1,0:T(8,128)(2,1)} %get-tuple-element.202.grad_ref) | copy-start | bytes 6291460 | tf_op jit(solution)/shard_map/cond
  147.0 33.3 %copy-start.3 = (f32[1024,128]{1,0:T(8,128)S(1)}, f32[1024,128]{1,0:T(8,128)}, u32[]{:S(2)}) copy-start(f32[1024,128]{1,0:T(8,128)} %get-tuple-element.209.cosine_ref) | copy-start | bytes 1572868 | tf_op jit(solution)/shard_map/cond
  147.0 33.3 %copy-start.5 = (f32[1024,128]{1,0:T(8,128)S(1)}, f32[1024,128]{1,0:T(8,128)}, u32[]{:S(2)}) copy-start(f32[1024,128]{1,0:T(8,128)} %get-tuple-element.210.sine_ref) | copy-start | bytes 1572868 | tf_op jit(solution)/shard_map/cond
  215.2 15.4 %collective-permute-start.3 = (f32[16,512,256]{2,1,0:T(8,128)}, f32[16,512,256]{2,1,0:T(8,128)}, u32[]{:S(2)}, u32[]{:S(2)}) collective-permute-start(f32[16,512,256]{2,1,0:T(8,128)} %get-tuple-element.297), channel_id=1, source_target_pairs={{1,0},{3,2},{5,4},{7,6},{9,8},{11,10},{13,12},{15,14},{17,16},{19,... | collective-permute-start | bytes 25165832 | tf_op jit(solution)/shard_map/ppermute | solution.py:1193
  216.5 403.1 %collective-permute-start.2 = (f32[1024,1024]{1,0:T(8,128)}, f32[1024,1024]{1,0:T(8,128)}, u32[]{:S(2)}, u32[]{:S(2)}) collective-permute-start(f32[1024,1024]{1,0:T(8,128)} %get-tuple-element.290.own_ref), channel_id=1, source_target_pairs={{0,1},{1,0},{2,3},{3,2},{4,5},{5,4},{6,7},{7,6},{8,9},{9,8},{10,11... | collective-permute-start | bytes 12582920 | tf_op jit(solution)/shard_map/ppermute | solution.py:1191
  612.9 102.5 %collective-permute-start.4 = (f32[2,2,2,528,256]{4,3,2,1,0:T(8,128)}, f32[2,2,2,528,256]{4,3,2,1,0:T(8,128)}, u32[]{:S(2)}, u32[]{:S(2)}) collective-permute-start(f32[2,2,2,528,256]{4,3,2,1,0:T(8,128)} %get-tuple-element.299), channel_id=1, source_target_pairs={{0,2},{2,0},{4,6},{6,4},{8,10},{10,8},{12,14},{14,12},{16,18},{18,... | collective-permute-start | bytes 12976136 | tf_op jit(solution)/shard_map/ppermute | solution.py:1049
  615.9 99.5 %collective-permute-start.5 = (f32[2,2,2,528,256]{4,3,2,1,0:T(8,128)}, f32[2,2,2,528,256]{4,3,2,1,0:T(8,128)}, u32[]{:S(2)}, u32[]{:S(2)}) collective-permute-start(f32[2,2,2,528,256]{4,3,2,1,0:T(8,128)} %get-tuple-element.300), channel_id=1, source_target_pairs={{0,4},{2,6},{4,0},{6,2},{8,12},{10,14},{12,8},{14,10},{16,20},{18,... | collective-permute-start | bytes 12976136 | tf_op jit(solution)/shard_map/ppermute | solution.py:1049
  617.4 98.0 %collective-permute-start.6 = (f32[2,2,2,480,256]{4,3,2,1,0:T(8,128)}, f32[2,2,2,480,256]{4,3,2,1,0:T(8,128)}, u32[]{:S(2)}, u32[]{:S(2)}) collective-permute-start(f32[2,2,2,480,256]{4,3,2,1,0:T(8,128)} %get-tuple-element.301), channel_id=1, source_target_pairs={{0,8},{2,10},{4,12},{6,14},{8,0},{10,2},{12,4},{14,6},{16,24},{18,... | collective-permute-start | bytes 11796488 | tf_op jit(solution)/shard_map/ppermute | solution.py:1049
  619.6 8.7 copy-start.7
  628.5 1.3 copy-start.8
  641.2 33.3 %copy-start.4 = (f32[1024,128]{1,0:T(8,128)S(1)}, f32[1024,128]{1,0:T(8,128)}, u32[]{:S(2)}) copy-start(f32[1024,128]{1,0:T(8,128)} %get-tuple-element.234.cosine_ref) | copy-start | bytes 1572868 | tf_op jit(solution)/shard_map/cond
  641.2 33.3 %copy-start.6 = (f32[1024,128]{1,0:T(8,128)S(1)}, f32[1024,128]{1,0:T(8,128)}, u32[]{:S(2)}) copy-start(f32[1024,128]{1,0:T(8,128)} %get-tuple-element.235.sine_ref) | copy-start | bytes 1572868 | tf_op jit(solution)/shard_map/cond
  641.2 33.3 %copy-start.9 = (bf16[1024,1024]{1,0:T(8,128)(2,1)S(1)}, bf16[1024,1024]{1,0:T(8,128)(2,1)}, u32[]{:S(2)}) copy-start(bf16[1024,1024]{1,0:T(8,128)(2,1)} %copy-done.8) | copy-start | bytes 6291460 | tf_op jit(solution)/shard_map/cond
  709.4 39.5 %collective-permute-start.8 = (f32[16,512,256]{2,1,0:T(8,128)}, f32[16,512,256]{2,1,0:T(8,128)}, u32[]{:S(2)}, u32[]{:S(2)}) collective-permute-start(f32[16,512,256]{2,1,0:T(8,128)} %get-tuple-element.304), channel_id=1, source_target_pairs={{1,0},{3,2},{5,4},{7,6},{9,8},{11,10},{13,12},{15,14},{17,16},{19,... | collective-permute-start | bytes 25165832 | tf_op jit(solution)/shard_map/ppermute | solution.py:1193
  711.0 19.8 %collective-permute-start.1 = (f32[1024,1024]{1,0:T(8,128)}, f32[1024,1024]{1,0:T(8,128)}, u32[]{:S(2)}, u32[]{:S(2)}) collective-permute-start(f32[1024,1024]{1,0:T(8,128)} %get-tuple-element.286), channel_id=1, source_target_pairs={{0,1},{1,0},{2,3},{3,2},{4,5},{5,4},{6,7},{7,6},{8,9},{9,8},{10,11... | collective-permute-start | bytes 12582920 | tf_op jit(solution)/shard_map/ppermute | solution.py:1160
  715.5 24.0 %collective-permute-start.7 = (f32[1024,1024]{1,0:T(8,128)}, f32[1024,1024]{1,0:T(8,128)}, u32[]{:S(2)}, u32[]{:S(2)}) collective-permute-start(f32[1024,1024]{1,0:T(8,128)} %after.1.own_ref), channel_id=1, source_target_pairs={{0,1},{1,0},{2,3},{3,2},{4,5},{5,4},{6,7},{7,6},{8,9},{9,8},{10,11... | collective-permute-start | bytes 12582920 | tf_op jit(solution)/shard_map/ppermute | solution.py:1191
  716.4 23.0 %copy-start.2 = (f32[1024,1024]{1,0:T(8,128)S(1)}, f32[1024,1024]{1,0:T(8,128)}, u32[]{:S(2)}) copy-start(f32[1024,1024]{1,0:T(8,128)} %after.1.own_ref) | copy-start | bytes 12582916
  1037.3 5.9 copy-start.10
  (1 other events, 0.8 us)

commit v4 on v3

--- a/solution.py
+++ b/solution.py
@@ -172,17 +172,12 @@
 
 
 def gelu_parts(units):
-    grown = jnp.exp(-0.5 * units * units)
-    inverse = 1.0 / (1.0 + (0.3275911 * math.sqrt(0.5)) * jnp.abs(units))
-    series = 0.5 * 1.061405429
-    for factor in (-1.453152027, 1.421413741, -0.284496736, 0.254829592):
-        series = series * inverse + 0.5 * factor
-    tail = series * inverse * grown
-    below = jnp.where(units >= 0.0, 1.0 - tail, tail)
-    return below, grown * (1.0 / math.sqrt(2.0 * math.pi))
-
-
-FF_BLOCK = 512
+    below = 0.5 + 0.5 * lax.erf(units * math.sqrt(0.5))
+    return below, jnp.exp(-0.5 * units * units) * (1.0 / math.sqrt(2.0 * math.pi))
+
+
+FF_BLOCK = 1024
+FF_ROWS = 512
 
 
 def mlp_forward_kernel(count, *refs):
@@ -200,8 +195,8 @@
         start_layer(stream, x_ref, h_ref, gain_ref, offset_ref)
         part_ref[...] = jnp.broadcast_to(down_bias_ref[...].astype(F32), part_ref.shape)
 
-    for first in range(0, h_ref.shape[0], ROWS):
-        rows = slice(first, first + ROWS)
+    for first in range(0, h_ref.shape[0], FF_ROWS):
+        rows = slice(first, first + FF_ROWS)
         units = dot_nt(h_ref[rows], up_ref[0]) + bias_ref[0]
         below, density = gelu_parts(units)
         active = (units * below).astype(BF16)
@@ -329,98 +324,6 @@
     return jnp.where(same, 1.0, 0.0).astype(BF16)
 
 
-def project_kernel(count, *refs):
-    stream, refs = refs[:count], refs[count:]
-    gain_ref, offset_ref, weight_ref, bias_ref = refs[:4]
-    upper_ref, lower_ref, scale_ref, cosine_ref, sine_ref = refs[4:9]
-    refs = refs[9:]
-    x_ref = None
-    if count > 1:
-        x_ref, refs = refs[0], refs[1:]
-    h_ref, state_ref, keys = refs
-    step = pl.program_id(0)
-    kind, group = step // QUADS, step % QUADS
-    length = h_ref.shape[0]
-
-    @pl.when(step == 0)
-    def _():
-        start_layer(stream, x_ref, h_ref, gain_ref, offset_ref)
-
-    def features(values, rows):
-        cosine = jnp.concatenate([cosine_ref[rows]] * (WIDE // PAIR), axis=1)
-        sine = jnp.concatenate([sine_ref[rows]] * (WIDE // PAIR), axis=1)
-        upper, lower = split(turn(values, cosine, sine))
-        table_up, table_low = upper_ref[0, 0], lower_ref[0, 0]
-        return dot_nn(upper, table_up) + (dot_nn(lower, table_up) + dot_nn(upper, table_low))
-
-    @pl.when(kind == 0)
-    def _():
-        for first in range(0, length, ROWS):
-            rows = slice(first, first + ROWS)
-            values = dot_nt(h_ref[rows], weight_ref[0, 0]) + bias_ref[0]
-            state_ref[0, rows] = jnp.exp(features(values, rows)).astype(BF16)
-
-    @pl.when(kind == 1)
-    def _():
-        ones = same_head_ones()
-        for first in range(0, length, ROWS):
-            rows = slice(first, first + ROWS)
-            values = dot_nt(h_ref[rows], weight_ref[0, 0]) + bias_ref[0]
-            keys[group, rows] = values.astype(BF16)
-            squares = head_sums(values * values, ones)
-            logs = features(values, rows) - (0.5 / math.sqrt(DH)) * squares
-            state_ref[0, rows] = (scale_ref[0, 0] * jnp.exp(logs)).astype(BF16)
-
-    @pl.when(kind == 2)
-    def _():
-        state_ref[0] = keys[group]
-
-    @pl.when(kind == 3)
-    def _():
-        for first in range(0, length, ROWS):
-            rows = slice(first, first + ROWS)
-            values = dot_nt(h_ref[rows], weight_ref[0, 0]) + bias_ref[0]
-            state_ref[0, rows] = values.astype(BF16)
-
-
-def project_forward(layer, stream, gain, offset, weight, biases, tables, rotary):
-    length, width = stream[0].shape
-    full = jax.ShapeDtypeStruct((length, width), F32)
-    state = jax.ShapeDtypeStruct((4, length, width), BF16)
-    out_shape = [jax.ShapeDtypeStruct((length, width), BF16), state]
-    out_specs = [whole((length, width)), plane_block(length, WIDE)]
-    if len(stream) > 1:
-        out_shape, out_specs = [full] + out_shape, [whole((length, width))] + out_specs
-
-    def source(j):
-        return jnp.where(j < 2 * QUADS, j, jnp.maximum(j - QUADS, 2 * QUADS - 1))
-
-    def table(j):
-        return jnp.where(j < 2 * QUADS, j % QUADS, QUADS - 1)
-
-    return pl.pallas_call(
-        functools.partial(project_kernel, len(stream)),
-        grid=(4 * QUADS,),
-        in_specs=[whole((length, width))] * len(stream)
-        + [
-            whole((1, width)),
-            whole((1, width)),
-            pl.BlockSpec((1, 1, WIDE, width), lambda j: (0, layer, source(j), 0)),
-            pl.BlockSpec((1, 1, WIDE), lambda j: (source(j), 0, 0)),
-            pl.BlockSpec((1, 1, WIDE, WIDE), lambda j: (layer, table(j), 0, 0)),
-            pl.BlockSpec((1, 1, WIDE, WIDE), lambda j: (layer, table(j), 0, 0)),
-            pl.BlockSpec((1, 1, 1, WIDE), lambda j: (layer, table(j), 0, 0)),
-            whole((length, PAIR)),
-            whole((length, PAIR)),
-        ],
-        out_specs=out_specs,
-        out_shape=out_shape,
-        scratch_shapes=[pltpu.VMEM((QUADS, length, WIDE), BF16)],
-        compiler_params=params(),
-        name="project_forward",
-    )(*stream, gain, offset, weight, biases.reshape(-1, 1, WIDE), *tables, *rotary)
-
-
 def write_mask(starts_ref, mask_ref, flipped):
     length = mask_ref.shape[0]
     keys = lane_index(1, length)
@@ -435,12 +338,47 @@
         mask_ref[first : first + ROWS] = jnp.where(seen, 1.0, 0.0).astype(BF16)
 
 
-def attend_kernel(starts_ref, state_ref, out_ref, mask_ref):
+def wide_rotary(cosine_ref, sine_ref, rows):
+    return tuple(
+        jnp.concatenate([ref[rows]] * (WIDE // PAIR), axis=1) for ref in (cosine_ref, sine_ref)
+    )
+
+
+def attention_forward_kernel(count, *refs):
+    stream, refs = refs[:count], refs[count:]
+    starts_ref, gain_ref, offset_ref, weight_ref, bias_ref, out_bias_ref = refs[:6]
+    upper_ref, lower_ref, scale_ref, cosine_ref, sine_ref = refs[6:11]
+    refs = refs[11:]
+    x_ref = None
+    if count > 1:
+        x_ref, refs = refs[0], refs[1:]
+    part_ref, h_ref, state_ref, mixed_ref, mask_ref = refs
+    length = h_ref.shape[0]
+
     @pl.when(pl.program_id(0) == 0)
     def _():
+        start_layer(stream, x_ref, h_ref, gain_ref, offset_ref)
         write_mask(starts_ref, mask_ref, False)
-
-    length = mask_ref.shape[0]
+        part_ref[...] = jnp.broadcast_to(out_bias_ref[...], part_ref.shape)
+
+    ones = same_head_ones()
+    table_up, table_low = upper_ref[0, 0], lower_ref[0, 0]
+
+    def features(values, rows):
+        upper, lower = split(turn(values, *wide_rotary(cosine_ref, sine_ref, rows)))
+        return dot_nn(upper, table_up) + (dot_nn(lower, table_up) + dot_nn(upper, table_low))
+
+    for first in range(0, length, ROWS):
+        rows = slice(first, first + ROWS)
+        queries, keys, values = [
+            dot_nt(h_ref[rows], weight_ref[0, 0, kind, 0]) + bias_ref[kind, 0] for kind in range(3)
+        ]
+        state_ref[0, rows] = jnp.exp(features(queries, rows)).astype(BF16)
+        logs = features(keys, rows) - (0.5 / math.sqrt(DH)) * head_sums(keys * keys, ones)
+        state_ref[1, rows] = (scale_ref[0, 0] * jnp.exp(logs)).astype(BF16)
+        state_ref[2, rows] = keys.astype(BF16)
+        state_ref[3, rows] = values.astype(BF16)
+
     zero = jnp.zeros((), BF16)
     one = jnp.ones((), BF16)
     for first in range(0, length, ROWS):
@@ -448,260 +386,210 @@
         finish = first + ROWS
         left = lane_index(finish, PAIR) < DH
         seen = mask_ref[rows, :finish] > zero
-        sums = []
-        for own in (left, ~left):
-            keys = jnp.where(own, state_ref[1, :finish], zero)
-            scores = dot_nt(state_ref[0, rows], keys).astype(BF16)
-            scores = jnp.where(seen, scores, zero)
-            sums.append(dot_nn(scores, jnp.where(own, state_ref[3, :finish], one)))
-        left = lane_index(ROWS, PAIR) < DH
-        numer = jnp.where(left, sums[0], sums[1])
-        denom = jnp.where(left, pltpu.roll(sums[0], DH, 1), pltpu.roll(sums[1], DH, 1))
-        inverse = 1.0 / denom
-        out_ref[0, rows] = (numer * inverse).astype(BF16)
-        out_ref[1, rows], out_ref[2, rows] = split(inverse)
-
-
-def attend_forward(starts, state):
-    _, length, width = state.shape
-    block = pl.BlockSpec((4, length, PAIR), lambda p: (0, 0, p))
+        for pair in range(WIDE // PAIR):
+            lanes = slice(pair * PAIR, (pair + 1) * PAIR)
+            sums = []
+            for own in (left, ~left):
+                keys = jnp.where(own, state_ref[1, :finish, lanes], zero)
+                scores = dot_nt(state_ref[0, rows, lanes], keys).astype(BF16)
+                scores = jnp.where(seen, scores, zero)
+                sums.append(dot_nn(scores, jnp.where(own, state_ref[3, :finish, lanes], one)))
+            mine = lane_index(ROWS, PAIR) < DH
+            numer = jnp.where(mine, sums[0], sums[1])
+            denom = jnp.where(mine, pltpu.roll(sums[0], DH, 1), pltpu.roll(sums[1], DH, 1))
+            inverse = 1.0 / denom
+            mixed_ref[0, rows, lanes] = (numer * inverse).astype(BF16)
+            mixed_ref[1, rows, lanes], mixed_ref[2, rows, lanes] = split(inverse)
+        part_ref[rows] += dot_nn(mixed_ref[0, rows], weight_ref[0, 0, 3, 0])
+
+
+def kinds_of(weight):
+    return weight.reshape(weight.shape[:2] + (4, QUADS, WIDE, weight.shape[3]))
+
+
+def attention_forward(layer, stream, starts, gain, offset, weight, biases, tables, rotary):
+    length, width = stream[0].shape
+    full = jax.ShapeDtypeStruct((length, width), F32)
+    state = jax.ShapeDtypeStruct((4, length, width), BF16)
+    out_shape = [full, jax.ShapeDtypeStruct((length, width), BF16), state, state]
+    four = pl.BlockSpec((4, length, WIDE), lambda g: (0, 0, g))
+    out_specs = [whole((length, width)), whole((length, width)), four, four]
+    if len(stream) > 1:
+        out_shape, out_specs = [full] + out_shape, [whole((length, width))] + out_specs
     return pl.pallas_call(
-        attend_kernel,
-        grid=(PAIRS,),
-        in_specs=[pl.BlockSpec(memory_space=pltpu.SMEM), block],
-        out_specs=block,
-        out_shape=jax.ShapeDtypeStruct(state.shape, BF16),
+        functools.partial(attention_forward_kernel, len(stream)),
+        grid=(QUADS,),
+        in_specs=[whole((length, width))] * len(stream)
+        + [
+            pl.BlockSpec(memory_space=pltpu.SMEM),
+            whole((1, width)),
+            whole((1, width)),
+            pl.BlockSpec((1, 1, 4, 1, WIDE, width), lambda g: (0, layer, 0, g, 0, 0)),
+            pl.BlockSpec((4, 1, 1, WIDE), lambda g: (0, g, 0, 0)),
+            whole((1, width)),
+            pl.BlockSpec((1, 1, WIDE, WIDE), lambda g: (layer, g, 0, 0)),
+            pl.BlockSpec((1, 1, WIDE, WIDE), lambda g: (layer, g, 0, 0)),
+            pl.BlockSpec((1, 1, 1, WIDE), lambda g: (layer, g, 0, 0)),
+            whole((length, PAIR)),
+            whole((length, PAIR)),
+        ],
+        out_specs=out_specs,
+        out_shape=out_shape,
         scratch_shapes=[pltpu.VMEM((length, length), BF16)],
         compiler_params=params(),
-        name="attend_forward",
-    )(starts, state)
-
-
-def mix_kernel(mixed_ref, weight_ref, bias_ref, part_ref):
-    part_ref[...] = dot_nn(mixed_ref[0], weight_ref[0, 0]) + bias_ref[0]
-
-
-def mix_forward(layer, mixed, weight, biases):
-    _, length, width = mixed.shape
-    return pl.pallas_call(
-        mix_kernel,
-        grid=(QUADS,),
-        in_specs=[
-            pl.BlockSpec((1, length, width), lambda j: (0, 0, 0), pipeline_mode=pl.Buffered(1)),
-            pl.BlockSpec((1, 1, width, WIDE), lambda j: (0, layer, 3, j)),
-            pl.BlockSpec((1, 1, WIDE), lambda j: (3 * QUADS + j, 0, 0)),
-        ],
-        out_specs=pl.BlockSpec((length, WIDE), lambda j: (0, j)),
-        out_shape=jax.ShapeDtypeStruct((length, width), F32),
-        compiler_params=params(),
-        name="mix_forward",
-    )(mixed, weight, biases.reshape(-1, 1, WIDE))
-
-
-def mix_backward_kernel(grad_ref, weight_ref, mixed_ref, out_ref):
-    row, lane = row_index(WIDE, WIDE), lane_index(WIDE, WIDE)
-    partner = (row // PAIR == lane // PAIR) & (row // DH != lane // DH)
-    ones = jnp.where(partner, 1.0, 0.0).astype(BF16)
-    length = grad_ref.shape[0]
-    for first in range(0, length, ROWS):
-        rows = slice(first, first + ROWS)
-        grad = dot_nt(grad_ref[rows], weight_ref[0, 0]).astype(BF16).astype(F32)
-        inverse = mixed_ref[1, rows].astype(F32) + mixed_ref[2, rows].astype(F32)
-        scaled = grad * inverse
-        upper, lower = split(-head_sums(scaled * mixed_ref[0, rows].astype(F32), ones))
-        numer = scaled.astype(BF16)
-        lane = lane_index(ROWS, WIDE)
-        spare = jnp.where(
-            lane % DH == 0, upper, jnp.where(lane % DH == 1, lower, jnp.zeros((), BF16))
-        )
-        left = lane % PAIR < DH
-        out_ref[0, rows] = jnp.where(left, numer, spare)
-        out_ref[1, rows] = jnp.where(left, spare, numer)
-
-
-def mix_backward(layer, grad, weight, mixed):
-    _, length, width = mixed.shape
-    return pl.pallas_call(
-        mix_backward_kernel,
-        grid=(QUADS,),
-        in_specs=[
-            whole((length, width)),
-            pl.BlockSpec((1, 1, WIDE, width), lambda j: (0, layer, 3 * QUADS + j, 0)),
-            pl.BlockSpec((4, length, WIDE), lambda j: (0, 0, j)),
-        ],
-        out_specs=pl.BlockSpec((2, length, WIDE), lambda j: (0, 0, j)),
-        out_shape=jax.ShapeDtypeStruct((2, length, width), BF16),
-        compiler_params=params(),
-        name="mix_backward",
-    )(grad, weight, mixed)
-
-
-def attend_backward_kernel(starts_ref, state_ref, numer_ref, out_ref, mask_ref, query_t):
+        name="attention_forward",
+    )(
+        *stream, starts, gain, offset, kinds_of(weight),
+        biases.reshape(4, QUADS, 1, WIDE), biases[None, 3 * width :], *tables, *rotary,
+    )
+
+
+def attention_backward_kernel(
+    starts_ref, grad_ref, h_ref, state_ref, mixed_ref, table_ref, cosine_ref, sine_ref, weight_ref,
+    part_ref, out_ref, bias_ref, near_ref, far_ref,
+    mask_ref, grad_t, h_t, numer_ref, feat_ref, flow, query_t,
+):
+    del near_ref, far_ref
+    length = h_ref.shape[0]
+
     @pl.when(pl.program_id(0) == 0)
     def _():
         write_mask(starts_ref, mask_ref, True)
-
-    length = mask_ref.shape[0]
-    zero = jnp.zeros((), BF16)
-    one = jnp.ones((), BF16)
-    query_t[...] = jnp.zeros_like(query_t)
-    for first in range(0, length, ROWS):
-        rows = slice(first, first + ROWS)
-        seen = mask_ref[rows, first:] > zero
-        lane = lane_index(ROWS, PAIR)
-        left = lane < DH
-        spare = jnp.where(lane % DH < 2, one, zero)
-        keys, values = state_ref[1, rows], state_ref[3, rows]
-        queries = state_ref[0, first:]
-        numer = jnp.where(lane_index(length - first, PAIR) < DH, numer_ref[0, first:], numer_ref[1, first:])
-        grads = []
-        for head, own in enumerate((left, ~left)):
-            own_keys = jnp.where(own, keys, zero)
-            scores = dot_nt(own_keys, queries).astype(BF16)
-            scores = jnp.where(seen, scores, zero)
-            grad_value = dot_nn(scores, numer)
-            grad_scores = dot_nt(jnp.where(own, values, spare), numer_ref[head, first:]).astype(BF16)
-            grad_scores = jnp.where(seen, grad_scores, zero)
-            grad_key = dot_nn(grad_scores, queries)
-            query_t[head, :, first:] += dot_nn(own_keys.T[head * DH : (head + 1) * DH], grad_scores)
-            grads.append((grad_value, grad_key))
-        out_ref[2, rows] = jnp.where(left, grads[0][0], grads[1][0]).astype(BF16)
-        grad_key = jnp.where(left, grads[0][1], grads[1][1])
-        out_ref[1, rows] = (grad_key * keys.astype(F32)).astype(BF16)
-    for first in range(0, length, ROWS):
-        rows = slice(first, first + ROWS)
-        grad_query = jnp.concatenate([query_t[0, :, rows], query_t[1, :, rows]], axis=0).T
-        out_ref[0, rows] = (grad_query * state_ref[0, rows].astype(F32)).astype(BF16)
-
-
-def attend_backward(starts, state, numer):
-    _, length, width = state.shape
-    return pl.pallas_call(
-        attend_backward_kernel,
-        grid=(PAIRS,),
-        in_specs=[
-            pl.BlockSpec(memory_space=pltpu.SMEM),
-            pl.BlockSpec((4, length, PAIR), lambda p: (0, 0, p)),
-            pl.BlockSpec((2, length, PAIR), lambda p: (0, 0, p)),
-        ],
-        out_specs=pl.BlockSpec((3, length, PAIR), lambda p: (0, 0, p)),
-        out_shape=jax.ShapeDtypeStruct((3, length, width), BF16),
-        scratch_shapes=[
-            pltpu.VMEM((length, length), BF16),
-            pltpu.VMEM((2, DH, length), F32),
-        ],
-        compiler_params=params(),
-        name="attend_backward",
-    )(starts, state, numer)
-
-
-def project_backward_kernel(
-    grad_ref, h_ref, mixed_ref, feat_ref, keys_ref, table_ref, cosine_ref, sine_ref, weight_ref,
-    part_ref, out_ref, bias_ref, near_ref, far_ref, grad_t, h_t, flow,
-):
-    del near_ref, far_ref
-    step = pl.program_id(0)
-    kind, length = step // QUADS, h_ref.shape[0]
-
-    @pl.when(step == 0)
-    def _():
         grad_t[...] = grad_ref[...].T
         h_t[...] = h_ref[...].T
         part_ref[...] = jnp.zeros_like(part_ref)
 
-    def project_back(rows):
-        cosine = jnp.concatenate([cosine_ref[rows]] * (WIDE // PAIR), axis=1)
-        sine = jnp.concatenate([sine_ref[rows]] * (WIDE // PAIR), axis=1)
-        return turn_back(dot_nt(feat_ref[0, rows], table_ref[0, 0]), cosine, sine)
-
-    @pl.when(kind == 0)
-    def _():
-        flow[...] = mixed_ref[0]
-        bias_ref[0] = jnp.sum(feat_ref[0, :1].astype(F32), axis=0, keepdims=True)
-
-    @pl.when(kind == 1)
-    def _():
+    row, lane = row_index(WIDE, WIDE), lane_index(WIDE, WIDE)
+    partner = (row // PAIR == lane // PAIR) & (row // DH != lane // DH)
+    partner = jnp.where(partner, 1.0, 0.0).astype(BF16)
+    zero = jnp.zeros((), BF16)
+    one = jnp.ones((), BF16)
+    for first in range(0, length, ROWS):
+        rows = slice(first, first + ROWS)
+        grad = dot_nt(grad_ref[rows], weight_ref[0, 0, 3, 0]).astype(BF16).astype(F32)
+        inverse = mixed_ref[1, rows].astype(F32) + mixed_ref[2, rows].astype(F32)
+        scaled = grad * inverse
+        upper, lower = split(-head_sums(scaled * mixed_ref[0, rows].astype(F32), partner))
+        numer = scaled.astype(BF16)
+        lane = lane_index(ROWS, WIDE)
+        spare = jnp.where(lane % DH == 0, upper, jnp.where(lane % DH == 1, lower, zero))
+        left = lane % PAIR < DH
+        numer_ref[0, rows] = jnp.where(left, numer, spare)
+        numer_ref[1, rows] = jnp.where(left, spare, numer)
+
+    for pair in range(WIDE // PAIR):
+        lanes = slice(pair * PAIR, (pair + 1) * PAIR)
+        query_t[...] = jnp.zeros_like(query_t)
         for first in range(0, length, ROWS):
             rows = slice(first, first + ROWS)
-            flow[rows] = project_back(rows).astype(BF16)
-
-    @pl.when(kind == 2)
-    def _():
-        ones = same_head_ones()
+            seen = mask_ref[rows, first:] > zero
+            lane = lane_index(ROWS, PAIR)
+            left = lane < DH
+            spare = jnp.where(lane % DH < 2, one, zero)
+            keys, values = state_ref[1, rows, lanes], state_ref[3, rows, lanes]
+            queries = state_ref[0, first:, lanes]
+            numer = jnp.where(
+                lane_index(length - first, PAIR) < DH,
+                numer_ref[0, first:, lanes],
+                numer_ref[1, first:, lanes],
+            )
+            grads = []
+            for head, own in enumerate((left, ~left)):
+                own_keys = jnp.where(own, keys, zero)
+                scores = dot_nt(own_keys, queries).astype(BF16)
+                scores = jnp.where(seen, scores, zero)
+                grad_value = dot_nn(scores, numer)
+                grad_scores = dot_nt(
+                    jnp.where(own, values, spare), numer_ref[head, first:, lanes]
+                ).astype(BF16)
+                grad_scores = jnp.where(seen, grad_scores, zero)
+                grad_key = dot_nn(grad_scores, queries)
+                query_t[head, :, first:] += dot_nn(
+                    own_keys.T[head * DH : (head + 1) * DH], grad_scores
+                )
+                grads.append((grad_value, grad_key))
+            flow[2, rows, lanes] = jnp.where(left, grads[0][0], grads[1][0]).astype(BF16)
+            grad_key = jnp.where(left, grads[0][1], grads[1][1])
+            feat_ref[1, rows, lanes] = (grad_key * keys.astype(F32)).astype(BF16)
         for first in range(0, length, ROWS):
             rows = slice(first, first + ROWS)
-            shrink = dot_nn(feat_ref[0, rows], ones) * (1.0 / math.sqrt(DH))
-            flow[rows] = (project_back(rows) - keys_ref[0, rows].astype(F32) * shrink).astype(BF16)
-
-    @pl.when(kind == 3)
-    def _():
-        flow[...] = feat_ref[0]
-
-    @pl.when(kind > 0)
-    def _():
-        bias = jnp.zeros((1, WIDE), F32)
-        for first in range(0, length, ROWS):
-            rows = slice(first, first + ROWS)
-            bias += jnp.sum(flow[rows].astype(F32), axis=0, keepdims=True)
-            part_ref[rows] += dot_nn(flow[rows], weight_ref[0, 0])
-            out_ref[0, rows] = dot_nn(h_t[rows], flow[...])
-        bias_ref[0] = bias
-
-    @pl.when(kind == 0)
-    def _():
-        for first in range(0, length, ROWS):
-            rows = slice(first, first + ROWS)
-            out_ref[0, rows] = dot_nn(grad_t[rows], flow[...])
-
-
-def project_backward(layer, grad, h, mixed, feats, state, tables, rotary, weight):
+            grad_query = jnp.concatenate([query_t[0, :, rows], query_t[1, :, rows]], axis=0).T
+            feat_ref[0, rows, lanes] = (
+                grad_query * state_ref[0, rows, lanes].astype(F32)
+            ).astype(BF16)
+
+    ones = same_head_ones()
+    table = table_ref[0, 0]
+    sums = [jnp.zeros((1, WIDE), F32)] * 3
+    for first in range(0, length, ROWS):
+        rows = slice(first, first + ROWS)
+        cosine, sine = wide_rotary(cosine_ref, sine_ref, rows)
+        flow[0, rows] = turn_back(dot_nt(feat_ref[0, rows], table), cosine, sine).astype(BF16)
+        shrink = dot_nn(feat_ref[1, rows], ones) * (1.0 / math.sqrt(DH))
+        turned = turn_back(dot_nt(feat_ref[1, rows], table), cosine, sine)
+        flow[1, rows] = (turned - state_ref[2, rows].astype(F32) * shrink).astype(BF16)
+        total = part_ref[rows]
+        for kind in range(3):
+            block = flow[kind, rows]
+            sums[kind] = sums[kind] + jnp.sum(block.astype(F32), axis=0, keepdims=True)
+            total = total + dot_nn(block, weight_ref[0, 0, kind, 0])
+        part_ref[rows] = total
+    for kind in range(3):
+        bias_ref[kind, 0] = sums[kind]
+    bias_ref[3, 0] = jnp.zeros((1, WIDE), F32)
+    for first in range(0, h_t.shape[0], ROWS):
+        rows = slice(first, first + ROWS)
+        for kind in range(3):
+            out_ref[kind, 0, rows] = dot_nn(h_t[rows], flow[kind])
+        out_ref[3, 0, rows] = dot_nn(grad_t[rows], mixed_ref[0])
+
+
+def attention_backward(layer, starts, grad, h, state, mixed, tables, rotary, weight):
     _, length, width = state.shape
     blocks = 4 * QUADS
-
-    def at(j):
-        return jnp.maximum(j - QUADS, 0)
-
-    def target(j):
-        return jnp.where(j < QUADS, 3 * QUADS + j, j - QUADS)
-
-    return pl.pallas_call(
-        project_backward_kernel,
-        grid=(blocks,),
+    four = pl.BlockSpec((4, length, WIDE), lambda g: (0, 0, g))
+    halves = jax.ShapeDtypeStruct((blocks, width // 2, WIDE), F32)
+    part, out, bias, near, far = pl.pallas_call(
+        attention_backward_kernel,
+        grid=(QUADS,),
         in_specs=[
+            pl.BlockSpec(memory_space=pltpu.SMEM),
             whole((length, width)),
             whole((length, width)),
-            pl.BlockSpec((1, length, WIDE), lambda j: (0, 0, jnp.minimum(j, QUADS - 1))),
-            pl.BlockSpec((1, length, WIDE), lambda j: (at(j) // QUADS, 0, at(j) % QUADS)),
-            pl.BlockSpec(
-                (1, length, WIDE), lambda j: (2, 0, jnp.clip(j - 2 * QUADS, 0, QUADS - 1))
-            ),
-            pl.BlockSpec((1, 1, WIDE, WIDE), lambda j: (layer, at(j) % QUADS, 0, 0)),
+            four,
+            four,
+            pl.BlockSpec((1, 1, WIDE, WIDE), lambda g: (layer, g, 0, 0)),
             whole((length, PAIR)),
             whole((length, PAIR)),
-            pl.BlockSpec((1, 1, WIDE, width), lambda j: (0, layer, at(j), 0)),
+            pl.BlockSpec((1, 1, 4, 1, WIDE, width), lambda g: (0, layer, 0, g, 0, 0)),
         ],
         out_specs=[
             whole((length, width)),
-            pl.BlockSpec((1, width, WIDE), lambda j: (target(j), 0, 0)),
-            pl.BlockSpec((1, 1, WIDE), lambda j: (target(j), 0, 0)),
+            pl.BlockSpec((4, 1, width, WIDE), lambda g: (0, g, 0, 0)),
+            pl.BlockSpec((4, 1, 1, WIDE), lambda g: (0, g, 0, 0)),
             pl.BlockSpec(memory_space=pl.ANY),
             pl.BlockSpec(memory_space=pl.ANY),
         ],
         out_shape=[
             jax.ShapeDtypeStruct((length, width), F32),
-            jax.ShapeDtypeStruct((blocks, width, WIDE), F32),
-            jax.ShapeDtypeStruct((blocks, 1, WIDE), F32),
-            jax.ShapeDtypeStruct((blocks, width // 2, WIDE), F32),
-            jax.ShapeDtypeStruct((blocks, width // 2, WIDE), F32),
+            jax.ShapeDtypeStruct((4, QUADS, width, WIDE), F32),
+            jax.ShapeDtypeStruct((4, QUADS, 1, WIDE), F32),
+            halves,
+            halves,
         ],
         scratch_shapes=[
+            pltpu.VMEM((length, length), BF16),
             pltpu.VMEM((width, length), BF16),
             pltpu.VMEM((width, length), BF16),
-            pltpu.VMEM((length, WIDE), BF16),
+            pltpu.VMEM((2, length, WIDE), BF16),
+            pltpu.VMEM((2, length, WIDE), BF16),
+            pltpu.VMEM((3, length, WIDE), BF16),
+            pltpu.VMEM((2, DH, length), F32),
         ],
         compiler_params=params(),
-        name="project_backward",
-    )(grad, h, mixed, feats, state, tables[0], *rotary, weight)
+        name="attention_backward",
+    )(starts, grad, h, state, mixed, tables[0], *rotary, kinds_of(weight))
+    return part, out.reshape(blocks, width, WIDE), near, far, bias.reshape(blocks, WIDE)
 
 
 def norm_backward_kernel(x_ref, own_ref, other_ref, grad_ref, gain_ref, out_ref, sums_ref):
@@ -1004,28 +892,40 @@
     ranges = [first_rows(length) for length in rows]
 
     def kernel(weight_ref, near_ref, far_ref, *refs):
-        outs, sems = refs[:3], refs[3]
+        outs, held, loads, stores = refs[:3], refs[3:6], refs[6], refs[7]
         me, core = lax.axis_index("batch"), lax.axis_index("stream")
 
-        def copies(source, is_up):
-            for bit in range(3):
-                first, finish = ranges[is_up][bit]
-                base = ranges[0][bit][1] - ranges[0][bit][0] if is_up else 0
-                at = [slice(None)] * bits + [pl.ds(first, finish - first)]
-                at[bits - 1 - bit] = 1 - bit_of(me, bit)
-                to = (slice(None),) * (bits - 1) + (pl.ds(base, finish - first),)
-                yield pltpu.make_async_copy(
-                    source.at[tuple(at)], outs[bit].at[to], sems.at[is_up, bit]
-                )
+        def load(source, is_up, bit, part):
+            first, finish = ranges[is_up][bit]
+            base = ranges[0][bit][1] - ranges[0][bit][0] if is_up else 0
+            others = [dim for dim in range(bits) if dim != bits - 1 - bit]
+            at = [slice(None)] * bits + [pl.ds(first, finish - first)]
+            at[bits - 1 - bit] = 1 - bit_of(me, bit)
+            at[others[0]] = part
+            to = (part,) + (slice(None),) * (bits - 2) + (pl.ds(base, finish - first),)
+            return pltpu.make_async_copy(
+                source.at[tuple(at)], held[bit].at[to], loads.at[is_up, bit, part]
+            )
 
         def start(source, is_up):
-            for copy in copies(source, is_up):
-                copy.start()
+            for part in range(2):
+                for bit in range(3):
+                    load(source, is_up, bit, part).start()
 
         start(weight_ref, 0)
         for side, source in enumerate((near_ref, far_ref)):
             pl.when(core == side)(functools.partial(start, source, 1))
-        for copy in list(copies(weight_ref, 0)) + list(copies(near_ref, 1)):
+        copies = []
+        for part in range(2):
+            for bit in range(3):
+                load(weight_ref, 0, bit, part).wait()
+                load(near_ref, 1, bit, part).wait()
+                copy = pltpu.make_async_copy(
+                    held[bit].at[part], outs[bit].at[part], stores.at[bit, part]
+                )
+                copy.start()
+                copies.append(copy)
+        for copy in copies:
             copy.wait()
 
     shapes = [
@@ -1036,7 +936,9 @@
         in_specs=[pl.BlockSpec(memory_space=pltpu.HBM)] * 3,
         out_specs=[pl.BlockSpec(memory_space=pltpu.HBM)] * 3,
         out_shape=[jax.ShapeDtypeStruct(shape, F32) for shape in shapes],
-        scratch_shapes=[pltpu.SemaphoreType.DMA((2, 3))],
+        scratch_shapes=[pltpu.VMEM(shape, F32) for shape in shapes]
+        + [pltpu.SemaphoreType.DMA((2, 3, 2)), pltpu.SemaphoreType.DMA((3, 2))],
+        compiler_params=params(),
         name="pack_halves",
     )(*[array.reshape((2,) * bits + array.shape[1:]) for array in (weight, near, far)])
 
@@ -1131,12 +1033,12 @@
 
     def attention(layer, stream):
         gain, offset = norm_gain[layer : layer + 1], norm_bias[layer : layer + 1]
-        *x, h, state = project_forward(
-            layer, stream, gain, offset, branch_weight, biases[layer], tables, rotary
-        )
-        mixed = attend_forward(doc_starts, state)
-        part = mix_forward(layer, mixed, branch_weight, biases[layer])
-        return tuple(x) + (part, h, state, mixed)
+        return tuple(
+            attention_forward(
+                layer, stream, doc_starts, gain, offset, branch_weight, biases[layer], tables,
+                rotary,
+            )
+        )
 
     def feed_forward(layer, stream):
         gain, offset = norm_gain[layer : layer + 1], norm_bias[layer : layer + 1]
@@ -1162,12 +1064,9 @@
 
     def attention_back(layer, grad):
         h, state, mixed = kept[layer]
-        numer = mix_backward(layer, grad, branch_weight, mixed)
-        feats = attend_backward(doc_starts, state, numer)
-        part, weight, bias, near, far = project_backward(
-            layer, grad, h, mixed, feats, state, tables, rotary, branch_weight
-        )
-        return part, weight, near, far, bias.reshape(-1, WIDE)
+        return attention_backward(
+            layer, doc_starts, grad, h, state, mixed, tables, rotary, branch_weight
+        )
 
     def feed_forward_back(layer, grad):
         h, act, slope = kept[layer]

time: 1050 us -> 629 us (0.60)
  Pallas kernels: 965 us -> 537 us
    pallas_call x1, Pallas kernels: 382 us -> 8.48 us  [pack_halves(): pl.pallas_call(kernel, in_specs=[pl.BlockSpec(memory_space=pltpu.HBM)] *...]
    pallas_call x12 -> x4, Pallas kernels: 269 us -> 216 us  [the longest x2 135 us: attention_backward(): pl.pallas_call(attention_backward_kernel, grid=(QUADS,), in_specs=[pl.Blo...]
  transfers between devices with their start and end apart: 9 -> 9, of which waited for: 3 -> 6; matrix products, arithmetic and copies ran while one was open for 1% -> 2% of each run, Pallas kernels for 46% -> 15%
where the time goes in v4:
time: 629 us; the launch traced here: 623 us
  Pallas kernels  537 us (85%)
  waiting for transfers between devices  31.8 us (5%)
  starting transfers between devices  17.6 us (3%)
  local copies, waits for them, and re-layouts  17.2 us (3%)
  other arithmetic  11.2 us (2%)
  loops' own time  7.67 us (1%)
    pallas_call x1, Pallas kernels, reduce_scatter(): pl.pallas_call(functools.partial(scatter_kernel, bits, flows, layers), in...  288 us
    pallas_call x2, Pallas kernels, attention_backward(): pl.pallas_call(attention_backward_kernel, grid=(QUADS,), in_specs=[pl.Blo...  135 us
    pallas_call x2, Pallas kernels, attention_forward(): pl.pallas_call(functools.partial(attention_forward_kernel, len(stream)),...  80.6 us
    pallas_call x2, Pallas kernels, norm_backward(): pl.pallas_call(norm_backward_kernel, grid=(length // ROWS,), in_specs=[bl...  15.2 us
    ppermute x2, waiting for transfers between devices, shards(): stream = (inputs[-1], part, lax.ppermute(part, 'stream', swap))  12.7 us
  transfers between devices with their start and end apart: 9, of which 6 were waited for; matrix products, arithmetic and copies ran while one was open for 2% of the time, Pallas kernels for 15%

profile of v4, /device:TPU:0, one launch (start us, length us, event | category | flops | bytes accessed | tf_op | source)
XLA Modules:
  0.0 623.4 jit_solution(10011154872613889128)
XLA Ops:
  1.6 11.9 %conditional.5 = ((bf16[2,4,256,256]{3,2,1,0:T(8,128)(2,1)S(1)}, bf16[2,4,256,256]{3,2,1,0:T(8,128)(2,1)}, f32[2,4,1,256]{3,2,1,0:T(1,128)S(1)})) conditional(s32[]{:T(128)} %convert_element_type.15, () %tuple.44, (s32[2,16,64]{2,1,0:T(8,128)}) %tuple.55), branch_computations={%region_0.0_spmd, %region_1.0_spmd.clone} | conditional | bytes 2105384 | solution.py:1023
  1.6 2.7 reshape.133.seeds_ref
  4.3 9.2 %feature_tables.1 = (bf16[2,4,256,256]{3,2,1,0:T(8,128)(2,1)S(1)}, bf16[2,4,256,256]{3,2,1,0:T(8,128)(2,1)}, f32[2,4,1,256]{3,2,1,0:T(1,128)S(1)}) custom-call(s32[2,1024,1]{2,1,0:T(8,128)} %reshape.133.seeds_ref, f32[256,256]{1,0:T(8,128)} %constant.22.clone.2.cosine_ref), custom_call_target="tpu_custom_call" | custom-call | tf_op jit(solution)/shard_map/cond/branch_1_fun/feature_tables/pallas_call | solution.py:108
  13.5 40.8 %conditional.6 = ((f32[1024,1024]{1,0:T(8,128)}, bf16[1024,1024]{1,0:T(8,128)(2,1)}, bf16[4,1024,1024]{2,1,0:T(8,128)(2,1)}, bf16[4,1024,1024]{2,1,0:T(8,128)(2,1)})) conditional(s32[]{:T(128)} %convert_element_type.15, (bf16[2,1024]{1,0:T(2,128)(2,1)S(1)}, bf16[2,1024]{1,0:T(2,128)(2,1)S(1)}, f32[2,4096]{1,0:T(2,128)S(1)}, ...), branch_computations={%region_2.0_spmd, %region_3.0_spmd} | conditional | bytes 40968 | solution.py:1055
  14.9 39.4 %attention_forward.2 = (f32[1024,1024]{1,0:T(8,128)}, bf16[1024,1024]{1,0:T(8,128)(2,1)}, bf16[4,1024,1024]{2,1,0:T(8,128)(2,1)}, bf16[4,1024,1024]{2,1,0:T(8,128)(2,1)}) custom-call(bf16[1024,1024]{1,0:T(8,128)(2,1)S(1)} %get-tuple-element.153.refs_0_, s32[1,4]{1,0:T(1,128)S(1)} %get-tuple-element.154.refs_1_, bf16[1,1024]{1,0:T(2,128)(2,1)S(1)} %bitcast.53, ...), custom_call_target="tpu_custom_call" | custom-call | tf_op jit(solution)/shard_map/cond/branch_1_fun/attention_forward/pallas_call | solution.py:419
  54.4 7.4 %collective-permute-done = f32[1024,1024]{1,0:T(8,128)S(1)} collective-permute-done((f32[1024,1024]{1,0:T(8,128)}, f32[1024,1024]{1,0:T(8,128)S(1)}, u32[]{:S(2)}, u32[]{:S(2)}) %collective-permute-start) | collective-permute-done | bytes 4194336 | tf_op jit(solution)/shard_map/ppermute | solution.py:1062
  61.7 50.3 %conditional.7 = ((f32[1024,1024]{1,0:T(8,128)}, f32[1024,1024]{1,0:T(8,128)}, bf16[1024,1024]{1,0:T(8,128)(2,1)}, bf16[4,1024,1024]{2,1,0:T(8,128)(2,1)}, bf16[4,1024,1024]{2,1,0:T(8,128)(2,1)})) conditional(s32[]{:T(128)} %convert_element_type.15, (bf16[2,1024]{1,0:T(2,128)(2,1)S(1)}, bf16[2,1024]{1,0:T(2,128)(2,1)S(1)}, f32[2,4096]{1,0:T(2,128)S(1)}, ...), branch_computations={%region_4.0_spmd, %region_5.0_spmd} | conditional | bytes 49160 | solution.py:1055
  70.8 41.2 %attention_forward.3 = (f32[1024,1024]{1,0:T(8,128)}, f32[1024,1024]{1,0:T(8,128)}, bf16[1024,1024]{1,0:T(8,128)(2,1)}, bf16[4,1024,1024]{2,1,0:T(8,128)(2,1)}, bf16[4,1024,1024]{2,1,0:T(8,128)(2,1)}) custom-call(bf16[1024,1024]{1,0:T(8,128)(2,1)S(1)} %get-tuple-element.173.refs_0_, f32[1024,1024]{1,0:T(8,128)} %get-tuple-element.174.refs_1_, ...), custom_call_target="tpu_custom_call" | custom-call | tf_op jit(solution)/shard_map/cond/branch_1_fun/attention_forward/pallas_call | solution.py:419
  112.0 69.1 %conditional.8 = (f32[1024,1024]{1,0:T(8,128)}, f32[16,1024,256]{2,1,0:T(8,128)}, f32[16,512,256]{2,1,0:T(8,128)}, f32[16,512,256]{2,1,0:T(8,128)}, f32[16,256]{1,0:T(8,128)S(1)}) conditional(s32[]{:T(128)} %convert_element_type.15, (bf16[1024,1024]{1,0:T(8,128)(2,1)}, bf16[1024,1024]{1,0:T(8,128)(2,1)}, bf16[4,1024,1024]{2,1,0:T(8,128)(2,1)}, ...), branch_computations={%region_6.0_spmd, %region_7.0_spmd} | conditional | bytes 65580 | solution.py:1083
  112.2 67.7 %attention_backward.2 = (f32[1024,1024]{1,0:T(8,128)}, f32[4,4,1024,256]{3,2,1,0:T(8,128)}, f32[4,4,1,256]{3,2,1,0:T(1,128)}, f32[16,512,256]{2,1,0:T(8,128)}, f32[16,512,256]{2,1,0:T(8,128)}) custom-call(s32[1,4]{1,0:T(1,128)S(1)} %get-tuple-element.197.starts_ref, bf16[1024,1024]{1,0:T(8,128)(2,1)} %get-tuple-element.198.grad_ref, ...), custom_call_target="tpu_custom_call" | custom-call | tf_op jit(solution)/shard_map/cond/branch_1_fun/attention_backward/pallas_call | solution.py:552
  182.4 4.4 collective-permute-start.2
  186.9 9.7 %collective-permute-done.3 = f32[16,512,256]{2,1,0:T(8,128)} collective-permute-done((f32[16,512,256]{2,1,0:T(8,128)}, f32[16,512,256]{2,1,0:T(8,128)}, u32[]{:S(2)}, u32[]{:S(2)}) %collective-permute-start.3) | collective-permute-done | bytes 8388640 | tf_op jit(solution)/shard_map/ppermute | solution.py:1092
  196.5 8.5 %pack_halves.1 = (f32[2,2,2,528,256]{4,3,2,1,0:T(8,128)}, f32[2,2,2,528,256]{4,3,2,1,0:T(8,128)}, f32[2,2,2,480,256]{4,3,2,1,0:T(8,128)}) custom-call(f32[2,2,2,2,1024,256]{5,4,3,2,1,0:T(8,128)} %bitcast.43, f32[2,2,2,2,512,256]{5,4,3,2,1,0:T(8,128)} %bitcast.13.near_ref.refs_1_, f32[2,2,2,2,512,256]{5,4,3,2,1,0:T(8,128)} %bitcast.45), custom_call_target="tpu_custom_call" | custom-call | tf_op jit(solution)/shard_map/pack_halves/pallas_call | solution.py:934
  205.0 3.0 collective-permute-start.4
  211.7 8.3 %norm_backward.2 = (bf16[1024,1024]{1,0:T(8,128)(2,1)}, f32[8,1024]{1,0:T(8,128)}) custom-call(f32[1024,1024]{1,0:T(8,128)} %get-tuple-element.280.x_ref, f32[1024,1024]{1,0:T(8,128)} %get-tuple-element.285.own_ref, f32[1024,1024]{1,0:T(8,128)} %collective-permute-done.2.other_ref, bf16[1024,1024]{1,0:T(8,128)(2,1)S(1)} %copy-done.1, ...), custom_call_target="tpu_custom_call" | custom-call | tf_op jit(solution)/shard_map/norm_backward/pallas_call | solution.py:621
  220.0 68.4 %conditional.9 = (f32[1024,1024]{1,0:T(8,128)}, f32[16,1024,256]{2,1,0:T(8,128)}, f32[16,512,256]{2,1,0:T(8,128)}, f32[16,512,256]{2,1,0:T(8,128)}, f32[16,256]{1,0:T(8,128)S(1)}) conditional(s32[]{:T(128)} %convert_element_type.15, (bf16[1024,1024]{1,0:T(8,128)(2,1)}, bf16[1024,1024]{1,0:T(8,128)(2,1)S(1)}, bf16[4,1024,1024]{2,1,0:T(8,128)(2,1)}, ...), branch_computations={%region_8.9_spmd, %region_9.10_spmd} | conditional | bytes 65580 | solution.py:1083
  220.0 67.4 %attention_backward.3 = (f32[1024,1024]{1,0:T(8,128)}, f32[4,4,1024,256]{3,2,1,0:T(8,128)}, f32[4,4,1,256]{3,2,1,0:T(1,128)}, f32[16,512,256]{2,1,0:T(8,128)}, f32[16,512,256]{2,1,0:T(8,128)}) custom-call(s32[1,4]{1,0:T(1,128)S(1)} %get-tuple-element.222.starts_ref, bf16[1024,1024]{1,0:T(8,128)(2,1)} %get-tuple-element.223.grad_ref, ...), custom_call_target="tpu_custom_call" | custom-call | tf_op jit(solution)/shard_map/cond/branch_1_fun/attention_backward/pallas_call | solution.py:552
  289.7 4.4 collective-permute-start.1
  296.3 5.7 collective-permute-done.4.refs_1_.refs_6_
  304.4 5.4 collective-permute-done.1
  309.8 8.6 %add_add_fusion = f32[1024,1024]{1,0:T(8,128)} fusion(f32[1024,1024]{1,0:T(8,128)} %get-tuple-element.280.x_ref, f32[1024,1024]{1,0:T(8,128)} %get-tuple-element.281, f32[1024,1024]{1,0:T(8,128)} %collective-permute-done.1), kind=kLoop, calls=%fused_computation | loop fusion | flops 2097152 | bytes 16777216 | tf_op jit(solution)/shard_map/add | solution.py:1063
  318.4 6.9 %norm_backward.3 = (f32[1024,1024]{1,0:T(8,128)}, f32[8,1024]{1,0:T(8,128)}) custom-call(bf16[1024,1024]{1,0:T(8,128)(2,1)S(1)} %copy-done, f32[1024,1024]{1,0:T(8,128)S(1)} %copy-done.2, f32[1024,1024]{1,0:T(8,128)} %collective-permute-done.7.other_ref, bf16[1024,1024]{1,0:T(8,128)(2,1)} %get-tuple-element.286.grad_ref, ...), custom_call_target="tpu_custom_call" | custom-call | tf_op jit(solution)/shard_map/norm_backward/pallas_call | solution.py:621
  327.9 288.4 %reduce_scatter.1 = (f32[2,256,1024]{2,1,0:T(8,128)}, f32[2,128,1024]{2,1,0:T(8,128)}, f32[8,128]{1,0:T(8,128)}) custom-call(f32[2,2,2,2,1024,256]{5,4,3,2,1,0:T(8,128)} %bitcast.44, f32[2,2,2,2,512,256]{5,4,3,2,1,0:T(8,128)} %bitcast.13.near_ref.refs_1_, f32[2,2,2,2,512,256]{5,4,3,2,1,0:T(8,128)} %bitcast.46, f32[2,2,2,2,1024,256]{5,4,3,2,1,0:T(8,128)} %bitcast.48, ...), custom_call_target="tpu_custom_call" | custom-call | tf_op jit(solution)/shard_map/reduce_scatter/pallas_call | solution.py:996
  619.1 3.2 copy.88
  (69 shorter events, 23.3 us)
Async XLA Ops:
  0.6 12.9 %copy-start.5 = (bf16[2,1024]{1,0:T(2,128)(2,1)S(1)}, bf16[2,1024]{1,0:T(2,128)(2,1)}, u32[]{:S(2)}) copy-start(bf16[2,1024]{1,0:T(2,128)(2,1)} %param.29) | copy-start | bytes 12292
  0.6 12.8 %copy-start.6 = (bf16[2,1024]{1,0:T(2,128)(2,1)S(1)}, bf16[2,1024]{1,0:T(2,128)(2,1)}, u32[]{:S(2)}) copy-start(bf16[2,1024]{1,0:T(2,128)(2,1)} %param.30) | copy-start | bytes 12292
  0.7 12.8 %copy-start.7 = (bf16[2,1024]{1,0:T(2,128)(2,1)S(1)}, bf16[2,1024]{1,0:T(2,128)(2,1)}, u32[]{:S(2)}) copy-start(bf16[2,1024]{1,0:T(2,128)(2,1)} %param.28) | copy-start | bytes 12292
  0.7 12.8 %copy-start = (bf16[1024,1024]{1,0:T(8,128)(2,1)S(1)}, bf16[1024,1024]{1,0:T(8,128)(2,1)}, u32[]{:S(2)}) copy-start(bf16[1024,1024]{1,0:T(8,128)(2,1)} %x_ref.1) | copy-start | bytes 6291460
  0.7 12.8 %copy-start.9 = (s32[1,4]{1,0:T(1,128)S(1)}, s32[1,4]{1,0:T(1,128)}, u32[]{:S(2)}) copy-start(s32[1,4]{1,0:T(1,128)} %param.32) | copy-start | bytes 52
  54.3 7.4 %collective-permute-start = (f32[1024,1024]{1,0:T(8,128)}, f32[1024,1024]{1,0:T(8,128)S(1)}, u32[]{:S(2)}, u32[]{:S(2)}) collective-permute-start(f32[1024,1024]{1,0:T(8,128)} %get-tuple-element.279), channel_id=1, source_target_pairs={{0,1},{1,0},{2,3},{3,2},{4,5},{5,4},{6,7},{7,6},{8,9},{9,8},{10,11... | collective-permute-start | bytes 12582920 | tf_op jit(solution)/shard_map/ppermute | solution.py:1062
  181.1 15.4 %collective-permute-start.3 = (f32[16,512,256]{2,1,0:T(8,128)}, f32[16,512,256]{2,1,0:T(8,128)}, u32[]{:S(2)}, u32[]{:S(2)}) collective-permute-start(f32[16,512,256]{2,1,0:T(8,128)} %get-tuple-element.292), channel_id=1, source_target_pairs={{1,0},{3,2},{5,4},{7,6},{9,8},{11,10},{13,12},{15,14},{17,16},{19,... | collective-permute-start | bytes 25165832 | tf_op jit(solution)/shard_map/ppermute | solution.py:1092
  182.4 29.3 %collective-permute-start.2 = (f32[1024,1024]{1,0:T(8,128)}, f32[1024,1024]{1,0:T(8,128)}, u32[]{:S(2)}, u32[]{:S(2)}) collective-permute-start(f32[1024,1024]{1,0:T(8,128)} %get-tuple-element.285.own_ref), channel_id=1, source_target_pairs={{0,1},{1,0},{2,3},{3,2},{4,5},{5,4},{6,7},{7,6},{8,9},{9,8},{10,11... | collective-permute-start | bytes 12582920 | tf_op jit(solution)/shard_map/ppermute | solution.py:1090
  196.5 15.2 %copy-start.1 = (bf16[1024,1024]{1,0:T(8,128)(2,1)S(1)}, bf16[1024,1024]{1,0:T(8,128)(2,1)}, u32[]{:S(2)}) copy-start(bf16[1024,1024]{1,0:T(8,128)(2,1)} %grad_ref.1) | copy-start | bytes 6291460
  205.0 97.0 %collective-permute-start.4 = (f32[2,2,2,528,256]{4,3,2,1,0:T(8,128)}, f32[2,2,2,528,256]{4,3,2,1,0:T(8,128)}, u32[]{:S(2)}, u32[]{:S(2)}) collective-permute-start(f32[2,2,2,528,256]{4,3,2,1,0:T(8,128)} %get-tuple-element.294), channel_id=1, source_target_pairs={{0,2},{2,0},{4,6},{6,4},{8,10},{10,8},{12,14},{14,12},{16,18},{18,... | collective-permute-start | bytes 12976136 | tf_op jit(solution)/shard_map/ppermute | solution.py:951
  208.0 95.5 %collective-permute-start.5 = (f32[2,2,2,528,256]{4,3,2,1,0:T(8,128)}, f32[2,2,2,528,256]{4,3,2,1,0:T(8,128)}, u32[]{:S(2)}, u32[]{:S(2)}) collective-permute-start(f32[2,2,2,528,256]{4,3,2,1,0:T(8,128)} %get-tuple-element.295), channel_id=1, source_target_pairs={{0,4},{2,6},{4,0},{6,2},{8,12},{10,14},{12,8},{14,10},{16,20},{18,... | collective-permute-start | bytes 12976136 | tf_op jit(solution)/shard_map/ppermute | solution.py:951
  209.5 86.8 %collective-permute-start.6 = (f32[2,2,2,480,256]{4,3,2,1,0:T(8,128)}, f32[2,2,2,480,256]{4,3,2,1,0:T(8,128)}, u32[]{:S(2)}, u32[]{:S(2)}) collective-permute-start(f32[2,2,2,480,256]{4,3,2,1,0:T(8,128)} %get-tuple-element.296), channel_id=1, source_target_pairs={{0,8},{2,10},{4,12},{6,14},{8,0},{10,2},{12,4},{14,6},{16,24},{18,... | collective-permute-start | bytes 11796488 | tf_op jit(solution)/shard_map/ppermute | solution.py:951
  211.7 8.3 %copy-start.3 = (bf16[1024,1024]{1,0:T(8,128)(2,1)S(1)}, bf16[1024,1024]{1,0:T(8,128)(2,1)}, u32[]{:S(2)}) copy-start(bf16[1024,1024]{1,0:T(8,128)(2,1)} %get-tuple-element.287) | copy-start | bytes 6291460
  288.4 39.5 %collective-permute-start.8 = (f32[16,512,256]{2,1,0:T(8,128)}, f32[16,512,256]{2,1,0:T(8,128)}, u32[]{:S(2)}, u32[]{:S(2)}) collective-permute-start(f32[16,512,256]{2,1,0:T(8,128)} %get-tuple-element.299), channel_id=1, source_target_pairs={{1,0},{3,2},{5,4},{7,6},{9,8},{11,10},{13,12},{15,14},{17,16},{19,... | collective-permute-start | bytes 25165832 | tf_op jit(solution)/shard_map/ppermute | solution.py:1092
  289.7 20.1 %collective-permute-start.1 = (f32[1024,1024]{1,0:T(8,128)}, f32[1024,1024]{1,0:T(8,128)}, u32[]{:S(2)}, u32[]{:S(2)}) collective-permute-start(f32[1024,1024]{1,0:T(8,128)} %get-tuple-element.281), channel_id=1, source_target_pairs={{0,1},{1,0},{2,3},{3,2},{4,5},{5,4},{6,7},{7,6},{8,9},{9,8},{10,11... | collective-permute-start | bytes 12582920 | tf_op jit(solution)/shard_map/ppermute | solution.py:1062
  303.5 0.8 copy-start.8
  303.5 14.9 %collective-permute-start.7 = (f32[1024,1024]{1,0:T(8,128)}, f32[1024,1024]{1,0:T(8,128)}, u32[]{:S(2)}, u32[]{:S(2)}) collective-permute-start(f32[1024,1024]{1,0:T(8,128)} %after.1.own_ref), channel_id=1, source_target_pairs={{0,1},{1,0},{2,3},{3,2},{4,5},{5,4},{6,7},{7,6},{8,9},{9,8},{10,11... | collective-permute-start | bytes 12582920 | tf_op jit(solution)/shard_map/ppermute | solution.py:1090
  304.4 14.0 %copy-start.2 = (f32[1024,1024]{1,0:T(8,128)S(1)}, f32[1024,1024]{1,0:T(8,128)}, u32[]{:S(2)}) copy-start(f32[1024,1024]{1,0:T(8,128)} %after.1.own_ref) | copy-start | bytes 12582916
  616.4 5.9 copy-start.4

commit v5 on v4

--- a/solution.py
+++ b/solution.py
@@ -241,8 +241,8 @@
 
 
 def mlp_backward_kernel(
-    grad_ref, h_ref, act_ref, slope_ref, down_ref, up_ref,
-    part_ref, weight_ref, near_ref, far_ref, bias_ref, grad_t, h_t,
+    place_ref, grad_ref, h_ref, act_ref, slope_ref, down_ref, up_ref,
+    part_ref, along_x, kept_x, along_y, kept_y, along_z, kept_z, bias_ref, grad_t, h_t, units,
 ):
     step = pl.program_id(0)
 
@@ -252,66 +252,83 @@
         h_t[...] = h_ref[...].T
         part_ref[...] = jnp.zeros_like(part_ref)
 
-    length = h_ref.shape[0]
     bias = jnp.zeros((1, FF_BLOCK), F32)
-    pieces = []
-    for first in range(0, length, ROWS):
+    for first in range(0, h_ref.shape[0], ROWS):
         rows = slice(first, first + ROWS)
         grad_act = dot_nt(grad_ref[rows], down_ref[0, 0])
         grad_unit = (grad_act * slope_ref[0, rows].astype(F32)).astype(BF16)
         bias += jnp.sum(grad_unit.astype(F32), axis=0, keepdims=True)
-        pieces.append(grad_unit)
+        units[rows] = grad_unit
         part_ref[rows] += dot_nn(grad_unit, up_ref[0])
-    bias_ref[0] = bias
-    units = jnp.concatenate(pieces, axis=0)
-    folded, half = near_ref.shape[1], near_ref.shape[2] // 2
-    for first in range(0, h_t.shape[0], ROWS):
+    bias_ref[pl.ds(step, 1)] = bias
+
+    def block(y, x):
+        return pl.ds(pl.multiple_of((2 * y + x) * WIDE, WIDE), WIDE)
+
+    near_x, near_y = place_ref[0], place_ref[1]
+    split_rows = along_x.shape[2]
+    for first in range(0, split_rows, ROWS):
         rows = slice(first, first + ROWS)
-        for block in range(FF_BLOCK // WIDE):
-            lanes = slice(block * WIDE, (block + 1) * WIDE)
-            weight_ref[block, rows] = dot_nn(grad_t[rows], act_ref[0, :, lanes])
-            up_grad = dot_nn(h_t[rows], units[:, lanes])
-            side = 0 if first < folded else half
-            place = slice(first % folded, first % folded + ROWS)
-            near_ref[block, place, side : side + half] = up_grad[:, :half]
-            far_ref[block, place, side : side + half] = up_grad[:, half:]
-
-
-def mlp_backward(layer, grad, h, act, slope, down_weight, up):
+        other = slice(split_rows + first, split_rows + first + ROWS)
+        for side in range(2):
+            for target, x in ((along_x, 1 - near_x), (kept_x, near_x)):
+                target[0, side, rows] = dot_nn(grad_t[rows], act_ref[0, :, block(side, x)])
+            for target, y in ((along_y, 1 - near_y), (kept_y, near_y)):
+                target[0, side, rows] = dot_nn(grad_t[other], act_ref[0, :, block(y, side)])
+
+    def up_grads(target):
+        for first in range(0, h_t.shape[0], ROWS):
+            rows = slice(first, first + ROWS)
+            for index in range(FF_BLOCK // WIDE):
+                lanes = slice(index * WIDE, (index + 1) * WIDE)
+                target[0, index, rows] = dot_nn(h_t[rows], units[:, lanes])
+
+    stays = lax.rem(step, 2) == place_ref[2]
+    pl.when(stays)(functools.partial(up_grads, kept_z))
+    pl.when(jnp.logical_not(stays))(functools.partial(up_grads, along_z))
+
+
+def halves_of(width):
+    pair = (4, 2, width // 2, WIDE)
+    single = (2, 4, width, WIDE)
+    return [jax.ShapeDtypeStruct(shape, F32) for shape in (pair,) * 4 + (single,) * 2]
+
+
+def mlp_backward(layer, place, grad, h, act, slope, down_weight, up):
     length, width = h.shape
     hidden = up.shape[1]
     blocks = hidden // FF_BLOCK
-    per = FF_BLOCK // WIDE
-    halves = jax.ShapeDtypeStruct((hidden // WIDE, width // 2, WIDE), F32)
+    pair = pl.BlockSpec((1, 2, width // 2, WIDE), lambda j, *_: (j, 0, 0, 0))
+    single = pl.BlockSpec(
+        (1, 4, width, WIDE), lambda j, *_: (j // 2, 0, 0, 0), pipeline_mode=pl.Buffered(1)
+    )
+    plane = pl.BlockSpec((1, length, FF_BLOCK), lambda j, *_: (j, 0, 0))
     return pl.pallas_call(
         mlp_backward_kernel,
-        grid=(blocks,),
-        in_specs=[
-            whole((length, width)),
-            whole((length, width)),
-            plane_block(length, FF_BLOCK),
-            plane_block(length, FF_BLOCK),
-            pl.BlockSpec((1, 1, FF_BLOCK, width), lambda j: (0, layer, j, 0)),
-            pl.BlockSpec((1, FF_BLOCK, width), lambda j: (layer, j, 0)),
-        ],
-        out_specs=[
-            whole((length, width)),
-            pl.BlockSpec((per, width, WIDE), lambda j: (j, 0, 0)),
-            pl.BlockSpec((per, width // 2, WIDE), lambda j: (j, 0, 0)),
-            pl.BlockSpec((per, width // 2, WIDE), lambda j: (j, 0, 0)),
-            pl.BlockSpec((1, 1, FF_BLOCK), lambda j: (j, 0, 0)),
-        ],
-        out_shape=[
-            jax.ShapeDtypeStruct((length, width), F32),
-            jax.ShapeDtypeStruct((hidden // WIDE, width, WIDE), F32),
-            halves,
-            halves,
-            jax.ShapeDtypeStruct((blocks, 1, FF_BLOCK), F32),
-        ],
-        scratch_shapes=[pltpu.VMEM((width, length), BF16), pltpu.VMEM((width, length), BF16)],
+        grid_spec=pltpu.PrefetchScalarGridSpec(
+            num_scalar_prefetch=1,
+            grid=(blocks,),
+            in_specs=[
+                whole((length, width)),
+                whole((length, width)),
+                plane,
+                plane,
+                pl.BlockSpec((1, 1, FF_BLOCK, width), lambda j, *_: (0, layer, j, 0)),
+                pl.BlockSpec((1, FF_BLOCK, width), lambda j, *_: (layer, j, 0)),
+            ],
+            out_specs=[whole((length, width))] + [pair] * 4 + [single] * 2
+            + [whole((blocks, FF_BLOCK))],
+            scratch_shapes=[
+                pltpu.VMEM((width, length), BF16),
+                pltpu.VMEM((width, length), BF16),
+                pltpu.VMEM((length, FF_BLOCK), BF16),
+            ],
+        ),
+        out_shape=[jax.ShapeDtypeStruct((length, width), F32)] + halves_of(width)
+        + [jax.ShapeDtypeStruct((blocks, FF_BLOCK), F32)],
         compiler_params=params(),
         name="mlp_backward",
-    )(grad, h, act, slope, down_weight, up)
+    )(place, grad, h, act, slope, down_weight, up)
 
 
 def head_sums(values, ones):
@@ -445,11 +462,12 @@
 
 
 def attention_backward_kernel(
-    starts_ref, grad_ref, h_ref, state_ref, mixed_ref, table_ref, cosine_ref, sine_ref, weight_ref,
-    part_ref, out_ref, bias_ref, near_ref, far_ref,
+    place_ref, starts_ref, grad_ref, h_ref, state_ref, mixed_ref, table_ref, cosine_ref, sine_ref,
+    weight_ref, part_ref, along_x, kept_x, along_y, kept_y, along_z, kept_z, bias_ref,
     mask_ref, grad_t, h_t, numer_ref, feat_ref, flow, query_t,
 ):
-    del near_ref, far_ref
+    del along_z, kept_z
+    group = pl.program_id(0)
     length = h_ref.shape[0]
 
     @pl.when(pl.program_id(0) == 0)
@@ -535,84 +553,105 @@
             total = total + dot_nn(block, weight_ref[0, 0, kind, 0])
         part_ref[rows] = total
     for kind in range(3):
-        bias_ref[kind, 0] = sums[kind]
-    bias_ref[3, 0] = jnp.zeros((1, WIDE), F32)
-    for first in range(0, h_t.shape[0], ROWS):
-        rows = slice(first, first + ROWS)
-        for kind in range(3):
-            out_ref[kind, 0, rows] = dot_nn(h_t[rows], flow[kind])
-        out_ref[3, 0, rows] = dot_nn(grad_t[rows], mixed_ref[0])
-
-
-def attention_backward(layer, starts, grad, h, state, mixed, tables, rotary, weight):
+        bias_ref[kind : kind + 1] = sums[kind]
+    lanes = pl.ds(pl.multiple_of(group * WIDE, WIDE), WIDE)
+    bias_ref[3:4] = jnp.sum(grad_ref[:, lanes].astype(F32), axis=0, keepdims=True)
+    split_rows = along_x.shape[2]
+
+    def weights(target, base):
+        for first in range(0, split_rows, ROWS):
+            rows = slice(first, first + ROWS)
+            held = slice(base + first, base + first + ROWS)
+            for kind in range(3):
+                target[kind, 0, rows] = dot_nn(h_t[held], flow[kind])
+            target[3, 0, rows] = dot_nn(grad_t[held], mixed_ref[0])
+
+    stays = lax.rem(group, 2) == place_ref[0]
+    pl.when(stays)(functools.partial(weights, kept_x, 0))
+    pl.when(jnp.logical_not(stays))(functools.partial(weights, along_x, 0))
+    stays = group // 2 == place_ref[1]
+    pl.when(stays)(functools.partial(weights, kept_y, split_rows))
+    pl.when(jnp.logical_not(stays))(functools.partial(weights, along_y, split_rows))
+
+
+def attention_backward(layer, place, starts, grad, h, state, mixed, tables, rotary, weight):
     _, length, width = state.shape
-    blocks = 4 * QUADS
-    four = pl.BlockSpec((4, length, WIDE), lambda g: (0, 0, g))
-    halves = jax.ShapeDtypeStruct((blocks, width // 2, WIDE), F32)
-    part, out, bias, near, far = pl.pallas_call(
+    four = pl.BlockSpec((4, length, WIDE), lambda g, *_: (0, 0, g))
+    shape = (4, 1, width // 2, WIDE)
+    first = pl.BlockSpec(shape, lambda g, *_: (0, g // 2, 0, 0))
+
+    def second(side):
+        def index(g, place_ref):
+            y, chosen = g // 2, place_ref[1] if side else 1 - place_ref[1]
+            at = jnp.where(y == chosen, g % 2, jnp.where(y < chosen, 0, 1))
+            return 0, at, 0, 0
+
+        return pl.BlockSpec(shape, index)
+
+    return pl.pallas_call(
         attention_backward_kernel,
-        grid=(QUADS,),
-        in_specs=[
-            pl.BlockSpec(memory_space=pltpu.SMEM),
-            whole((length, width)),
-            whole((length, width)),
-            four,
-            four,
-            pl.BlockSpec((1, 1, WIDE, WIDE), lambda g: (layer, g, 0, 0)),
-            whole((length, PAIR)),
-            whole((length, PAIR)),
-            pl.BlockSpec((1, 1, 4, 1, WIDE, width), lambda g: (0, layer, 0, g, 0, 0)),
-        ],
-        out_specs=[
-            whole((length, width)),
-            pl.BlockSpec((4, 1, width, WIDE), lambda g: (0, g, 0, 0)),
-            pl.BlockSpec((4, 1, 1, WIDE), lambda g: (0, g, 0, 0)),
-            pl.BlockSpec(memory_space=pl.ANY),
-            pl.BlockSpec(memory_space=pl.ANY),
-        ],
-        out_shape=[
-            jax.ShapeDtypeStruct((length, width), F32),
-            jax.ShapeDtypeStruct((4, QUADS, width, WIDE), F32),
-            jax.ShapeDtypeStruct((4, QUADS, 1, WIDE), F32),
-            halves,
-            halves,
-        ],
-        scratch_shapes=[
-            pltpu.VMEM((length, length), BF16),
-            pltpu.VMEM((width, length), BF16),
-            pltpu.VMEM((width, length), BF16),
-            pltpu.VMEM((2, length, WIDE), BF16),
-            pltpu.VMEM((2, length, WIDE), BF16),
-            pltpu.VMEM((3, length, WIDE), BF16),
-            pltpu.VMEM((2, DH, length), F32),
-        ],
+        grid_spec=pltpu.PrefetchScalarGridSpec(
+            num_scalar_prefetch=1,
+            grid=(QUADS,),
+            in_specs=[
+                pl.BlockSpec(memory_space=pltpu.SMEM),
+                whole((length, width)),
+                whole((length, width)),
+                four,
+                four,
+                pl.BlockSpec((1, 1, WIDE, WIDE), lambda g, *_: (layer, g, 0, 0)),
+                whole((length, PAIR)),
+                whole((length, PAIR)),
+                pl.BlockSpec((1, 1, 4, 1, WIDE, width), lambda g, *_: (0, layer, 0, g, 0, 0)),
+            ],
+            out_specs=[whole((length, width)), first, first, second(False), second(True)]
+            + [pl.BlockSpec(memory_space=pl.ANY)] * 2
+            + [pl.BlockSpec((4, WIDE), lambda g, *_: (0, g))],
+            scratch_shapes=[
+                pltpu.VMEM((length, length), BF16),
+                pltpu.VMEM((width, length), BF16),
+                pltpu.VMEM((width, length), BF16),
+                pltpu.VMEM((2, length, WIDE), BF16),
+                pltpu.VMEM((2, length, WIDE), BF16),
+                pltpu.VMEM((3, length, WIDE), BF16),
+                pltpu.VMEM((2, DH, length), F32),
+            ],
+        ),
+        out_shape=[jax.ShapeDtypeStruct((length, width), F32)] + halves_of(width)
+        + [jax.ShapeDtypeStruct((4, width), F32)],
         compiler_params=params(),
         name="attention_backward",
-    )(starts, grad, h, state, mixed, tables[0], *rotary, kinds_of(weight))
-    return part, out.reshape(blocks, width, WIDE), near, far, bias.reshape(blocks, WIDE)
-
-
-def norm_backward_kernel(x_ref, own_ref, other_ref, grad_ref, gain_ref, out_ref, sums_ref):
-    @pl.when(pl.program_id(0) == 0)
-    def _():
-        sums_ref[...] = jnp.zeros_like(sums_ref)
-
-    values = x_ref[...].astype(F32)
+    )(place, starts, grad, h, state, mixed, tables[0], *rotary, kinds_of(weight))
+
+
+def norm_gradient(values, incoming, grad, gain, sums_ref):
     average = jnp.mean(values, -1, keepdims=True)
     centered = values - average
     variance = jnp.mean(centered * centered, -1, keepdims=True)
     inverse = lax.rsqrt(variance + EPSILON)
     unit = centered * inverse
-    incoming = own_ref[...] + other_ref[...]
-    grad_unit = incoming * gain_ref[...].astype(F32)
+    grad_unit = incoming * gain
     first = jnp.mean(grad_unit, -1, keepdims=True)
     second = jnp.mean(grad_unit * unit, -1, keepdims=True)
-    grad = grad_ref[...].astype(F32)
-    out = grad + inverse * (grad_unit - first - unit * second)
-    out_ref[...] = out.astype(out_ref.dtype)
     sums_ref[0:1] += jnp.sum(incoming * unit, axis=0, keepdims=True)
     sums_ref[1:2] += jnp.sum(incoming, axis=0, keepdims=True)
     sums_ref[2:3] += jnp.sum(grad, axis=0, keepdims=True)
+    return grad + inverse * (grad_unit - first - unit * second)
+
+
+def norm_backward_kernel(x_ref, own_ref, other_ref, grad_ref, gain_ref, out_ref, sums_ref):
+    @pl.when(pl.program_id(0) == 0)
+    def _():
+        sums_ref[...] = jnp.zeros_like(sums_ref)
+
+    out = norm_gradient(
+        x_ref[...].astype(F32),
+        own_ref[...] + other_ref[...],
+        grad_ref[...].astype(F32),
+        gain_ref[...].astype(F32),
+        sums_ref,
+    )
+    out_ref[...] = out.astype(out_ref.dtype)
 
 
 def norm_backward(x, own, other, grad, gain, kind):
@@ -636,57 +675,34 @@
 UNIT = 8
 SLOTS = 4
 LAG = 1
+JOB = 128
 
 
 class Flow(NamedTuple):
     order: tuple
+    family: int
     layer: int
-    begun: int
+    row: int
+    units: int
     start: int
-    segments: tuple
-
-
-def first_rows(rows):
-    cuts = (0, rows * 11 // 32, rows * 22 // 32, rows)
-    return tuple(zip(cuts[:-1], cuts[1:]))
-
-
-def begun_flows(rows, layer):
-    orders = (((0, 1, 2, 3),) * 2, ((1, 0, 2, 3),) * 2, ((2, 0, 1, 3), (2, 1, 0, 3)))
-    flows = []
-    for way in range(3):
-        for part in range(2):
-            segments = []
-            for is_up in range(2):
-                first, finish = first_rows(rows[is_up])[way]
-                half = (finish - first) // 2
-                base = first_rows(rows[0])[way]
-                base = base[1] - base[0] if is_up else 0
-                segments.append(
-                    (bool(is_up), first + part * half, half // UNIT, base + part * half)
-                )
-            flows.append(Flow(orders[way][part], layer, way, 0, tuple(segments)))
-    return flows
-
-
-def fresh_flows(rows, layer, start):
-    orders = ((0, 1, 2, 3), (1, 0, 2, 3)) + ((0, 2, 3, 1), (1, 2, 3, 0)) * 2
-    count = len(orders)
-    flows, at = [], [0, 0]
-    for index, order in enumerate(orders):
-        segments = []
-        for is_up in range(2):
-            units = rows[is_up] // UNIT
-            place = index if is_up == 0 else count - 1 - index
-            share = units // count + (place < units % count)
-            segments.append((bool(is_up), at[is_up] * UNIT, share, 0))
-            at[is_up] += share
-        flows.append(Flow(order, layer, -1, start, tuple(segments)))
-    return flows
-
-
-def units_of(flow):
-    return sum(segment[2] for segment in flow.segments)
+
+
+def flows_of(width, layer, start):
+    rows = width // 4
+    kinds = (
+        ((0, 1, 2, 3), 0, 0),
+        ((1, 0, 2, 3), 1, 0),
+        ((2, 0, 1, 3), 2, 0),
+        ((2, 1, 0, 3), 2, 1),
+        ((0, 1, 2, 3), 0, 1),
+        ((1, 0, 2, 3), 1, 1),
+        ((2, 0, 1, 3), 2, 2),
+        ((2, 1, 0, 3), 2, 3),
+    )
+    return [
+        Flow(order, family, layer, part * rows, rows // UNIT, start)
+        for order, family, part in kinds
+    ]
 
 
 def bit_of(index, bit):
@@ -697,26 +713,135 @@
     return index + (1 << bit) * (1 - 2 * bit_of(index, bit))
 
 
-def scatter_kernel(bits, flows, layers, *refs):
-    sources, refs = refs[: 3 * layers], refs[3 * layers :]
-    halves, refs = refs[:3], refs[3:]
-    small_ref, weight_out, up_out, small_out = refs[:4]
+def finish_kernel(
+    bits, flows,
+    kept_x1, kept_y1, kept_z1, came_x1, came_y1, came_z1,
+    kept_x0, kept_y0, kept_z0, sent_x0, sent_y0, sent_z0,
+    part_ref, tokens_ref, grad_ref, x_ref, own_ref, other_ref,
+    bias0_ref, bias1_ref, sums1_ref, gain_ref,
+    weight_out, up_out, small_out, result_out, grad_out,
+    weight_sum, up_sum, up_turned, up_came, part, part_came, tokens, grad, x, own, other, sums,
+    *scratch,
+):
     stages = bits
-    weight_sum, up_sum = refs[4:6]
-    small_held = refs[6 : 6 + stages]
-    held = refs[6 + stages :]
-    held, sems = held[: len(flows) * (stages + 1)], held[len(flows) * (stages + 1) :]
-    load_sem, send_sem, recv_sem, credit, small_send, small_recv = sems
+    kept = ((kept_x1, kept_y1, kept_z1), (kept_x0, kept_y0, kept_z0))
+    moved = ((came_x1, came_y1, came_z1), (sent_x0, sent_y0, sent_z0))
+    held = scratch[: len(flows) * (stages + 1)]
     held = [held[f * (stages + 1) : (f + 1) * (stages + 1)] for f in range(len(flows))]
+    small = scratch[len(flows) * (stages + 1) :][: stages + 1]
+    small_came = scratch[len(flows) * (stages + 1) + stages + 1 :][:stages]
+    load_sem, send_sem, recv_sem, credit, small_send, small_recv, job_sem, near_send, near_recv = (
+        scratch[len(flows) * (stages + 1) + 2 * stages + 1 :]
+    )
     me, core = lax.axis_index("batch"), lax.axis_index("stream")
-    totals = [units_of(flow) for flow in flows]
 
     barrier = pltpu.get_barrier_semaphore()
     for bit in range(bits):
         pl.semaphore_signal(
             barrier, inc=1, device_id={"batch": flip(me, bit)}, device_id_type=MESH
         )
-    pl.semaphore_wait(barrier, bits)
+    pl.semaphore_signal(barrier, inc=1, device_id={"stream": 1 - core}, device_id_type=MESH)
+    pl.semaphore_wait(barrier, bits + 1)
+
+    exchange = pltpu.make_async_remote_copy(
+        src_ref=part_ref,
+        dst_ref=part_came,
+        send_sem=near_send.at[2],
+        recv_sem=near_recv.at[2],
+        device_id={"stream": 1 - core},
+        device_id_type=MESH,
+    )
+    loads = [
+        pltpu.make_async_copy(source, target, job_sem.at[index])
+        for index, (source, target) in enumerate(
+            ((part_ref, part), (tokens_ref, tokens), (grad_ref, grad), (x_ref, x),
+             (own_ref, own), (other_ref, other))
+        )
+    ]
+    stores = [
+        pltpu.make_async_copy(part, grad_out, job_sem.at[len(loads)]),
+        pltpu.make_async_copy(x, result_out, job_sem.at[len(loads) + 1]),
+    ]
+    exchange.start()
+    for copy in loads:
+        copy.start()
+    jobs = part.shape[0] // JOB
+    norm_start, result_start = 3, 3 + jobs
+    small_start = result_start + 1
+    turn_start = max(flow.start + flow.units for flow in flows[: len(flows) // 2]) + stages + 1
+
+    def norm_job(index):
+        rows = pl.ds(pl.multiple_of((index - norm_start) * JOB, JOB), JOB)
+
+        @pl.when(index == norm_start)
+        def _():
+            exchange.wait()
+            for copy in loads[:3]:
+                copy.wait()
+            sums[...] = jnp.zeros_like(sums)
+
+        part[rows] = norm_gradient(
+            tokens[rows].astype(F32),
+            part[rows] + part_came[rows],
+            grad[rows].astype(F32),
+            gain_ref[...].astype(F32),
+            sums,
+        )
+
+    def result_job(index):
+        rows = pl.ds(pl.multiple_of((index - result_start) * JOB, JOB), JOB)
+
+        @pl.when(index == result_start)
+        def _():
+            stores[0].start()
+            for copy in loads[3:]:
+                copy.wait()
+
+        x[rows] = x[rows] + (own[rows] + other[rows])
+
+    def near_copy(layer):
+        return pltpu.make_async_remote_copy(
+            src_ref=up_turned.at[layer],
+            dst_ref=up_came.at[layer],
+            send_sem=near_send.at[layer],
+            recv_sem=near_recv.at[layer],
+            device_id={"stream": 0},
+            device_id_type=MESH,
+        )
+
+    def turn_weights(layer):
+        weight_out[len(moved) - 1 - layer] = weight_sum[layer].T
+
+        @pl.when(core == 1)
+        def _():
+            up_turned[layer] = up_sum[layer, :, : WIDE // 2].T
+            near_copy(layer).start()
+            up_out[len(moved) - 1 - layer] = up_sum[layer, :, WIDE // 2 :].T
+
+    def small_copy(stage):
+        return pltpu.make_async_remote_copy(
+            src_ref=small[stage],
+            dst_ref=small_came[stage],
+            send_sem=small_send.at[stage],
+            recv_sem=small_recv.at[stage],
+            device_id={"batch": flip(me, stage)},
+            device_id_type=MESH,
+        )
+
+    def small_step(stage):
+        if stage == 0:
+            rows = bias0_ref.shape[0]
+            small[0][0:rows] = bias0_ref[...]
+            small[0][rows : 2 * rows] = bias1_ref[...]
+            small[0][2 * rows : 2 * rows + 8] = sums1_ref[...]
+            small[0][2 * rows + 8 : 2 * rows + 16] = sums[...]
+        else:
+            small_copy(stage - 1).wait()
+            small[stage][...] = small[stage - 1][...] + small_came[stage - 1][...]
+        if stage < stages:
+            small_copy(stage).start()
+        else:
+            small_out[...] = small[stage][...]
 
     def view(order, stage, mine):
         left = sorted(set(range(bits)) - set(order[:stage]), reverse=True)
@@ -724,267 +849,158 @@
         pick = pick if mine else 1 - pick
         return tuple(pick if bit == order[stage] else slice(None) for bit in left)
 
-    def remote(flow, stage, slot, source):
+    def remote(place, stage, slot, source):
         return pltpu.make_async_remote_copy(
             src_ref=source,
-            dst_ref=held[flow][stage + 1].at[slot],
-            send_sem=send_sem.at[flow, stage, slot],
-            recv_sem=recv_sem.at[flow, stage, slot],
-            device_id={"batch": flip(me, flows[flow].order[stage])},
+            dst_ref=held[place][stage + 1].at[slot],
+            send_sem=send_sem.at[place, stage, slot],
+            recv_sem=recv_sem.at[place, stage, slot],
+            device_id={"batch": flip(me, flows[place].order[stage])},
             device_id_type=MESH,
         )
 
-    def sent_from(flow, stage, slot):
+    def sent_from(place, stage, slot):
         if stage == 0:
-            return held[flow][0].at[slot]
-        return held[flow][stage].at[(slot,) + view(flows[flow].order, stage, False)]
-
-    def load(flow, slot, source):
-        return pltpu.make_async_copy(source, held[flow][0].at[slot], load_sem.at[flow, slot])
-
-    def load_half(flow, slot, source):
+            return held[place][0].at[slot]
+        return held[place][stage].at[(slot,) + view(flows[place].order, stage, False)]
+
+    def load(place, slot, source):
+        return pltpu.make_async_copy(source, held[place][0].at[slot], load_sem.at[place, slot])
+
+    def load_came(place, slot, source):
         return pltpu.make_async_copy(
-            source, held[flow][1].at[slot], recv_sem.at[flow, 0, slot]
-        )
-
-    def return_credit(flow, stage, unit):
-        if stage == 0 and flows[flow].begun >= 0:
+            source, held[place][1].at[slot], recv_sem.at[place, 0, slot]
+        )
+
+    def return_credit(place, stage, unit):
+        if stage == 0 and flows[place].layer == 0:
             return
 
-        @pl.when(unit + SLOTS < totals[flow])
+        @pl.when(unit + SLOTS < flows[place].units)
         def _():
             pl.semaphore_signal(
-                credit.at[flow, stage],
+                credit.at[place, stage],
                 inc=1,
-                device_id={"batch": flip(me, flows[flow].order[stage])},
+                device_id={"batch": flip(me, flows[place].order[stage])},
                 device_id_type=MESH,
             )
 
-    def take_credit(flow, stage, unit):
+    def take_credit(place, stage, unit):
         @pl.when(unit >= SLOTS)
         def _():
-            pl.semaphore_wait(credit.at[flow, stage], 1)
-
-    def places(flow, unit, act):
-        base = 0
-        for is_up, row, units, half_row in flows[flow].segments:
-            offset = (unit - base) * UNIT
-            pl.when((unit >= base) & (unit < base + units))(
-                functools.partial(act, is_up, row + offset, half_row + offset)
-            )
-            base += units
-
-    def begin(flow, unit):
+            pl.semaphore_wait(credit.at[place, stage], 1)
+
+    def begin(place, unit):
         slot = lax.rem(unit, SLOTS)
-        order, layer, begun = flows[flow][:3]
-        if begun < 0:
-            take_credit(flow, 0, unit)
-
-        def start(source, row):
-            at = (pl.ds(pl.multiple_of(row, UNIT), UNIT),)
-            load(flow, slot, source.at[view(order, 0, True) + at]).start()
-            if begun < 0:
-                remote(flow, 0, slot, source.at[view(order, 0, False) + at]).start()
-
-        def act(is_up, row, half_row):
-            if begun >= 0:
-                at = (slice(None),) * (bits - 1)
-                at += (pl.ds(pl.multiple_of(half_row, UNIT), UNIT),)
-                load_half(flow, slot, halves[begun].at[at]).start()
-            if not is_up:
-                start(sources[3 * layer], row)
-            else:
-                for side in range(2):
-                    pl.when(core == side)(
-                        functools.partial(start, sources[3 * layer + 1 + side], row)
-                    )
-
-        places(flow, unit, act)
-
-    def advance(flow, stage, unit):
+        _, family, layer, row, _, _ = flows[place]
+        at = (slice(None),) * (bits - 1)
+        at += (pl.ds(pl.multiple_of(row + unit * UNIT, UNIT), UNIT),)
+        load(place, slot, kept[layer][family].at[at]).start()
+        if layer == 0:
+            load_came(place, slot, moved[layer][family].at[at]).start()
+        else:
+            take_credit(place, 0, unit)
+            remote(place, 0, slot, moved[layer][family].at[at]).start()
+
+    def advance(place, stage, unit):
         slot = lax.rem(unit, SLOTS)
-        order, layer, begun = flows[flow][:3]
-        buffer = held[flow][stage]
-        copy = remote(flow, stage - 1, slot, sent_from(flow, stage - 1, slot))
-        if stage == 1 and begun >= 0:
-            load_half(flow, slot, held[flow][0].at[slot]).wait()
+        order, family, layer, row, _, _ = flows[place]
+        buffer = held[place][stage]
+        copy = remote(place, stage - 1, slot, sent_from(place, stage - 1, slot))
+        if stage == 1 and layer == 0:
+            load_came(place, slot, held[place][0].at[slot]).wait()
         else:
             copy.wait_recv()
         if stage == 1:
-            load(flow, slot, held[flow][1].at[slot]).wait()
-            mine = held[flow][0][slot]
+            load(place, slot, held[place][1].at[slot]).wait()
+            mine = held[place][0][slot]
         else:
-            mine = held[flow][stage - 1][(slot,) + view(order, stage - 1, True)]
+            mine = held[place][stage - 1][(slot,) + view(order, stage - 1, True)]
         value = buffer[slot] + mine
         if stage < stages:
             buffer[slot] = value
-            take_credit(flow, stage, unit)
-            remote(flow, stage, slot, sent_from(flow, stage, slot)).start()
+            take_credit(place, stage, unit)
+            remote(place, stage, slot, sent_from(place, stage, slot)).start()
         else:
-
-            def act(is_up, row, half_row):
-                target = up_sum if is_up else weight_sum
-                target[layer, pl.ds(pl.multiple_of(row, UNIT), UNIT)] = value
-
-            places(flow, unit, act)
-        if stage > 1 or begun < 0:
+            target = up_sum if family == 2 else weight_sum
+            base = row + (weight_sum.shape[1] // 2 if family == 1 else 0)
+            target[layer, pl.ds(pl.multiple_of(base + unit * UNIT, UNIT), UNIT)] = value
+        if stage > 1 or layer > 0:
             copy.wait_send()
         if stage >= 2:
-            return_credit(flow, stage - 2, unit)
+            return_credit(place, stage - 2, unit)
         if stage == stages:
-            return_credit(flow, stage - 1, unit)
-
-    small_order = tuple(range(bits))
-
-    def small_copy(stage):
-        source = small_ref if stage == 0 else small_held[stage - 1]
-        return pltpu.make_async_remote_copy(
-            src_ref=source.at[view(small_order, stage, False)],
-            dst_ref=small_held[stage],
-            send_sem=small_send.at[stage],
-            recv_sem=small_recv.at[stage],
-            device_id={"batch": flip(me, small_order[stage])},
-            device_id_type=MESH,
-        )
-
-    def small_step(stage):
-        if stage > 0:
-            small_copy(stage - 1).wait()
-            source = small_ref if stage == 1 else small_held[stage - 2]
-            sums = small_held[stage - 1][...] + source[view(small_order, stage - 1, True)]
-            if stage == stages:
-                small_out[...] = sums
-            else:
-                small_held[stage - 1][...] = sums
-        if stage < stages:
-            small_copy(stage).start()
+            return_credit(place, stage - 1, unit)
+
+    def within(place, unit):
+        inside = (unit >= 0) & (unit < flows[place].units)
+        return inside & (core == 1) if flows[place].family == 2 else inside
 
     def step(index, carry):
         for place, flow in enumerate(flows):
             unit = index - flow.start
-            pl.when((unit >= 0) & (unit < totals[place]))(
-                functools.partial(begin, place, unit)
-            )
+            pl.when(within(place, unit))(functools.partial(begin, place, unit))
         for place, flow in enumerate(flows):
             for stage in range(1, stages + 1):
                 unit = index - flow.start - LAG * stage
-                pl.when((unit >= 0) & (unit < totals[place]))(
-                    functools.partial(advance, place, stage, unit)
-                )
+                pl.when(within(place, unit))(functools.partial(advance, place, stage, unit))
+        pl.when((index >= norm_start) & (index < norm_start + jobs))(
+            functools.partial(norm_job, index)
+        )
+        pl.when((index >= result_start) & (index < result_start + jobs))(
+            functools.partial(result_job, index)
+        )
         for stage in range(stages + 1):
-            pl.when(index == stages + 2 * stage)(functools.partial(small_step, stage))
+            pl.when(index == small_start + 2 * stage)(functools.partial(small_step, stage))
+        pl.when(index == turn_start)(functools.partial(turn_weights, 0))
         return carry
 
-    last = max(flow.start + total for flow, total in zip(flows, totals))
+    last = max(flow.start + flow.units for flow in flows)
     lax.fori_loop(0, last + LAG * stages, step, 0)
-    half = WIDE // 2
-    for layer in range(layers):
-        weight_out[layers - 1 - layer] = weight_sum[layer].T
-        folded = up_sum.shape[1]
-        up_out[layers - 1 - layer, :, :folded] = up_sum[layer, :, :half].T
-        up_out[layers - 1 - layer, :, folded:] = up_sum[layer, :, half:].T
-
-
-def pack_halves(weight, near, far):
-    count, width, lanes = weight.shape
-    bits = count.bit_length() - 1
-    rows = (width, near.shape[1])
-    ranges = [first_rows(length) for length in rows]
-
-    def kernel(weight_ref, near_ref, far_ref, *refs):
-        outs, held, loads, stores = refs[:3], refs[3:6], refs[6], refs[7]
-        me, core = lax.axis_index("batch"), lax.axis_index("stream")
-
-        def load(source, is_up, bit, part):
-            first, finish = ranges[is_up][bit]
-            base = ranges[0][bit][1] - ranges[0][bit][0] if is_up else 0
-            others = [dim for dim in range(bits) if dim != bits - 1 - bit]
-            at = [slice(None)] * bits + [pl.ds(first, finish - first)]
-            at[bits - 1 - bit] = 1 - bit_of(me, bit)
-            at[others[0]] = part
-            to = (part,) + (slice(None),) * (bits - 2) + (pl.ds(base, finish - first),)
-            return pltpu.make_async_copy(
-                source.at[tuple(at)], held[bit].at[to], loads.at[is_up, bit, part]
-            )
-
-        def start(source, is_up):
-            for part in range(2):
-                for bit in range(3):
-                    load(source, is_up, bit, part).start()
-
-        start(weight_ref, 0)
-        for side, source in enumerate((near_ref, far_ref)):
-            pl.when(core == side)(functools.partial(start, source, 1))
-        copies = []
-        for part in range(2):
-            for bit in range(3):
-                load(weight_ref, 0, bit, part).wait()
-                load(near_ref, 1, bit, part).wait()
-                copy = pltpu.make_async_copy(
-                    held[bit].at[part], outs[bit].at[part], stores.at[bit, part]
-                )
-                copy.start()
-                copies.append(copy)
-        for copy in copies:
-            copy.wait()
-
-    shapes = [
-        (2,) * (bits - 1) + (sum(r[bit][1] - r[bit][0] for r in ranges), lanes) for bit in range(3)
-    ]
-    return pl.pallas_call(
-        kernel,
-        in_specs=[pl.BlockSpec(memory_space=pltpu.HBM)] * 3,
-        out_specs=[pl.BlockSpec(memory_space=pltpu.HBM)] * 3,
-        out_shape=[jax.ShapeDtypeStruct(shape, F32) for shape in shapes],
-        scratch_shapes=[pltpu.VMEM(shape, F32) for shape in shapes]
-        + [pltpu.SemaphoreType.DMA((2, 3, 2)), pltpu.SemaphoreType.DMA((3, 2))],
-        compiler_params=params(),
-        name="pack_halves",
-    )(*[array.reshape((2,) * bits + array.shape[1:]) for array in (weight, near, far)])
-
-
-def send_halves(weight, near, far):
-    count = weight.shape[0]
-    received = []
-    for bit, part in enumerate(pack_halves(weight, near, far)):
-        pairs = [(source, flip(source, bit)) for source in range(count)]
-        received.append(lax.ppermute(part, "batch", pairs))
-    return received
-
-
-def after(first, others):
-    def kernel(*refs):
-        del refs
-
-    return pl.pallas_call(
-        kernel,
-        in_specs=[pl.BlockSpec(memory_space=pltpu.HBM)] * (1 + len(others)),
-        out_specs=pl.BlockSpec(memory_space=pltpu.HBM),
-        out_shape=jax.ShapeDtypeStruct(first.shape, first.dtype),
-        input_output_aliases={0: 0},
-        name="after",
-    )(first, *others)
-
-
-def reduce_scatter(grads, halves, small):
-    layers = len(grads) // 3
-    count, width = grads[0].shape[:2]
-    folded = grads[1].shape[1]
-    bits = count.bit_length() - 1
-    small = jnp.pad(small, ((0, 0), (0, -small.shape[1] % 1024)))
-    small = small.reshape((2,) * bits + (-1, 128))
-    flows = begun_flows((width, folded), 0)
-    for layer in range(1, layers):
-        start = max(flow.start + units_of(flow) for flow in flows)
-        flows = flows + fresh_flows((width, folded), layer, start)
-    scratch = [pltpu.VMEM((layers, width, WIDE), F32), pltpu.VMEM((layers, folded, WIDE), F32)]
-    scratch += [
-        pltpu.VMEM((2,) * (bits - 1 - stage) + small.shape[-2:], F32) for stage in range(bits)
+    stores[1].start()
+    turn_weights(1)
+    for layer in range(len(moved)):
+
+        @pl.when(core == 0)
+        def _():
+            near_copy(layer).wait_recv()
+            up_out[len(moved) - 1 - layer] = up_came[layer]
+
+        @pl.when(core == 1)
+        def _():
+            near_copy(layer).wait_send()
+
+    for copy in stores:
+        copy.wait()
+
+
+def finish(last, first, came, part, tokens, grad, x, own, other, biases, sums, gain):
+    length, width = tokens.shape
+    bits = 4
+    split = (2,) * (bits - 1)
+    flows = flows_of(width, 0, 0)
+    flows += flows_of(width, 1, max(flow.start + flow.units for flow in flows))
+    small = (2 * biases[0].shape[0] + 16, width)
+    full = (length, width)
+    scratch = [
+        pltpu.VMEM((2, width, WIDE), F32),
+        pltpu.VMEM((2, width, WIDE), F32),
+        pltpu.VMEM((2, WIDE // 2, width), F32),
+        pltpu.VMEM((2, WIDE // 2, width), F32),
+        pltpu.VMEM(full, F32),
+        pltpu.VMEM(full, F32),
+        pltpu.VMEM(full, BF16),
+        pltpu.VMEM(full, BF16),
+        pltpu.VMEM(full, F32),
+        pltpu.VMEM(full, F32),
+        pltpu.VMEM(full, F32),
+        pltpu.VMEM((8, width), F32),
     ]
     for _ in flows:
         for stage in range(bits + 1):
             lead = (SLOTS,) + (2,) * (bits - 1 - max(stage - 1, 0))
             scratch.append(pltpu.VMEM(lead + (UNIT, WIDE), F32))
+    scratch += [pltpu.VMEM(small, F32)] * (2 * bits + 1)
     scratch += [
         pltpu.SemaphoreType.DMA((len(flows), SLOTS)),
         pltpu.SemaphoreType.DMA((len(flows), bits, SLOTS)),
@@ -992,24 +1008,46 @@
         pltpu.SemaphoreType.REGULAR((len(flows), bits)),
         pltpu.SemaphoreType.DMA((bits,)),
         pltpu.SemaphoreType.DMA((bits,)),
+        pltpu.SemaphoreType.DMA((8,)),
+        pltpu.SemaphoreType.DMA((3,)),
+        pltpu.SemaphoreType.DMA((3,)),
     ]
-    weight, up, small = pl.pallas_call(
-        functools.partial(scatter_kernel, bits, flows, layers),
-        in_specs=[pl.BlockSpec(memory_space=pltpu.HBM)] * (len(grads) + len(halves))
-        + [pl.BlockSpec(memory_space=pltpu.VMEM)],
-        out_specs=[pl.BlockSpec(memory_space=pltpu.VMEM)] * 3,
+    large = [last[1], last[3], last[5], *came, first[1], first[3], first[5]]
+    large += [first[0], first[2], first[4]]
+    large = [array.reshape(split + array.shape[2:]) for array in large]
+    return pl.pallas_call(
+        functools.partial(finish_kernel, bits, flows),
+        in_specs=[pl.BlockSpec(memory_space=pltpu.HBM)] * (len(large) + 6)
+        + [pl.BlockSpec(memory_space=pltpu.VMEM)] * 4,
+        out_specs=[pl.BlockSpec(memory_space=pltpu.VMEM)] * 3
+        + [pl.BlockSpec(memory_space=pltpu.HBM)] * 2,
         out_shape=[
-            jax.ShapeDtypeStruct((layers, WIDE, width), F32),
-            jax.ShapeDtypeStruct((layers, WIDE // 2, width), F32),
-            jax.ShapeDtypeStruct(small.shape[-2:], F32),
+            jax.ShapeDtypeStruct((2, WIDE, width), F32),
+            jax.ShapeDtypeStruct((2, WIDE // 2, width), F32),
+            jax.ShapeDtypeStruct(small, F32),
+            jax.ShapeDtypeStruct(full, F32),
+            jax.ShapeDtypeStruct(full, F32),
         ],
         scratch_shapes=scratch,
         compiler_params=pltpu.CompilerParams(
             collective_id=0, has_side_effects=True, vmem_limit_bytes=VMEM_LIMIT
         ),
-        name="reduce_scatter",
-    )(*[array.reshape((2,) * bits + array.shape[1:]) for array in grads], *halves, small)
-    return weight, up, small.reshape(-1)
+        name="finish",
+    )(*large, part, tokens, grad, x, own, other, biases[0], biases[1], sums, gain)
+
+
+def send_first(halves):
+    count = lax.axis_size("batch")
+    received = []
+    for bit, part in enumerate(halves[0::2]):
+        streams = (1,) if bit == 2 else (0, 1)
+        pairs = [
+            (2 * source + stream, 2 * flip(source, bit) + stream)
+            for source in range(count)
+            for stream in streams
+        ]
+        received.append(lax.ppermute(part, ("batch", "stream"), pairs))
+    return received
 
 
 def shards(
@@ -1062,65 +1100,60 @@
         stream = (inputs[-1], part, lax.ppermute(part, "stream", swap))
     result = stream[0] + (stream[1] + stream[2])
 
+    count = lax.axis_size("batch")
+    blocked = count == branch_weight.shape[2] // WIDE
+    me = lax.axis_index("batch") if blocked else 0
+    place = jnp.stack([jnp.asarray(bit_of(me, bit), jnp.int32) for bit in range(3)])
+
     def attention_back(layer, grad):
         h, state, mixed = kept[layer]
         return attention_backward(
-            layer, doc_starts, grad, h, state, mixed, tables, rotary, branch_weight
+            layer, place, doc_starts, grad, h, state, mixed, tables, rotary, branch_weight
         )
 
     def feed_forward_back(layer, grad):
         h, act, slope = kept[layer]
-        part, weight, near, far, bias = mlp_backward(
-            layer, grad, h, act, slope, branch_weight, up_weight
-        )
-        return part, weight, near, far, bias.reshape(-1, WIDE)
-
-    grad = cotangent
-    count = lax.axis_size("batch")
-    blocked = count == branch_weight.shape[2] // WIDE
-    grads, vectors = [], []
-    for layer in reversed(range(LAYERS)):
-        part, weight, near, far, bias = lax.cond(
+        return mlp_backward(layer, place, grad, h, act, slope, branch_weight, up_weight)
+
+    def back(layer, grad):
+        part, *halves, bias = lax.cond(
             is_attention,
             functools.partial(attention_back, layer, grad),
             functools.partial(feed_forward_back, layer, grad),
         )
-        if blocked and layer < LAYERS - 1:
-            part = after(part, halves)
+        return part, halves, bias
+
+    def norm_back(layer, part, grad, kind):
         other = lax.ppermute(part, "stream", swap)
-        if blocked:
-            near = lax.ppermute(near, "stream", [(1, 0)])
-            if layer == LAYERS - 1:
-                halves = send_halves(weight, near, far)
-        kind = BF16 if layer else F32
-        new_grad, sums = norm_backward(
+        return norm_backward(
             inputs[layer], part, other, grad, norm_gain[layer : layer + 1], kind
         )
-        bias = jnp.where(
-            is_attention & (jnp.arange(bias.shape[0])[:, None] >= 3 * QUADS),
-            jnp.tile(sums[2].reshape(QUADS, WIDE), (bias.shape[0] // QUADS, 1)),
-            bias,
-        )
-        vectors = [bias.reshape(count, -1), sums[:3].reshape(3, count, -1)] + vectors
-        grads += [weight, near, far]
-        grad = new_grad
-    small = jnp.concatenate(
-        [part.reshape(count, -1) for part in vectors[0::2]]
-        + [jnp.moveaxis(part, 0, 1).reshape(count, -1) for part in vectors[1::2]],
-        axis=1,
-    )
+
+    part1, halves1, bias1 = back(1, cotangent)
     if blocked:
-        weight, up, small = reduce_scatter(grads, halves, small)
+        came = send_first(halves1)
+    grad0, sums1 = norm_back(1, part1, cotangent, BF16)
+    part0, halves0, bias0 = back(0, grad0)
+    if blocked:
+        weight, up, small, result, input_grad = finish(
+            halves1, halves0, came, part0, tokens, grad0, *stream, (bias0, bias1), sums1,
+            norm_gain[:1],
+        )
     else:
-        weight, up, small = scatter_rows(grads, small)
-    each = branch_weight.shape[2] // count
-    bias, sums = small[: LAYERS * each], small[LAYERS * each :]
-    sums = sums[: LAYERS * 3 * (width // count)].reshape(LAYERS, 3, -1)
+        result = stream[0] + (stream[1] + stream[2])
+        input_grad, sums0 = norm_back(0, part0, grad0, F32)
+        weight, up = scatter_rows((halves0, halves1))
+        small = lax.psum(jnp.concatenate([bias0, bias1, sums1, sums0]), "batch")
+    index, rows = lax.axis_index("batch"), bias0.shape[0]
+    each, own = branch_weight.shape[2] // count, width // count
+    biases = small[: 2 * rows].reshape(LAYERS, -1)
+    sums = small[2 * rows :].reshape(LAYERS, 8, width)[::-1]
+    sums = lax.dynamic_slice_in_dim(sums, index * own, own, axis=2)
     return (
         result,
-        grad,
+        input_grad,
         weight[None],
-        bias.reshape(1, LAYERS, -1),
+        lax.dynamic_slice_in_dim(biases, index * each, each, axis=1)[None],
         up,
         sums[:, 2],
         sums[:, 0],
@@ -1128,23 +1161,18 @@
     )
 
 
-def scatter_rows(grads, small):
-    scatter = functools.partial(
-        lax.psum_scatter, axis_name="batch", scatter_dimension=0, tiled=True
-    )
+def scatter_rows(layers):
     weights, ups = [], []
-    for weight, near, far in zip(grads[0::3], grads[1::3], grads[2::3]):
-        half = near.shape[2] // 2
-        whole_up = [
-            jnp.concatenate([side[..., :half], side[..., half:]], axis=1) for side in (near, far)
-        ]
-        whole_up = rows_of(jnp.concatenate(whole_up, axis=2))
-        whole_up = jnp.where(lax.axis_index("stream") == 1, whole_up, 0.0)
-        weights.append(scatter(rows_of(weight)))
-        ups.append(
-            lax.psum_scatter(whole_up, ("batch", "stream"), scatter_dimension=0, tiled=True)
-        )
-    return jnp.stack(weights[::-1]), jnp.stack(ups[::-1]), scatter(small)[0]
+    for along_x, kept_x, along_y, kept_y, along_z, kept_z in layers:
+        width = kept_z.shape[2]
+        part_x = jnp.stack([kept_x, along_x], axis=2).reshape(-1, width // 2, WIDE)
+        part_y = jnp.stack([kept_y, along_y], axis=1).reshape(-1, width // 2, WIDE)
+        weight = rows_of(jnp.concatenate([part_x, part_y], axis=1))
+        up = rows_of(jnp.stack([kept_z, along_z], axis=1).reshape(-1, width, WIDE))
+        up = jnp.where(lax.axis_index("stream") == 1, up, 0.0)
+        weights.append(lax.psum_scatter(weight, "batch", scatter_dimension=0, tiled=True))
+        ups.append(lax.psum_scatter(up, ("batch", "stream"), scatter_dimension=0, tiled=True))
+    return jnp.stack(weights), jnp.stack(ups)
 
 
 def rows_of(blocks):

time: 629 us -> 617 us (0.981)
  Pallas kernels: 537 us -> 555 us
  waiting for transfers between devices: 31.8 us -> 17.9 us
  other arithmetic: 11.2 us -> 0.95 us
  starting transfers between devices: 17.6 us -> 8.5 us
    pallas_call x5 -> x3, Pallas kernels: 432 us -> 455 us  [the longest x1 300 us: finish(): pl.pallas_call(functools.partial(finish_kernel, bits, flows), in_specs=[p...]
    add x1 -> x0, other arithmetic: 8.62 us -> none  [shards(): result = stream[0] + (stream[1] + stream[2])]
    ppermute x7 -> x4, waiting for transfers between devices: 19 us -> 10.5 us  [the longest x3 8.08 us: send_first(): received.append(lax.ppermute(part, ('batch', 'stream'), pairs))]
    pallas_call x2 -> x1, Pallas kernels: 15.2 us -> 8.68 us  [norm_backward(): pl.pallas_call(norm_backward_kernel, grid=(length // ROWS,), in_specs=[bl...]
    ppermute x7 -> x4, starting transfers between devices: 13.1 us -> 8.43 us  [the longest x3 8.42 us: send_first(): received.append(lax.ppermute(part, ('batch', 'stream'), pairs))]
  transfers between devices with their start and end apart: 9 -> 6, of which waited for: 6 -> 4; matrix products, arithmetic and copies ran while one was open for 2% -> 0% of each run, Pallas kernels for 15% -> 13%
where the time goes in v5:
time: 617 us; the launch traced here: 612 us
  Pallas kernels  555 us (90%)
  local copies, waits for them, and re-layouts  20.6 us (3%)
  waiting for transfers between devices  17.9 us (3%)
  starting transfers between devices  8.5 us (1%)
  loops' own time  7.54 us (1%)
    pallas_call x1, Pallas kernels, finish(): pl.pallas_call(functools.partial(finish_kernel, bits, flows), in_specs=[p...  300 us
    pallas_call x2, Pallas kernels, attention_backward(): pl.pallas_call(attention_backward_kernel, grid_spec=pltpu.PrefetchScalarG...  155 us
    pallas_call x2, Pallas kernels, attention_forward(): pl.pallas_call(functools.partial(attention_forward_kernel, len(stream)),...  81.8 us
  transfers between devices with their start and end apart: 6, of which 4 were waited for; matrix products, arithmetic and copies ran while one was open for 0% of the time, Pallas kernels for 13%

profile of v5, /device:TPU:0, one launch (start us, length us, event | category | flops | bytes accessed | tf_op | source)
XLA Modules:
  0.0 611.6 jit_solution(12355123358087806839)
XLA Ops:
  1.6 11.9 %conditional.5 = ((bf16[2,4,256,256]{3,2,1,0:T(8,128)(2,1)S(1)}, bf16[2,4,256,256]{3,2,1,0:T(8,128)(2,1)}, f32[2,4,1,256]{3,2,1,0:T(1,128)S(1)})) conditional(s32[]{:T(128)} %convert_element_type.13, () %tuple.62, (s32[2,16,64]{2,1,0:T(8,128)}) %tuple.73), branch_computations={%region_0.0_spmd, %region_1.0_spmd.clone} | conditional | bytes 2105384 | solution.py:1061
  1.6 2.7 reshape.104.seeds_ref
  4.3 9.2 %feature_tables.1 = (bf16[2,4,256,256]{3,2,1,0:T(8,128)(2,1)S(1)}, bf16[2,4,256,256]{3,2,1,0:T(8,128)(2,1)}, f32[2,4,1,256]{3,2,1,0:T(1,128)S(1)}) custom-call(s32[2,1024,1]{2,1,0:T(8,128)} %reshape.104.seeds_ref, f32[256,256]{1,0:T(8,128)} %constant.80.clone.2.cosine_ref), custom_call_target="tpu_custom_call" | custom-call | tf_op jit(solution)/shard_map/cond/branch_1_fun/feature_tables/pallas_call | solution.py:108
  13.5 40.8 %conditional.6 = ((f32[1024,1024]{1,0:T(8,128)}, bf16[1024,1024]{1,0:T(8,128)(2,1)}, bf16[4,1024,1024]{2,1,0:T(8,128)(2,1)}, bf16[4,1024,1024]{2,1,0:T(8,128)(2,1)})) conditional(s32[]{:T(128)} %convert_element_type.13, (bf16[2,1024]{1,0:T(2,128)(2,1)S(1)}, bf16[2,1024]{1,0:T(2,128)(2,1)S(1)}, f32[2,4096]{1,0:T(2,128)S(1)}, ...), branch_computations={%region_2.0_spmd, %region_3.0_spmd} | conditional | bytes 40968 | solution.py:1093
  14.9 39.4 %attention_forward.2 = (f32[1024,1024]{1,0:T(8,128)}, bf16[1024,1024]{1,0:T(8,128)(2,1)}, bf16[4,1024,1024]{2,1,0:T(8,128)(2,1)}, bf16[4,1024,1024]{2,1,0:T(8,128)(2,1)}) custom-call(bf16[1024,1024]{1,0:T(8,128)(2,1)S(1)} %get-tuple-element.202.refs_0_, s32[1,4]{1,0:T(1,128)S(1)} %get-tuple-element.203.refs_1_, bf16[1,1024]{1,0:T(2,128)(2,1)S(1)} %bitcast.71, ...), custom_call_target="tpu_custom_call" | custom-call | tf_op jit(solution)/shard_map/cond/branch_1_fun/attention_forward/pallas_call | solution.py:436
  54.5 7.4 %collective-permute-done = f32[1024,1024]{1,0:T(8,128)} collective-permute-done((f32[1024,1024]{1,0:T(8,128)}, f32[1024,1024]{1,0:T(8,128)}, u32[]{:S(2)}, u32[]{:S(2)}) %collective-permute-start) | collective-permute-done | bytes 4194336 | tf_op jit(solution)/shard_map/ppermute | solution.py:1100
  61.9 51.5 %conditional.7 = ((f32[1024,1024]{1,0:T(8,128)}, f32[1024,1024]{1,0:T(8,128)}, bf16[1024,1024]{1,0:T(8,128)(2,1)}, bf16[4,1024,1024]{2,1,0:T(8,128)(2,1)}, bf16[4,1024,1024]{2,1,0:T(8,128)(2,1)})) conditional(s32[]{:T(128)} %convert_element_type.13, (bf16[2,1024]{1,0:T(2,128)(2,1)S(1)}, bf16[2,1024]{1,0:T(2,128)(2,1)S(1)}, f32[2,4096]{1,0:T(2,128)S(1)}, ...), branch_computations={%region_4.0_spmd, %region_5.0_spmd} | conditional | bytes 49160 | solution.py:1093
  71.0 42.4 %attention_forward.3 = (f32[1024,1024]{1,0:T(8,128)}, f32[1024,1024]{1,0:T(8,128)}, bf16[1024,1024]{1,0:T(8,128)(2,1)}, bf16[4,1024,1024]{2,1,0:T(8,128)(2,1)}, bf16[4,1024,1024]{2,1,0:T(8,128)(2,1)}) custom-call(bf16[1024,1024]{1,0:T(8,128)(2,1)S(1)} %get-tuple-element.222.refs_0_, f32[1024,1024]{1,0:T(8,128)} %get-tuple-element.223.refs_1_, ...), custom_call_target="tpu_custom_call" | custom-call | tf_op jit(solution)/shard_map/cond/branch_1_fun/attention_forward/pallas_call | solution.py:436
  113.4 83.7 %conditional.8 = (f32[1024,1024]{1,0:T(8,128)}, f32[4,2,512,256]{3,2,1,0:T(8,128)}, f32[4,2,512,256]{3,2,1,0:T(8,128)}, f32[2,4,1024,256]{3,2,1,0:T(8,128)}, f32...) conditional(s32[]{:T(128)} %convert_element_type.13, ...), branch_computations={%region_6.7_spmd, %region_7.8_spmd} | conditional | bytes 64 | solution.py:1119
  113.6 83.4 %attention_backward.2 = (f32[1024,1024]{1,0:T(8,128)}, f32[4,2,512,256]{3,2,1,0:T(8,128)}, f32[4,2,512,256]{3,2,1,0:T(8,128)}, f32[4,2,512,256]{3,2,1,0:T(8,128)...) custom-call(s32[3]{0:T(128)S(1)} %get-tuple-element.250.place_ref, ...), custom_call_target="tpu_custom_call" | custom-call | tf_op jit(solution)/shard_map/cond/branch_1_fun/attention_backward/pallas_call | solution.py:591
  197.1 4.0 collective-permute-start.3
  201.1 3.0 collective-permute-start.1
  204.0 1.5 collective-permute-start.2
  206.2 2.4 collective-permute-done.4.other_ref
  208.6 8.7 %norm_backward.1 = (bf16[1024,1024]{1,0:T(8,128)(2,1)}, f32[8,1024]{1,0:T(8,128)}) custom-call(f32[1024,1024]{1,0:T(8,128)} %get-tuple-element.357.x_ref, f32[1024,1024]{1,0:T(8,128)} %get-tuple-element.358.own_ref, f32[1024,1024]{1,0:T(8,128)} %collective-permute-done.4.other_ref, bf16[1024,1024]{1,0:T(8,128)(2,1)} %grad_ref.1, ...), custom_call_target="tpu_custom_call" | custom-call | tf_op jit(solution)/shard_map/norm_backward/pallas_call | solution.py:660
  217.3 71.7 %conditional.9 = (f32[1024,1024]{1,0:T(8,128)}, f32[4,1024]{1,0:T(4,128)S(1)}, f32[2,2,2,512,256]{4,3,2,1,0:T(8,128)}, f32[2,2,2,512,256]{4,3,2,1,0:T(8,128)}, f...) conditional(s32[]{:T(128)} %convert_element_type.13, ...), branch_computations={%region_8.9_spmd, %region_9.10_spmd} | conditional | bytes 64 | solution.py:1119
  217.3 71.4 %attention_backward.3 = (f32[1024,1024]{1,0:T(8,128)}, f32[4,2,512,256]{3,2,1,0:T(8,128)}, f32[4,2,512,256]{3,2,1,0:T(8,128)}, f32[4,2,512,256]{3,2,1,0:T(8,128)...) custom-call(s32[3]{0:T(128)S(1)} %get-tuple-element.283.place_ref, ...), custom_call_target="tpu_custom_call" | custom-call | tf_op jit(solution)/shard_map/cond/branch_1_fun/attention_backward/pallas_call | solution.py:591
  289.0 6.6 %collective-permute-done.1 = f32[4,2,512,256]{3,2,1,0:T(8,128)} collective-permute-done((f32[4,2,512,256]{3,2,1,0:T(8,128)}, f32[4,2,512,256]{3,2,1,0:T(8,128)}, u32[]{:S(2)}, u32[]{:S(2)}) %collective-permute-start.1) | collective-permute-done | bytes 4194336 | tf_op jit(solution)/shard_map/ppermute | solution.py:1049
  295.6 1.5 collective-permute-done.2
  297.1 300.4 %finish.1 = (f32[2,256,1024]{2,1,0:T(8,128)}, f32[2,128,1024]{2,1,0:T(8,128)}, f32[24,1024]{1,0:T(8,128)}, f32[1024,1024]{1,0:T(8,128)}, f32[1024,1024]{1,0:T(8,128)}) custom-call(f32[2,2,2,512,256]{4,3,2,1,0:T(8,128)} %get-tuple-element.351.kept_x1, f32[2,2,2,512,256]{4,3,2,1,0:T(8,128)} %get-tuple-element.352.kept_y1, ...), custom_call_target="tpu_custom_call" | custom-call | tf_op jit(solution)/shard_map/finish/pallas_call | solution.py:1018
  600.8 4.9 copy.88
  605.7 2.1 copy.89
  608.8 1.3 copy.90
  610.2 1.0 copy.91
  (43 shorter events, 9.6 us)
Async XLA Ops:
  0.6 12.8 %copy-start = (bf16[1024,1024]{1,0:T(8,128)(2,1)S(1)}, bf16[1024,1024]{1,0:T(8,128)(2,1)}, u32[]{:S(2)}) copy-start(bf16[1024,1024]{1,0:T(8,128)(2,1)} %tokens_ref.1) | copy-start | bytes 6291460
  0.6 12.8 %copy-start.7 = (bf16[2,1024]{1,0:T(2,128)(2,1)S(1)}, bf16[2,1024]{1,0:T(2,128)(2,1)}, u32[]{:S(2)}) copy-start(bf16[2,1024]{1,0:T(2,128)(2,1)} %param.29) | copy-start | bytes 12292
  0.7 12.8 %copy-start.8 = (bf16[2,1024]{1,0:T(2,128)(2,1)S(1)}, bf16[2,1024]{1,0:T(2,128)(2,1)}, u32[]{:S(2)}) copy-start(bf16[2,1024]{1,0:T(2,128)(2,1)} %param.30) | copy-start | bytes 12292
  0.7 12.8 %copy-start.9 = (bf16[2,1024]{1,0:T(2,128)(2,1)S(1)}, bf16[2,1024]{1,0:T(2,128)(2,1)}, u32[]{:S(2)}) copy-start(bf16[2,1024]{1,0:T(2,128)(2,1)} %param.28) | copy-start | bytes 12292
  0.7 12.8 %copy-start.10 = (s32[1,4]{1,0:T(1,128)S(1)}, s32[1,4]{1,0:T(1,128)}, u32[]{:S(2)}) copy-start(s32[1,4]{1,0:T(1,128)} %param.32) | copy-start | bytes 52
  54.3 7.6 %collective-permute-start = (f32[1024,1024]{1,0:T(8,128)}, f32[1024,1024]{1,0:T(8,128)}, u32[]{:S(2)}, u32[]{:S(2)}) collective-permute-start(f32[1024,1024]{1,0:T(8,128)} %get-tuple-element.347), channel_id=1, source_target_pairs={{0,1},{1,0},{2,3},{3,2},{4,5},{5,4},{6,7},{7,6},{8,9},{9,8},{10,11... | collective-permute-start | bytes 12582920 | tf_op jit(solution)/shard_map/ppermute | solution.py:1100
  197.1 99.9 %collective-permute-start.3 = (f32[2,4,1024,256]{3,2,1,0:T(8,128)}, f32[2,4,1024,256]{3,2,1,0:T(8,128)}, u32[]{:S(2)}, u32[]{:S(2)}) collective-permute-start(f32[2,4,1024,256]{3,2,1,0:T(8,128)} %get-tuple-element.356), channel_id=1, source_target_pairs={{1,9},{3,11},{5,13},{7,15},{9,1},{11,3},{13,5},{15,7},{17,25},{19,... | collective-permute-start | bytes 25165832 | tf_op jit(solution)/shard_map/ppermute | solution.py:1049
  201.1 7.5 %collective-permute-start.4 = (f32[1024,1024]{1,0:T(8,128)}, f32[1024,1024]{1,0:T(8,128)}, u32[]{:S(2)}, u32[]{:S(2)}) collective-permute-start(f32[1024,1024]{1,0:T(8,128)} %get-tuple-element.358.own_ref), channel_id=1, source_target_pairs={{0,1},{1,0},{2,3},{3,2},{4,5},{5,4},{6,7},{7,6},{8,9},{9,8},{10,11... | collective-permute-start | bytes 12582920 | tf_op jit(solution)/shard_map/ppermute | solution.py:1127
  201.1 94.5 %collective-permute-start.1 = (f32[4,2,512,256]{3,2,1,0:T(8,128)}, f32[4,2,512,256]{3,2,1,0:T(8,128)}, u32[]{:S(2)}, u32[]{:S(2)}) collective-permute-start(f32[4,2,512,256]{3,2,1,0:T(8,128)} %get-tuple-element.354), channel_id=1, source_target_pairs={{0,2},{1,3},{2,0},{3,1},{4,6},{5,7},{6,4},{7,5},{8,10},{9,11},{10,... | collective-permute-start | bytes 12582920 | tf_op jit(solution)/shard_map/ppermute | solution.py:1049
  204.0 93.0 %collective-permute-start.2 = (f32[4,2,512,256]{3,2,1,0:T(8,128)}, f32[4,2,512,256]{3,2,1,0:T(8,128)}, u32[]{:S(2)}, u32[]{:S(2)}) collective-permute-start(f32[4,2,512,256]{3,2,1,0:T(8,128)} %get-tuple-element.355), channel_id=1, source_target_pairs={{0,4},{1,5},{2,6},{3,7},{4,0},{5,1},{6,2},{7,3},{8,12},{9,13},{10,... | collective-permute-start | bytes 12582920 | tf_op jit(solution)/shard_map/ppermute | solution.py:1049
  205.5 91.5 %collective-permute-start.5 = (f32[1024,1024]{1,0:T(8,128)}, f32[1024,1024]{1,0:T(8,128)}, u32[]{:S(2)}, u32[]{:S(2)}) collective-permute-start(f32[1024,1024]{1,0:T(8,128)} %get-tuple-element.370.own_ref), channel_id=1, source_target_pairs={{0,1},{1,0},{2,3},{3,2},{4,5},{5,4},{6,7},{7,6},{8,9},{9,8},{10,11... | collective-permute-start | bytes 12582920 | tf_op jit(solution)/shard_map/ppermute | solution.py:1100
  208.6 8.7 %copy-start.1 = (f32[1024,128]{1,0:T(8,128)S(1)}, f32[1024,128]{1,0:T(8,128)}, u32[]{:S(2)}) copy-start(f32[1024,128]{1,0:T(8,128)} %constant.78.clone) | copy-start | bytes 1572868
  208.6 8.7 %copy-start.2 = (f32[1024,128]{1,0:T(8,128)S(1)}, f32[1024,128]{1,0:T(8,128)}, u32[]{:S(2)}) copy-start(f32[1024,128]{1,0:T(8,128)} %constant.79.clone) | copy-start | bytes 1572868
  208.6 8.7 %copy-start.3 = (bf16[1024,1024]{1,0:T(8,128)(2,1)S(1)}, bf16[1024,1024]{1,0:T(8,128)(2,1)}, u32[]{:S(2)}) copy-start(bf16[1024,1024]{1,0:T(8,128)(2,1)} %get-tuple-element.360) | copy-start | bytes 6291460
  600.8 4.9 copy-start.4
  605.7 3.1 copy-start.5
  605.7 4.4 copy-start.6

commit v6 on v5

--- a/solution.py
+++ b/solution.py
@@ -40,6 +40,10 @@
     return lax.dot_general(left, right, (((1,), (0,)), ((), ())), preferred_element_type=F32)
 
 
+def dot_tn(left, right):
+    return lax.dot_general(left, right, (((0,), (0,)), ((), ())), preferred_element_type=F32)
+
+
 def dot_nt(left, right):
     return lax.dot_general(left, right, (((1,), (1,)), ((), ())), preferred_element_type=F32)
 
@@ -81,41 +85,53 @@
 
 
 def tables_kernel(seeds_ref, cosine_ref, upper_ref, lower_ref, weight_ref):
-    feature = lane_index(WIDE, WIDE)
-    lattice = (feature % FEAT) * seeds_ref[0] % FEAT
-    prob = (lattice.astype(F32) + 0.5) / FEAT
-    radius = jnp.sqrt(-2.0 * jnp.log(jnp.minimum(prob, 1.0 - prob)))
-    above = 2.515517 + 0.802853 * radius + 0.010328 * radius * radius
-    below = (
-        1.0 + 1.432788 * radius + 0.189269 * radius * radius + 0.001308 * radius * radius * radius
-    )
-    magnitude = radius - above / below
-    same_head = row_index(WIDE, WIDE) // DH == feature // FEAT
-    omega = jnp.where(same_head, jnp.where(prob > 0.5, magnitude, -magnitude), 0.0)
-    project = jnp.dot(cosine_ref[...], omega, precision=HIGH, preferred_element_type=F32)
-    upper_ref[0, 0], lower_ref[0, 0] = split(project)
-    grown = jnp.exp(-0.5 / DH * jnp.sum(omega * omega, axis=0, keepdims=True))
-    total = jnp.dot(
-        jnp.broadcast_to(grown, (8, WIDE)),
-        same_head.astype(F32),
-        precision=HIGH,
-        preferred_element_type=F32,
-    )
-    weight_ref[0, 0] = FEAT * grown / total[:1]
+    own = row_index(WIDE, DH) % DH == lane_index(WIDE, DH)
+    feature = lane_index(WIDE, PAIR) % FEAT
+    same_head = row_index(WIDE, WIDE) // DH == lane_index(WIDE, WIDE) // FEAT
+    for group in range(QUADS):
+        heads = [
+            jnp.broadcast_to(seeds_ref[0, head : head + 1], (DH, DH))
+            for head in range(group * QUADS, (group + 1) * QUADS)
+        ]
+        seeds = jnp.where(own, jnp.concatenate(heads, axis=0), 0)
+        seeds = jnp.sum(seeds.astype(F32), axis=1, keepdims=True).astype(jnp.int32)
+        lattice = (feature * seeds) & (FEAT - 1)
+        prob = (lattice.astype(F32) + 0.5) * (1.0 / FEAT)
+        radius = jnp.sqrt(-2.0 * jnp.log(jnp.minimum(prob, 1.0 - prob)))
+        above = 2.515517 + 0.802853 * radius + 0.010328 * radius * radius
+        below = (
+            1.0
+            + 1.432788 * radius
+            + 0.189269 * radius * radius
+            + 0.001308 * radius * radius * radius
+        )
+        magnitude = radius - above / below
+        omega = jnp.where(prob > 0.5, magnitude, -magnitude)
+        omega = jnp.where(same_head, jnp.concatenate([omega] * (WIDE // PAIR), axis=1), 0.0)
+        project = jnp.dot(cosine_ref[...], omega, precision=HIGH, preferred_element_type=F32)
+        upper_ref[0, group], lower_ref[0, group] = split(project)
+        grown = jnp.exp(-0.5 / DH * jnp.sum(omega * omega, axis=0, keepdims=True))
+        total = jnp.dot(
+            jnp.broadcast_to(grown, (8, WIDE)),
+            same_head.astype(F32),
+            precision=HIGH,
+            preferred_element_type=F32,
+        )
+        weight_ref[0, group] = FEAT * grown / total[:1]
 
 
 def feature_tables(seeds):
     return pl.pallas_call(
         tables_kernel,
-        grid=(LAYERS, QUADS),
+        grid=(LAYERS,),
         in_specs=[
-            pl.BlockSpec((1, WIDE, 1), lambda l, g: (l, g, 0)),
+            pl.BlockSpec((1, HEADS, DH), lambda l: (l, 0, 0)),
             whole((WIDE, WIDE)),
         ],
         out_specs=[
-            pl.BlockSpec((1, 1, WIDE, WIDE), lambda l, g: (l, g, 0, 0)),
-            pl.BlockSpec((1, 1, WIDE, WIDE), lambda l, g: (l, g, 0, 0)),
-            pl.BlockSpec((1, 1, 1, WIDE), lambda l, g: (l, g, 0, 0)),
+            pl.BlockSpec((1, QUADS, WIDE, WIDE), lambda l: (l, 0, 0, 0)),
+            pl.BlockSpec((1, QUADS, WIDE, WIDE), lambda l: (l, 0, 0, 0)),
+            pl.BlockSpec((1, QUADS, 1, WIDE), lambda l: (l, 0, 0, 0)),
         ],
         out_shape=[
             jax.ShapeDtypeStruct((LAYERS, QUADS, WIDE, WIDE), BF16),
@@ -124,7 +140,7 @@
         ],
         compiler_params=params(),
         name="feature_tables",
-    )(seeds.reshape(LAYERS, HEADS * DH, 1), jnp.asarray(cosine_block()))
+    )(seeds, jnp.asarray(cosine_block()))
 
 
 def turn(values, cosine, sine):
@@ -240,11 +256,28 @@
     )(*stream, gain, offset, up, biases.reshape(blocks, 1, FF_BLOCK), down_weight, down_bias)
 
 
-def mlp_backward_kernel(
-    place_ref, grad_ref, h_ref, act_ref, slope_ref, down_ref, up_ref,
-    part_ref, along_x, kept_x, along_y, kept_y, along_z, kept_z, bias_ref, grad_t, h_t, units,
-):
+def add_stream(stream, result_ref):
+    if stream:
+        result_ref[...] = stream[0][...] + (stream[1][...] + stream[2][...])
+
+
+def stream_specs(stream):
+    specs = [
+        pl.BlockSpec((part.shape[0] // 4, part.shape[1]), lambda j, *_: (j, 0)) for part in stream
+    ]
+    shapes = [jax.ShapeDtypeStruct(part.shape, F32) for part in stream[:1]]
+    return specs, specs[:1], shapes
+
+
+def mlp_backward_kernel(count, place_ref, *refs):
+    stream, refs = refs[:count], refs[count:]
+    grad_ref, h_ref, act_ref, slope_ref, down_ref, up_ref = refs[:6]
+    result_ref, refs = (refs[6], refs[7:]) if count else (None, refs[6:])
+    part_ref, along_x, kept_x, along_y, kept_y, along_z, kept_z, bias_ref = refs[:8]
+    grad_t, h_t, units = refs[8:]
+    del along_z, kept_z
     step = pl.program_id(0)
+    add_stream(stream, result_ref)
 
     @pl.when(step == 0)
     def _():
@@ -266,49 +299,34 @@
         return pl.ds(pl.multiple_of((2 * y + x) * WIDE, WIDE), WIDE)
 
     near_x, near_y = place_ref[0], place_ref[1]
-    split_rows = along_x.shape[2]
-    for first in range(0, split_rows, ROWS):
+    for first in range(0, h_t.shape[0], ROWS):
         rows = slice(first, first + ROWS)
-        other = slice(split_rows + first, split_rows + first + ROWS)
         for side in range(2):
             for target, x in ((along_x, 1 - near_x), (kept_x, near_x)):
                 target[0, side, rows] = dot_nn(grad_t[rows], act_ref[0, :, block(side, x)])
             for target, y in ((along_y, 1 - near_y), (kept_y, near_y)):
-                target[0, side, rows] = dot_nn(grad_t[other], act_ref[0, :, block(y, side)])
-
-    def up_grads(target):
-        for first in range(0, h_t.shape[0], ROWS):
-            rows = slice(first, first + ROWS)
-            for index in range(FF_BLOCK // WIDE):
-                lanes = slice(index * WIDE, (index + 1) * WIDE)
-                target[0, index, rows] = dot_nn(h_t[rows], units[:, lanes])
-
-    stays = lax.rem(step, 2) == place_ref[2]
-    pl.when(stays)(functools.partial(up_grads, kept_z))
-    pl.when(jnp.logical_not(stays))(functools.partial(up_grads, along_z))
+                target[0, side, rows] = dot_nn(h_t[rows], units[:, block(y, side)])
 
 
 def halves_of(width):
-    pair = (4, 2, width // 2, WIDE)
-    single = (2, 4, width, WIDE)
-    return [jax.ShapeDtypeStruct(shape, F32) for shape in (pair,) * 4 + (single,) * 2]
-
-
-def mlp_backward(layer, place, grad, h, act, slope, down_weight, up):
+    shapes = ((4, 2, width, WIDE),) * 4 + ((2, 4, width, WIDE),) * 2
+    return [jax.ShapeDtypeStruct(shape, F32) for shape in shapes]
+
+
+def mlp_backward(layer, place, grad, h, act, slope, down_weight, up, stream=()):
     length, width = h.shape
     hidden = up.shape[1]
     blocks = hidden // FF_BLOCK
-    pair = pl.BlockSpec((1, 2, width // 2, WIDE), lambda j, *_: (j, 0, 0, 0))
-    single = pl.BlockSpec(
-        (1, 4, width, WIDE), lambda j, *_: (j // 2, 0, 0, 0), pipeline_mode=pl.Buffered(1)
-    )
+    pair = pl.BlockSpec((1, 2, width, WIDE), lambda j, *_: (j, 0, 0, 0))
     plane = pl.BlockSpec((1, length, FF_BLOCK), lambda j, *_: (j, 0, 0))
+    stream_in, stream_out, stream_shape = stream_specs(stream)
     return pl.pallas_call(
-        mlp_backward_kernel,
+        functools.partial(mlp_backward_kernel, len(stream)),
         grid_spec=pltpu.PrefetchScalarGridSpec(
             num_scalar_prefetch=1,
             grid=(blocks,),
-            in_specs=[
+            in_specs=stream_in
+            + [
                 whole((length, width)),
                 whole((length, width)),
                 plane,
@@ -316,7 +334,10 @@
                 pl.BlockSpec((1, 1, FF_BLOCK, width), lambda j, *_: (0, layer, j, 0)),
                 pl.BlockSpec((1, FF_BLOCK, width), lambda j, *_: (layer, j, 0)),
             ],
-            out_specs=[whole((length, width))] + [pair] * 4 + [single] * 2
+            out_specs=stream_out
+            + [whole((length, width))]
+            + [pair] * 4
+            + [pl.BlockSpec(memory_space=pl.ANY)] * 2
             + [whole((blocks, FF_BLOCK))],
             scratch_shapes=[
                 pltpu.VMEM((width, length), BF16),
@@ -324,11 +345,13 @@
                 pltpu.VMEM((length, FF_BLOCK), BF16),
             ],
         ),
-        out_shape=[jax.ShapeDtypeStruct((length, width), F32)] + halves_of(width)
+        out_shape=stream_shape
+        + [jax.ShapeDtypeStruct((length, width), F32)]
+        + halves_of(width)
         + [jax.ShapeDtypeStruct((blocks, FF_BLOCK), F32)],
         compiler_params=params(),
         name="mlp_backward",
-    )(place, grad, h, act, slope, down_weight, up)
+    )(place, *stream, grad, h, act, slope, down_weight, up)
 
 
 def head_sums(values, ones):
@@ -341,18 +364,27 @@
     return jnp.where(same, 1.0, 0.0).astype(BF16)
 
 
+def document_of(starts_ref, positions):
+    return sum((starts_ref[0, i] <= positions).astype(jnp.int32) for i in range(starts_ref.shape[1]))
+
+
 def write_mask(starts_ref, mask_ref, flipped):
-    length = mask_ref.shape[0]
-    keys = lane_index(1, length)
-    documents = sum((starts_ref[0, i] <= keys).astype(jnp.int32) for i in range(starts_ref.shape[1]))
+    for first in range(0, mask_ref.shape[0], ROWS):
+        lanes = lane_index(1, ROWS) + first
+        own = row_index(ROWS, 1) + first
+        order = (own <= lanes) if flipped else (lanes <= own)
+        seen = (document_of(starts_ref, own) == document_of(starts_ref, lanes)) & order
+        mask_ref[first : first + ROWS] = jnp.where(seen, 1.0, 0.0).astype(BF16)
+
+
+def document_edges(starts_ref, length):
+    edges = []
     for first in range(0, length, ROWS):
-        own = row_index(ROWS, 1) + first
-        document = sum(
-            (starts_ref[0, i] <= own).astype(jnp.int32) for i in range(starts_ref.shape[1])
-        )
-        order = (own <= keys) if flipped else (keys <= own)
-        seen = (document == documents) & order
-        mask_ref[first : first + ROWS] = jnp.where(seen, 1.0, 0.0).astype(BF16)
+        rows = document_of(starts_ref, row_index(ROWS, 1) + first)
+        here = document_of(starts_ref, first)
+        later = document_of(starts_ref, first + ROWS)
+        edges.append((rows == here, rows == later, here == later))
+    return edges
 
 
 def wide_rotary(cosine_ref, sine_ref, rows):
@@ -398,25 +430,41 @@
 
     zero = jnp.zeros((), BF16)
     one = jnp.ones((), BF16)
-    for first in range(0, length, ROWS):
-        rows = slice(first, first + ROWS)
-        finish = first + ROWS
-        left = lane_index(finish, PAIR) < DH
-        seen = mask_ref[rows, :finish] > zero
-        for pair in range(WIDE // PAIR):
-            lanes = slice(pair * PAIR, (pair + 1) * PAIR)
+    left = lane_index(ROWS, PAIR) < DH
+    row, lane = row_index(PAIR, 2 * PAIR), lane_index(PAIR, 2 * PAIR)
+    same = row // DH == lane // PAIR
+    edges = document_edges(starts_ref, length)
+    for pair in range(WIDE // PAIR):
+        lanes = slice(pair * PAIR, (pair + 1) * PAIR)
+        before = None
+        for block, (same_first, same_next, goes_on) in enumerate(edges):
+            rows = slice(block * ROWS, (block + 1) * ROWS)
+            seen = mask_ref[rows] > zero
+            queries, keys = state_ref[0, rows, lanes], state_ref[1, rows, lanes]
+            values = [jnp.where(own, state_ref[3, rows, lanes], one) for own in (left, ~left)]
+            if block > 0:
+                earlier = dot_nn(queries, before.astype(BF16))
+                earlier = jnp.where(same_first, earlier, 0.0)
             sums = []
-            for own in (left, ~left):
-                keys = jnp.where(own, state_ref[1, :finish, lanes], zero)
-                scores = dot_nt(state_ref[0, rows, lanes], keys).astype(BF16)
-                scores = jnp.where(seen, scores, zero)
-                sums.append(dot_nn(scores, jnp.where(own, state_ref[3, :finish, lanes], one)))
-            mine = lane_index(ROWS, PAIR) < DH
-            numer = jnp.where(mine, sums[0], sums[1])
-            denom = jnp.where(mine, pltpu.roll(sums[0], DH, 1), pltpu.roll(sums[1], DH, 1))
+            for head, own in enumerate((left, ~left)):
+                scores = dot_nt(queries, jnp.where(own, keys, zero)).astype(BF16)
+                total = dot_nn(jnp.where(seen, scores, zero), values[head])
+                if block > 0:
+                    total = total + earlier[:, head * PAIR : (head + 1) * PAIR]
+                sums.append(total)
+            if block + 1 < len(edges):
+                kept = jnp.where(same_next, keys, zero)
+                added = jnp.where(same, dot_tn(kept, jnp.concatenate(values, axis=1)), 0.0)
+                if block > 0:
+                    added = added + jnp.where(goes_on, before, 0.0)
+                before = added
+            numer = jnp.where(left, sums[0], sums[1])
+            denom = jnp.where(left, pltpu.roll(sums[0], DH, 1), pltpu.roll(sums[1], DH, 1))
             inverse = 1.0 / denom
             mixed_ref[0, rows, lanes] = (numer * inverse).astype(BF16)
             mixed_ref[1, rows, lanes], mixed_ref[2, rows, lanes] = split(inverse)
+    for first in range(0, length, ROWS):
+        rows = slice(first, first + ROWS)
         part_ref[rows] += dot_nn(mixed_ref[0, rows], weight_ref[0, 0, 3, 0])
 
 
@@ -452,7 +500,7 @@
         ],
         out_specs=out_specs,
         out_shape=out_shape,
-        scratch_shapes=[pltpu.VMEM((length, length), BF16)],
+        scratch_shapes=[pltpu.VMEM((length, ROWS), BF16)],
         compiler_params=params(),
         name="attention_forward",
     )(
@@ -461,20 +509,23 @@
     )
 
 
-def attention_backward_kernel(
-    place_ref, starts_ref, grad_ref, h_ref, state_ref, mixed_ref, table_ref, cosine_ref, sine_ref,
-    weight_ref, part_ref, along_x, kept_x, along_y, kept_y, along_z, kept_z, bias_ref,
-    mask_ref, grad_t, h_t, numer_ref, feat_ref, flow, query_t,
-):
-    del along_z, kept_z
+def attention_backward_kernel(count, place_ref, *refs):
+    stream, refs = refs[:count], refs[count:]
+    starts_ref, grad_ref, h_ref, state_ref, mixed_ref, table_ref = refs[:6]
+    cosine_ref, sine_ref, weight_ref = refs[6:9]
+    result_ref, refs = (refs[9], refs[10:]) if count else (None, refs[9:])
+    part_ref, along_x, kept_x, along_y, kept_y, along_z, kept_z, bias_ref = refs[:8]
+    mask_ref, upright, numer_ref, feat_ref, flow = refs[8:]
+    del along_x, kept_x, along_y, kept_y
     group = pl.program_id(0)
-    length = h_ref.shape[0]
+    length, width = h_ref.shape
+    add_stream(stream, result_ref)
 
     @pl.when(pl.program_id(0) == 0)
     def _():
         write_mask(starts_ref, mask_ref, True)
-        grad_t[...] = grad_ref[...].T
-        h_t[...] = h_ref[...].T
+        upright[0] = h_ref[...].T
+        upright[1] = grad_ref[...].T
         part_ref[...] = jnp.zeros_like(part_ref)
 
     row, lane = row_index(WIDE, WIDE), lane_index(WIDE, WIDE)
@@ -495,46 +546,79 @@
         numer_ref[0, rows] = jnp.where(left, numer, spare)
         numer_ref[1, rows] = jnp.where(left, spare, numer)
 
+    left = lane_index(ROWS, PAIR) < DH
+    spare = jnp.where(lane_index(ROWS, PAIR) % DH < 2, one, zero)
+    row, lane = row_index(2 * PAIR, PAIR), lane_index(2 * PAIR, PAIR)
+    same = row // PAIR == lane // DH
+    row, lane = row_index(PAIR, PAIR), lane_index(PAIR, PAIR)
+    same_head = row // DH == lane // DH
+    edges = document_edges(starts_ref, length)
+    blocks = range(len(edges))
+
+    def both(upper_and_lower, sums):
+        upper, lower = split(sums)
+        return dot_nn(upper_and_lower, upper) + dot_nn(upper_and_lower, lower)
+
     for pair in range(WIDE // PAIR):
         lanes = slice(pair * PAIR, (pair + 1) * PAIR)
-        query_t[...] = jnp.zeros_like(query_t)
-        for first in range(0, length, ROWS):
-            rows = slice(first, first + ROWS)
-            seen = mask_ref[rows, first:] > zero
-            lane = lane_index(ROWS, PAIR)
-            left = lane < DH
-            spare = jnp.where(lane % DH < 2, one, zero)
-            keys, values = state_ref[1, rows, lanes], state_ref[3, rows, lanes]
-            queries = state_ref[0, first:, lanes]
-            numer = jnp.where(
-                lane_index(length - first, PAIR) < DH,
-                numer_ref[0, first:, lanes],
-                numer_ref[1, first:, lanes],
-            )
+
+        def rows_of_block(block):
+            rows = slice(block * ROWS, (block + 1) * ROWS)
+            numers = [numer_ref[head, rows, lanes] for head in range(2)]
+            values = state_ref[3, rows, lanes]
+            values = [jnp.where(own, values, spare) for own in (left, ~left)]
+            return rows, state_ref[0, rows, lanes], state_ref[1, rows, lanes], values, numers
+
+        before, after = {}, {}
+        for block in blocks[1:]:
+            rows, queries, keys, values, numers = rows_of_block(block - 1)
+            _, same_next, goes_on = edges[block - 1]
+            kept = jnp.where(same_next, keys, zero)
+            added = jnp.where(same, dot_tn(jnp.concatenate(values, axis=1), kept), 0.0)
+            if block > 1:
+                added = added + jnp.where(goes_on, before[block - 1], 0.0)
+            before[block] = added
+        for block in blocks[::-1][:-1]:
+            rows, queries, keys, values, numers = rows_of_block(block)
+            same_first, _, goes_on = edges[block]
+            kept = jnp.where(same_first, queries, zero)
+            keys_sum = jnp.where(same, dot_tn(jnp.concatenate(numers, axis=1), kept), 0.0)
+            values_sum = dot_tn(kept, jnp.where(left, numers[0], numers[1]))
+            values_sum = jnp.where(same_head, values_sum, 0.0)
+            if block + 1 < len(edges):
+                keys_sum = keys_sum + jnp.where(goes_on, after[block + 1][0], 0.0)
+                values_sum = values_sum + jnp.where(goes_on, after[block + 1][1], 0.0)
+            after[block] = (keys_sum, values_sum)
+        for block in blocks:
+            rows, queries, keys, values, numers = rows_of_block(block)
+            same_first, same_next, _ = edges[block]
+            seen = mask_ref[rows] > zero
+            numer = jnp.where(left, numers[0], numers[1])
             grads = []
+            grad_query = None
             for head, own in enumerate((left, ~left)):
                 own_keys = jnp.where(own, keys, zero)
                 scores = dot_nt(own_keys, queries).astype(BF16)
-                scores = jnp.where(seen, scores, zero)
-                grad_value = dot_nn(scores, numer)
-                grad_scores = dot_nt(
-                    jnp.where(own, values, spare), numer_ref[head, first:, lanes]
-                ).astype(BF16)
+                grad_value = dot_nn(jnp.where(seen, scores, zero), numer)
+                grad_scores = dot_nt(values[head], numers[head]).astype(BF16)
                 grad_scores = jnp.where(seen, grad_scores, zero)
-                grad_key = dot_nn(grad_scores, queries)
-                query_t[head, :, first:] += dot_nn(
-                    own_keys.T[head * DH : (head + 1) * DH], grad_scores
-                )
-                grads.append((grad_value, grad_key))
-            flow[2, rows, lanes] = jnp.where(left, grads[0][0], grads[1][0]).astype(BF16)
+                grads.append((grad_value, dot_nn(grad_scores, queries)))
+                from_head = dot_tn(grad_scores, own_keys)
+                grad_query = from_head if head == 0 else grad_query + from_head
+            grad_value = jnp.where(left, grads[0][0], grads[1][0])
             grad_key = jnp.where(left, grads[0][1], grads[1][1])
+            if block + 1 < len(edges):
+                keys_sum, values_sum = after[block + 1]
+                late = both(jnp.concatenate(values, axis=1), keys_sum)
+                grad_key = grad_key + jnp.where(same_next, late, 0.0)
+                late = dot_nn(keys, values_sum.astype(BF16))
+                grad_value = grad_value + jnp.where(same_next, late, 0.0)
+            if block > 0:
+                early = both(jnp.concatenate(numers, axis=1), before[block])
+                grad_query = grad_query + jnp.where(same_first, early, 0.0)
+            flow[2, rows, lanes] = grad_value.astype(BF16)
             feat_ref[1, rows, lanes] = (grad_key * keys.astype(F32)).astype(BF16)
-        for first in range(0, length, ROWS):
-            rows = slice(first, first + ROWS)
-            grad_query = jnp.concatenate([query_t[0, :, rows], query_t[1, :, rows]], axis=0).T
-            feat_ref[0, rows, lanes] = (
-                grad_query * state_ref[0, rows, lanes].astype(F32)
-            ).astype(BF16)
+            feat_ref[0, rows, lanes] = (grad_query * queries.astype(F32)).astype(BF16)
 
     ones = same_head_ones()
     table = table_ref[0, 0]
@@ -556,44 +640,29 @@
         bias_ref[kind : kind + 1] = sums[kind]
     lanes = pl.ds(pl.multiple_of(group * WIDE, WIDE), WIDE)
     bias_ref[3:4] = jnp.sum(grad_ref[:, lanes].astype(F32), axis=0, keepdims=True)
-    split_rows = along_x.shape[2]
-
-    def weights(target, base):
-        for first in range(0, split_rows, ROWS):
-            rows = slice(first, first + ROWS)
-            held = slice(base + first, base + first + ROWS)
-            for kind in range(3):
-                target[kind, 0, rows] = dot_nn(h_t[held], flow[kind])
-            target[3, 0, rows] = dot_nn(grad_t[held], mixed_ref[0])
-
-    stays = lax.rem(group, 2) == place_ref[0]
-    pl.when(stays)(functools.partial(weights, kept_x, 0))
-    pl.when(jnp.logical_not(stays))(functools.partial(weights, along_x, 0))
-    stays = group // 2 == place_ref[1]
-    pl.when(stays)(functools.partial(weights, kept_y, split_rows))
-    pl.when(jnp.logical_not(stays))(functools.partial(weights, along_y, split_rows))
-
-
-def attention_backward(layer, place, starts, grad, h, state, mixed, tables, rotary, weight):
+    flow[3] = mixed_ref[0]
+    for first in range(0, width, ROWS):
+        rows = slice(first, first + ROWS)
+        for far in range(2):
+            for target, near in ((along_z, 1 - place_ref[2]), (kept_z, place_ref[2])):
+                kind = 2 * far + near
+                target[far, 0, rows] = dot_nn(upright[kind // 3, rows], flow[kind])
+
+
+def attention_backward(
+    layer, place, starts, grad, h, state, mixed, tables, rotary, weight, stream=()
+):
     _, length, width = state.shape
     four = pl.BlockSpec((4, length, WIDE), lambda g, *_: (0, 0, g))
-    shape = (4, 1, width // 2, WIDE)
-    first = pl.BlockSpec(shape, lambda g, *_: (0, g // 2, 0, 0))
-
-    def second(side):
-        def index(g, place_ref):
-            y, chosen = g // 2, place_ref[1] if side else 1 - place_ref[1]
-            at = jnp.where(y == chosen, g % 2, jnp.where(y < chosen, 0, 1))
-            return 0, at, 0, 0
-
-        return pl.BlockSpec(shape, index)
-
+    halves = pl.BlockSpec((2, 1, width, WIDE), lambda g, *_: (0, g, 0, 0))
+    stream_in, stream_out, stream_shape = stream_specs(stream)
     return pl.pallas_call(
-        attention_backward_kernel,
+        functools.partial(attention_backward_kernel, len(stream)),
         grid_spec=pltpu.PrefetchScalarGridSpec(
             num_scalar_prefetch=1,
             grid=(QUADS,),
-            in_specs=[
+            in_specs=stream_in
+            + [
                 pl.BlockSpec(memory_space=pltpu.SMEM),
                 whole((length, width)),
                 whole((length, width)),
@@ -604,24 +673,26 @@
                 whole((length, PAIR)),
                 pl.BlockSpec((1, 1, 4, 1, WIDE, width), lambda g, *_: (0, layer, 0, g, 0, 0)),
             ],
-            out_specs=[whole((length, width)), first, first, second(False), second(True)]
-            + [pl.BlockSpec(memory_space=pl.ANY)] * 2
+            out_specs=stream_out
+            + [whole((length, width))]
+            + [pl.BlockSpec(memory_space=pl.ANY)] * 4
+            + [halves, halves]
             + [pl.BlockSpec((4, WIDE), lambda g, *_: (0, g))],
             scratch_shapes=[
-                pltpu.VMEM((length, length), BF16),
-                pltpu.VMEM((width, length), BF16),
-                pltpu.VMEM((width, length), BF16),
+                pltpu.VMEM((length, ROWS), BF16),
+                pltpu.VMEM((2, width, length), BF16),
                 pltpu.VMEM((2, length, WIDE), BF16),
                 pltpu.VMEM((2, length, WIDE), BF16),
-                pltpu.VMEM((3, length, WIDE), BF16),
-                pltpu.VMEM((2, DH, length), F32),
+                pltpu.VMEM((4, length, WIDE), BF16),
             ],
         ),
-        out_shape=[jax.ShapeDtypeStruct((length, width), F32)] + halves_of(width)
+        out_shape=stream_shape
+        + [jax.ShapeDtypeStruct((length, width), F32)]
+        + halves_of(width)
         + [jax.ShapeDtypeStruct((4, width), F32)],
         compiler_params=params(),
         name="attention_backward",
-    )(place, starts, grad, h, state, mixed, tables[0], *rotary, kinds_of(weight))
+    )(place, *stream, starts, grad, h, state, mixed, tables[0], *rotary, kinds_of(weight))
 
 
 def norm_gradient(values, incoming, grad, gain, sums_ref):
@@ -672,7 +743,7 @@
 
 
 MESH = pl.DeviceIdType.MESH
-UNIT = 8
+UNIT = 16
 SLOTS = 4
 LAG = 1
 JOB = 128
@@ -680,28 +751,28 @@
 
 class Flow(NamedTuple):
     order: tuple
+    core: int
     family: int
     layer: int
     row: int
     units: int
     start: int
+    place: int
 
 
 def flows_of(width, layer, start):
-    rows = width // 4
+    rows = width // 2
     kinds = (
-        ((0, 1, 2, 3), 0, 0),
-        ((1, 0, 2, 3), 1, 0),
-        ((2, 0, 1, 3), 2, 0),
-        ((2, 1, 0, 3), 2, 1),
-        ((0, 1, 2, 3), 0, 1),
-        ((1, 0, 2, 3), 1, 1),
-        ((2, 0, 1, 3), 2, 2),
-        ((2, 1, 0, 3), 2, 3),
+        ((0, 1, 2, 3), 1, 0, 0, 0),
+        ((1, 0, 2, 3), 1, 1, 0, 1),
+        ((0, 1, 2, 3), 1, 0, 1, 2),
+        ((1, 0, 2, 3), 1, 1, 1, 3),
+        ((2, 0, 1, 3), 0, 2, 0, 0),
+        ((2, 1, 0, 3), 0, 2, 1, 1),
     )
     return [
-        Flow(order, family, layer, part * rows, rows // UNIT, start)
-        for order, family, part in kinds
+        Flow(order, core, family, layer, part * rows, rows // UNIT, start, 4 * layer + place)
+        for order, core, family, part, place in kinds
     ]
 
 
@@ -717,21 +788,21 @@
     bits, flows,
     kept_x1, kept_y1, kept_z1, came_x1, came_y1, came_z1,
     kept_x0, kept_y0, kept_z0, sent_x0, sent_y0, sent_z0,
-    part_ref, tokens_ref, grad_ref, x_ref, own_ref, other_ref,
+    part_ref, tokens_ref, grad_ref,
     bias0_ref, bias1_ref, sums1_ref, gain_ref,
-    weight_out, up_out, small_out, result_out, grad_out,
-    weight_sum, up_sum, up_turned, up_came, part, part_came, tokens, grad, x, own, other, sums,
+    weight_out, up_out, small_out, grad_out,
+    weight_sum, up_sum, up_turned, up_came, part, part_came, tokens, grad, sums,
     *scratch,
 ):
     stages = bits
     kept = ((kept_x1, kept_y1, kept_z1), (kept_x0, kept_y0, kept_z0))
     moved = ((came_x1, came_y1, came_z1), (sent_x0, sent_y0, sent_z0))
-    held = scratch[: len(flows) * (stages + 1)]
-    held = [held[f * (stages + 1) : (f + 1) * (stages + 1)] for f in range(len(flows))]
-    small = scratch[len(flows) * (stages + 1) :][: stages + 1]
-    small_came = scratch[len(flows) * (stages + 1) + stages + 1 :][:stages]
+    places = 1 + max(flow.place for flow in flows)
+    held, scratch = scratch[: places * (stages + 1)], scratch[places * (stages + 1) :]
+    held = [held[f * (stages + 1) : (f + 1) * (stages + 1)] for f in range(places)]
+    small, small_came = scratch[: stages + 1], scratch[stages + 1 : 2 * stages + 1]
     load_sem, send_sem, recv_sem, credit, small_send, small_recv, job_sem, near_send, near_recv = (
-        scratch[len(flows) * (stages + 1) + 2 * stages + 1 :]
+        scratch[2 * stages + 1 :]
     )
     me, core = lax.axis_index("batch"), lax.axis_index("stream")
 
@@ -754,21 +825,17 @@
     loads = [
         pltpu.make_async_copy(source, target, job_sem.at[index])
         for index, (source, target) in enumerate(
-            ((part_ref, part), (tokens_ref, tokens), (grad_ref, grad), (x_ref, x),
-             (own_ref, own), (other_ref, other))
+            ((part_ref, part), (tokens_ref, tokens), (grad_ref, grad))
         )
     ]
-    stores = [
-        pltpu.make_async_copy(part, grad_out, job_sem.at[len(loads)]),
-        pltpu.make_async_copy(x, result_out, job_sem.at[len(loads) + 1]),
-    ]
+    store = pltpu.make_async_copy(part, grad_out, job_sem.at[len(loads)])
     exchange.start()
     for copy in loads:
         copy.start()
     jobs = part.shape[0] // JOB
-    norm_start, result_start = 3, 3 + jobs
-    small_start = result_start + 1
-    turn_start = max(flow.start + flow.units for flow in flows[: len(flows) // 2]) + stages + 1
+    norm_start = 3
+    small_start = norm_start + jobs
+    turn_start = max(flow.start + flow.units for flow in flows if flow.layer == 0) + stages + 1
 
     def norm_job(index):
         rows = pl.ds(pl.multiple_of((index - norm_start) * JOB, JOB), JOB)
@@ -776,7 +843,7 @@
         @pl.when(index == norm_start)
         def _():
             exchange.wait()
-            for copy in loads[:3]:
+            for copy in loads:
                 copy.wait()
             sums[...] = jnp.zeros_like(sums)
 
@@ -787,17 +854,6 @@
             gain_ref[...].astype(F32),
             sums,
         )
-
-    def result_job(index):
-        rows = pl.ds(pl.multiple_of((index - result_start) * JOB, JOB), JOB)
-
-        @pl.when(index == result_start)
-        def _():
-            stores[0].start()
-            for copy in loads[3:]:
-                copy.wait()
-
-        x[rows] = x[rows] + (own[rows] + other[rows])
 
     def near_copy(layer):
         return pltpu.make_async_remote_copy(
@@ -830,6 +886,7 @@
 
     def small_step(stage):
         if stage == 0:
+            store.start()
             rows = bias0_ref.shape[0]
             small[0][0:rows] = bias0_ref[...]
             small[0][rows : 2 * rows] = bias1_ref[...]
@@ -849,106 +906,103 @@
         pick = pick if mine else 1 - pick
         return tuple(pick if bit == order[stage] else slice(None) for bit in left)
 
-    def remote(place, stage, slot, source):
+    def remote(flow, stage, slot, source):
+        place = flow.place
         return pltpu.make_async_remote_copy(
             src_ref=source,
             dst_ref=held[place][stage + 1].at[slot],
             send_sem=send_sem.at[place, stage, slot],
             recv_sem=recv_sem.at[place, stage, slot],
-            device_id={"batch": flip(me, flows[place].order[stage])},
+            device_id={"batch": flip(me, flow.order[stage])},
             device_id_type=MESH,
         )
 
-    def sent_from(place, stage, slot):
+    def sent_from(flow, stage, slot):
         if stage == 0:
-            return held[place][0].at[slot]
-        return held[place][stage].at[(slot,) + view(flows[place].order, stage, False)]
-
-    def load(place, slot, source):
+            return held[flow.place][0].at[slot]
+        return held[flow.place][stage].at[(slot,) + view(flow.order, stage, False)]
+
+    def load(flow, slot, source):
+        place = flow.place
         return pltpu.make_async_copy(source, held[place][0].at[slot], load_sem.at[place, slot])
 
-    def load_came(place, slot, source):
+    def load_came(flow, slot, source):
         return pltpu.make_async_copy(
-            source, held[place][1].at[slot], recv_sem.at[place, 0, slot]
-        )
-
-    def return_credit(place, stage, unit):
-        if stage == 0 and flows[place].layer == 0:
+            source, held[flow.place][1].at[slot], recv_sem.at[flow.place, 0, slot]
+        )
+
+    def return_credit(flow, stage, unit):
+        if stage == 0 and flow.layer == 0:
             return
 
-        @pl.when(unit + SLOTS < flows[place].units)
+        @pl.when(unit + SLOTS < flow.units)
         def _():
             pl.semaphore_signal(
-                credit.at[place, stage],
+                credit.at[flow.place, stage],
                 inc=1,
-                device_id={"batch": flip(me, flows[place].order[stage])},
+                device_id={"batch": flip(me, flow.order[stage])},
                 device_id_type=MESH,
             )
 
-    def take_credit(place, stage, unit):
+    def take_credit(flow, stage, unit):
         @pl.when(unit >= SLOTS)
         def _():
-            pl.semaphore_wait(credit.at[place, stage], 1)
-
-    def begin(place, unit):
+            pl.semaphore_wait(credit.at[flow.place, stage], 1)
+
+    def begin(flow, unit):
         slot = lax.rem(unit, SLOTS)
-        _, family, layer, row, _, _ = flows[place]
         at = (slice(None),) * (bits - 1)
-        at += (pl.ds(pl.multiple_of(row + unit * UNIT, UNIT), UNIT),)
-        load(place, slot, kept[layer][family].at[at]).start()
-        if layer == 0:
-            load_came(place, slot, moved[layer][family].at[at]).start()
+        at += (pl.ds(pl.multiple_of(flow.row + unit * UNIT, UNIT), UNIT),)
+        load(flow, slot, kept[flow.layer][flow.family].at[at]).start()
+        source = moved[flow.layer][flow.family].at[at]
+        if flow.layer == 0:
+            load_came(flow, slot, source).start()
         else:
-            take_credit(place, 0, unit)
-            remote(place, 0, slot, moved[layer][family].at[at]).start()
-
-    def advance(place, stage, unit):
+            take_credit(flow, 0, unit)
+            remote(flow, 0, slot, source).start()
+
+    def advance(flow, stage, unit):
         slot = lax.rem(unit, SLOTS)
-        order, family, layer, row, _, _ = flows[place]
-        buffer = held[place][stage]
-        copy = remote(place, stage - 1, slot, sent_from(place, stage - 1, slot))
-        if stage == 1 and layer == 0:
-            load_came(place, slot, held[place][0].at[slot]).wait()
+        buffers, begun = held[flow.place], flow.layer == 0
+        copy = remote(flow, stage - 1, slot, sent_from(flow, stage - 1, slot))
+        if stage == 1 and begun:
+            load_came(flow, slot, buffers[0].at[slot]).wait()
         else:
             copy.wait_recv()
         if stage == 1:
-            load(place, slot, held[place][1].at[slot]).wait()
-            mine = held[place][0][slot]
+            load(flow, slot, buffers[1].at[slot]).wait()
+            mine = buffers[0][slot]
         else:
-            mine = held[place][stage - 1][(slot,) + view(order, stage - 1, True)]
-        value = buffer[slot] + mine
+            mine = buffers[stage - 1][(slot,) + view(flow.order, stage - 1, True)]
+        value = buffers[stage][slot] + mine
         if stage < stages:
-            buffer[slot] = value
-            take_credit(place, stage, unit)
-            remote(place, stage, slot, sent_from(place, stage, slot)).start()
+            buffers[stage][slot] = value
+            take_credit(flow, stage, unit)
+            remote(flow, stage, slot, sent_from(flow, stage, slot)).start()
         else:
-            target = up_sum if family == 2 else weight_sum
-            base = row + (weight_sum.shape[1] // 2 if family == 1 else 0)
-            target[layer, pl.ds(pl.multiple_of(base + unit * UNIT, UNIT), UNIT)] = value
-        if stage > 1 or layer > 0:
+            target = up_sum if flow.family == 1 else weight_sum
+            at = pl.ds(pl.multiple_of(flow.row + unit * UNIT, UNIT), UNIT)
+            target[flow.layer, at] = value
+        if stage > 1 or not begun:
             copy.wait_send()
         if stage >= 2:
-            return_credit(place, stage - 2, unit)
+            return_credit(flow, stage - 2, unit)
         if stage == stages:
-            return_credit(place, stage - 1, unit)
-
-    def within(place, unit):
-        inside = (unit >= 0) & (unit < flows[place].units)
-        return inside & (core == 1) if flows[place].family == 2 else inside
+            return_credit(flow, stage - 1, unit)
+
+    def within(flow, unit):
+        return (unit >= 0) & (unit < flow.units) & (core == flow.core)
 
     def step(index, carry):
-        for place, flow in enumerate(flows):
+        for flow in flows:
             unit = index - flow.start
-            pl.when(within(place, unit))(functools.partial(begin, place, unit))
-        for place, flow in enumerate(flows):
+            pl.when(within(flow, unit))(functools.partial(begin, flow, unit))
+        for flow in flows:
             for stage in range(1, stages + 1):
                 unit = index - flow.start - LAG * stage
-                pl.when(within(place, unit))(functools.partial(advance, place, stage, unit))
+                pl.when(within(flow, unit))(functools.partial(advance, flow, stage, unit))
         pl.when((index >= norm_start) & (index < norm_start + jobs))(
             functools.partial(norm_job, index)
-        )
-        pl.when((index >= result_start) & (index < result_start + jobs))(
-            functools.partial(result_job, index)
         )
         for stage in range(stages + 1):
             pl.when(index == small_start + 2 * stage)(functools.partial(small_step, stage))
@@ -957,7 +1011,6 @@
 
     last = max(flow.start + flow.units for flow in flows)
     lax.fori_loop(0, last + LAG * stages, step, 0)
-    stores[1].start()
     turn_weights(1)
     for layer in range(len(moved)):
 
@@ -970,11 +1023,10 @@
         def _():
             near_copy(layer).wait_send()
 
-    for copy in stores:
-        copy.wait()
-
-
-def finish(last, first, came, part, tokens, grad, x, own, other, biases, sums, gain):
+    store.wait()
+
+
+def finish(last, first, came, part, tokens, grad, biases, sums, gain):
     length, width = tokens.shape
     bits = 4
     split = (2,) * (bits - 1)
@@ -991,24 +1043,22 @@
         pltpu.VMEM(full, F32),
         pltpu.VMEM(full, BF16),
         pltpu.VMEM(full, BF16),
-        pltpu.VMEM(full, F32),
-        pltpu.VMEM(full, F32),
-        pltpu.VMEM(full, F32),
         pltpu.VMEM((8, width), F32),
     ]
-    for _ in flows:
+    places = 1 + max(flow.place for flow in flows)
+    for _ in range(places):
         for stage in range(bits + 1):
             lead = (SLOTS,) + (2,) * (bits - 1 - max(stage - 1, 0))
             scratch.append(pltpu.VMEM(lead + (UNIT, WIDE), F32))
     scratch += [pltpu.VMEM(small, F32)] * (2 * bits + 1)
     scratch += [
-        pltpu.SemaphoreType.DMA((len(flows), SLOTS)),
-        pltpu.SemaphoreType.DMA((len(flows), bits, SLOTS)),
-        pltpu.SemaphoreType.DMA((len(flows), bits, SLOTS)),
-        pltpu.SemaphoreType.REGULAR((len(flows), bits)),
+        pltpu.SemaphoreType.DMA((places, SLOTS)),
+        pltpu.SemaphoreType.DMA((places, bits, SLOTS)),
+        pltpu.SemaphoreType.DMA((places, bits, SLOTS)),
+        pltpu.SemaphoreType.REGULAR((places, bits)),
         pltpu.SemaphoreType.DMA((bits,)),
         pltpu.SemaphoreType.DMA((bits,)),
-        pltpu.SemaphoreType.DMA((8,)),
+        pltpu.SemaphoreType.DMA((4,)),
         pltpu.SemaphoreType.DMA((3,)),
         pltpu.SemaphoreType.DMA((3,)),
     ]
@@ -1017,15 +1067,14 @@
     large = [array.reshape(split + array.shape[2:]) for array in large]
     return pl.pallas_call(
         functools.partial(finish_kernel, bits, flows),
-        in_specs=[pl.BlockSpec(memory_space=pltpu.HBM)] * (len(large) + 6)
+        in_specs=[pl.BlockSpec(memory_space=pltpu.HBM)] * (len(large) + 3)
         + [pl.BlockSpec(memory_space=pltpu.VMEM)] * 4,
         out_specs=[pl.BlockSpec(memory_space=pltpu.VMEM)] * 3
-        + [pl.BlockSpec(memory_space=pltpu.HBM)] * 2,
+        + [pl.BlockSpec(memory_space=pltpu.HBM)],
         out_shape=[
             jax.ShapeDtypeStruct((2, WIDE, width), F32),
             jax.ShapeDtypeStruct((2, WIDE // 2, width), F32),
             jax.ShapeDtypeStruct(small, F32),
-            jax.ShapeDtypeStruct(full, F32),
             jax.ShapeDtypeStruct(full, F32),
         ],
         scratch_shapes=scratch,
@@ -1033,18 +1082,16 @@
             collective_id=0, has_side_effects=True, vmem_limit_bytes=VMEM_LIMIT
         ),
         name="finish",
-    )(*large, part, tokens, grad, x, own, other, biases[0], biases[1], sums, gain)
+    )(*large, part, tokens, grad, biases[0], biases[1], sums, gain)
 
 
 def send_first(halves):
     count = lax.axis_size("batch")
     received = []
     for bit, part in enumerate(halves[0::2]):
-        streams = (1,) if bit == 2 else (0, 1)
+        stream = 0 if bit == 2 else 1
         pairs = [
-            (2 * source + stream, 2 * flip(source, bit) + stream)
-            for source in range(count)
-            for stream in streams
+            (2 * source + stream, 2 * flip(source, bit) + stream) for source in range(count)
         ]
         received.append(lax.ppermute(part, ("batch", "stream"), pairs))
     return received
@@ -1105,23 +1152,25 @@
     me = lax.axis_index("batch") if blocked else 0
     place = jnp.stack([jnp.asarray(bit_of(me, bit), jnp.int32) for bit in range(3)])
 
-    def attention_back(layer, grad):
+    def attention_back(layer, grad, stream):
         h, state, mixed = kept[layer]
         return attention_backward(
-            layer, place, doc_starts, grad, h, state, mixed, tables, rotary, branch_weight
-        )
-
-    def feed_forward_back(layer, grad):
+            layer, place, doc_starts, grad, h, state, mixed, tables, rotary, branch_weight, stream
+        )
+
+    def feed_forward_back(layer, grad, stream):
         h, act, slope = kept[layer]
-        return mlp_backward(layer, place, grad, h, act, slope, branch_weight, up_weight)
-
-    def back(layer, grad):
-        part, *halves, bias = lax.cond(
+        return mlp_backward(
+            layer, place, grad, h, act, slope, branch_weight, up_weight, stream
+        )
+
+    def back(layer, grad, stream=()):
+        *result, part, a, b, c, d, e, f, bias = lax.cond(
             is_attention,
-            functools.partial(attention_back, layer, grad),
-            functools.partial(feed_forward_back, layer, grad),
-        )
-        return part, halves, bias
+            functools.partial(attention_back, layer, grad, stream),
+            functools.partial(feed_forward_back, layer, grad, stream),
+        )
+        return *result, part, (a, b, c, d, e, f), bias
 
     def norm_back(layer, part, grad, kind):
         other = lax.ppermute(part, "stream", swap)
@@ -1133,14 +1182,12 @@
     if blocked:
         came = send_first(halves1)
     grad0, sums1 = norm_back(1, part1, cotangent, BF16)
-    part0, halves0, bias0 = back(0, grad0)
+    result, part0, halves0, bias0 = back(0, grad0, stream)
     if blocked:
-        weight, up, small, result, input_grad = finish(
-            halves1, halves0, came, part0, tokens, grad0, *stream, (bias0, bias1), sums1,
-            norm_gain[:1],
+        weight, up, small, input_grad = finish(
+            halves1, halves0, came, part0, tokens, grad0, (bias0, bias1), sums1, norm_gain[:1]
         )
     else:
-        result = stream[0] + (stream[1] + stream[2])
         input_grad, sums0 = norm_back(0, part0, grad0, F32)
         weight, up = scatter_rows((halves0, halves1))
         small = lax.psum(jnp.concatenate([bias0, bias1, sums1, sums0]), "batch")
@@ -1164,11 +1211,14 @@
 def scatter_rows(layers):
     weights, ups = [], []
     for along_x, kept_x, along_y, kept_y, along_z, kept_z in layers:
-        width = kept_z.shape[2]
-        part_x = jnp.stack([kept_x, along_x], axis=2).reshape(-1, width // 2, WIDE)
-        part_y = jnp.stack([kept_y, along_y], axis=1).reshape(-1, width // 2, WIDE)
-        weight = rows_of(jnp.concatenate([part_x, part_y], axis=1))
-        up = rows_of(jnp.stack([kept_z, along_z], axis=1).reshape(-1, width, WIDE))
+        blocks = (-1,) + kept_x.shape[2:]
+        weight = jnp.where(
+            lax.axis_index("stream") == 1,
+            jnp.stack([kept_x, along_x], axis=2).reshape(blocks),
+            jnp.stack([kept_z, along_z], axis=1).reshape(blocks),
+        )
+        weight = rows_of(weight)
+        up = rows_of(jnp.stack([kept_y, along_y], axis=1).reshape(blocks))
         up = jnp.where(lax.axis_index("stream") == 1, up, 0.0)
         weights.append(lax.psum_scatter(weight, "batch", scatter_dimension=0, tiled=True))
         ups.append(lax.psum_scatter(up, ("batch", "stream"), scatter_dimension=0, tiled=True))

time: 617 us -> 560 us (0.908)
  Pallas kernels: 555 us -> 492 us
  waiting for transfers between devices: 17.9 us -> 28 us
  loops' own time: 7.54 us -> 1.36 us
    pallas_call x3, Pallas kernels: 164 us -> 126 us  [the longest x2 121 us: attention_backward(): pl.pallas_call(functools.partial(attention_backward_kernel, len(stream)),...]
    pallas_call x2, Pallas kernels: 81.8 us -> 67.7 us  [attention_forward(): pl.pallas_call(functools.partial(attention_forward_kernel, len(stream)),...]
    pallas_call x1, Pallas kernels: 300 us -> 290 us  [finish(): pl.pallas_call(functools.partial(finish_kernel, bits, flows), in_specs=[p...]
    another operation x2, loops' own time: 6.92 us -> 0.56 us  [shards(): lax.cond(is_attention, functools.partial(attention, layer, stream), funct...]
  transfers between devices with their start and end apart: 6 -> 6, of which waited for: 4 -> 3; matrix products, arithmetic and copies ran while one was open for 0% -> 0% of each run, Pallas kernels for 13% -> 13%
where the time goes in v6:
time: 560 us; the launch traced here: 554 us
  Pallas kernels  492 us (88%)
  waiting for transfers between devices  28 us (5%)
  local copies, waits for them, and re-layouts  17.1 us (3%)
  starting transfers between devices  13.4 us (2%)
    pallas_call x1, Pallas kernels, finish(): pl.pallas_call(functools.partial(finish_kernel, bits, flows), in_specs=[p...  290 us
    pallas_call x2, Pallas kernels, attention_backward(): pl.pallas_call(functools.partial(attention_backward_kernel, len(stream)),...  121 us
    pallas_call x2, Pallas kernels, attention_forward(): pl.pallas_call(functools.partial(attention_forward_kernel, len(stream)),...  67.7 us
    ppermute x3, waiting for transfers between devices, send_first(): received.append(lax.ppermute(part, ('batch', 'stream'), pairs))  14.2 us
    ppermute x3, starting transfers between devices, send_first(): received.append(lax.ppermute(part, ('batch', 'stream'), pairs))  12.8 us
  transfers between devices with their start and end apart: 6, of which 3 were waited for; matrix products, arithmetic and copies ran while one was open for 0% of the time, Pallas kernels for 13%

profile of v6, /device:TPU:0, one launch (start us, length us, event | category | flops | bytes accessed | tf_op | source)
XLA Modules:
  0.0 554.1 jit_solution(14582502191843955315)
XLA Ops:
  1.4 5.1 conditional.5
  1.4 5.1 feature_tables.1
  7.5 33.7 %conditional.6 = ((f32[1024,1024]{1,0:T(8,128)}, bf16[1024,1024]{1,0:T(8,128)(2,1)}, bf16[4,1024,1024]{2,1,0:T(8,128)(2,1)}, bf16[4,1024,1024]{2,1,0:T(8,128)(2,1)})) conditional(s32[]{:T(128)} %convert_element_type.13, (bf16[2,1024]{1,0:T(2,128)(2,1)}, bf16[2,1024]{1,0:T(2,128)(2,1)}, f32[2,4096]{1,0:T(2,128)S(1)}, bf16[2,1024]{1,0:T(2,128)(2,1)}, ...), branch_computations={%region_2.0_spmd, %region_3.0_spmd} | conditional | bytes 40968 | solution.py:1140
  8.8 32.3 %attention_forward.2 = (f32[1024,1024]{1,0:T(8,128)}, bf16[1024,1024]{1,0:T(8,128)(2,1)}, bf16[4,1024,1024]{2,1,0:T(8,128)(2,1)}, bf16[4,1024,1024]{2,1,0:T(8,128)(2,1)}) custom-call(bf16[1024,1024]{1,0:T(8,128)(2,1)} %get-tuple-element.216.refs_0_, s32[1,4]{1,0:T(1,128)} %get-tuple-element.217.refs_1_, bf16[1,1024]{1,0:T(2,128)(2,1)} %bitcast.75, ...), custom_call_target="tpu_custom_call" | custom-call | tf_op jit(solution)/shard_map/cond/branch_1_fun/attention_forward/pallas_call | solution.py:484
  41.4 7.4 %collective-permute-done = f32[1024,1024]{1,0:T(8,128)} collective-permute-done((f32[1024,1024]{1,0:T(8,128)}, f32[1024,1024]{1,0:T(8,128)}, u32[]{:S(2)}, u32[]{:S(2)}) %collective-permute-start) | collective-permute-done | bytes 4194336 | tf_op jit(solution)/shard_map/ppermute | solution.py:1147
  48.7 39.6 %conditional.7 = ((f32[1024,1024]{1,0:T(8,128)}, f32[1024,1024]{1,0:T(8,128)}, bf16[1024,1024]{1,0:T(8,128)(2,1)}, bf16[4,1024,1024]{2,1,0:T(8,128)(2,1)}, bf16[4,1024,1024]{2,1,0:T(8,128)(2,1)})) conditional(s32[]{:T(128)} %convert_element_type.13, (bf16[2,1024]{1,0:T(2,128)(2,1)}, bf16[2,1024]{1,0:T(2,128)(2,1)}, f32[2,4096]{1,0:T(2,128)S(1)}, ...), branch_computations={%region_4.0_spmd, %region_5.0_spmd} | conditional | bytes 49160 | solution.py:1140
  50.3 1.3 slice.62.refs_4_
  51.6 1.3 slice.63.refs_5_
  52.9 35.4 %attention_forward.3 = (f32[1024,1024]{1,0:T(8,128)}, f32[1024,1024]{1,0:T(8,128)}, bf16[1024,1024]{1,0:T(8,128)(2,1)}, bf16[4,1024,1024]{2,1,0:T(8,128)(2,1)}, bf16[4,1024,1024]{2,1,0:T(8,128)(2,1)}) custom-call(bf16[1024,1024]{1,0:T(8,128)(2,1)} %get-tuple-element.236.refs_0_, f32[1024,1024]{1,0:T(8,128)} %get-tuple-element.237.refs_1_, ...), custom_call_target="tpu_custom_call" | custom-call | tf_op jit(solution)/shard_map/cond/branch_1_fun/attention_forward/pallas_call | solution.py:484
  88.3 60.3 %conditional.8 = (f32[1024,1024]{1,0:T(8,128)}, f32[4,2,1024,256]{3,2,1,0:T(8,128)}, f32[4,2,1024,256]{3,2,1,0:T(8,128)}, f32[2,4,1024,256]{3,2,1,0:T(8,128)}, f...) conditional(s32[]{:T(128)} %convert_element_type.13, ...), branch_computations={%region_6.7_spmd, %region_7.8_spmd} | conditional | bytes 64 | solution.py:1168
  88.5 59.7 %attention_backward.2 = (f32[1024,1024]{1,0:T(8,128)}, f32[4,2,1024,256]{3,2,1,0:T(8,128)}, f32[4,2,1024,256]{3,2,1,0:T(8,128)}, f32[4,2,1024,256]{3,2,1,0:T(8,1...) custom-call(s32[3]{0:T(128)S(1)} %get-tuple-element.264.place_ref, ...), custom_call_target="tpu_custom_call" | custom-call | tf_op jit(solution)/shard_map/cond/branch_1_fun/attention_backward/pallas_call | solution.py:659
  148.6 4.0 collective-permute-start.3
  152.6 3.9 collective-permute-start.4
  156.5 4.9 collective-permute-start.5
  162.6 6.4 %collective-permute-done.2.other_ref = f32[1024,1024]{1,0:T(8,128)} collective-permute-done((f32[1024,1024]{1,0:T(8,128)}, f32[1024,1024]{1,0:T(8,128)}, u32[]{:S(2)}, u32[]{:S(2)}) %collective-permute-start.2) | collective-permute-done | bytes 4194336 | tf_op jit(solution)/shard_map/ppermute | solution.py:1176
  169.0 8.1 %norm_backward.1 = (bf16[1024,1024]{1,0:T(8,128)(2,1)}, f32[8,1024]{1,0:T(8,128)}) custom-call(f32[1024,1024]{1,0:T(8,128)} %get-tuple-element.370.x_ref, f32[1024,1024]{1,0:T(8,128)} %get-tuple-element.375.own_ref, f32[1024,1024]{1,0:T(8,128)} %collective-permute-done.2.other_ref, bf16[1024,1024]{1,0:T(8,128)(2,1)S(1)} %copy-done.2, ...), custom_call_target="tpu_custom_call" | custom-call | tf_op jit(solution)/shard_map/norm_backward/pallas_call | solution.py:731
  177.1 61.7 %conditional.9 = (f32[1024,1024]{1,0:T(8,128)}, f32[1024,1024]{1,0:T(8,128)}, f32[4,1024]{1,0:T(4,128)S(1)}, f32[2,2,2,1024,256]{4,3,2,1,0:T(8,128)}, f32[2,2,2,...) conditional(s32[]{:T(128)} %convert_element_type.13, ...), branch_computations={%region_8.9_spmd, %region_9.10_spmd} | conditional | bytes 72 | solution.py:1168
  177.1 61.5 %attention_backward.3 = (f32[1024,1024]{1,0:T(8,128)}, f32[1024,1024]{1,0:T(8,128)}, f32[4,2,1024,256]{3,2,1,0:T(8,128)}, f32[4,2,1024,256]{3,2,1,0:T(8,128)}, f...) custom-call(s32[3]{0:T(128)S(1)} %get-tuple-element.301.place_ref, ...), custom_call_target="tpu_custom_call" | custom-call | tf_op jit(solution)/shard_map/cond/branch_1_fun/attention_backward/pallas_call | solution.py:659
  238.9 14.2 %collective-permute-done.5 = f32[2,4,1024,256]{3,2,1,0:T(8,128)} collective-permute-done((f32[2,4,1024,256]{3,2,1,0:T(8,128)}, f32[2,4,1024,256]{3,2,1,0:T(8,128)}, u32[]{:S(2)}, u32[]{:S(2)}) %collective-permute-start.5) | collective-permute-done | bytes 8388640 | tf_op jit(solution)/shard_map/ppermute | solution.py:1096
  253.1 290.1 %finish.1 = (f32[2,256,1024]{2,1,0:T(8,128)}, f32[2,128,1024]{2,1,0:T(8,128)}, f32[24,1024]{1,0:T(8,128)}, f32[1024,1024]{1,0:T(8,128)}) custom-call(f32[2,2,2,1024,256]{4,3,2,1,0:T(8,128)} %get-tuple-element.381.kept_x1, f32[2,2,2,1024,256]{4,3,2,1,0:T(8,128)} %get-tuple-element.382.kept_y1, f32[2,2,2,1024,256]{4,3,2,1,0:T(8,128)} %get-tuple-element.383.kept_z1, ...), custom_call_target="tpu_custom_call" | custom-call | tf_op jit(solution)/shard_map/finish/pallas_call | solution.py:1068
  543.3 1.0 slice_bitcast_fusion
  546.7 4.8 copy.87
  551.5 1.3 copy.88
  552.9 1.0 copy.89
  (37 shorter events, 7.9 us)
Async XLA Ops:
  6.5 1.0 copy-start.3
  41.2 7.6 %collective-permute-start = (f32[1024,1024]{1,0:T(8,128)}, f32[1024,1024]{1,0:T(8,128)}, u32[]{:S(2)}, u32[]{:S(2)}) collective-permute-start(f32[1024,1024]{1,0:T(8,128)} %get-tuple-element.369), channel_id=1, source_target_pairs={{0,1},{1,0},{2,3},{3,2},{4,5},{5,4},{6,7},{7,6},{8,9},{9,8},{10,11... | collective-permute-start | bytes 12582920 | tf_op jit(solution)/shard_map/ppermute | solution.py:1147
  48.7 39.6 %copy-start.2 = (bf16[1024,1024]{1,0:T(8,128)(2,1)S(1)}, bf16[1024,1024]{1,0:T(8,128)(2,1)}, u32[]{:S(2)}) copy-start(bf16[1024,1024]{1,0:T(8,128)(2,1)} %grad_ref.1) | copy-start | bytes 6291460
  88.3 73.7 %copy-start.7 = (bf16[2,1024]{1,0:T(2,128)(2,1)S(1)}, bf16[2,1024]{1,0:T(2,128)(2,1)}, u32[]{:S(2)}) copy-start(bf16[2,1024]{1,0:T(2,128)(2,1)} %param.29) | copy-start | bytes 12292
  148.6 28.5 %copy-start.8 = (s32[1,4]{1,0:T(1,128)S(1)}, s32[1,4]{1,0:T(1,128)}, u32[]{:S(2)}) copy-start(s32[1,4]{1,0:T(1,128)} %param.32) | copy-start | bytes 52
  148.6 90.3 %collective-permute-start.3 = (f32[4,2,1024,256]{3,2,1,0:T(8,128)}, f32[4,2,1024,256]{3,2,1,0:T(8,128)}, u32[]{:S(2)}, u32[]{:S(2)}) collective-permute-start(f32[4,2,1024,256]{3,2,1,0:T(8,128)} %get-tuple-element.384), channel_id=1, source_target_pairs={{1,3},{3,1},{5,7},{7,5},{9,11},{11,9},{13,15},{15,13},{17,19},{19,... | collective-permute-start | bytes 25165832 | tf_op jit(solution)/shard_map/ppermute | solution.py:1096
  152.6 86.3 %collective-permute-start.4 = (f32[4,2,1024,256]{3,2,1,0:T(8,128)}, f32[4,2,1024,256]{3,2,1,0:T(8,128)}, u32[]{:S(2)}, u32[]{:S(2)}) collective-permute-start(f32[4,2,1024,256]{3,2,1,0:T(8,128)} %get-tuple-element.385), channel_id=1, source_target_pairs={{1,5},{3,7},{5,1},{7,3},{9,13},{11,15},{13,9},{15,11},{17,21},{19,... | collective-permute-start | bytes 25165832 | tf_op jit(solution)/shard_map/ppermute | solution.py:1096
  156.5 96.7 %collective-permute-start.5 = (f32[2,4,1024,256]{3,2,1,0:T(8,128)}, f32[2,4,1024,256]{3,2,1,0:T(8,128)}, u32[]{:S(2)}, u32[]{:S(2)}) collective-permute-start(f32[2,4,1024,256]{3,2,1,0:T(8,128)} %get-tuple-element.386), channel_id=1, source_target_pairs={{0,8},{2,10},{4,12},{6,14},{8,0},{10,2},{12,4},{14,6},{16,24},{18,... | collective-permute-start | bytes 25165832 | tf_op jit(solution)/shard_map/ppermute | solution.py:1096
  161.4 7.6 %collective-permute-start.2 = (f32[1024,1024]{1,0:T(8,128)}, f32[1024,1024]{1,0:T(8,128)}, u32[]{:S(2)}, u32[]{:S(2)}) collective-permute-start(f32[1024,1024]{1,0:T(8,128)} %get-tuple-element.375.own_ref), channel_id=1, source_target_pairs={{0,1},{1,0},{2,3},{3,2},{4,5},{5,4},{6,7},{7,6},{8,9},{9,8},{10,11... | collective-permute-start | bytes 12582920 | tf_op jit(solution)/shard_map/ppermute | solution.py:1176
  161.5 15.6 %collective-permute-start.1 = (f32[1024,1024]{1,0:T(8,128)}, f32[1024,1024]{1,0:T(8,128)}, u32[]{:S(2)}, u32[]{:S(2)}) collective-permute-start(f32[1024,1024]{1,0:T(8,128)} %get-tuple-element.371), channel_id=1, source_target_pairs={{0,1},{1,0},{2,3},{3,2},{4,5},{5,4},{6,7},{7,6},{8,9},{9,8},{10,11... | collective-permute-start | bytes 12582920 | tf_op jit(solution)/shard_map/ppermute | solution.py:1147
  162.0 15.1 %copy-start.1 = (f32[1024,1024]{1,0:T(8,128)S(1)}, f32[1024,1024]{1,0:T(8,128)}, u32[]{:S(2)}) copy-start(f32[1024,1024]{1,0:T(8,128)} %get-tuple-element.370.x_ref) | copy-start | bytes 12582916
  162.0 15.1 %copy-start.4 = (f32[1024,128]{1,0:T(8,128)S(1)}, f32[1024,128]{1,0:T(8,128)}, u32[]{:S(2)}) copy-start(f32[1024,128]{1,0:T(8,128)} %constant.78.clone) | copy-start | bytes 1572868
  177.1 76.0 %copy-start = (bf16[1024,1024]{1,0:T(8,128)(2,1)S(1)}, bf16[1024,1024]{1,0:T(8,128)(2,1)}, u32[]{:S(2)}) copy-start(bf16[1024,1024]{1,0:T(8,128)(2,1)} %tokens_ref.1) | copy-start | bytes 6291460
  543.3 8.3 %copy-start.5 = (f32[2,256,1024]{2,1,0:T(8,128)S(1)}, f32[2,256,1024]{2,1,0:T(8,128)}, u32[]{:S(2)}) copy-start(f32[2,256,1024]{2,1,0:T(8,128)} %get-tuple-element.398) | copy-start | bytes 6291460
  543.3 9.6 %copy-start.6 = (f32[2,128,1024]{2,1,0:T(8,128)S(1)}, f32[2,128,1024]{2,1,0:T(8,128)}, u32[]{:S(2)}) copy-start(f32[2,128,1024]{2,1,0:T(8,128)} %get-tuple-element.482) | copy-start | bytes 3145732

commit v7 on v6

--- a/solution.py
+++ b/solution.py
@@ -196,9 +196,12 @@
 FF_ROWS = 512
 
 
-def mlp_forward_kernel(count, *refs):
+def mlp_forward_kernel(layer, count, *refs):
     stream, refs = refs[:count], refs[count:]
     gain_ref, offset_ref, up_ref, bias_ref, down_ref, down_bias_ref = refs[:6]
+    gain_ref, offset_ref, down_bias_ref = [
+        ref.at[layer : layer + 1] for ref in (gain_ref, offset_ref, down_bias_ref)
+    ]
     refs = refs[6:]
     x_ref = None
     if count > 1:
@@ -238,22 +241,22 @@
     if len(stream) > 1:
         out_shape, out_specs = [full] + out_shape, [whole((length, width))] + out_specs
     return pl.pallas_call(
-        functools.partial(mlp_forward_kernel, len(stream)),
+        functools.partial(mlp_forward_kernel, layer, len(stream)),
         grid=(blocks,),
         in_specs=[whole((length, width))] * len(stream)
         + [
-            whole((1, width)),
-            whole((1, width)),
+            whole((LAYERS, width)),
+            whole((LAYERS, width)),
             pl.BlockSpec((1, FF_BLOCK, width), lambda j: (layer, j, 0)),
-            pl.BlockSpec((1, 1, FF_BLOCK), lambda j: (j, 0, 0)),
+            pl.BlockSpec((1, 1, FF_BLOCK), lambda j: (layer * blocks + j, 0, 0)),
             pl.BlockSpec((1, 1, FF_BLOCK, width), lambda j: (0, layer, j, 0)),
-            whole((1, width)),
+            whole((LAYERS, width)),
         ],
         out_specs=out_specs,
         out_shape=out_shape,
         compiler_params=params(),
         name="mlp_forward",
-    )(*stream, gain, offset, up, biases.reshape(blocks, 1, FF_BLOCK), down_weight, down_bias)
+    )(*stream, gain, offset, up, biases, down_weight, down_bias)
 
 
 def add_stream(stream, result_ref):
@@ -273,9 +276,8 @@
     stream, refs = refs[:count], refs[count:]
     grad_ref, h_ref, act_ref, slope_ref, down_ref, up_ref = refs[:6]
     result_ref, refs = (refs[6], refs[7:]) if count else (None, refs[6:])
-    part_ref, along_x, kept_x, along_y, kept_y, along_z, kept_z, bias_ref = refs[:8]
-    grad_t, h_t, units = refs[8:]
-    del along_z, kept_z
+    part_ref, along_x, kept_x, along_y, kept_y, bias_ref = refs[:6]
+    grad_t, h_t, units = refs[6:]
     step = pl.program_id(0)
     add_stream(stream, result_ref)
 
@@ -308,9 +310,14 @@
                 target[0, side, rows] = dot_nn(h_t[rows], units[:, block(y, side)])
 
 
-def halves_of(width):
-    shapes = ((4, 2, width, WIDE),) * 4 + ((2, 4, width, WIDE),) * 2
+def halves_of(width, weight):
+    shapes = (weight,) * 2 + ((4, 2, width, WIDE),) * 2
     return [jax.ShapeDtypeStruct(shape, F32) for shape in shapes]
+
+
+def flat_halves(part, sent, kept, sent_up, kept_up, bias):
+    halves = [half.reshape((-1,) + half.shape[2:]) for half in (sent, kept, sent_up, kept_up)]
+    return (part, *halves, bias)
 
 
 def mlp_backward(layer, place, grad, h, act, slope, down_weight, up, stream=()):
@@ -337,7 +344,6 @@
             out_specs=stream_out
             + [whole((length, width))]
             + [pair] * 4
-            + [pl.BlockSpec(memory_space=pl.ANY)] * 2
             + [whole((blocks, FF_BLOCK))],
             scratch_shapes=[
                 pltpu.VMEM((width, length), BF16),
@@ -347,7 +353,7 @@
         ),
         out_shape=stream_shape
         + [jax.ShapeDtypeStruct((length, width), F32)]
-        + halves_of(width)
+        + halves_of(width, (4, 2, width, WIDE))
         + [jax.ShapeDtypeStruct((blocks, FF_BLOCK), F32)],
         compiler_params=params(),
         name="mlp_backward",
@@ -393,11 +399,13 @@
     )
 
 
-def attention_forward_kernel(count, *refs):
+def attention_forward_kernel(layer, count, *refs):
     stream, refs = refs[:count], refs[count:]
-    starts_ref, gain_ref, offset_ref, weight_ref, bias_ref, out_bias_ref = refs[:6]
-    upper_ref, lower_ref, scale_ref, cosine_ref, sine_ref = refs[6:11]
-    refs = refs[11:]
+    starts_ref, gain_ref, offset_ref, weight_ref, bias_ref = refs[:5]
+    gain_ref, offset_ref = [ref.at[layer : layer + 1] for ref in (gain_ref, offset_ref)]
+    kind_rows = bias_ref.shape[0] // LAYERS
+    upper_ref, lower_ref, scale_ref, cosine_ref, sine_ref = refs[5:10]
+    refs = refs[10:]
     x_ref = None
     if count > 1:
         x_ref, refs = refs[0], refs[1:]
@@ -408,10 +416,12 @@
     def _():
         start_layer(stream, x_ref, h_ref, gain_ref, offset_ref)
         write_mask(starts_ref, mask_ref, False)
-        part_ref[...] = jnp.broadcast_to(out_bias_ref[...], part_ref.shape)
+        last = layer * kind_rows + 3
+        part_ref[...] = jnp.broadcast_to(bias_ref[last], part_ref.shape)
 
     ones = same_head_ones()
     table_up, table_low = upper_ref[0, 0], lower_ref[0, 0]
+    lanes_of_step = pl.ds(pl.multiple_of(pl.program_id(0) * WIDE, WIDE), WIDE)
 
     def features(values, rows):
         upper, lower = split(turn(values, *wide_rotary(cosine_ref, sine_ref, rows)))
@@ -420,7 +430,9 @@
     for first in range(0, length, ROWS):
         rows = slice(first, first + ROWS)
         queries, keys, values = [
-            dot_nt(h_ref[rows], weight_ref[0, 0, kind, 0]) + bias_ref[kind, 0] for kind in range(3)
+            dot_nt(h_ref[rows], weight_ref[0, 0, kind, 0])
+            + bias_ref[layer * kind_rows + kind, :, lanes_of_step]
+            for kind in range(3)
         ]
         state_ref[0, rows] = jnp.exp(features(queries, rows)).astype(BF16)
         logs = features(keys, rows) - (0.5 / math.sqrt(DH)) * head_sums(keys * keys, ones)
@@ -482,16 +494,15 @@
     if len(stream) > 1:
         out_shape, out_specs = [full] + out_shape, [whole((length, width))] + out_specs
     return pl.pallas_call(
-        functools.partial(attention_forward_kernel, len(stream)),
+        functools.partial(attention_forward_kernel, layer, len(stream)),
         grid=(QUADS,),
         in_specs=[whole((length, width))] * len(stream)
         + [
             pl.BlockSpec(memory_space=pltpu.SMEM),
-            whole((1, width)),
-            whole((1, width)),
+            whole((LAYERS, width)),
+            whole((LAYERS, width)),
             pl.BlockSpec((1, 1, 4, 1, WIDE, width), lambda g: (0, layer, 0, g, 0, 0)),
-            pl.BlockSpec((4, 1, 1, WIDE), lambda g: (0, g, 0, 0)),
-            whole((1, width)),
+            whole((LAYERS * 4, 1, width)),
             pl.BlockSpec((1, 1, WIDE, WIDE), lambda g: (layer, g, 0, 0)),
             pl.BlockSpec((1, 1, WIDE, WIDE), lambda g: (layer, g, 0, 0)),
             pl.BlockSpec((1, 1, 1, WIDE), lambda g: (layer, g, 0, 0)),
@@ -505,7 +516,7 @@
         name="attention_forward",
     )(
         *stream, starts, gain, offset, kinds_of(weight),
-        biases.reshape(4, QUADS, 1, WIDE), biases[None, 3 * width :], *tables, *rotary,
+        biases, *tables, *rotary,
     )
 
 
@@ -514,9 +525,8 @@
     starts_ref, grad_ref, h_ref, state_ref, mixed_ref, table_ref = refs[:6]
     cosine_ref, sine_ref, weight_ref = refs[6:9]
     result_ref, refs = (refs[9], refs[10:]) if count else (None, refs[9:])
-    part_ref, along_x, kept_x, along_y, kept_y, along_z, kept_z, bias_ref = refs[:8]
-    mask_ref, upright, numer_ref, feat_ref, flow = refs[8:]
-    del along_x, kept_x, along_y, kept_y
+    part_ref, along_z, kept_z, _, _, bias_ref = refs[:6]
+    mask_ref, upright, numer_ref, feat_ref, flow = refs[6:]
     group = pl.program_id(0)
     length, width = h_ref.shape
     add_stream(stream, result_ref)
@@ -675,8 +685,8 @@
             ],
             out_specs=stream_out
             + [whole((length, width))]
-            + [pl.BlockSpec(memory_space=pl.ANY)] * 4
             + [halves, halves]
+            + [pl.BlockSpec(memory_space=pl.ANY)] * 2
             + [pl.BlockSpec((4, WIDE), lambda g, *_: (0, g))],
             scratch_shapes=[
                 pltpu.VMEM((length, ROWS), BF16),
@@ -688,7 +698,7 @@
         ),
         out_shape=stream_shape
         + [jax.ShapeDtypeStruct((length, width), F32)]
-        + halves_of(width)
+        + halves_of(width, (2, 4, width, WIDE))
         + [jax.ShapeDtypeStruct((4, width), F32)],
         compiler_params=params(),
         name="attention_backward",
@@ -710,7 +720,7 @@
     return grad + inverse * (grad_unit - first - unit * second)
 
 
-def norm_backward_kernel(x_ref, own_ref, other_ref, grad_ref, gain_ref, out_ref, sums_ref):
+def norm_backward_kernel(layer, x_ref, own_ref, other_ref, grad_ref, gain_ref, out_ref, sums_ref):
     @pl.when(pl.program_id(0) == 0)
     def _():
         sums_ref[...] = jnp.zeros_like(sums_ref)
@@ -719,19 +729,19 @@
         x_ref[...].astype(F32),
         own_ref[...] + other_ref[...],
         grad_ref[...].astype(F32),
-        gain_ref[...].astype(F32),
+        gain_ref[layer : layer + 1].astype(F32),
         sums_ref,
     )
     out_ref[...] = out.astype(out_ref.dtype)
 
 
-def norm_backward(x, own, other, grad, gain, kind):
+def norm_backward(layer, x, own, other, grad, gain, kind):
     length, width = own.shape
     block = pl.BlockSpec((ROWS, width), lambda i: (i, 0))
     return pl.pallas_call(
-        norm_backward_kernel,
+        functools.partial(norm_backward_kernel, layer),
         grid=(length // ROWS,),
-        in_specs=[block, block, block, block, whole((1, width))],
+        in_specs=[block, block, block, block, whole((LAYERS, width))],
         out_specs=[block, whole((8, width))],
         out_shape=[
             jax.ShapeDtypeStruct((length, width), kind),
@@ -744,15 +754,14 @@
 
 MESH = pl.DeviceIdType.MESH
 UNIT = 16
-SLOTS = 4
-LAG = 1
-JOB = 128
+SLOTS = 6
+LAG = 2
 
 
 class Flow(NamedTuple):
     order: tuple
     core: int
-    family: int
+    is_up: int
     layer: int
     row: int
     units: int
@@ -767,12 +776,12 @@
         ((1, 0, 2, 3), 1, 1, 0, 1),
         ((0, 1, 2, 3), 1, 0, 1, 2),
         ((1, 0, 2, 3), 1, 1, 1, 3),
-        ((2, 0, 1, 3), 0, 2, 0, 0),
-        ((2, 1, 0, 3), 0, 2, 1, 1),
+        ((2, 0, 1, 3), 0, 0, 0, 0),
+        ((2, 1, 0, 3), 0, 0, 1, 1),
     )
     return [
-        Flow(order, core, family, layer, part * rows, rows // UNIT, start, 4 * layer + place)
-        for order, core, family, part, place in kinds
+        Flow(order, core, is_up, layer, part * rows, rows // UNIT, start, 4 * layer + place)
+        for order, core, is_up, part, place in kinds
     ]
 
 
@@ -786,22 +795,22 @@
 
 def finish_kernel(
     bits, flows,
-    kept_x1, kept_y1, kept_z1, came_x1, came_y1, came_z1,
-    kept_x0, kept_y0, kept_z0, sent_x0, sent_y0, sent_z0,
-    part_ref, tokens_ref, grad_ref,
-    bias0_ref, bias1_ref, sums1_ref, gain_ref,
-    weight_out, up_out, small_out, grad_out,
-    weight_sum, up_sum, up_turned, up_came, part, part_came, tokens, grad, sums,
+    kept_weight1, kept_up1, came_weight1, came_up1,
+    kept_weight0, kept_up0, sent_weight0, sent_up0,
+    bias0_ref, bias1_ref, sums1_ref, sums0_ref,
+    weight_out, up_out, small_out,
+    weight_sum, up_sum, up_turned, up_came,
     *scratch,
 ):
     stages = bits
-    kept = ((kept_x1, kept_y1, kept_z1), (kept_x0, kept_y0, kept_z0))
-    moved = ((came_x1, came_y1, came_z1), (sent_x0, sent_y0, sent_z0))
+    kept = ((kept_weight1, kept_up1), (kept_weight0, kept_up0))
+    moved = ((came_weight1, came_up1), (sent_weight0, sent_up0))
+    small_parts = (bias0_ref, bias1_ref, sums1_ref, sums0_ref)
     places = 1 + max(flow.place for flow in flows)
     held, scratch = scratch[: places * (stages + 1)], scratch[places * (stages + 1) :]
     held = [held[f * (stages + 1) : (f + 1) * (stages + 1)] for f in range(places)]
     small, small_came = scratch[: stages + 1], scratch[stages + 1 : 2 * stages + 1]
-    load_sem, send_sem, recv_sem, credit, small_send, small_recv, job_sem, near_send, near_recv = (
+    load_sem, send_sem, recv_sem, credit, small_send, small_recv, near_send, near_recv = (
         scratch[2 * stages + 1 :]
     )
     me, core = lax.axis_index("batch"), lax.axis_index("stream")
@@ -814,46 +823,9 @@
     pl.semaphore_signal(barrier, inc=1, device_id={"stream": 1 - core}, device_id_type=MESH)
     pl.semaphore_wait(barrier, bits + 1)
 
-    exchange = pltpu.make_async_remote_copy(
-        src_ref=part_ref,
-        dst_ref=part_came,
-        send_sem=near_send.at[2],
-        recv_sem=near_recv.at[2],
-        device_id={"stream": 1 - core},
-        device_id_type=MESH,
-    )
-    loads = [
-        pltpu.make_async_copy(source, target, job_sem.at[index])
-        for index, (source, target) in enumerate(
-            ((part_ref, part), (tokens_ref, tokens), (grad_ref, grad))
-        )
-    ]
-    store = pltpu.make_async_copy(part, grad_out, job_sem.at[len(loads)])
-    exchange.start()
-    for copy in loads:
-        copy.start()
-    jobs = part.shape[0] // JOB
-    norm_start = 3
-    small_start = norm_start + jobs
-    turn_start = max(flow.start + flow.units for flow in flows if flow.layer == 0) + stages + 1
-
-    def norm_job(index):
-        rows = pl.ds(pl.multiple_of((index - norm_start) * JOB, JOB), JOB)
-
-        @pl.when(index == norm_start)
-        def _():
-            exchange.wait()
-            for copy in loads:
-                copy.wait()
-            sums[...] = jnp.zeros_like(sums)
-
-        part[rows] = norm_gradient(
-            tokens[rows].astype(F32),
-            part[rows] + part_came[rows],
-            grad[rows].astype(F32),
-            gain_ref[...].astype(F32),
-            sums,
-        )
+    small_start = 2
+    turn_start = max(flow.start + flow.units for flow in flows if flow.layer == 1)
+    turn_start += LAG * stages + 1
 
     def near_copy(layer):
         return pltpu.make_async_remote_copy(
@@ -886,12 +858,10 @@
 
     def small_step(stage):
         if stage == 0:
-            store.start()
-            rows = bias0_ref.shape[0]
-            small[0][0:rows] = bias0_ref[...]
-            small[0][rows : 2 * rows] = bias1_ref[...]
-            small[0][2 * rows : 2 * rows + 8] = sums1_ref[...]
-            small[0][2 * rows + 8 : 2 * rows + 16] = sums[...]
+            row = 0
+            for part in small_parts:
+                small[0][row : row + part.shape[0]] = part[...]
+                row += part.shape[0]
         else:
             small_copy(stage - 1).wait()
             small[stage][...] = small[stage - 1][...] + small_came[stage - 1][...]
@@ -953,8 +923,8 @@
         slot = lax.rem(unit, SLOTS)
         at = (slice(None),) * (bits - 1)
         at += (pl.ds(pl.multiple_of(flow.row + unit * UNIT, UNIT), UNIT),)
-        load(flow, slot, kept[flow.layer][flow.family].at[at]).start()
-        source = moved[flow.layer][flow.family].at[at]
+        load(flow, slot, kept[flow.layer][flow.is_up].at[at]).start()
+        source = moved[flow.layer][flow.is_up].at[at]
         if flow.layer == 0:
             load_came(flow, slot, source).start()
         else:
@@ -980,7 +950,7 @@
             take_credit(flow, stage, unit)
             remote(flow, stage, slot, sent_from(flow, stage, slot)).start()
         else:
-            target = up_sum if flow.family == 1 else weight_sum
+            target = up_sum if flow.is_up else weight_sum
             at = pl.ds(pl.multiple_of(flow.row + unit * UNIT, UNIT), UNIT)
             target[flow.layer, at] = value
         if stage > 1 or not begun:
@@ -1001,17 +971,14 @@
             for stage in range(1, stages + 1):
                 unit = index - flow.start - LAG * stage
                 pl.when(within(flow, unit))(functools.partial(advance, flow, stage, unit))
-        pl.when((index >= norm_start) & (index < norm_start + jobs))(
-            functools.partial(norm_job, index)
-        )
         for stage in range(stages + 1):
             pl.when(index == small_start + 2 * stage)(functools.partial(small_step, stage))
-        pl.when(index == turn_start)(functools.partial(turn_weights, 0))
+        pl.when(index == turn_start)(functools.partial(turn_weights, 1))
         return carry
 
     last = max(flow.start + flow.units for flow in flows)
     lax.fori_loop(0, last + LAG * stages, step, 0)
-    turn_weights(1)
+    turn_weights(0)
     for layer in range(len(moved)):
 
         @pl.when(core == 0)
@@ -1023,27 +990,19 @@
         def _():
             near_copy(layer).wait_send()
 
-    store.wait()
-
-
-def finish(last, first, came, part, tokens, grad, biases, sums, gain):
-    length, width = tokens.shape
+
+def finish(last, first, came, smalls):
+    width = last[0].shape[1]
     bits = 4
     split = (2,) * (bits - 1)
-    flows = flows_of(width, 0, 0)
-    flows += flows_of(width, 1, max(flow.start + flow.units for flow in flows))
-    small = (2 * biases[0].shape[0] + 16, width)
-    full = (length, width)
+    flows = flows_of(width, 1, 0)
+    flows += flows_of(width, 0, max(flow.start + flow.units for flow in flows))
+    small = (sum(part.shape[0] for part in smalls), width)
     scratch = [
         pltpu.VMEM((2, width, WIDE), F32),
         pltpu.VMEM((2, width, WIDE), F32),
         pltpu.VMEM((2, WIDE // 2, width), F32),
         pltpu.VMEM((2, WIDE // 2, width), F32),
-        pltpu.VMEM(full, F32),
-        pltpu.VMEM(full, F32),
-        pltpu.VMEM(full, BF16),
-        pltpu.VMEM(full, BF16),
-        pltpu.VMEM((8, width), F32),
     ]
     places = 1 + max(flow.place for flow in flows)
     for _ in range(places):
@@ -1058,43 +1017,40 @@
         pltpu.SemaphoreType.REGULAR((places, bits)),
         pltpu.SemaphoreType.DMA((bits,)),
         pltpu.SemaphoreType.DMA((bits,)),
-        pltpu.SemaphoreType.DMA((4,)),
-        pltpu.SemaphoreType.DMA((3,)),
-        pltpu.SemaphoreType.DMA((3,)),
+        pltpu.SemaphoreType.DMA((2,)),
+        pltpu.SemaphoreType.DMA((2,)),
     ]
-    large = [last[1], last[3], last[5], *came, first[1], first[3], first[5]]
-    large += [first[0], first[2], first[4]]
-    large = [array.reshape(split + array.shape[2:]) for array in large]
+    large = [last[1], last[3], *came, first[1], first[3], first[0], first[2]]
+    large = [array.reshape(split + array.shape[1:]) for array in large]
     return pl.pallas_call(
         functools.partial(finish_kernel, bits, flows),
-        in_specs=[pl.BlockSpec(memory_space=pltpu.HBM)] * (len(large) + 3)
-        + [pl.BlockSpec(memory_space=pltpu.VMEM)] * 4,
-        out_specs=[pl.BlockSpec(memory_space=pltpu.VMEM)] * 3
-        + [pl.BlockSpec(memory_space=pltpu.HBM)],
+        in_specs=[pl.BlockSpec(memory_space=pltpu.HBM)] * len(large)
+        + [pl.BlockSpec(memory_space=pltpu.VMEM)] * len(smalls),
+        out_specs=[pl.BlockSpec(memory_space=pltpu.VMEM)] * 3,
         out_shape=[
             jax.ShapeDtypeStruct((2, WIDE, width), F32),
             jax.ShapeDtypeStruct((2, WIDE // 2, width), F32),
             jax.ShapeDtypeStruct(small, F32),
-            jax.ShapeDtypeStruct(full, F32),
         ],
         scratch_shapes=scratch,
         compiler_params=pltpu.CompilerParams(
             collective_id=0, has_side_effects=True, vmem_limit_bytes=VMEM_LIMIT
         ),
         name="finish",
-    )(*large, part, tokens, grad, biases[0], biases[1], sums, gain)
+    )(*large, *smalls)
 
 
 def send_first(halves):
     count = lax.axis_size("batch")
-    received = []
-    for bit, part in enumerate(halves[0::2]):
-        stream = 0 if bit == 2 else 1
-        pairs = [
-            (2 * source + stream, 2 * flip(source, bit) + stream) for source in range(count)
-        ]
-        received.append(lax.ppermute(part, ("batch", "stream"), pairs))
-    return received
+
+    def pairs(stream, bit):
+        return [(2 * source + stream, 2 * flip(source, bit) + stream) for source in range(count)]
+
+    axes = ("batch", "stream")
+    return [
+        lax.ppermute(halves[0], axes, pairs(0, 2) + pairs(1, 0)),
+        lax.ppermute(halves[2], axes, pairs(1, 1)),
+    ]
 
 
 def shards(
@@ -1104,7 +1060,7 @@
     is_attention = lax.axis_index("stream") == 0
     length, width = tokens.shape
     rotary = tuple(jnp.asarray(table) for table in rotary_rows(length))
-    biases = branch_bias[0].astype(F32)
+    biases = branch_bias[0].astype(F32).reshape(-1, 1, width)
     tables = lax.cond(
         is_attention,
         lambda: tuple(feature_tables(freq_seeds)),
@@ -1117,20 +1073,17 @@
     swap = [(0, 1), (1, 0)]
 
     def attention(layer, stream):
-        gain, offset = norm_gain[layer : layer + 1], norm_bias[layer : layer + 1]
         return tuple(
             attention_forward(
-                layer, stream, doc_starts, gain, offset, branch_weight, biases[layer], tables,
+                layer, stream, doc_starts, norm_gain, norm_bias, branch_weight, biases, tables,
                 rotary,
             )
         )
 
     def feed_forward(layer, stream):
-        gain, offset = norm_gain[layer : layer + 1], norm_bias[layer : layer + 1]
         return tuple(
             mlp_forward(
-                layer, stream, gain, offset, up_weight, biases[layer], branch_weight,
-                down_bias[layer : layer + 1],
+                layer, stream, norm_gain, norm_bias, up_weight, biases, branch_weight, down_bias
             )
         )
 
@@ -1154,41 +1107,39 @@
 
     def attention_back(layer, grad, stream):
         h, state, mixed = kept[layer]
-        return attention_backward(
+        *result, part, a, b, c, d, bias = attention_backward(
             layer, place, doc_starts, grad, h, state, mixed, tables, rotary, branch_weight, stream
         )
+        return *result, *flat_halves(part, a, b, c, d, bias)
 
     def feed_forward_back(layer, grad, stream):
         h, act, slope = kept[layer]
-        return mlp_backward(
+        *result, part, a, b, c, d, bias = mlp_backward(
             layer, place, grad, h, act, slope, branch_weight, up_weight, stream
         )
+        return *result, *flat_halves(part, a, b, c, d, bias)
 
     def back(layer, grad, stream=()):
-        *result, part, a, b, c, d, e, f, bias = lax.cond(
+        *result, part, a, b, c, d, bias = lax.cond(
             is_attention,
             functools.partial(attention_back, layer, grad, stream),
             functools.partial(feed_forward_back, layer, grad, stream),
         )
-        return *result, part, (a, b, c, d, e, f), bias
+        return *result, part, (a, b, c, d), bias
 
     def norm_back(layer, part, grad, kind):
         other = lax.ppermute(part, "stream", swap)
-        return norm_backward(
-            inputs[layer], part, other, grad, norm_gain[layer : layer + 1], kind
-        )
+        return norm_backward(layer, inputs[layer], part, other, grad, norm_gain, kind)
 
     part1, halves1, bias1 = back(1, cotangent)
     if blocked:
         came = send_first(halves1)
     grad0, sums1 = norm_back(1, part1, cotangent, BF16)
     result, part0, halves0, bias0 = back(0, grad0, stream)
+    input_grad, sums0 = norm_back(0, part0, grad0, F32)
     if blocked:
-        weight, up, small, input_grad = finish(
-            halves1, halves0, came, part0, tokens, grad0, (bias0, bias1), sums1, norm_gain[:1]
-        )
+        weight, up, small = finish(halves1, halves0, came, (bias0, bias1, sums1, sums0))
     else:
-        input_grad, sums0 = norm_back(0, part0, grad0, F32)
         weight, up = scatter_rows((halves0, halves1))
         small = lax.psum(jnp.concatenate([bias0, bias1, sums1, sums0]), "batch")
     index, rows = lax.axis_index("batch"), bias0.shape[0]
@@ -1210,15 +1161,17 @@
 
 def scatter_rows(layers):
     weights, ups = [], []
-    for along_x, kept_x, along_y, kept_y, along_z, kept_z in layers:
-        blocks = (-1,) + kept_x.shape[2:]
+    for sent, kept, sent_up, kept_up in layers:
+        blocks = (-1,) + kept.shape[1:]
+        wide, far = (4, 2) + kept.shape[1:], (2, 4) + kept.shape[1:]
         weight = jnp.where(
             lax.axis_index("stream") == 1,
-            jnp.stack([kept_x, along_x], axis=2).reshape(blocks),
-            jnp.stack([kept_z, along_z], axis=1).reshape(blocks),
+            jnp.stack([kept.reshape(wide), sent.reshape(wide)], axis=2).reshape(blocks),
+            jnp.stack([kept.reshape(far), sent.reshape(far)], axis=1).reshape(blocks),
         )
         weight = rows_of(weight)
-        up = rows_of(jnp.stack([kept_y, along_y], axis=1).reshape(blocks))
+        up = jnp.stack([kept_up.reshape(wide), sent_up.reshape(wide)], axis=1)
+        up = rows_of(up.reshape(blocks))
         up = jnp.where(lax.axis_index("stream") == 1, up, 0.0)
         weights.append(lax.psum_scatter(weight, "batch", scatter_dimension=0, tiled=True))
         ups.append(lax.psum_scatter(up, ("batch", "stream"), scatter_dimension=0, tiled=True))

time: 560 us -> 534 us (0.954)
  waiting for transfers between devices: 28 us -> 17.8 us
  local copies, waits for them, and re-layouts: 17.1 us -> 10.5 us
  starting transfers between devices: 13.4 us -> 7.64 us
    ppermute x3 -> x2, waiting for transfers between devices: 14.2 us -> 2.95 us  [the longest x1 2.94 us: send_first(): lax.ppermute(halves[0], axes, pairs(0, 2) + pairs(1, 0))]
    pallas_call x1, Pallas kernels: 290 us -> 280 us  [finish(): pl.pallas_call(functools.partial(finish_kernel, bits, flows), in_specs=[p...]
    pallas_call x3 -> x4, Pallas kernels: 75.8 us -> 83.2 us  [the longest x2 67.7 us: attention_forward(): pl.pallas_call(functools.partial(attention_forward_kernel, layer, len(str...]
    ppermute x3 -> x2, starting transfers between devices: 12.8 us -> 6.93 us  [the longest x1 3.91 us: send_first(): lax.ppermute(halves[2], axes, pairs(1, 1))]
  transfers between devices with their start and end apart: 6 -> 6, of which waited for: 3 -> 4; matrix products, arithmetic and copies ran while one was open for 0% -> 0% of each run, Pallas kernels for 13% -> 15%
where the time goes in v7:
time: 534 us; the launch traced here: 528 us
  Pallas kernels  490 us (92%)
  waiting for transfers between devices  17.8 us (3%)
  local copies, waits for them, and re-layouts  10.5 us (2%)
  starting transfers between devices  7.64 us (1%)
    pallas_call x1, Pallas kernels, finish(): pl.pallas_call(functools.partial(finish_kernel, bits, flows), in_specs=[p...  280 us
    pallas_call x2, Pallas kernels, attention_backward(): pl.pallas_call(functools.partial(attention_backward_kernel, len(stream)),...  121 us
    pallas_call x2, Pallas kernels, attention_forward(): pl.pallas_call(functools.partial(attention_forward_kernel, layer, len(str...  67.7 us
    pallas_call x2, Pallas kernels, norm_backward(): pl.pallas_call(functools.partial(norm_backward_kernel, layer), grid=(leng...  15.5 us
  transfers between devices with their start and end apart: 6, of which 4 were waited for; matrix products, arithmetic and copies ran while one was open for 0% of the time, Pallas kernels for 15%

profile of v7, /device:TPU:0, one launch (start us, length us, event | category | flops | bytes accessed | tf_op | source)
XLA Modules:
  0.0 528.1 jit_solution(11674016928091417746)
XLA Ops:
  0.6 0.8 reshape.122
  1.4 5.1 conditional.5
  1.4 5.1 feature_tables.1
  6.5 1.0 copy-done.3
  7.5 32.5 %conditional.6 = ((f32[1024,1024]{1,0:T(8,128)}, bf16[1024,1024]{1,0:T(8,128)(2,1)}, bf16[4,1024,1024]{2,1,0:T(8,128)(2,1)}, bf16[4,1024,1024]{2,1,0:T(8,128)(2,1)})) conditional(s32[]{:T(128)} %convert_element_type.20, (bf16[1024,1024]{1,0:T(8,128)(2,1)}, bf16[2,1024]{1,0:T(2,128)(2,1)}, bf16[2,1024]{1,0:T(2,128)(2,1)}, ...), branch_computations={%region_2.0_spmd, %region_3.0_spmd} | conditional | bytes 8 | solution.py:1093
  7.7 32.3 %attention_forward.2 = (f32[1024,1024]{1,0:T(8,128)}, bf16[1024,1024]{1,0:T(8,128)(2,1)}, bf16[4,1024,1024]{2,1,0:T(8,128)(2,1)}, bf16[4,1024,1024]{2,1,0:T(8,128)(2,1)}) custom-call(bf16[1024,1024]{1,0:T(8,128)(2,1)} %get-tuple-element.184.refs_0_, s32[1,4]{1,0:T(1,128)} %get-tuple-element.185.refs_1_, bf16[2,1024]{1,0:T(2,128)(2,1)} %get-tuple-element.186.refs_2_, ...), custom_call_target="tpu_custom_call" | custom-call | tf_op jit(solution)/shard_map/cond/branch_1_fun/attention_forward/pallas_call | solution.py:496
  40.2 7.4 %collective-permute-done = f32[1024,1024]{1,0:T(8,128)} collective-permute-done((f32[1024,1024]{1,0:T(8,128)}, f32[1024,1024]{1,0:T(8,128)}, u32[]{:S(2)}, u32[]{:S(2)}) %collective-permute-start) | collective-permute-done | bytes 4194336 | tf_op jit(solution)/shard_map/ppermute | solution.py:1100
  47.5 35.8 %conditional.7 = ((f32[1024,1024]{1,0:T(8,128)}, f32[1024,1024]{1,0:T(8,128)}, bf16[1024,1024]{1,0:T(8,128)(2,1)}, bf16[4,1024,1024]{2,1,0:T(8,128)(2,1)}, bf16[4,1024,1024]{2,1,0:T(8,128)(2,1)})) conditional(s32[]{:T(128)} %convert_element_type.20, (bf16[1024,1024]{1,0:T(8,128)(2,1)}, f32[1024,1024]{1,0:T(8,128)}, f32[1024,1024]{1,0:T(8,128)}, ...), branch_computations={%region_4.0_spmd, %region_5.0_spmd} | conditional | bytes 8 | solution.py:1093
  47.9 35.4 %attention_forward.3 = (f32[1024,1024]{1,0:T(8,128)}, f32[1024,1024]{1,0:T(8,128)}, bf16[1024,1024]{1,0:T(8,128)(2,1)}, bf16[4,1024,1024]{2,1,0:T(8,128)(2,1)}, bf16[4,1024,1024]{2,1,0:T(8,128)(2,1)}) custom-call(bf16[1024,1024]{1,0:T(8,128)(2,1)} %get-tuple-element.204.refs_0_, f32[1024,1024]{1,0:T(8,128)} %get-tuple-element.205.refs_1_, ...), custom_call_target="tpu_custom_call" | custom-call | tf_op jit(solution)/shard_map/cond/branch_1_fun/attention_forward/pallas_call | solution.py:496
  83.4 60.3 %conditional.8 = (f32[1024,1024]{1,0:T(8,128)}, f32[8,1024,256]{2,1,0:T(8,128)}, f32[4,1024]{1,0:T(4,128)S(1)}, f32[4,2,1024,256]{3,2,1,0:T(8,128)}, f32[4,2,102...) conditional(s32[]{:T(128)} %convert_element_type.20, (s32[3]{0:T(128)S(1)}, bf16[1024,1024]{1,0:T(8,128)(2,1)S(1)}, ...), branch_computations={%region_6.7_spmd, %region_7.8_spmd} | conditional | bytes 48 | solution.py:1123
  83.6 59.7 %attention_backward.2 = (f32[1024,1024]{1,0:T(8,128)}, f32[2,4,1024,256]{3,2,1,0:T(8,128)}, f32[2,4,1024,256]{3,2,1,0:T(8,128)}, f32[4,2,1024,256]{3,2,1,0:T(8,1...) custom-call(s32[3]{0:T(128)S(1)} %get-tuple-element.230.place_ref, s32[1,4]{1,0:T(1,128)} %get-tuple-element.231.refs_0_, ...), custom_call_target="tpu_custom_call" | custom-call | tf_op jit(solution)/shard_map/cond/branch_1_fun/attention_backward/pallas_call | solution.py:669
  144.3 3.0 collective-permute-start.4
  147.3 3.9 collective-permute-start.5
  151.3 7.7 %norm_backward.2 = (bf16[1024,1024]{1,0:T(8,128)(2,1)}, f32[8,1024]{1,0:T(8,128)}) custom-call(f32[1024,1024]{1,0:T(8,128)} %get-tuple-element.327.x_ref, f32[1024,1024]{1,0:T(8,128)} %get-tuple-element.332.own_ref, f32[1024,1024]{1,0:T(8,128)} %collective-permute-done.2.other_ref, bf16[1024,1024]{1,0:T(8,128)(2,1)S(1)} %copy-done.2, ...), custom_call_target="tpu_custom_call" | custom-call | tf_op jit(solution)/shard_map/norm_backward/pallas_call | solution.py:741
  159.0 61.7 %conditional.9 = (f32[1024,1024]{1,0:T(8,128)}, f32[1024,1024]{1,0:T(8,128)}, f32[4,1024]{1,0:T(4,128)S(1)}, f32[2,2,2,1024,256]{4,3,2,1,0:T(8,128)}, f32[2,2,2,...) conditional(s32[]{:T(128)} %convert_element_type.20, ...), branch_computations={%region_8.9_spmd, %region_9.10_spmd} | conditional | bytes 56 | solution.py:1123
  159.0 61.5 %attention_backward.3 = (f32[1024,1024]{1,0:T(8,128)}, f32[1024,1024]{1,0:T(8,128)}, f32[2,4,1024,256]{3,2,1,0:T(8,128)}, f32[2,4,1024,256]{3,2,1,0:T(8,128)}, f...) custom-call(s32[3]{0:T(128)S(1)} %get-tuple-element.263.place_ref, ...), custom_call_target="tpu_custom_call" | custom-call | tf_op jit(solution)/shard_map/cond/branch_1_fun/attention_backward/pallas_call | solution.py:669
  220.8 7.5 %collective-permute-done.3.other_ref = f32[1024,1024]{1,0:T(8,128)} collective-permute-done((f32[1024,1024]{1,0:T(8,128)}, f32[1024,1024]{1,0:T(8,128)}, u32[]{:S(2)}, u32[]{:S(2)}) %collective-permute-start.3) | collective-permute-done | bytes 4194336 | tf_op jit(solution)/shard_map/ppermute | solution.py:1131
  228.3 7.8 %norm_backward.3 = (f32[1024,1024]{1,0:T(8,128)}, f32[8,1024]{1,0:T(8,128)}) custom-call(bf16[1024,1024]{1,0:T(8,128)(2,1)S(1)} %copy-done, f32[1024,1024]{1,0:T(8,128)} %get-tuple-element.338.own_ref, f32[1024,1024]{1,0:T(8,128)} %collective-permute-done.3.other_ref, bf16[1024,1024]{1,0:T(8,128)(2,1)} %get-tuple-element.333.grad_ref, ...), custom_call_target="tpu_custom_call" | custom-call | tf_op jit(solution)/shard_map/norm_backward/pallas_call | solution.py:741
  236.1 2.9 collective-permute-done.4
  239.0 280.1 %finish.1 = (f32[2,256,1024]{2,1,0:T(8,128)}, f32[2,128,1024]{2,1,0:T(8,128)}, f32[24,1024]{1,0:T(8,128)}) custom-call(f32[2,2,2,1024,256]{4,3,2,1,0:T(8,128)} %get-tuple-element.340.kept_weight1, f32[2,2,2,1024,256]{4,3,2,1,0:T(8,128)} %bitcast.48, f32[2,2,2,1024,256]{4,3,2,1,0:T(8,128)} %bitcast.20.came_weight1, f32[2,2,2,1024,256]{4,3,2,1,0:T(8,128)} %bitcast.22.came_up1, ...), custom_call_target="tpu_custom_call" | custom-call | tf_op jit(solution)/shard_map/finish/pallas_call | solution.py:1025
  519.1 0.8 slice_bitcast_fusion
  520.0 0.8 slice.15
  522.4 3.2 copy.78
  525.6 2.3 copy.79
  (26 shorter events, 2.6 us)
Async XLA Ops:
  6.5 1.0 copy-start.3
  40.0 7.6 %collective-permute-start = (f32[1024,1024]{1,0:T(8,128)}, f32[1024,1024]{1,0:T(8,128)}, u32[]{:S(2)}, u32[]{:S(2)}) collective-permute-start(f32[1024,1024]{1,0:T(8,128)} %get-tuple-element.326), channel_id=1, source_target_pairs={{0,1},{1,0},{2,3},{3,2},{4,5},{5,4},{6,7},{7,6},{8,9},{9,8},{10,11... | collective-permute-start | bytes 12582920 | tf_op jit(solution)/shard_map/ppermute | solution.py:1100
  47.5 35.8 %copy-start.2 = (bf16[1024,1024]{1,0:T(8,128)(2,1)S(1)}, bf16[1024,1024]{1,0:T(8,128)(2,1)}, u32[]{:S(2)}) copy-start(bf16[1024,1024]{1,0:T(8,128)(2,1)} %grad_ref.1) | copy-start | bytes 6291460
  83.4 67.9 %copy-start.5 = (bf16[2,1024]{1,0:T(2,128)(2,1)S(1)}, bf16[2,1024]{1,0:T(2,128)(2,1)}, u32[]{:S(2)}) copy-start(bf16[2,1024]{1,0:T(2,128)(2,1)} %gain_ref.3) | copy-start | bytes 12292
  143.7 15.3 %copy-start.1 = (f32[1024,1024]{1,0:T(8,128)S(1)}, f32[1024,1024]{1,0:T(8,128)}, u32[]{:S(2)}) copy-start(f32[1024,1024]{1,0:T(8,128)} %get-tuple-element.327.x_ref) | copy-start | bytes 12582916
  143.7 15.3 %copy-start.4 = (f32[1024,128]{1,0:T(8,128)S(1)}, f32[1024,128]{1,0:T(8,128)}, u32[]{:S(2)}) copy-start(f32[1024,128]{1,0:T(8,128)} %constant.78.clone) | copy-start | bytes 1572868
  143.7 15.3 %copy-start.6 = (s32[1,4]{1,0:T(1,128)S(1)}, s32[1,4]{1,0:T(1,128)}, u32[]{:S(2)}) copy-start(s32[1,4]{1,0:T(1,128)} %param.32) | copy-start | bytes 52
  143.7 7.6 %collective-permute-start.2 = (f32[1024,1024]{1,0:T(8,128)}, f32[1024,1024]{1,0:T(8,128)}, u32[]{:S(2)}, u32[]{:S(2)}) collective-permute-start(f32[1024,1024]{1,0:T(8,128)} %get-tuple-element.332.own_ref), channel_id=1, source_target_pairs={{0,1},{1,0},{2,3},{3,2},{4,5},{5,4},{6,7},{7,6},{8,9},{9,8},{10,11... | collective-permute-start | bytes 12582920 | tf_op jit(solution)/shard_map/ppermute | solution.py:1131
  143.8 15.2 %collective-permute-start.1 = (f32[1024,1024]{1,0:T(8,128)}, f32[1024,1024]{1,0:T(8,128)}, u32[]{:S(2)}, u32[]{:S(2)}) collective-permute-start(f32[1024,1024]{1,0:T(8,128)} %get-tuple-element.328), channel_id=1, source_target_pairs={{0,1},{1,0},{2,3},{3,2},{4,5},{5,4},{6,7},{7,6},{8,9},{9,8},{10,11... | collective-permute-start | bytes 12582920 | tf_op jit(solution)/shard_map/ppermute | solution.py:1100
  144.3 94.8 %collective-permute-start.4 = (f32[8,1024,256]{2,1,0:T(8,128)}, f32[8,1024,256]{2,1,0:T(8,128)}, u32[]{:S(2)}, u32[]{:S(2)}) collective-permute-start(f32[8,1024,256]{2,1,0:T(8,128)} %get-tuple-element.342), channel_id=1, source_target_pairs={{0,8},{2,10},{4,12},{6,14},{8,0},{10,2},{12,4},{14,6},{16,24},{18,... | collective-permute-start | bytes 25165832 | tf_op jit(solution)/shard_map/ppermute | solution.py:1051
  147.3 91.7 %collective-permute-start.5 = (f32[8,1024,256]{2,1,0:T(8,128)}, f32[8,1024,256]{2,1,0:T(8,128)}, u32[]{:S(2)}, u32[]{:S(2)}) collective-permute-start(f32[8,1024,256]{2,1,0:T(8,128)} %bitcast.52), channel_id=1, source_target_pairs={{1,5},{3,7},{5,1},{7,3},{9,13},{11,15},{13,9},{15,11},{17,21},{19,... | collective-permute-start | bytes 25165832 | tf_op jit(solution)/shard_map/ppermute | solution.py:1052
  159.0 69.3 %copy-start = (bf16[1024,1024]{1,0:T(8,128)(2,1)S(1)}, bf16[1024,1024]{1,0:T(8,128)(2,1)}, u32[]{:S(2)}) copy-start(bf16[1024,1024]{1,0:T(8,128)(2,1)} %x_ref.1) | copy-start | bytes 6291460
  220.7 7.6 %collective-permute-start.3 = (f32[1024,1024]{1,0:T(8,128)}, f32[1024,1024]{1,0:T(8,128)}, u32[]{:S(2)}, u32[]{:S(2)}) collective-permute-start(f32[1024,1024]{1,0:T(8,128)} %get-tuple-element.338.own_ref), channel_id=1, source_target_pairs={{0,1},{1,0},{2,3},{3,2},{4,5},{5,4},{6,7},{7,6},{8,9},{9,8},{10,11... | collective-permute-start | bytes 12582920 | tf_op jit(solution)/shard_map/ppermute | solution.py:1131

commit v8 on v7

--- a/solution.py
+++ b/solution.py
@@ -185,6 +185,53 @@
         h_ref[rows] = normalized(
             values, gain_ref[...].astype(F32), offset_ref[...].astype(F32)
         ).astype(BF16)
+
+
+JOB = 128
+
+
+def start_last_layer(stream, x_hbm, buffers, loads, stores, h_ref, gain_ref, offset_ref):
+    gain, offset = gain_ref[...].astype(F32), offset_ref[...].astype(F32)
+    jobs = h_ref.shape[0] // JOB
+
+    def rows_at(index):
+        return pl.ds(pl.multiple_of(index * JOB, JOB), JOB)
+
+    def load(part, index):
+        rows = rows_at(index)
+        return pltpu.make_async_copy(
+            stream[part].at[rows], buffers[part].at[rows], loads.at[part, index]
+        )
+
+    def store(index):
+        rows = rows_at(index)
+        return pltpu.make_async_copy(buffers[1].at[rows], x_hbm.at[rows], stores.at[index])
+
+    @pl.loop(0, jobs)
+    def _(index):
+        for part in range(len(stream)):
+            load(part, index).start()
+
+    @pl.loop(0, jobs)
+    def _(index):
+        rows = rows_at(index)
+        for part in range(len(stream)):
+            load(part, index).wait()
+        values = buffers[0][rows].astype(F32) + (buffers[1][rows] + buffers[2][rows])
+        buffers[1][rows] = values
+        store(index).start()
+        h_ref[rows] = normalized(values, gain, offset).astype(BF16)
+
+    @pl.loop(0, jobs)
+    def _(index):
+        store(index).wait()
+
+
+def chunk_semaphores(length):
+    return [
+        pltpu.SemaphoreType.DMA((3, length // JOB)),
+        pltpu.SemaphoreType.DMA((length // JOB,)),
+    ]
 
 
 def gelu_parts(units):
@@ -297,6 +344,12 @@
         part_ref[rows] += dot_nn(grad_unit, up_ref[0])
     bias_ref[pl.ds(step, 1)] = bias
 
+    mlp_weights(
+        place_ref, grad_t, h_t, act_ref.at[0], units, along_x, kept_x, along_y, kept_y
+    )
+
+
+def mlp_weights(place_ref, grad_t, h_t, act, units, along_x, kept_x, along_y, kept_y):
     def block(y, x):
         return pl.ds(pl.multiple_of((2 * y + x) * WIDE, WIDE), WIDE)
 
@@ -305,9 +358,86 @@
         rows = slice(first, first + ROWS)
         for side in range(2):
             for target, x in ((along_x, 1 - near_x), (kept_x, near_x)):
-                target[0, side, rows] = dot_nn(grad_t[rows], act_ref[0, :, block(side, x)])
+                target[0, side, rows] = dot_nn(grad_t[rows], act[:, block(side, x)])
             for target, y in ((along_y, 1 - near_y), (kept_y, near_y)):
                 target[0, side, rows] = dot_nn(h_t[rows], units[:, block(y, side)])
+
+
+def mlp_last_kernel(layer, place_ref, *refs):
+    stream, refs = refs[:3], refs[3:]
+    gain_ref, offset_ref, up_ref, bias_ref, down_ref, down_bias_ref, grad_ref = refs[:7]
+    gain_ref, offset_ref, down_bias_ref = [
+        ref.at[layer : layer + 1] for ref in (gain_ref, offset_ref, down_bias_ref)
+    ]
+    x_hbm, part_ref, grad_part, along_x, kept_x, along_y, kept_y, bias_out = refs[7:15]
+    h_ref, grad_t, h_t, act, units, loads, stores = refs[15:]
+    step = pl.program_id(0)
+
+    @pl.when(step == 0)
+    def _():
+        buffers = (act, part_ref, grad_part)
+        start_last_layer(stream, x_hbm, buffers, loads, stores, h_ref, gain_ref, offset_ref)
+        part_ref[...] = jnp.broadcast_to(down_bias_ref[...].astype(F32), part_ref.shape)
+        grad_part[...] = jnp.zeros_like(grad_part)
+        grad_t[...] = grad_ref[...].T
+        h_t[...] = h_ref[...].T
+
+    bias = jnp.zeros((1, FF_BLOCK), F32)
+    for first in range(0, h_ref.shape[0], ROWS):
+        rows = slice(first, first + ROWS)
+        hidden = dot_nt(h_ref[rows], up_ref[0]) + bias_ref[0]
+        below, density = gelu_parts(hidden)
+        active = (hidden * below).astype(BF16)
+        act[rows] = active
+        part_ref[rows] += dot_nn(active, down_ref[0, 0])
+        grad_act = dot_nt(grad_ref[rows], down_ref[0, 0])
+        grad_unit = (grad_act * (below + hidden * density)).astype(BF16)
+        bias += jnp.sum(grad_unit.astype(F32), axis=0, keepdims=True)
+        units[rows] = grad_unit
+        grad_part[rows] += dot_nn(grad_unit, up_ref[0])
+    bias_out[pl.ds(step, 1)] = bias
+    mlp_weights(place_ref, grad_t, h_t, act, units, along_x, kept_x, along_y, kept_y)
+
+
+def mlp_last(layer, place, stream, gain, offset, up, biases, down_weight, down_bias, grad):
+    length, width = stream[0].shape
+    blocks = up.shape[1] // FF_BLOCK
+    full = jax.ShapeDtypeStruct((length, width), F32)
+    pair = pl.BlockSpec((1, 2, width, WIDE), lambda j, *_: (j, 0, 0, 0))
+    return pl.pallas_call(
+        functools.partial(mlp_last_kernel, layer),
+        grid_spec=pltpu.PrefetchScalarGridSpec(
+            num_scalar_prefetch=1,
+            grid=(blocks,),
+            in_specs=[pl.BlockSpec(memory_space=pltpu.HBM)] * 3
+            + [
+                whole((LAYERS, width)),
+                whole((LAYERS, width)),
+                pl.BlockSpec((1, FF_BLOCK, width), lambda j, *_: (layer, j, 0)),
+                pl.BlockSpec((1, 1, FF_BLOCK), lambda j, *_: (layer * blocks + j, 0, 0)),
+                pl.BlockSpec((1, 1, FF_BLOCK, width), lambda j, *_: (0, layer, j, 0)),
+                whole((LAYERS, width)),
+                whole((length, width)),
+            ],
+            out_specs=[pl.BlockSpec(memory_space=pltpu.HBM)]
+            + [whole((length, width))] * 2
+            + [pair] * 4
+            + [whole((blocks, FF_BLOCK))],
+            scratch_shapes=[
+                pltpu.VMEM((length, width), BF16),
+                pltpu.VMEM((width, length), BF16),
+                pltpu.VMEM((width, length), BF16),
+                pltpu.VMEM((length, FF_BLOCK), BF16),
+                pltpu.VMEM((length, FF_BLOCK), BF16),
+            ]
+            + chunk_semaphores(length),
+        ),
+        out_shape=[full, full, full]
+        + halves_of(width, (4, 2, width, WIDE))
+        + [jax.ShapeDtypeStruct((blocks, FF_BLOCK), F32)],
+        compiler_params=params(),
+        name="mlp_last",
+    )(place, *stream, gain, offset, up, biases, down_weight, down_bias, grad)
 
 
 def halves_of(width, weight):
@@ -399,26 +529,11 @@
     )
 
 
-def attention_forward_kernel(layer, count, *refs):
-    stream, refs = refs[:count], refs[count:]
-    starts_ref, gain_ref, offset_ref, weight_ref, bias_ref = refs[:5]
-    gain_ref, offset_ref = [ref.at[layer : layer + 1] for ref in (gain_ref, offset_ref)]
-    kind_rows = bias_ref.shape[0] // LAYERS
-    upper_ref, lower_ref, scale_ref, cosine_ref, sine_ref = refs[5:10]
-    refs = refs[10:]
-    x_ref = None
-    if count > 1:
-        x_ref, refs = refs[0], refs[1:]
-    part_ref, h_ref, state_ref, mixed_ref, mask_ref = refs
+def attend_heads(
+    first_bias, starts_ref, weight_ref, bias_ref, upper_ref, lower_ref, scale_ref, cosine_ref,
+    sine_ref, part_ref, h_ref, state_ref, mixed_ref, mask_ref,
+):
     length = h_ref.shape[0]
-
-    @pl.when(pl.program_id(0) == 0)
-    def _():
-        start_layer(stream, x_ref, h_ref, gain_ref, offset_ref)
-        write_mask(starts_ref, mask_ref, False)
-        last = layer * kind_rows + 3
-        part_ref[...] = jnp.broadcast_to(bias_ref[last], part_ref.shape)
-
     ones = same_head_ones()
     table_up, table_low = upper_ref[0, 0], lower_ref[0, 0]
     lanes_of_step = pl.ds(pl.multiple_of(pl.program_id(0) * WIDE, WIDE), WIDE)
@@ -431,7 +546,7 @@
         rows = slice(first, first + ROWS)
         queries, keys, values = [
             dot_nt(h_ref[rows], weight_ref[0, 0, kind, 0])
-            + bias_ref[layer * kind_rows + kind, :, lanes_of_step]
+            + bias_ref[first_bias + kind, :, lanes_of_step]
             for kind in range(3)
         ]
         state_ref[0, rows] = jnp.exp(features(queries, rows)).astype(BF16)
@@ -480,6 +595,30 @@
         part_ref[rows] += dot_nn(mixed_ref[0, rows], weight_ref[0, 0, 3, 0])
 
 
+def attention_forward_kernel(layer, count, *refs):
+    stream, refs = refs[:count], refs[count:]
+    starts_ref, gain_ref, offset_ref, weight_ref, bias_ref = refs[:5]
+    gain_ref, offset_ref = [ref.at[layer : layer + 1] for ref in (gain_ref, offset_ref)]
+    first_bias = layer * (bias_ref.shape[0] // LAYERS)
+    upper_ref, lower_ref, scale_ref, cosine_ref, sine_ref = refs[5:10]
+    refs = refs[10:]
+    x_ref = None
+    if count > 1:
+        x_ref, refs = refs[0], refs[1:]
+    part_ref, h_ref, state_ref, mixed_ref, mask_ref = refs
+
+    @pl.when(pl.program_id(0) == 0)
+    def _():
+        start_layer(stream, x_ref, h_ref, gain_ref, offset_ref)
+        write_mask(starts_ref, mask_ref, False)
+        part_ref[...] = jnp.broadcast_to(bias_ref[first_bias + 3], part_ref.shape)
+
+    attend_heads(
+        first_bias, starts_ref, weight_ref, bias_ref, upper_ref, lower_ref, scale_ref, cosine_ref,
+        sine_ref, part_ref, h_ref, state_ref, mixed_ref, mask_ref,
+    )
+
+
 def kinds_of(weight):
     return weight.reshape(weight.shape[:2] + (4, QUADS, WIDE, weight.shape[3]))
 
@@ -520,24 +659,12 @@
     )
 
 
-def attention_backward_kernel(count, place_ref, *refs):
-    stream, refs = refs[:count], refs[count:]
-    starts_ref, grad_ref, h_ref, state_ref, mixed_ref, table_ref = refs[:6]
-    cosine_ref, sine_ref, weight_ref = refs[6:9]
-    result_ref, refs = (refs[9], refs[10:]) if count else (None, refs[9:])
-    part_ref, along_z, kept_z, _, _, bias_ref = refs[:6]
-    mask_ref, upright, numer_ref, feat_ref, flow = refs[6:]
+def attend_heads_back(
+    place_ref, starts_ref, grad_ref, state_ref, mixed_ref, table_ref, cosine_ref, sine_ref,
+    weight_ref, part_ref, along_z, kept_z, bias_ref, mask_ref, upright, numer_ref, feat_ref, flow,
+):
     group = pl.program_id(0)
-    length, width = h_ref.shape
-    add_stream(stream, result_ref)
-
-    @pl.when(pl.program_id(0) == 0)
-    def _():
-        write_mask(starts_ref, mask_ref, True)
-        upright[0] = h_ref[...].T
-        upright[1] = grad_ref[...].T
-        part_ref[...] = jnp.zeros_like(part_ref)
-
+    length, width = grad_ref.shape
     row, lane = row_index(WIDE, WIDE), lane_index(WIDE, WIDE)
     partner = (row // PAIR == lane // PAIR) & (row // DH != lane // DH)
     partner = jnp.where(partner, 1.0, 0.0).astype(BF16)
@@ -659,6 +786,29 @@
                 target[far, 0, rows] = dot_nn(upright[kind // 3, rows], flow[kind])
 
 
+def attention_backward_kernel(count, place_ref, *refs):
+    stream, refs = refs[:count], refs[count:]
+    starts_ref, grad_ref, h_ref, state_ref, mixed_ref, table_ref = refs[:6]
+    cosine_ref, sine_ref, weight_ref = refs[6:9]
+    result_ref, refs = (refs[9], refs[10:]) if count else (None, refs[9:])
+    part_ref, along_z, kept_z, _, _, bias_ref = refs[:6]
+    mask_ref, upright, numer_ref, feat_ref, flow = refs[6:]
+    add_stream(stream, result_ref)
+
+    @pl.when(pl.program_id(0) == 0)
+    def _():
+        write_mask(starts_ref, mask_ref, True)
+        upright[0] = h_ref[...].T
+        upright[1] = grad_ref[...].T
+        part_ref[...] = jnp.zeros_like(part_ref)
+
+    attend_heads_back(
+        place_ref, starts_ref, grad_ref, state_ref, mixed_ref, table_ref, cosine_ref, sine_ref,
+        weight_ref, part_ref, along_z, kept_z, bias_ref, mask_ref, upright, numer_ref, feat_ref,
+        flow,
+    )
+
+
 def attention_backward(
     layer, place, starts, grad, h, state, mixed, tables, rotary, weight, stream=()
 ):
@@ -703,6 +853,91 @@
         compiler_params=params(),
         name="attention_backward",
     )(place, *stream, starts, grad, h, state, mixed, tables[0], *rotary, kinds_of(weight))
+
+
+def attention_last_kernel(layer, place_ref, *refs):
+    stream, refs = refs[:3], refs[3:]
+    starts_ref, gain_ref, offset_ref, weight_ref, bias_ref = refs[:5]
+    gain_ref, offset_ref = [ref.at[layer : layer + 1] for ref in (gain_ref, offset_ref)]
+    first_bias = layer * (bias_ref.shape[0] // LAYERS)
+    upper_ref, lower_ref, scale_ref, cosine_ref, sine_ref, grad_ref = refs[5:11]
+    x_hbm, part_ref, grad_part, along_z, kept_z, _, _, bias_out = refs[11:19]
+    h_ref, state_ref, mixed_ref, mask_ref, mask_back = refs[19:24]
+    upright, numer_ref, feat_ref, flow, loads, stores = refs[24:]
+
+    @pl.when(pl.program_id(0) == 0)
+    def _():
+        buffers = (upright.at[0], part_ref, grad_part)
+        start_last_layer(stream, x_hbm, buffers, loads, stores, h_ref, gain_ref, offset_ref)
+        write_mask(starts_ref, mask_ref, False)
+        write_mask(starts_ref, mask_back, True)
+        part_ref[...] = jnp.broadcast_to(bias_ref[first_bias + 3], part_ref.shape)
+        grad_part[...] = jnp.zeros_like(grad_part)
+        upright[0] = h_ref[...].T
+        upright[1] = grad_ref[...].T
+
+    attend_heads(
+        first_bias, starts_ref, weight_ref, bias_ref, upper_ref, lower_ref, scale_ref, cosine_ref,
+        sine_ref, part_ref, h_ref, state_ref, mixed_ref, mask_ref,
+    )
+    attend_heads_back(
+        place_ref, starts_ref, grad_ref, state_ref, mixed_ref, upper_ref, cosine_ref, sine_ref,
+        weight_ref, grad_part, along_z, kept_z, bias_out, mask_back, upright, numer_ref, feat_ref,
+        flow,
+    )
+
+
+def attention_last(
+    layer, place, stream, starts, gain, offset, weight, biases, tables, rotary, grad
+):
+    length, width = stream[0].shape
+    full = jax.ShapeDtypeStruct((length, width), F32)
+    halves = pl.BlockSpec((2, 1, width, WIDE), lambda g, *_: (0, g, 0, 0))
+    return pl.pallas_call(
+        functools.partial(attention_last_kernel, layer),
+        grid_spec=pltpu.PrefetchScalarGridSpec(
+            num_scalar_prefetch=1,
+            grid=(QUADS,),
+            in_specs=[pl.BlockSpec(memory_space=pltpu.HBM)] * 3
+            + [
+                pl.BlockSpec(memory_space=pltpu.SMEM),
+                whole((LAYERS, width)),
+                whole((LAYERS, width)),
+                pl.BlockSpec((1, 1, 4, 1, WIDE, width), lambda g, *_: (0, layer, 0, g, 0, 0)),
+                whole((LAYERS * 4, 1, width)),
+                pl.BlockSpec((1, 1, WIDE, WIDE), lambda g, *_: (layer, g, 0, 0)),
+                pl.BlockSpec((1, 1, WIDE, WIDE), lambda g, *_: (layer, g, 0, 0)),
+                pl.BlockSpec((1, 1, 1, WIDE), lambda g, *_: (layer, g, 0, 0)),
+                whole((length, PAIR)),
+                whole((length, PAIR)),
+                whole((length, width)),
+            ],
+            out_specs=[pl.BlockSpec(memory_space=pltpu.HBM)]
+            + [whole((length, width))] * 2
+            + [halves, halves]
+            + [pl.BlockSpec(memory_space=pl.ANY)] * 2
+            + [pl.BlockSpec((4, WIDE), lambda g, *_: (0, g))],
+            scratch_shapes=[
+                pltpu.VMEM((length, width), BF16),
+                pltpu.VMEM((4, length, WIDE), BF16),
+                pltpu.VMEM((3, length, WIDE), BF16),
+                pltpu.VMEM((length, ROWS), BF16),
+                pltpu.VMEM((length, ROWS), BF16),
+                pltpu.VMEM((2, width, length), BF16),
+                pltpu.VMEM((2, length, WIDE), BF16),
+                pltpu.VMEM((2, length, WIDE), BF16),
+                pltpu.VMEM((4, length, WIDE), BF16),
+            ]
+            + chunk_semaphores(length),
+        ),
+        out_shape=[full, full, full]
+        + halves_of(width, (2, 4, width, WIDE))
+        + [jax.ShapeDtypeStruct((4, width), F32)],
+        compiler_params=params(),
+        name="attention_last",
+    )(
+        place, *stream, starts, gain, offset, kinds_of(weight), biases, *tables, *rotary, grad
+    )
 
 
 def norm_gradient(values, incoming, grad, gain, sums_ref):
@@ -1087,33 +1322,44 @@
             )
         )
 
-    stream = (tokens,)
-    inputs, kept = [], []
-    for layer in range(LAYERS):
-        *x, part, h, state, mixed = lax.cond(
-            is_attention,
-            functools.partial(attention, layer, stream),
-            functools.partial(feed_forward, layer, stream),
-        )
-        inputs.append(x[0] if x else tokens)
-        kept.append((h, state, mixed))
-        stream = (inputs[-1], part, lax.ppermute(part, "stream", swap))
-    result = stream[0] + (stream[1] + stream[2])
-
     count = lax.axis_size("batch")
     blocked = count == branch_weight.shape[2] // WIDE
     me = lax.axis_index("batch") if blocked else 0
     place = jnp.stack([jnp.asarray(bit_of(me, bit), jnp.int32) for bit in range(3)])
 
+    part, *kept = lax.cond(
+        is_attention,
+        functools.partial(attention, 0, (tokens,)),
+        functools.partial(feed_forward, 0, (tokens,)),
+    )
+    stream = (tokens, part, lax.ppermute(part, "stream", swap))
+
+    def attention_ends():
+        x, part, *back = attention_last(
+            1, place, stream, doc_starts, norm_gain, norm_bias, branch_weight, biases, tables,
+            rotary, cotangent,
+        )
+        return x, part, *flat_halves(*back)
+
+    def feed_forward_ends():
+        x, part, *back = mlp_last(
+            1, place, stream, norm_gain, norm_bias, up_weight, biases, branch_weight, down_bias,
+            cotangent,
+        )
+        return x, part, *flat_halves(*back)
+
+    x1, part, part1, *halves1, bias1 = lax.cond(is_attention, attention_ends, feed_forward_ends)
+    stream = (x1, part, lax.ppermute(part, "stream", swap))
+
     def attention_back(layer, grad, stream):
-        h, state, mixed = kept[layer]
+        h, state, mixed = kept
         *result, part, a, b, c, d, bias = attention_backward(
             layer, place, doc_starts, grad, h, state, mixed, tables, rotary, branch_weight, stream
         )
         return *result, *flat_halves(part, a, b, c, d, bias)
 
     def feed_forward_back(layer, grad, stream):
-        h, act, slope = kept[layer]
+        h, act, slope = kept
         *result, part, a, b, c, d, bias = mlp_backward(
             layer, place, grad, h, act, slope, branch_weight, up_weight, stream
         )
@@ -1127,16 +1373,15 @@
         )
         return *result, part, (a, b, c, d), bias
 
-    def norm_back(layer, part, grad, kind):
+    def norm_back(layer, x, part, grad, kind):
         other = lax.ppermute(part, "stream", swap)
-        return norm_backward(layer, inputs[layer], part, other, grad, norm_gain, kind)
-
-    part1, halves1, bias1 = back(1, cotangent)
+        return norm_backward(layer, x, part, other, grad, norm_gain, kind)
+
     if blocked:
         came = send_first(halves1)
-    grad0, sums1 = norm_back(1, part1, cotangent, BF16)
+    grad0, sums1 = norm_back(1, x1, part1, cotangent, BF16)
     result, part0, halves0, bias0 = back(0, grad0, stream)
-    input_grad, sums0 = norm_back(0, part0, grad0, F32)
+    input_grad, sums0 = norm_back(0, tokens, part0, grad0, F32)
     if blocked:
         weight, up, small = finish(halves1, halves0, came, (bias0, bias1, sums1, sums0))
     else:

time: 534 us -> 539 us (level)
  loops' own time: 1.36 us -> 14.7 us
  Pallas kernels: 490 us -> 481 us
    pallas_call x0 -> x1, Pallas kernels: none -> 86.9 us  [attention_last(): pl.pallas_call(functools.partial(attention_last_kernel, layer), grid_spec...]
    pallas_call x2 -> x1, Pallas kernels: 121 us -> 61.5 us  [attention_backward(): pl.pallas_call(functools.partial(attention_backward_kernel, len(stream)),...]
    pallas_call x2 -> x1, Pallas kernels: 67.7 us -> 32.5 us  [attention_forward(): pl.pallas_call(functools.partial(attention_forward_kernel, layer, len(str...]
    another operation x2, loops' own time: 0.55 us -> 14.4 us  [the longest x1 14.2 us: shards(): lax.cond(is_attention, attention_ends, feed_forward_ends)]
  transfers between devices with their start and end apart: 6 -> 6, of which waited for: 4 -> 4; matrix products, arithmetic and copies ran while one was open for 0% -> 0% of each run, Pallas kernels for 15% -> 14%
where the time goes in v8:
time: 539 us; the launch traced here: 533 us
  Pallas kernels  481 us (89%)
  waiting for transfers between devices  18.8 us (3%)
  loops' own time  14.7 us (3%)
  local copies, waits for them, and re-layouts  9.53 us (2%)
  starting transfers between devices  7.63 us (1%)
    pallas_call x1, Pallas kernels, finish(): pl.pallas_call(functools.partial(finish_kernel, bits, flows), in_specs=[p...  280 us
    pallas_call x1, Pallas kernels, attention_last(): pl.pallas_call(functools.partial(attention_last_kernel, layer), grid_spec...  86.9 us
    pallas_call x1, Pallas kernels, attention_backward(): pl.pallas_call(functools.partial(attention_backward_kernel, len(stream)),...  61.5 us
    pallas_call x1, Pallas kernels, attention_forward(): pl.pallas_call(functools.partial(attention_forward_kernel, layer, len(str...  32.5 us
    pallas_call x2, Pallas kernels, norm_backward(): pl.pallas_call(functools.partial(norm_backward_kernel, layer), grid=(leng...  14.6 us
    another operation x1, loops' own time, shards(): lax.cond(is_attention, attention_ends, feed_forward_ends)  14.2 us
  transfers between devices with their start and end apart: 6, of which 4 were waited for; matrix products, arithmetic and copies ran while one was open for 0% of the time, Pallas kernels for 14%

profile of v8, /device:TPU:0, one launch (start us, length us, event | category | flops | bytes accessed | tf_op | source)
XLA Modules:
  0.0 533.2 jit_solution(4269742968668107389)
XLA Ops:
  0.6 0.8 reshape.119
  1.4 5.9 %conditional.4 = ((bf16[2,4,256,256]{3,2,1,0:T(8,128)(2,1)S(1)}, bf16[2,4,256,256]{3,2,1,0:T(8,128)(2,1)}, f32[2,4,1,256]{3,2,1,0:T(1,128)S(1)})) conditional(s32[]{:T(128)} %convert_element_type.19, () %tuple.51, (s32[2,16,64]{2,1,0:T(8,128)}) %tuple.60), branch_computations={%region_0.0_spmd, %region_1.0_spmd.clone} | conditional | bytes 2105384 | solution.py:1299
  1.4 5.9 %feature_tables.1 = (bf16[2,4,256,256]{3,2,1,0:T(8,128)(2,1)S(1)}, bf16[2,4,256,256]{3,2,1,0:T(8,128)(2,1)}, f32[2,4,1,256]{3,2,1,0:T(1,128)S(1)}) custom-call(s32[2,16,64]{2,1,0:T(8,128)} %get-tuple-element.320.seeds_ref, f32[256,256]{1,0:T(8,128)} %constant.80.clone.2.cosine_ref), custom_call_target="tpu_custom_call" | custom-call | tf_op jit(solution)/shard_map/cond/branch_1_fun/feature_tables/pallas_call | solution.py:124
  7.3 32.7 %conditional.5 = ((f32[1024,1024]{1,0:T(8,128)}, bf16[1024,1024]{1,0:T(8,128)(2,1)}, bf16[4,1024,1024]{2,1,0:T(8,128)(2,1)}, bf16[4,1024,1024]{2,1,0:T(8,128)(2,1)})) conditional(s32[]{:T(128)} %convert_element_type.19, (bf16[1024,1024]{1,0:T(8,128)(2,1)}, bf16[2,1024]{1,0:T(2,128)(2,1)}, bf16[2,1024]{1,0:T(2,128)(2,1)}, ...), branch_computations={%region_2.3_spmd, %region_3.4_spmd} | conditional | bytes 8 | solution.py:1330
  7.5 32.5 %attention_forward.1 = (f32[1024,1024]{1,0:T(8,128)}, bf16[1024,1024]{1,0:T(8,128)(2,1)}, bf16[4,1024,1024]{2,1,0:T(8,128)(2,1)}, bf16[4,1024,1024]{2,1,0:T(8,128)(2,1)}) custom-call(bf16[1024,1024]{1,0:T(8,128)(2,1)} %get-tuple-element.160.refs_0_, s32[1,4]{1,0:T(1,128)} %get-tuple-element.161.refs_1_, bf16[2,1024]{1,0:T(2,128)(2,1)} %get-tuple-element.162.refs_2_, ...), custom_call_target="tpu_custom_call" | custom-call | tf_op jit(solution)/shard_map/cond/branch_1_fun/attention_forward/pallas_call | solution.py:635
  40.2 7.4 %collective-permute-done = f32[1024,1024]{1,0:T(8,128)} collective-permute-done((f32[1024,1024]{1,0:T(8,128)}, f32[1024,1024]{1,0:T(8,128)}, u32[]{:S(2)}, u32[]{:S(2)}) %collective-permute-start) | collective-permute-done | bytes 4194336 | tf_op jit(solution)/shard_map/ppermute | solution.py:1335
  47.6 101.1 %conditional.6 = (f32[1024,1024]{1,0:T(8,128)S(1)}, f32[1024,1024]{1,0:T(8,128)}, f32[1024,1024]{1,0:T(8,128)}, f32[8,1024,256]{2,1,0:T(8,128)}, f32[4,1024]{1,0...) conditional(s32[]{:T(128)} %convert_element_type.19, ...), branch_computations={%region_4.5_spmd, %region_5.6_spmd} | conditional | bytes 64 | solution.py:1351
  61.4 86.9 %attention_last.1 = (f32[1024,1024]{1,0:T(8,128)S(1)}, f32[1024,1024]{1,0:T(8,128)}, f32[1024,1024]{1,0:T(8,128)}, f32[2,4,1024,256]{3,2,1,0:T(8,128)}, f32[2,4,...) custom-call(s32[3]{0:T(128)S(1)} %get-tuple-element.190.place_ref, ...), custom_call_target="tpu_custom_call" | custom-call | tf_op jit(solution)/shard_map/cond/branch_1_fun/attention_last/pallas_call | solution.py:896
  148.8 0.5 collective-permute-start.1
  149.3 3.0 collective-permute-start.4
  152.3 3.9 collective-permute-start.5
  156.3 6.8 %norm_backward.2 = (bf16[1024,1024]{1,0:T(8,128)(2,1)}, f32[8,1024]{1,0:T(8,128)}) custom-call(f32[1024,1024]{1,0:T(8,128)S(1)} %get-tuple-element.291.x_ref, f32[1024,1024]{1,0:T(8,128)} %get-tuple-element.293.own_ref, f32[1024,1024]{1,0:T(8,128)} %collective-permute-done.2.other_ref, bf16[1024,1024]{1,0:T(8,128)(2,1)S(1)} %copy-done.1, ...), custom_call_target="tpu_custom_call" | custom-call | tf_op jit(solution)/shard_map/norm_backward/pallas_call | solution.py:976
  163.1 61.7 %conditional.7 = (f32[1024,1024]{1,0:T(8,128)}, f32[1024,1024]{1,0:T(8,128)}, f32[4,1024]{1,0:T(4,128)S(1)}, f32[2,2,2,1024,256]{4,3,2,1,0:T(8,128)}, f32[2,2,2,...) conditional(s32[]{:T(128)} %convert_element_type.19, ...), branch_computations={%region_6.7_spmd, %region_7.8_spmd} | conditional | bytes 56 | solution.py:1369
  163.2 61.5 %attention_backward.1 = (f32[1024,1024]{1,0:T(8,128)}, f32[1024,1024]{1,0:T(8,128)}, f32[2,4,1024,256]{3,2,1,0:T(8,128)}, f32[2,4,1024,256]{3,2,1,0:T(8,128)}, f...) custom-call(s32[3]{0:T(128)S(1)} %get-tuple-element.230.place_ref, ...), custom_call_target="tpu_custom_call" | custom-call | tf_op jit(solution)/shard_map/cond/branch_1_fun/attention_backward/pallas_call | solution.py:819
  224.9 7.5 %collective-permute-done.3.other_ref = f32[1024,1024]{1,0:T(8,128)} collective-permute-done((f32[1024,1024]{1,0:T(8,128)}, f32[1024,1024]{1,0:T(8,128)}, u32[]{:S(2)}, u32[]{:S(2)}) %collective-permute-start.3) | collective-permute-done | bytes 4194336 | tf_op jit(solution)/shard_map/ppermute | solution.py:1377
  232.4 7.8 %norm_backward.3 = (f32[1024,1024]{1,0:T(8,128)}, f32[8,1024]{1,0:T(8,128)}) custom-call(bf16[1024,1024]{1,0:T(8,128)(2,1)S(1)} %copy-done, f32[1024,1024]{1,0:T(8,128)} %get-tuple-element.299.own_ref, f32[1024,1024]{1,0:T(8,128)} %collective-permute-done.3.other_ref, bf16[1024,1024]{1,0:T(8,128)(2,1)} %get-tuple-element.294.grad_ref, ...), custom_call_target="tpu_custom_call" | custom-call | tf_op jit(solution)/shard_map/norm_backward/pallas_call | solution.py:976
  240.2 3.9 collective-permute-done.4
  244.1 280.2 %finish.1 = (f32[2,256,1024]{2,1,0:T(8,128)}, f32[2,128,1024]{2,1,0:T(8,128)}, f32[24,1024]{1,0:T(8,128)}) custom-call(f32[2,2,2,1024,256]{4,3,2,1,0:T(8,128)} %get-tuple-element.301.kept_weight1, f32[2,2,2,1024,256]{4,3,2,1,0:T(8,128)} %bitcast.38, f32[2,2,2,1024,256]{4,3,2,1,0:T(8,128)} %bitcast.19.came_weight1, f32[2,2,2,1024,256]{4,3,2,1,0:T(8,128)} %bitcast.21.came_up1, ...), custom_call_target="tpu_custom_call" | custom-call | tf_op jit(solution)/shard_map/finish/pallas_call | solution.py:1260
  524.2 0.8 slice_bitcast_fusion
  525.1 0.8 slice.15
  526.3 0.6 dynamic-slice_bitcast_fusion
  526.9 0.6 dynamic-slice_bitcast_fusion.1
  527.5 3.2 copy.72
  530.7 2.3 copy.73
  (20 shorter events, 0.8 us)
Async XLA Ops:
  7.3 40.2 %copy-start.1 = (bf16[1024,1024]{1,0:T(8,128)(2,1)S(1)}, bf16[1024,1024]{1,0:T(8,128)(2,1)}, u32[]{:S(2)}) copy-start(bf16[1024,1024]{1,0:T(8,128)(2,1)} %grad_ref.1) | copy-start | bytes 6291460
  40.0 7.6 %collective-permute-start = (f32[1024,1024]{1,0:T(8,128)}, f32[1024,1024]{1,0:T(8,128)}, u32[]{:S(2)}, u32[]{:S(2)}) collective-permute-start(f32[1024,1024]{1,0:T(8,128)} %get-tuple-element.290), channel_id=1, source_target_pairs={{0,1},{1,0},{2,3},{3,2},{4,5},{5,4},{6,7},{7,6},{8,9},{9,8},{10,11... | collective-permute-start | bytes 12582920 | tf_op jit(solution)/shard_map/ppermute | solution.py:1335
  148.7 14.4 %copy-start.2 = (f32[1024,128]{1,0:T(8,128)S(1)}, f32[1024,128]{1,0:T(8,128)}, u32[]{:S(2)}) copy-start(f32[1024,128]{1,0:T(8,128)} %constant.78.clone) | copy-start | bytes 1572868
  148.7 14.4 %copy-start.4 = (s32[1,4]{1,0:T(1,128)S(1)}, s32[1,4]{1,0:T(1,128)}, u32[]{:S(2)}) copy-start(s32[1,4]{1,0:T(1,128)} %param.30) | copy-start | bytes 52
  148.7 7.6 %collective-permute-start.2 = (f32[1024,1024]{1,0:T(8,128)}, f32[1024,1024]{1,0:T(8,128)}, u32[]{:S(2)}, u32[]{:S(2)}) collective-permute-start(f32[1024,1024]{1,0:T(8,128)} %get-tuple-element.293.own_ref), channel_id=1, source_target_pairs={{0,1},{1,0},{2,3},{3,2},{4,5},{5,4},{6,7},{7,6},{8,9},{9,8},{10,11... | collective-permute-start | bytes 12582920 | tf_op jit(solution)/shard_map/ppermute | solution.py:1377
  148.8 14.3 %collective-permute-start.1 = (f32[1024,1024]{1,0:T(8,128)}, f32[1024,1024]{1,0:T(8,128)}, u32[]{:S(2)}, u32[]{:S(2)}) collective-permute-start(f32[1024,1024]{1,0:T(8,128)} %get-tuple-element.292), channel_id=1, source_target_pairs={{0,1},{1,0},{2,3},{3,2},{4,5},{5,4},{6,7},{7,6},{8,9},{9,8},{10,11... | collective-permute-start | bytes 12582920 | tf_op jit(solution)/shard_map/ppermute | solution.py:1352
  149.3 94.8 %collective-permute-start.4 = (f32[8,1024,256]{2,1,0:T(8,128)}, f32[8,1024,256]{2,1,0:T(8,128)}, u32[]{:S(2)}, u32[]{:S(2)}) collective-permute-start(f32[8,1024,256]{2,1,0:T(8,128)} %get-tuple-element.303), channel_id=1, source_target_pairs={{0,8},{2,10},{4,12},{6,14},{8,0},{10,2},{12,4},{14,6},{16,24},{18,... | collective-permute-start | bytes 25165832 | tf_op jit(solution)/shard_map/ppermute | solution.py:1286
  152.3 91.7 %collective-permute-start.5 = (f32[8,1024,256]{2,1,0:T(8,128)}, f32[8,1024,256]{2,1,0:T(8,128)}, u32[]{:S(2)}, u32[]{:S(2)}) collective-permute-start(f32[8,1024,256]{2,1,0:T(8,128)} %bitcast.50), channel_id=1, source_target_pairs={{1,5},{3,7},{5,1},{7,3},{9,13},{11,15},{13,9},{15,11},{17,21},{19,... | collective-permute-start | bytes 25165832 | tf_op jit(solution)/shard_map/ppermute | solution.py:1287
  163.1 69.3 %copy-start = (bf16[1024,1024]{1,0:T(8,128)(2,1)S(1)}, bf16[1024,1024]{1,0:T(8,128)(2,1)}, u32[]{:S(2)}) copy-start(bf16[1024,1024]{1,0:T(8,128)(2,1)} %x_ref.1) | copy-start | bytes 6291460
  163.1 69.3 %copy-start.3 = (bf16[2,1024]{1,0:T(2,128)(2,1)S(1)}, bf16[2,1024]{1,0:T(2,128)(2,1)}, u32[]{:S(2)}) copy-start(bf16[2,1024]{1,0:T(2,128)(2,1)} %gain_ref.3) | copy-start | bytes 12292
  224.8 7.6 %collective-permute-start.3 = (f32[1024,1024]{1,0:T(8,128)}, f32[1024,1024]{1,0:T(8,128)}, u32[]{:S(2)}, u32[]{:S(2)}) collective-permute-start(f32[1024,1024]{1,0:T(8,128)} %get-tuple-element.299.own_ref), channel_id=1, source_target_pairs={{0,1},{1,0},{2,3},{3,2},{4,5},{5,4},{6,7},{7,6},{8,9},{9,8},{10,11... | collective-permute-start | bytes 12582920 | tf_op jit(solution)/shard_map/ppermute | solution.py:1377

commit v9 on v8

--- a/solution.py
+++ b/solution.py
@@ -66,7 +66,7 @@
     angles = math.pi * (samples[None, :] + 0.5) * samples[:, None] / DH
     table = np.cos(angles) * math.sqrt(2.0 / DH)
     table[0] *= math.sqrt(0.5)
-    return np.kron(np.eye(WIDE // DH), table.T * DH ** (-0.25)).astype(np.float32)
+    return (table.T * DH ** (-0.25)).astype(np.float32)
 
 
 def rotary_rows(length):
@@ -85,16 +85,14 @@
 
 
 def tables_kernel(seeds_ref, cosine_ref, upper_ref, lower_ref, weight_ref):
-    own = row_index(WIDE, DH) % DH == lane_index(WIDE, DH)
-    feature = lane_index(WIDE, PAIR) % FEAT
+    feature = lane_index(DH, WIDE) % FEAT
     same_head = row_index(WIDE, WIDE) // DH == lane_index(WIDE, WIDE) // FEAT
+    ones = jnp.where(same_head, 1.0, 0.0).astype(BF16)
+    pick = (row_index(QUADS, WIDE) == lane_index(QUADS, WIDE) // FEAT).astype(BF16)
+    cosine = cosine_ref[...]
     for group in range(QUADS):
-        heads = [
-            jnp.broadcast_to(seeds_ref[0, head : head + 1], (DH, DH))
-            for head in range(group * QUADS, (group + 1) * QUADS)
-        ]
-        seeds = jnp.where(own, jnp.concatenate(heads, axis=0), 0)
-        seeds = jnp.sum(seeds.astype(F32), axis=1, keepdims=True).astype(jnp.int32)
+        seeds = seeds_ref[0, group * QUADS : (group + 1) * QUADS].astype(F32).astype(BF16)
+        seeds = dot_tn(seeds, pick).astype(jnp.int32)
         lattice = (feature * seeds) & (FEAT - 1)
         prob = (lattice.astype(F32) + 0.5) * (1.0 / FEAT)
         radius = jnp.sqrt(-2.0 * jnp.log(jnp.minimum(prob, 1.0 - prob)))
@@ -107,16 +105,12 @@
         )
         magnitude = radius - above / below
         omega = jnp.where(prob > 0.5, magnitude, -magnitude)
-        omega = jnp.where(same_head, jnp.concatenate([omega] * (WIDE // PAIR), axis=1), 0.0)
-        project = jnp.dot(cosine_ref[...], omega, precision=HIGH, preferred_element_type=F32)
-        upper_ref[0, group], lower_ref[0, group] = split(project)
+        project = jnp.dot(cosine, omega, precision=HIGH, preferred_element_type=F32)
+        project = jnp.concatenate([project] * QUADS, axis=0)
+        upper_ref[0, group], lower_ref[0, group] = split(jnp.where(same_head, project, 0.0))
         grown = jnp.exp(-0.5 / DH * jnp.sum(omega * omega, axis=0, keepdims=True))
-        total = jnp.dot(
-            jnp.broadcast_to(grown, (8, WIDE)),
-            same_head.astype(F32),
-            precision=HIGH,
-            preferred_element_type=F32,
-        )
+        upper, rest = split(jnp.broadcast_to(grown, (8, WIDE)))
+        total = dot_nn(upper, ones) + dot_nn(rest, ones)
         weight_ref[0, group] = FEAT * grown / total[:1]
 
 
@@ -126,7 +120,7 @@
         grid=(LAYERS,),
         in_specs=[
             pl.BlockSpec((1, HEADS, DH), lambda l: (l, 0, 0)),
-            whole((WIDE, WIDE)),
+            whole((DH, DH)),
         ],
         out_specs=[
             pl.BlockSpec((1, QUADS, WIDE, WIDE), lambda l: (l, 0, 0, 0)),
@@ -354,8 +348,10 @@
         return pl.ds(pl.multiple_of((2 * y + x) * WIDE, WIDE), WIDE)
 
     near_x, near_y = place_ref[0], place_ref[1]
-    for first in range(0, h_t.shape[0], ROWS):
-        rows = slice(first, first + ROWS)
+
+    @pl.loop(0, h_t.shape[0] // ROWS)
+    def _(index):
+        rows = pl.ds(pl.multiple_of(index * ROWS, ROWS), ROWS)
         for side in range(2):
             for target, x in ((along_x, 1 - near_x), (kept_x, near_x)):
                 target[0, side, rows] = dot_nn(grad_t[rows], act[:, block(side, x)])
@@ -382,9 +378,12 @@
         grad_t[...] = grad_ref[...].T
         h_t[...] = h_ref[...].T
 
-    bias = jnp.zeros((1, FF_BLOCK), F32)
-    for first in range(0, h_ref.shape[0], ROWS):
-        rows = slice(first, first + ROWS)
+    here = pl.ds(step, 1)
+    bias_out[here] = jnp.zeros((1, FF_BLOCK), F32)
+
+    @pl.loop(0, h_ref.shape[0] // ROWS)
+    def _(index):
+        rows = pl.ds(pl.multiple_of(index * ROWS, ROWS), ROWS)
         hidden = dot_nt(h_ref[rows], up_ref[0]) + bias_ref[0]
         below, density = gelu_parts(hidden)
         active = (hidden * below).astype(BF16)
@@ -392,10 +391,9 @@
         part_ref[rows] += dot_nn(active, down_ref[0, 0])
         grad_act = dot_nt(grad_ref[rows], down_ref[0, 0])
         grad_unit = (grad_act * (below + hidden * density)).astype(BF16)
-        bias += jnp.sum(grad_unit.astype(F32), axis=0, keepdims=True)
+        bias_out[here] += jnp.sum(grad_unit.astype(F32), axis=0, keepdims=True)
         units[rows] = grad_unit
         grad_part[rows] += dot_nn(grad_unit, up_ref[0])
-    bias_out[pl.ds(step, 1)] = bias
     mlp_weights(place_ref, grad_t, h_t, act, units, along_x, kept_x, along_y, kept_y)
 
 
@@ -1033,8 +1031,8 @@
     kept_weight1, kept_up1, came_weight1, came_up1,
     kept_weight0, kept_up0, sent_weight0, sent_up0,
     bias0_ref, bias1_ref, sums1_ref, sums0_ref,
-    weight_out, up_out, small_out,
-    weight_sum, up_sum, up_turned, up_came,
+    weight_sum, up_out, small_out,
+    up_sum, up_near, up_came,
     *scratch,
 ):
     stages = bits
@@ -1064,7 +1062,7 @@
 
     def near_copy(layer):
         return pltpu.make_async_remote_copy(
-            src_ref=up_turned.at[layer],
+            src_ref=up_near.at[layer],
             dst_ref=up_came.at[layer],
             send_sem=near_send.at[layer],
             recv_sem=near_recv.at[layer],
@@ -1072,14 +1070,12 @@
             device_id_type=MESH,
         )
 
-    def turn_weights(layer):
-        weight_out[len(moved) - 1 - layer] = weight_sum[layer].T
-
+    def part_up(layer):
         @pl.when(core == 1)
         def _():
-            up_turned[layer] = up_sum[layer, :, : WIDE // 2].T
+            up_near[layer] = up_sum[layer, :, : WIDE // 2]
             near_copy(layer).start()
-            up_out[len(moved) - 1 - layer] = up_sum[layer, :, WIDE // 2 :].T
+            up_out[layer] = up_sum[layer, :, WIDE // 2 :]
 
     def small_copy(stage):
         return pltpu.make_async_remote_copy(
@@ -1208,18 +1204,18 @@
                 pl.when(within(flow, unit))(functools.partial(advance, flow, stage, unit))
         for stage in range(stages + 1):
             pl.when(index == small_start + 2 * stage)(functools.partial(small_step, stage))
-        pl.when(index == turn_start)(functools.partial(turn_weights, 1))
+        pl.when(index == turn_start)(functools.partial(part_up, 1))
         return carry
 
     last = max(flow.start + flow.units for flow in flows)
     lax.fori_loop(0, last + LAG * stages, step, 0)
-    turn_weights(0)
+    part_up(0)
     for layer in range(len(moved)):
 
         @pl.when(core == 0)
         def _():
             near_copy(layer).wait_recv()
-            up_out[len(moved) - 1 - layer] = up_came[layer]
+            up_out[layer] = up_came[layer]
 
         @pl.when(core == 1)
         def _():
@@ -1235,9 +1231,8 @@
     small = (sum(part.shape[0] for part in smalls), width)
     scratch = [
         pltpu.VMEM((2, width, WIDE), F32),
-        pltpu.VMEM((2, width, WIDE), F32),
-        pltpu.VMEM((2, WIDE // 2, width), F32),
-        pltpu.VMEM((2, WIDE // 2, width), F32),
+        pltpu.VMEM((2, width, WIDE // 2), F32),
+        pltpu.VMEM((2, width, WIDE // 2), F32),
     ]
     places = 1 + max(flow.place for flow in flows)
     for _ in range(places):
@@ -1263,8 +1258,8 @@
         + [pl.BlockSpec(memory_space=pltpu.VMEM)] * len(smalls),
         out_specs=[pl.BlockSpec(memory_space=pltpu.VMEM)] * 3,
         out_shape=[
-            jax.ShapeDtypeStruct((2, WIDE, width), F32),
-            jax.ShapeDtypeStruct((2, WIDE // 2, width), F32),
+            jax.ShapeDtypeStruct((2, width, WIDE), F32),
+            jax.ShapeDtypeStruct((2, width, WIDE // 2), F32),
             jax.ShapeDtypeStruct(small, F32),
         ],
         scratch_shapes=scratch,
@@ -1273,6 +1268,48 @@
         ),
         name="finish",
     )(*large, *smalls)
+
+
+def hand_out_kernel(
+    rows, own, index_ref, weight_ref, up_ref, small_ref,
+    weight_out, up_out, bias_out, down_out, gain_out, offset_out,
+):
+    index = index_ref[0]
+    layers = weight_ref.shape[0]
+    for layer in range(layers):
+        weight_out[layer] = weight_ref[layers - 1 - layer].T
+        up_out[layer] = up_ref[layers - 1 - layer].T
+        per_row = small_ref.shape[1] // WIDE
+        lanes = pl.ds(pl.multiple_of(lax.rem(index, per_row) * WIDE, WIDE), WIDE)
+        row = pl.ds(layer * rows + index // per_row, 1)
+        bias_out[layer : layer + 1] = small_ref[row, lanes]
+        first = 2 * rows + 8 * (layers - 1 - layer)
+        width = small_ref.shape[1]
+        sums = pltpu.roll(small_ref[first : first + 8], lax.rem(width - index * own, width), 1)
+        gain_out[layer : layer + 1] = sums[0:1, :own]
+        offset_out[layer : layer + 1] = sums[1:2, :own]
+        down_out[layer : layer + 1] = sums[2:3, :own]
+
+
+def hand_out(weight, up, small, rows, own):
+    layers, width, _ = weight.shape
+    vector = jax.ShapeDtypeStruct((layers, own), F32)
+    return pl.pallas_call(
+        functools.partial(hand_out_kernel, rows, own),
+        in_specs=[pl.BlockSpec(memory_space=pltpu.SMEM)]
+        + [pl.BlockSpec(memory_space=pltpu.VMEM)] * 3,
+        out_specs=[pl.BlockSpec(memory_space=pltpu.VMEM)] * 6,
+        out_shape=[
+            jax.ShapeDtypeStruct((layers, WIDE, width), F32),
+            jax.ShapeDtypeStruct((layers, WIDE // 2, width), F32),
+            jax.ShapeDtypeStruct((layers, WIDE), F32),
+            vector,
+            vector,
+            vector,
+        ],
+        compiler_params=params(),
+        name="hand_out",
+    )(lax.axis_index("batch").astype(jnp.int32).reshape(1), weight, up, small)
 
 
 def send_first(halves):
@@ -1348,7 +1385,9 @@
         )
         return x, part, *flat_halves(*back)
 
-    x1, part, part1, *halves1, bias1 = lax.cond(is_attention, attention_ends, feed_forward_ends)
+    x1, part, part1, *halves1, bias1 = lax.cond(
+        jnp.logical_not(is_attention), feed_forward_ends, attention_ends
+    )
     stream = (x1, part, lax.ppermute(part, "stream", swap))
 
     def attention_back(layer, grad, stream):
@@ -1389,19 +1428,16 @@
         small = lax.psum(jnp.concatenate([bias0, bias1, sums1, sums0]), "batch")
     index, rows = lax.axis_index("batch"), bias0.shape[0]
     each, own = branch_weight.shape[2] // count, width // count
-    biases = small[: 2 * rows].reshape(LAYERS, -1)
-    sums = small[2 * rows :].reshape(LAYERS, 8, width)[::-1]
-    sums = lax.dynamic_slice_in_dim(sums, index * own, own, axis=2)
-    return (
-        result,
-        input_grad,
-        weight[None],
-        lax.dynamic_slice_in_dim(biases, index * each, each, axis=1)[None],
-        up,
-        sums[:, 2],
-        sums[:, 0],
-        sums[:, 1],
-    )
+    if blocked:
+        weight, up, bias, down, gain, offset = hand_out(weight, up, small, rows, own)
+    else:
+        bias = lax.dynamic_slice_in_dim(
+            small[: 2 * rows].reshape(LAYERS, -1), index * each, each, axis=1
+        )
+        sums = small[2 * rows :].reshape(LAYERS, 8, width)[::-1]
+        sums = lax.dynamic_slice_in_dim(sums, index * own, own, axis=2)
+        down, gain, offset = sums[:, 2], sums[:, 0], sums[:, 1]
+    return result, input_grad, weight[None], bias[None], up, down, gain, offset
 
 
 def scatter_rows(layers):

time: 539 us -> 523 us (0.970)
  loops' own time: 14.7 us -> 5.99 us
  local copies, waits for them, and re-layouts: 9.53 us -> 2.75 us
    another operation x1, loops' own time: 14.2 us -> 5.27 us  [shards(): lax.cond(jnp.logical_not(is_attention), feed_forward_ends, attention_ends)]
  transfers between devices with their start and end apart: 6 -> 6, of which waited for: 4 -> 4; matrix products, arithmetic and copies ran while one was open for 0% -> 0% of each run, Pallas kernels for 14% -> 15%
where the time goes in v9:
time: 523 us; the launch traced here: 518 us
  Pallas kernels  484 us (93%)
  waiting for transfers between devices  16.7 us (3%)
  starting transfers between devices  7.63 us (1%)
  loops' own time  5.99 us (1%)
    pallas_call x1, Pallas kernels, finish(): pl.pallas_call(functools.partial(finish_kernel, bits, flows), in_specs=[p...  280 us
    pallas_call x1, Pallas kernels, attention_last(): pl.pallas_call(functools.partial(attention_last_kernel, layer), grid_spec...  86.9 us
    pallas_call x1, Pallas kernels, attention_backward(): pl.pallas_call(functools.partial(attention_backward_kernel, len(stream)),...  61.3 us
    pallas_call x1, Pallas kernels, attention_forward(): pl.pallas_call(functools.partial(attention_forward_kernel, layer, len(str...  32.5 us
    pallas_call x2, Pallas kernels, norm_backward(): pl.pallas_call(functools.partial(norm_backward_kernel, layer), grid=(leng...  14.6 us
  transfers between devices with their start and end apart: 6, of which 4 were waited for; matrix products, arithmetic and copies ran while one was open for 0% of the time, Pallas kernels for 15%

profile of v9, /device:TPU:0, one launch (start us, length us, event | category | flops | bytes accessed | tf_op | source)
XLA Modules:
  0.0 518.1 jit_solution(12789397582297406807)
XLA Ops:
  0.6 0.8 reshape.115
  1.4 4.5 conditional.4
  1.4 4.5 feature_tables.1
  5.9 32.7 %conditional.5 = ((f32[1024,1024]{1,0:T(8,128)}, bf16[1024,1024]{1,0:T(8,128)(2,1)}, bf16[4,1024,1024]{2,1,0:T(8,128)(2,1)}, bf16[4,1024,1024]{2,1,0:T(8,128)(2,1)})) conditional(s32[]{:T(128)} %convert_element_type.21, (bf16[1024,1024]{1,0:T(8,128)(2,1)}, bf16[2,1024]{1,0:T(2,128)(2,1)}, bf16[2,1024]{1,0:T(2,128)(2,1)}, ...), branch_computations={%region_2.3_spmd, %region_3.4_spmd} | conditional | bytes 8 | solution.py:1367
  6.2 32.5 %attention_forward.1 = (f32[1024,1024]{1,0:T(8,128)}, bf16[1024,1024]{1,0:T(8,128)(2,1)}, bf16[4,1024,1024]{2,1,0:T(8,128)(2,1)}, bf16[4,1024,1024]{2,1,0:T(8,128)(2,1)}) custom-call(bf16[1024,1024]{1,0:T(8,128)(2,1)} %get-tuple-element.160.refs_0_, s32[1,4]{1,0:T(1,128)} %get-tuple-element.161.refs_1_, bf16[2,1024]{1,0:T(2,128)(2,1)} %get-tuple-element.162.refs_2_, ...), custom_call_target="tpu_custom_call" | custom-call | tf_op jit(solution)/shard_map/cond/branch_1_fun/attention_forward/pallas_call | solution.py:633
  38.7 0.1 collective-permute-start
  38.8 0.1 pad_add_fusion
  38.9 7.3 %collective-permute-done = f32[1024,1024]{1,0:T(8,128)} collective-permute-done((f32[1024,1024]{1,0:T(8,128)}, f32[1024,1024]{1,0:T(8,128)}, u32[]{:S(2)}, u32[]{:S(2)}) %collective-permute-start) | collective-permute-done | bytes 4194336 | tf_op jit(solution)/shard_map/ppermute | solution.py:1372
  46.2 92.1 %conditional.6 = (f32[1024,1024]{1,0:T(8,128)S(1)}, f32[1024,1024]{1,0:T(8,128)}, f32[1024,1024]{1,0:T(8,128)}, f32[8,1024,256]{2,1,0:T(8,128)}, f32[4,1024]{1,0...) conditional(s32[]{:T(128)} %convert_element_type.22, ...), branch_computations={%region_4.5_spmd, %region_5.6_spmd} | conditional | bytes 64 | solution.py:1388
  46.2 86.9 %attention_last.1 = (f32[1024,1024]{1,0:T(8,128)S(1)}, f32[1024,1024]{1,0:T(8,128)}, f32[1024,1024]{1,0:T(8,128)}, f32[2,4,1024,256]{3,2,1,0:T(8,128)}, f32[2,4,...) custom-call(s32[3]{0:T(128)S(1)} %get-tuple-element.171.place_ref, ...), custom_call_target="tpu_custom_call" | custom-call | tf_op jit(solution)/shard_map/cond/branch_0_fun/attention_last/pallas_call | solution.py:894
  138.4 0.1 collective-permute-start.2
  138.5 0.5 collective-permute-start.1
  139.0 3.0 collective-permute-start.4
  142.0 3.9 collective-permute-start.5
  145.9 0.1 collective-permute-done.2.other_ref
  146.0 6.8 %norm_backward.2 = (bf16[1024,1024]{1,0:T(8,128)(2,1)}, f32[8,1024]{1,0:T(8,128)}) custom-call(f32[1024,1024]{1,0:T(8,128)S(1)} %get-tuple-element.297.x_ref, f32[1024,1024]{1,0:T(8,128)} %get-tuple-element.299.own_ref, f32[1024,1024]{1,0:T(8,128)} %collective-permute-done.2.other_ref, bf16[1024,1024]{1,0:T(8,128)(2,1)S(1)} %copy-done.1, ...), custom_call_target="tpu_custom_call" | custom-call | tf_op jit(solution)/shard_map/norm_backward/pallas_call | solution.py:974
  152.8 61.8 %conditional.7 = (f32[1024,1024]{1,0:T(8,128)}, f32[1024,1024]{1,0:T(8,128)}, f32[4,1024]{1,0:T(4,128)S(1)}, f32[2,2,2,1024,256]{4,3,2,1,0:T(8,128)}, f32[2,2,2,...) conditional(s32[]{:T(128)} %convert_element_type.21, ...), branch_computations={%region_6.7_spmd, %region_7.8_spmd} | conditional | bytes 56 | solution.py:1408
  153.1 61.3 %attention_backward.1 = (f32[1024,1024]{1,0:T(8,128)}, f32[1024,1024]{1,0:T(8,128)}, f32[2,4,1024,256]{3,2,1,0:T(8,128)}, f32[2,4,1024,256]{3,2,1,0:T(8,128)}, f...) custom-call(s32[3]{0:T(128)S(1)} %get-tuple-element.230.place_ref, ...), custom_call_target="tpu_custom_call" | custom-call | tf_op jit(solution)/shard_map/cond/branch_1_fun/attention_backward/pallas_call | solution.py:817
  214.7 7.4 %collective-permute-done.3.other_ref = f32[1024,1024]{1,0:T(8,128)S(1)} collective-permute-done((f32[1024,1024]{1,0:T(8,128)}, f32[1024,1024]{1,0:T(8,128)S(1)}, u32[]{:S(2)}, u32[]{:S(2)}) %collective-permute-start.3) | collective-permute-done | bytes 4194336 | tf_op jit(solution)/shard_map/ppermute | solution.py:1416
  222.1 2.0 copy-done.3
  224.1 7.8 %norm_backward.3 = (f32[1024,1024]{1,0:T(8,128)}, f32[8,1024]{1,0:T(8,128)}) custom-call(bf16[1024,1024]{1,0:T(8,128)(2,1)S(1)} %copy-done, f32[1024,1024]{1,0:T(8,128)} %get-tuple-element.305.own_ref, f32[1024,1024]{1,0:T(8,128)} %copy-done.3, bf16[1024,1024]{1,0:T(8,128)(2,1)} %get-tuple-element.300.grad_ref, bf16[2,1024]{1,0:T(2,128)(2,1)S(1)} %copy-done.4), custom_call_target="tpu_custom_call" | custom-call | tf_op jit(solution)/shard_map/norm_backward/pallas_call | solution.py:974
  231.9 1.9 collective-permute-done.4
  233.7 279.5 %finish.1 = (f32[2,1024,256]{2,1,0:T(8,128)}, f32[2,1024,128]{2,1,0:T(8,128)}, f32[24,1024]{1,0:T(8,128)}) custom-call(f32[2,2,2,1024,256]{4,3,2,1,0:T(8,128)} %get-tuple-element.307.kept_weight1, f32[2,2,2,1024,256]{4,3,2,1,0:T(8,128)} %bitcast.30, f32[2,2,2,1024,256]{4,3,2,1,0:T(8,128)} %bitcast.20.came_weight1, f32[2,2,2,1024,256]{4,3,2,1,0:T(8,128)} %bitcast.22.came_up1, ...), custom_call_target="tpu_custom_call" | custom-call | tf_op jit(solution)/shard_map/finish/pallas_call | solution.py:1255
  513.3 4.4 hand_out.1
  (14 shorter events, 0.1 us)
Async XLA Ops:
  5.9 40.3 %copy-start.1 = (bf16[1024,1024]{1,0:T(8,128)(2,1)S(1)}, bf16[1024,1024]{1,0:T(8,128)(2,1)}, u32[]{:S(2)}) copy-start(bf16[1024,1024]{1,0:T(8,128)(2,1)} %grad_ref.1) | copy-start | bytes 6291460
  38.7 7.6 %collective-permute-start = (f32[1024,1024]{1,0:T(8,128)}, f32[1024,1024]{1,0:T(8,128)}, u32[]{:S(2)}, u32[]{:S(2)}) collective-permute-start(f32[1024,1024]{1,0:T(8,128)} %get-tuple-element.296), channel_id=1, source_target_pairs={{0,1},{1,0},{2,3},{3,2},{4,5},{5,4},{6,7},{7,6},{8,9},{9,8},{10,11... | collective-permute-start | bytes 12582920 | tf_op jit(solution)/shard_map/ppermute | solution.py:1372
  138.4 14.4 %copy-start.2 = (f32[1024,128]{1,0:T(8,128)S(1)}, f32[1024,128]{1,0:T(8,128)}, u32[]{:S(2)}) copy-start(f32[1024,128]{1,0:T(8,128)} %constant.71.clone) | copy-start | bytes 1572868
  138.4 14.4 %copy-start.5 = (s32[1,4]{1,0:T(1,128)S(1)}, s32[1,4]{1,0:T(1,128)}, u32[]{:S(2)}) copy-start(s32[1,4]{1,0:T(1,128)} %param.30) | copy-start | bytes 52
  138.4 7.6 %collective-permute-start.2 = (f32[1024,1024]{1,0:T(8,128)}, f32[1024,1024]{1,0:T(8,128)}, u32[]{:S(2)}, u32[]{:S(2)}) collective-permute-start(f32[1024,1024]{1,0:T(8,128)} %get-tuple-element.299.own_ref), channel_id=1, source_target_pairs={{0,1},{1,0},{2,3},{3,2},{4,5},{5,4},{6,7},{7,6},{8,9},{9,8},{10,11... | collective-permute-start | bytes 12582920 | tf_op jit(solution)/shard_map/ppermute | solution.py:1416
  138.5 14.3 %collective-permute-start.1 = (f32[1024,1024]{1,0:T(8,128)}, f32[1024,1024]{1,0:T(8,128)}, u32[]{:S(2)}, u32[]{:S(2)}) collective-permute-start(f32[1024,1024]{1,0:T(8,128)} %get-tuple-element.298), channel_id=1, source_target_pairs={{0,1},{1,0},{2,3},{3,2},{4,5},{5,4},{6,7},{7,6},{8,9},{9,8},{10,11... | collective-permute-start | bytes 12582920 | tf_op jit(solution)/shard_map/ppermute | solution.py:1391
  139.0 94.8 %collective-permute-start.4 = (f32[8,1024,256]{2,1,0:T(8,128)}, f32[8,1024,256]{2,1,0:T(8,128)}, u32[]{:S(2)}, u32[]{:S(2)}) collective-permute-start(f32[8,1024,256]{2,1,0:T(8,128)} %get-tuple-element.309), channel_id=1, source_target_pairs={{0,8},{2,10},{4,12},{6,14},{8,0},{10,2},{12,4},{14,6},{16,24},{18,... | collective-permute-start | bytes 25165832 | tf_op jit(solution)/shard_map/ppermute | solution.py:1323
  142.0 91.7 %collective-permute-start.5 = (f32[8,1024,256]{2,1,0:T(8,128)}, f32[8,1024,256]{2,1,0:T(8,128)}, u32[]{:S(2)}, u32[]{:S(2)}) collective-permute-start(f32[8,1024,256]{2,1,0:T(8,128)} %bitcast.41), channel_id=1, source_target_pairs={{1,5},{3,7},{5,1},{7,3},{9,13},{11,15},{13,9},{15,11},{17,21},{19,... | collective-permute-start | bytes 25165832 | tf_op jit(solution)/shard_map/ppermute | solution.py:1324
  152.8 71.2 %copy-start = (bf16[1024,1024]{1,0:T(8,128)(2,1)S(1)}, bf16[1024,1024]{1,0:T(8,128)(2,1)}, u32[]{:S(2)}) copy-start(bf16[1024,1024]{1,0:T(8,128)(2,1)} %x_ref.1) | copy-start | bytes 6291460
  152.8 71.2 %copy-start.4 = (bf16[2,1024]{1,0:T(2,128)(2,1)S(1)}, bf16[2,1024]{1,0:T(2,128)(2,1)}, u32[]{:S(2)}) copy-start(bf16[2,1024]{1,0:T(2,128)(2,1)} %gain_ref.3) | copy-start | bytes 12292
  214.7 7.4 %collective-permute-start.3 = (f32[1024,1024]{1,0:T(8,128)}, f32[1024,1024]{1,0:T(8,128)S(1)}, u32[]{:S(2)}, u32[]{:S(2)}) collective-permute-start(f32[1024,1024]{1,0:T(8,128)} %get-tuple-element.305.own_ref), channel_id=1, source_target_pairs={{0,1},{1,0},{2,3},{3,2},{4,5},{5,4},{6,7},{7,6},{8,9},{9,8},{10,11... | collective-permute-start | bytes 12582920 | tf_op jit(solution)/shard_map/ppermute | solution.py:1416
  222.1 2.0 copy-start.3

commit v10 on v9

--- a/solution.py
+++ b/solution.py
@@ -167,7 +167,7 @@
 
 def start_layer(stream, x_ref, h_ref, gain_ref, offset_ref):
     length = h_ref.shape[0]
-    step = min(128, length)
+    step = min(256, length)
 
     @pl.loop(0, length // step)
     def _(index):
@@ -181,7 +181,7 @@
         ).astype(BF16)
 
 
-JOB = 128
+JOB = 256
 
 
 def start_last_layer(stream, x_hbm, buffers, loads, stores, h_ref, gain_ref, offset_ref):
@@ -352,7 +352,9 @@
     @pl.loop(0, h_t.shape[0] // ROWS)
     def _(index):
         rows = pl.ds(pl.multiple_of(index * ROWS, ROWS), ROWS)
-        for side in range(2):
+
+        @pl.loop(0, 2)
+        def _(side):
             for target, x in ((along_x, 1 - near_x), (kept_x, near_x)):
                 target[0, side, rows] = dot_nn(grad_t[rows], act[:, block(side, x)])
             for target, y in ((along_y, 1 - near_y), (kept_y, near_y)):
@@ -1198,8 +1200,8 @@
         for flow in flows:
             unit = index - flow.start
             pl.when(within(flow, unit))(functools.partial(begin, flow, unit))
-        for flow in flows:
-            for stage in range(1, stages + 1):
+        for stage in range(stages, 0, -1):
+            for flow in flows:
                 unit = index - flow.start - LAG * stage
                 pl.when(within(flow, unit))(functools.partial(advance, flow, stage, unit))
         for stage in range(stages + 1):

time: 523 us -> 513 us (0.981)
  Pallas kernels: 484 us -> 478 us
where the time goes in v10:
time: 513 us; the launch traced here: 508 us
  Pallas kernels  478 us (93%)
  waiting for transfers between devices  16.7 us (3%)
  starting transfers between devices  7.64 us (1%)
    pallas_call x1, Pallas kernels, finish(): pl.pallas_call(functools.partial(finish_kernel, bits, flows), in_specs=[p...  275 us
    pallas_call x1, Pallas kernels, attention_last(): pl.pallas_call(functools.partial(attention_last_kernel, layer), grid_spec...  86.9 us
    pallas_call x1, Pallas kernels, attention_backward(): pl.pallas_call(functools.partial(attention_backward_kernel, len(stream)),...  61.3 us
    pallas_call x1, Pallas kernels, attention_forward(): pl.pallas_call(functools.partial(attention_forward_kernel, layer, len(str...  32 us
    pallas_call x2, Pallas kernels, norm_backward(): pl.pallas_call(functools.partial(norm_backward_kernel, layer), grid=(leng...  14.6 us
  transfers between devices with their start and end apart: 6, of which 4 were waited for; matrix products, arithmetic and copies ran while one was open for 0% of the time, Pallas kernels for 15%

profile of v10, /device:TPU:0, one launch (start us, length us, event | category | flops | bytes accessed | tf_op | source)
XLA Modules:
  0.0 507.9 jit_solution(4011043400050628062)
XLA Ops:
  0.6 0.8 reshape.115
  1.4 4.5 conditional.4
  1.4 4.5 feature_tables.1
  5.9 32.3 %conditional.5 = ((f32[1024,1024]{1,0:T(8,128)}, bf16[1024,1024]{1,0:T(8,128)(2,1)}, bf16[4,1024,1024]{2,1,0:T(8,128)(2,1)}, bf16[4,1024,1024]{2,1,0:T(8,128)(2,1)})) conditional(s32[]{:T(128)} %convert_element_type.21, (bf16[1024,1024]{1,0:T(8,128)(2,1)}, bf16[2,1024]{1,0:T(2,128)(2,1)}, bf16[2,1024]{1,0:T(2,128)(2,1)}, ...), branch_computations={%region_2.3_spmd, %region_3.4_spmd} | conditional | bytes 8 | solution.py:1369
  6.3 32.0 %attention_forward.1 = (f32[1024,1024]{1,0:T(8,128)}, bf16[1024,1024]{1,0:T(8,128)(2,1)}, bf16[4,1024,1024]{2,1,0:T(8,128)(2,1)}, bf16[4,1024,1024]{2,1,0:T(8,128)(2,1)}) custom-call(bf16[1024,1024]{1,0:T(8,128)(2,1)} %get-tuple-element.160.refs_0_, s32[1,4]{1,0:T(1,128)} %get-tuple-element.161.refs_1_, bf16[2,1024]{1,0:T(2,128)(2,1)} %get-tuple-element.162.refs_2_, ...), custom_call_target="tpu_custom_call" | custom-call | tf_op jit(solution)/shard_map/cond/branch_1_fun/attention_forward/pallas_call | solution.py:635
  38.2 0.1 collective-permute-start
  38.4 0.1 pad_add_fusion
  38.4 7.3 %collective-permute-done = f32[1024,1024]{1,0:T(8,128)} collective-permute-done((f32[1024,1024]{1,0:T(8,128)}, f32[1024,1024]{1,0:T(8,128)}, u32[]{:S(2)}, u32[]{:S(2)}) %collective-permute-start) | collective-permute-done | bytes 4194336 | tf_op jit(solution)/shard_map/ppermute | solution.py:1374
  45.8 87.1 %conditional.6 = (f32[1024,1024]{1,0:T(8,128)S(1)}, f32[1024,1024]{1,0:T(8,128)}, f32[1024,1024]{1,0:T(8,128)}, f32[8,1024,256]{2,1,0:T(8,128)}, f32[4,1024]{1,0...) conditional(s32[]{:T(128)} %convert_element_type.22, ...), branch_computations={%region_4.5_spmd, %region_5.6_spmd} | conditional | bytes 64 | solution.py:1390
  45.8 86.9 %attention_last.1 = (f32[1024,1024]{1,0:T(8,128)S(1)}, f32[1024,1024]{1,0:T(8,128)}, f32[1024,1024]{1,0:T(8,128)}, f32[2,4,1024,256]{3,2,1,0:T(8,128)}, f32[2,4,...) custom-call(s32[3]{0:T(128)S(1)} %get-tuple-element.171.place_ref, ...), custom_call_target="tpu_custom_call" | custom-call | tf_op jit(solution)/shard_map/cond/branch_0_fun/attention_last/pallas_call | solution.py:896
  132.9 0.1 collective-permute-start.2
  133.0 0.5 collective-permute-start.1
  133.5 3.0 collective-permute-start.4
  136.5 3.9 collective-permute-start.5
  140.5 6.8 %norm_backward.2 = (bf16[1024,1024]{1,0:T(8,128)(2,1)}, f32[8,1024]{1,0:T(8,128)}) custom-call(f32[1024,1024]{1,0:T(8,128)S(1)} %get-tuple-element.297.x_ref, f32[1024,1024]{1,0:T(8,128)} %get-tuple-element.299.own_ref, f32[1024,1024]{1,0:T(8,128)} %collective-permute-done.2.other_ref, bf16[1024,1024]{1,0:T(8,128)(2,1)S(1)} %copy-done.1, ...), custom_call_target="tpu_custom_call" | custom-call | tf_op jit(solution)/shard_map/norm_backward/pallas_call | solution.py:976
  147.4 61.8 %conditional.7 = (f32[1024,1024]{1,0:T(8,128)}, f32[1024,1024]{1,0:T(8,128)}, f32[4,1024]{1,0:T(4,128)S(1)}, f32[2,2,2,1024,256]{4,3,2,1,0:T(8,128)}, f32[2,2,2,...) conditional(s32[]{:T(128)} %convert_element_type.21, ...), branch_computations={%region_6.7_spmd, %region_7.8_spmd} | conditional | bytes 56 | solution.py:1410
  147.6 61.3 %attention_backward.1 = (f32[1024,1024]{1,0:T(8,128)}, f32[1024,1024]{1,0:T(8,128)}, f32[2,4,1024,256]{3,2,1,0:T(8,128)}, f32[2,4,1024,256]{3,2,1,0:T(8,128)}, f...) custom-call(s32[3]{0:T(128)S(1)} %get-tuple-element.230.place_ref, ...), custom_call_target="tpu_custom_call" | custom-call | tf_op jit(solution)/shard_map/cond/branch_1_fun/attention_backward/pallas_call | solution.py:819
  209.2 0.1 collective-permute-start.3
  209.2 7.4 %collective-permute-done.3.other_ref = f32[1024,1024]{1,0:T(8,128)S(1)} collective-permute-done((f32[1024,1024]{1,0:T(8,128)}, f32[1024,1024]{1,0:T(8,128)S(1)}, u32[]{:S(2)}, u32[]{:S(2)}) %collective-permute-start.3) | collective-permute-done | bytes 4194336 | tf_op jit(solution)/shard_map/ppermute | solution.py:1418
  216.6 2.0 copy-done.3
  218.6 7.8 %norm_backward.3 = (f32[1024,1024]{1,0:T(8,128)}, f32[8,1024]{1,0:T(8,128)}) custom-call(bf16[1024,1024]{1,0:T(8,128)(2,1)S(1)} %copy-done, f32[1024,1024]{1,0:T(8,128)} %get-tuple-element.305.own_ref, f32[1024,1024]{1,0:T(8,128)} %copy-done.3, bf16[1024,1024]{1,0:T(8,128)(2,1)} %get-tuple-element.300.grad_ref, bf16[2,1024]{1,0:T(2,128)(2,1)S(1)} %copy-done.4), custom_call_target="tpu_custom_call" | custom-call | tf_op jit(solution)/shard_map/norm_backward/pallas_call | solution.py:976
  226.4 1.9 collective-permute-done.4
  228.3 274.8 %finish.1 = (f32[2,1024,256]{2,1,0:T(8,128)}, f32[2,1024,128]{2,1,0:T(8,128)}, f32[24,1024]{1,0:T(8,128)}) custom-call(f32[2,2,2,1024,256]{4,3,2,1,0:T(8,128)} %get-tuple-element.307.kept_weight1, f32[2,2,2,1024,256]{4,3,2,1,0:T(8,128)} %bitcast.30, f32[2,2,2,1024,256]{4,3,2,1,0:T(8,128)} %bitcast.20.came_weight1, f32[2,2,2,1024,256]{4,3,2,1,0:T(8,128)} %bitcast.22.came_up1, ...), custom_call_target="tpu_custom_call" | custom-call | tf_op jit(solution)/shard_map/finish/pallas_call | solution.py:1257
  503.0 4.4 hand_out.1
  (14 shorter events, 0.1 us)
Async XLA Ops:
  5.9 39.9 %copy-start.1 = (bf16[1024,1024]{1,0:T(8,128)(2,1)S(1)}, bf16[1024,1024]{1,0:T(8,128)(2,1)}, u32[]{:S(2)}) copy-start(bf16[1024,1024]{1,0:T(8,128)(2,1)} %grad_ref.1) | copy-start | bytes 6291460
  38.2 7.6 %collective-permute-start = (f32[1024,1024]{1,0:T(8,128)}, f32[1024,1024]{1,0:T(8,128)}, u32[]{:S(2)}, u32[]{:S(2)}) collective-permute-start(f32[1024,1024]{1,0:T(8,128)} %get-tuple-element.296), channel_id=1, source_target_pairs={{0,1},{1,0},{2,3},{3,2},{4,5},{5,4},{6,7},{7,6},{8,9},{9,8},{10,11... | collective-permute-start | bytes 12582920 | tf_op jit(solution)/shard_map/ppermute | solution.py:1374
  132.9 14.4 %copy-start.2 = (f32[1024,128]{1,0:T(8,128)S(1)}, f32[1024,128]{1,0:T(8,128)}, u32[]{:S(2)}) copy-start(f32[1024,128]{1,0:T(8,128)} %constant.71.clone) | copy-start | bytes 1572868
  132.9 14.4 %copy-start.5 = (s32[1,4]{1,0:T(1,128)S(1)}, s32[1,4]{1,0:T(1,128)}, u32[]{:S(2)}) copy-start(s32[1,4]{1,0:T(1,128)} %param.30) | copy-start | bytes 52
  132.9 7.6 %collective-permute-start.2 = (f32[1024,1024]{1,0:T(8,128)}, f32[1024,1024]{1,0:T(8,128)}, u32[]{:S(2)}, u32[]{:S(2)}) collective-permute-start(f32[1024,1024]{1,0:T(8,128)} %get-tuple-element.299.own_ref), channel_id=1, source_target_pairs={{0,1},{1,0},{2,3},{3,2},{4,5},{5,4},{6,7},{7,6},{8,9},{9,8},{10,11... | collective-permute-start | bytes 12582920 | tf_op jit(solution)/shard_map/ppermute | solution.py:1418
  133.0 14.3 %collective-permute-start.1 = (f32[1024,1024]{1,0:T(8,128)}, f32[1024,1024]{1,0:T(8,128)}, u32[]{:S(2)}, u32[]{:S(2)}) collective-permute-start(f32[1024,1024]{1,0:T(8,128)} %get-tuple-element.298), channel_id=1, source_target_pairs={{0,1},{1,0},{2,3},{3,2},{4,5},{5,4},{6,7},{7,6},{8,9},{9,8},{10,11... | collective-permute-start | bytes 12582920 | tf_op jit(solution)/shard_map/ppermute | solution.py:1393
  133.5 94.8 %collective-permute-start.4 = (f32[8,1024,256]{2,1,0:T(8,128)}, f32[8,1024,256]{2,1,0:T(8,128)}, u32[]{:S(2)}, u32[]{:S(2)}) collective-permute-start(f32[8,1024,256]{2,1,0:T(8,128)} %get-tuple-element.309), channel_id=1, source_target_pairs={{0,8},{2,10},{4,12},{6,14},{8,0},{10,2},{12,4},{14,6},{16,24},{18,... | collective-permute-start | bytes 25165832 | tf_op jit(solution)/shard_map/ppermute | solution.py:1325
  136.5 91.7 %collective-permute-start.5 = (f32[8,1024,256]{2,1,0:T(8,128)}, f32[8,1024,256]{2,1,0:T(8,128)}, u32[]{:S(2)}, u32[]{:S(2)}) collective-permute-start(f32[8,1024,256]{2,1,0:T(8,128)} %bitcast.41), channel_id=1, source_target_pairs={{1,5},{3,7},{5,1},{7,3},{9,13},{11,15},{13,9},{15,11},{17,21},{19,... | collective-permute-start | bytes 25165832 | tf_op jit(solution)/shard_map/ppermute | solution.py:1326
  147.3 71.2 %copy-start = (bf16[1024,1024]{1,0:T(8,128)(2,1)S(1)}, bf16[1024,1024]{1,0:T(8,128)(2,1)}, u32[]{:S(2)}) copy-start(bf16[1024,1024]{1,0:T(8,128)(2,1)} %x_ref.1) | copy-start | bytes 6291460
  147.3 71.2 %copy-start.4 = (bf16[2,1024]{1,0:T(2,128)(2,1)S(1)}, bf16[2,1024]{1,0:T(2,128)(2,1)}, u32[]{:S(2)}) copy-start(bf16[2,1024]{1,0:T(2,128)(2,1)} %gain_ref.3) | copy-start | bytes 12292
  209.2 7.4 %collective-permute-start.3 = (f32[1024,1024]{1,0:T(8,128)}, f32[1024,1024]{1,0:T(8,128)S(1)}, u32[]{:S(2)}, u32[]{:S(2)}) collective-permute-start(f32[1024,1024]{1,0:T(8,128)} %get-tuple-element.305.own_ref), channel_id=1, source_target_pairs={{0,1},{1,0},{2,3},{3,2},{4,5},{5,4},{6,7},{7,6},{8,9},{9,8},{10,11... | collective-permute-start | bytes 12582920 | tf_op jit(solution)/shard_map/ppermute | solution.py:1418
  216.6 2.0 copy-start.3

commit v11 on v10

--- a/solution.py
+++ b/solution.py
@@ -117,7 +117,7 @@
 def feature_tables(seeds):
     return pl.pallas_call(
         tables_kernel,
-        grid=(LAYERS,),
+        grid=(1,),
         in_specs=[
             pl.BlockSpec((1, HEADS, DH), lambda l: (l, 0, 0)),
             whole((DH, DH)),
@@ -128,9 +128,9 @@
             pl.BlockSpec((1, QUADS, 1, WIDE), lambda l: (l, 0, 0, 0)),
         ],
         out_shape=[
-            jax.ShapeDtypeStruct((LAYERS, QUADS, WIDE, WIDE), BF16),
-            jax.ShapeDtypeStruct((LAYERS, QUADS, WIDE, WIDE), BF16),
-            jax.ShapeDtypeStruct((LAYERS, QUADS, 1, WIDE), F32),
+            jax.ShapeDtypeStruct((1, QUADS, WIDE, WIDE), BF16),
+            jax.ShapeDtypeStruct((1, QUADS, WIDE, WIDE), BF16),
+            jax.ShapeDtypeStruct((1, QUADS, 1, WIDE), F32),
         ],
         compiler_params=params(),
         name="feature_tables",
@@ -662,6 +662,7 @@
 def attend_heads_back(
     place_ref, starts_ref, grad_ref, state_ref, mixed_ref, table_ref, cosine_ref, sine_ref,
     weight_ref, part_ref, along_z, kept_z, bias_ref, mask_ref, upright, numer_ref, feat_ref, flow,
+    mixed_grad=None,
 ):
     group = pl.program_id(0)
     length, width = grad_ref.shape
@@ -672,7 +673,10 @@
     one = jnp.ones((), BF16)
     for first in range(0, length, ROWS):
         rows = slice(first, first + ROWS)
-        grad = dot_nt(grad_ref[rows], weight_ref[0, 0, 3, 0]).astype(BF16).astype(F32)
+        if mixed_grad is None:
+            grad = dot_nt(grad_ref[rows], weight_ref[0, 0, 3, 0]).astype(BF16).astype(F32)
+        else:
+            grad = mixed_grad[rows].astype(F32)
         inverse = mixed_ref[1, rows].astype(F32) + mixed_ref[2, rows].astype(F32)
         scaled = grad * inverse
         upper, lower = split(-head_sums(scaled * mixed_ref[0, rows].astype(F32), partner))
@@ -861,20 +865,23 @@
     gain_ref, offset_ref = [ref.at[layer : layer + 1] for ref in (gain_ref, offset_ref)]
     first_bias = layer * (bias_ref.shape[0] // LAYERS)
     upper_ref, lower_ref, scale_ref, cosine_ref, sine_ref, grad_ref = refs[5:11]
-    x_hbm, part_ref, grad_part, along_z, kept_z, _, _, bias_out = refs[11:19]
-    h_ref, state_ref, mixed_ref, mask_ref, mask_back = refs[19:24]
-    upright, numer_ref, feat_ref, flow, loads, stores = refs[24:]
+    mixed_grad, grad_t = refs[11:13]
+    x_hbm, part_ref, grad_part, along_z, kept_z, _, _, bias_out = refs[13:21]
+    h_ref, state_ref, mixed_ref, mask_ref, mask_back = refs[21:26]
+    upright, numer_ref, feat_ref, flow, turned, loads, stores = refs[26:]
 
     @pl.when(pl.program_id(0) == 0)
     def _():
         buffers = (upright.at[0], part_ref, grad_part)
+        copy = pltpu.make_async_copy(grad_t, upright.at[1], turned)
+        copy.start()
         start_last_layer(stream, x_hbm, buffers, loads, stores, h_ref, gain_ref, offset_ref)
         write_mask(starts_ref, mask_ref, False)
         write_mask(starts_ref, mask_back, True)
         part_ref[...] = jnp.broadcast_to(bias_ref[first_bias + 3], part_ref.shape)
         grad_part[...] = jnp.zeros_like(grad_part)
         upright[0] = h_ref[...].T
-        upright[1] = grad_ref[...].T
+        copy.wait()
 
     attend_heads(
         first_bias, starts_ref, weight_ref, bias_ref, upper_ref, lower_ref, scale_ref, cosine_ref,
@@ -883,12 +890,13 @@
     attend_heads_back(
         place_ref, starts_ref, grad_ref, state_ref, mixed_ref, upper_ref, cosine_ref, sine_ref,
         weight_ref, grad_part, along_z, kept_z, bias_out, mask_back, upright, numer_ref, feat_ref,
-        flow,
+        flow, mixed_grad,
     )
 
 
 def attention_last(
-    layer, place, stream, starts, gain, offset, weight, biases, tables, rotary, grad
+    layer, place, stream, starts, gain, offset, weight, biases, tables, rotary, grad, mixed_grad,
+    grad_t,
 ):
     length, width = stream[0].shape
     full = jax.ShapeDtypeStruct((length, width), F32)
@@ -905,12 +913,14 @@
                 whole((LAYERS, width)),
                 pl.BlockSpec((1, 1, 4, 1, WIDE, width), lambda g, *_: (0, layer, 0, g, 0, 0)),
                 whole((LAYERS * 4, 1, width)),
-                pl.BlockSpec((1, 1, WIDE, WIDE), lambda g, *_: (layer, g, 0, 0)),
-                pl.BlockSpec((1, 1, WIDE, WIDE), lambda g, *_: (layer, g, 0, 0)),
-                pl.BlockSpec((1, 1, 1, WIDE), lambda g, *_: (layer, g, 0, 0)),
+                pl.BlockSpec((1, 1, WIDE, WIDE), lambda g, *_: (0, g, 0, 0)),
+                pl.BlockSpec((1, 1, WIDE, WIDE), lambda g, *_: (0, g, 0, 0)),
+                pl.BlockSpec((1, 1, 1, WIDE), lambda g, *_: (0, g, 0, 0)),
                 whole((length, PAIR)),
                 whole((length, PAIR)),
                 whole((length, width)),
+                pl.BlockSpec((length, WIDE), lambda g, *_: (0, g)),
+                pl.BlockSpec(memory_space=pltpu.HBM),
             ],
             out_specs=[pl.BlockSpec(memory_space=pltpu.HBM)]
             + [whole((length, width))] * 2
@@ -927,6 +937,7 @@
                 pltpu.VMEM((2, length, WIDE), BF16),
                 pltpu.VMEM((2, length, WIDE), BF16),
                 pltpu.VMEM((4, length, WIDE), BF16),
+                pltpu.SemaphoreType.DMA,
             ]
             + chunk_semaphores(length),
         ),
@@ -936,8 +947,53 @@
         compiler_params=params(),
         name="attention_last",
     )(
-        place, *stream, starts, gain, offset, kinds_of(weight), biases, *tables, *rotary, grad
-    )
+        place, *stream, starts, gain, offset, kinds_of(weight), biases, *tables, *rotary, grad,
+        mixed_grad, grad_t,
+    )
+
+
+def unread(shapes):
+    def kernel(*refs):
+        del refs
+
+    return tuple(
+        pl.pallas_call(
+            kernel,
+            out_specs=[pl.BlockSpec(memory_space=pl.ANY)] * len(shapes),
+            out_shape=list(shapes),
+            name="unread",
+        )()
+    )
+
+
+def prepare_kernel(part_ref, grad_ref, weight_ref, mixed_grad, grad_t):
+    del part_ref
+    mixed_grad[...] = dot_nt(grad_ref[...], weight_ref[0, 0]).astype(BF16)
+
+    @pl.when(pl.program_id(0) == 0)
+    def _():
+        grad_t[...] = grad_ref[...].T
+
+
+def prepare(layer, part, grad, weight):
+    length, width = grad.shape
+    lanes = width // 2
+    return pl.pallas_call(
+        prepare_kernel,
+        grid=(width // lanes,),
+        in_specs=[
+            pl.BlockSpec(memory_space=pltpu.HBM),
+            whole((length, width)),
+            pl.BlockSpec((1, 1, lanes, width), lambda j: (0, layer, 6 + j, 0)),
+        ],
+        out_specs=[pl.BlockSpec((length, lanes), lambda j: (0, j)), whole((width, length))],
+        out_shape=[
+            jax.ShapeDtypeStruct((length, width), BF16),
+            jax.ShapeDtypeStruct((width, length), BF16),
+        ],
+        compiler_params=params(),
+        name="prepare",
+    )(part, grad, weight)
 
 
 def norm_gradient(values, incoming, grad, gain, sums_ref):
@@ -1335,15 +1391,18 @@
     length, width = tokens.shape
     rotary = tuple(jnp.asarray(table) for table in rotary_rows(length))
     biases = branch_bias[0].astype(F32).reshape(-1, 1, width)
-    tables = lax.cond(
-        is_attention,
-        lambda: tuple(feature_tables(freq_seeds)),
-        lambda: (
-            jnp.zeros((LAYERS, QUADS, WIDE, WIDE), BF16),
-            jnp.zeros((LAYERS, QUADS, WIDE, WIDE), BF16),
-            jnp.zeros((LAYERS, QUADS, 1, WIDE), F32),
-        ),
-    )
+
+    def tables_of(layer):
+        return tuple(feature_tables(freq_seeds[layer : layer + 1]))
+
+    wide = jax.ShapeDtypeStruct((1, QUADS, WIDE, WIDE), BF16)
+    none = (wide, wide, jax.ShapeDtypeStruct((1, QUADS, 1, WIDE), F32))
+    square = jax.ShapeDtypeStruct((length, width), BF16)
+
+    def no_tables():
+        return unread(none)
+
+    tables = lax.cond(is_attention, lambda: tables_of(0), no_tables)
     swap = [(0, 1), (1, 0)]
 
     def attention(layer, stream):
@@ -1373,10 +1432,18 @@
     )
     stream = (tokens, part, lax.ppermute(part, "stream", swap))
 
+    def ready():
+        return *tables_of(1), *prepare(1, part, cotangent, branch_weight)
+
+    def not_ready():
+        return unread(none + (square, jax.ShapeDtypeStruct((width, length), BF16)))
+
+    *tables1, mixed_grad, grad_t = lax.cond(is_attention, ready, not_ready)
+
     def attention_ends():
         x, part, *back = attention_last(
-            1, place, stream, doc_starts, norm_gain, norm_bias, branch_weight, biases, tables,
-            rotary, cotangent,
+            1, place, stream, doc_starts, norm_gain, norm_bias, branch_weight, biases, tables1,
+            rotary, cotangent, mixed_grad, grad_t,
         )
         return x, part, *flat_halves(*back)
 
@@ -1390,8 +1457,6 @@
     x1, part, part1, *halves1, bias1 = lax.cond(
         jnp.logical_not(is_attention), feed_forward_ends, attention_ends
     )
-    stream = (x1, part, lax.ppermute(part, "stream", swap))
-
     def attention_back(layer, grad, stream):
         h, state, mixed = kept
         *result, part, a, b, c, d, bias = attention_backward(
@@ -1421,6 +1486,7 @@
     if blocked:
         came = send_first(halves1)
     grad0, sums1 = norm_back(1, x1, part1, cotangent, BF16)
+    stream = (x1, part, lax.ppermute(part, "stream", swap))
     result, part0, halves0, bias0 = back(0, grad0, stream)
     input_grad, sums0 = norm_back(0, tokens, part0, grad0, F32)
     if blocked:

time: 513 us -> 511 us (level)
  waiting for transfers between devices: 16.7 us -> 9.03 us
    pallas_call x1 -> x3, Pallas kernels: 4.51 us -> 12.5 us  [the longest x1 6.81 us: prepare(): pl.pallas_call(prepare_kernel, grid=(width // lanes,), in_specs=[pl.Block...]
    ppermute x1, waiting for transfers between devices: 7.35 us -> 0.01 us  [shards(): stream = (tokens, part, lax.ppermute(part, 'stream', swap))]
  transfers between devices with their start and end apart: 6 -> 6, of which waited for: 4 -> 3; matrix products, arithmetic and copies ran while one was open for 0% -> 0% of each run, Pallas kernels for 15% -> 17%
where the time goes in v11:
time: 511 us; the launch traced here: 506 us
  Pallas kernels  481 us (94%)
  waiting for transfers between devices  9.03 us (2%)
  starting transfers between devices  7.63 us (1%)
  local copies, waits for them, and re-layouts  5.46 us (1%)
    pallas_call x1, Pallas kernels, finish(): pl.pallas_call(functools.partial(finish_kernel, bits, flows), in_specs=[p...  275 us
    pallas_call x1, Pallas kernels, attention_last(): pl.pallas_call(functools.partial(attention_last_kernel, layer), grid_spec...  81.9 us
    pallas_call x1, Pallas kernels, attention_backward(): pl.pallas_call(functools.partial(attention_backward_kernel, len(stream)),...  61.3 us
    pallas_call x1, Pallas kernels, attention_forward(): pl.pallas_call(functools.partial(attention_forward_kernel, layer, len(str...  31.7 us
    pallas_call x2, Pallas kernels, norm_backward(): pl.pallas_call(functools.partial(norm_backward_kernel, layer), grid=(leng...  15 us
  transfers between devices with their start and end apart: 6, of which 3 were waited for; matrix products, arithmetic and copies ran while one was open for 0% of the time, Pallas kernels for 17%

profile of v11, /device:TPU:0, one launch (start us, length us, event | category | flops | bytes accessed | tf_op | source)
XLA Modules:
  0.0 506.0 jit_solution(4089524812571317873)
XLA Ops:
  0.6 0.8 reshape.115
  1.4 3.5 conditional.5
  1.4 1.3 slice.4.seeds_ref
  2.7 2.2 feature_tables.2
  5.0 0.8 copy-done.4
  5.7 32.1 %conditional.6 = ((f32[1024,1024]{1,0:T(8,128)}, bf16[1024,1024]{1,0:T(8,128)(2,1)}, bf16[4,1024,1024]{2,1,0:T(8,128)(2,1)}, bf16[4,1024,1024]{2,1,0:T(8,128)(2,1)})) conditional(s32[]{:T(128)} %convert_element_type.22, (bf16[1024,1024]{1,0:T(8,128)(2,1)}, bf16[2,1024]{1,0:T(2,128)(2,1)}, bf16[2,1024]{1,0:T(2,128)(2,1)}, ...), branch_computations={%region_2.3_spmd, %region_3.4_spmd} | conditional | bytes 8 | solution.py:1428
  6.1 31.7 %attention_forward.1 = (f32[1024,1024]{1,0:T(8,128)}, bf16[1024,1024]{1,0:T(8,128)(2,1)}, bf16[4,1024,1024]{2,1,0:T(8,128)(2,1)}, bf16[4,1024,1024]{2,1,0:T(8,128)(2,1)}) custom-call(bf16[1024,1024]{1,0:T(8,128)(2,1)} %get-tuple-element.174.refs_0_, s32[1,4]{1,0:T(1,128)} %get-tuple-element.175.refs_1_, bf16[2,1024]{1,0:T(2,128)(2,1)} %get-tuple-element.176.refs_2_, ...), custom_call_target="tpu_custom_call" | custom-call | tf_op jit(solution)/shard_map/cond/branch_1_fun/attention_forward/pallas_call | solution.py:635
  38.1 10.9 %conditional.7 = ((bf16[1,4,256,256]{3,2,1,0:T(8,128)(2,1)}, bf16[1,4,256,256]{3,2,1,0:T(8,128)(2,1)}, f32[1,4,1,256]{3,2,1,0:T(1,128)S(1)}, bf16[1024,1024]{1,0:T(8,128)(2,1)}, bf16[1024,1024]{1,0:T(8,128)(2,1)})) conditional(s32[]{:T(128)} %convert_element_type.22, () %tuple.60, (s32[2,16,64]{2,1,0:T(8,128)S(1)}, f32[64,64]{1,0:T(8,128)S(1)}, ...), branch_computations={%region_4.5_spmd, %region_5.6_spmd} | conditional | bytes 8240 | solution.py:1441
  38.1 0.6 slice.5.seeds_ref
  38.7 3.4 feature_tables.3
  42.1 6.8 %prepare.1 = (bf16[1024,1024]{1,0:T(8,128)(2,1)}, bf16[1024,1024]{1,0:T(8,128)(2,1)}) custom-call(f32[1024,1024]{1,0:T(8,128)} %get-tuple-element.190.part_ref, bf16[1024,1024]{1,0:T(8,128)(2,1)} %get-tuple-element.191.grad_ref, bf16[1,2,4096,1024]{3,2,1,0:T(8,128)(2,1)} %get-tuple-element.192.weight_ref), custom_call_target="tpu_custom_call" | custom-call | tf_op jit(solution)/shard_map/cond/branch_1_fun/prepare/pallas_call | solution.py:981
  49.1 82.1 %conditional.8 = (f32[1024,1024]{1,0:T(8,128)S(1)}, f32[1024,1024]{1,0:T(8,128)}, f32[1024,1024]{1,0:T(8,128)}, f32[8,1024,256]{2,1,0:T(8,128)}, f32[4,1024]{1,0...) conditional(s32[]{:T(128)} %convert_element_type.23, ...), branch_computations={%region_6.7_spmd, %region_7.8_spmd} | conditional | bytes 64 | solution.py:1457
  49.1 81.9 %attention_last.1 = (f32[1024,1024]{1,0:T(8,128)S(1)}, f32[1024,1024]{1,0:T(8,128)}, f32[1024,1024]{1,0:T(8,128)}, f32[2,4,1024,256]{3,2,1,0:T(8,128)}, f32[2,4,...) custom-call(s32[3]{0:T(128)S(1)} %get-tuple-element.195.place_ref, ...), custom_call_target="tpu_custom_call" | custom-call | tf_op jit(solution)/shard_map/cond/branch_0_fun/attention_last/pallas_call | solution.py:904
  131.8 3.0 collective-permute-start.4
  134.8 3.9 collective-permute-start.5
  138.8 7.2 %norm_backward.2 = (bf16[1024,1024]{1,0:T(8,128)(2,1)}, f32[8,1024]{1,0:T(8,128)}) custom-call(f32[1024,1024]{1,0:T(8,128)S(1)} %get-tuple-element.333.x_ref, f32[1024,1024]{1,0:T(8,128)} %get-tuple-element.335.own_ref, f32[1024,1024]{1,0:T(8,128)} %collective-permute-done.2.other_ref, bf16[1024,1024]{1,0:T(8,128)(2,1)} %grad_ref.1, ...), custom_call_target="tpu_custom_call" | custom-call | tf_op jit(solution)/shard_map/norm_backward/pallas_call | solution.py:1032
  146.0 61.7 %conditional.9 = (f32[1024,1024]{1,0:T(8,128)}, f32[1024,1024]{1,0:T(8,128)}, f32[4,1024]{1,0:T(4,128)S(1)}, f32[2,2,2,1024,256]{4,3,2,1,0:T(8,128)}, f32[2,2,2,...) conditional(s32[]{:T(128)} %convert_element_type.22, ...), branch_computations={%region_8.9_spmd, %region_9.10_spmd} | conditional | bytes 56 | solution.py:1475
  146.3 61.3 %attention_backward.1 = (f32[1024,1024]{1,0:T(8,128)}, f32[1024,1024]{1,0:T(8,128)}, f32[2,4,1024,256]{3,2,1,0:T(8,128)}, f32[2,4,1024,256]{3,2,1,0:T(8,128)}, f...) custom-call(s32[3]{0:T(128)S(1)} %get-tuple-element.256.place_ref, ...), custom_call_target="tpu_custom_call" | custom-call | tf_op jit(solution)/shard_map/cond/branch_1_fun/attention_backward/pallas_call | solution.py:823
  207.8 7.4 %collective-permute-done.3.other_ref = f32[1024,1024]{1,0:T(8,128)S(1)} collective-permute-done((f32[1024,1024]{1,0:T(8,128)}, f32[1024,1024]{1,0:T(8,128)S(1)}, u32[]{:S(2)}, u32[]{:S(2)}) %collective-permute-start.3) | collective-permute-done | bytes 4194336 | tf_op jit(solution)/shard_map/ppermute | solution.py:1483
  215.2 2.0 copy-done.3
  217.2 7.8 %norm_backward.3 = (f32[1024,1024]{1,0:T(8,128)}, f32[8,1024]{1,0:T(8,128)}) custom-call(bf16[1024,1024]{1,0:T(8,128)(2,1)S(1)} %copy-done, f32[1024,1024]{1,0:T(8,128)} %get-tuple-element.341.own_ref, f32[1024,1024]{1,0:T(8,128)} %copy-done.3, bf16[1024,1024]{1,0:T(8,128)(2,1)} %get-tuple-element.336.grad_ref, bf16[2,1024]{1,0:T(2,128)(2,1)S(1)} %copy-done.6), custom_call_target="tpu_custom_call" | custom-call | tf_op jit(solution)/shard_map/norm_backward/pallas_call | solution.py:1032
  224.9 1.6 collective-permute-done.4
  226.5 274.6 %finish.1 = (f32[2,1024,256]{2,1,0:T(8,128)}, f32[2,1024,128]{2,1,0:T(8,128)}, f32[24,1024]{1,0:T(8,128)}) custom-call(f32[2,2,2,1024,256]{4,3,2,1,0:T(8,128)} %get-tuple-element.343.kept_weight1, f32[2,2,2,1024,256]{4,3,2,1,0:T(8,128)} %bitcast.30, f32[2,2,2,1024,256]{4,3,2,1,0:T(8,128)} %bitcast.20.came_weight1, f32[2,2,2,1024,256]{4,3,2,1,0:T(8,128)} %bitcast.22.came_up1, ...), custom_call_target="tpu_custom_call" | custom-call | tf_op jit(solution)/shard_map/finish/pallas_call | solution.py:1313
  501.2 4.4 hand_out.1
  (31 shorter events, 0.9 us)
Async XLA Ops:
  4.9 0.8 copy-start.4
  5.0 33.0 %copy-start.7 = (f32[64,64]{1,0:T(8,128)S(1)}, f32[64,64]{1,0:T(8,128)}, u32[]{:S(2)}) copy-start(f32[64,64]{1,0:T(8,128)} %constant.68.clone) | copy-start | bytes 49156
  5.0 33.0 %copy-start.10 = (s32[2,16,64]{2,1,0:T(8,128)S(1)}, s32[2,16,64]{2,1,0:T(8,128)}, u32[]{:S(2)}) copy-start(s32[2,16,64]{2,1,0:T(8,128)} %param.32) | copy-start | bytes 24580
  37.8 11.2 %collective-permute-start = (f32[1024,1024]{1,0:T(8,128)}, f32[1024,1024]{1,0:T(8,128)}, u32[]{:S(2)}, u32[]{:S(2)}) collective-permute-start(f32[1024,1024]{1,0:T(8,128)} %get-tuple-element.327), channel_id=1, source_target_pairs={{0,1},{1,0},{2,3},{3,2},{4,5},{5,4},{6,7},{7,6},{8,9},{9,8},{10,11... | collective-permute-start | bytes 12582920 | tf_op jit(solution)/shard_map/ppermute | solution.py:1433
  38.0 11.0 %copy-start = (bf16[1024,1024]{1,0:T(8,128)(2,1)S(1)}, bf16[1024,1024]{1,0:T(8,128)(2,1)}, u32[]{:S(2)}) copy-start(bf16[1024,1024]{1,0:T(8,128)(2,1)} %x_ref.1) | copy-start | bytes 6291460
  38.0 11.0 %copy-start.1 = (f32[1024,128]{1,0:T(8,128)S(1)}, f32[1024,128]{1,0:T(8,128)}, u32[]{:S(2)}) copy-start(f32[1024,128]{1,0:T(8,128)} %constant.67.clone) | copy-start | bytes 1572868
  38.0 11.0 %copy-start.2 = (f32[1024,128]{1,0:T(8,128)S(1)}, f32[1024,128]{1,0:T(8,128)}, u32[]{:S(2)}) copy-start(f32[1024,128]{1,0:T(8,128)} %constant.66.clone) | copy-start | bytes 1572868
  38.0 11.0 %copy-start.6 = (bf16[2,1024]{1,0:T(2,128)(2,1)S(1)}, bf16[2,1024]{1,0:T(2,128)(2,1)}, u32[]{:S(2)}) copy-start(bf16[2,1024]{1,0:T(2,128)(2,1)} %gain_ref.3) | copy-start | bytes 12292
  38.0 11.0 %copy-start.8 = (bf16[2,1024]{1,0:T(2,128)(2,1)S(1)}, bf16[2,1024]{1,0:T(2,128)(2,1)}, u32[]{:S(2)}) copy-start(bf16[2,1024]{1,0:T(2,128)(2,1)} %param.31) | copy-start | bytes 12292
  38.0 11.0 %copy-start.9 = (bf16[2,1024]{1,0:T(2,128)(2,1)S(1)}, bf16[2,1024]{1,0:T(2,128)(2,1)}, u32[]{:S(2)}) copy-start(bf16[2,1024]{1,0:T(2,128)(2,1)} %param.29) | copy-start | bytes 12292
  38.1 11.0 %copy-start.11 = (s32[1,4]{1,0:T(1,128)S(1)}, s32[1,4]{1,0:T(1,128)}, u32[]{:S(2)}) copy-start(s32[1,4]{1,0:T(1,128)} %param.33) | copy-start | bytes 52
  131.2 7.6 %collective-permute-start.2 = (f32[1024,1024]{1,0:T(8,128)}, f32[1024,1024]{1,0:T(8,128)}, u32[]{:S(2)}, u32[]{:S(2)}) collective-permute-start(f32[1024,1024]{1,0:T(8,128)} %get-tuple-element.335.own_ref), channel_id=1, source_target_pairs={{0,1},{1,0},{2,3},{3,2},{4,5},{5,4},{6,7},{7,6},{8,9},{9,8},{10,11... | collective-permute-start | bytes 12582920 | tf_op jit(solution)/shard_map/ppermute | solution.py:1483
  131.3 14.7 %collective-permute-start.1 = (f32[1024,1024]{1,0:T(8,128)}, f32[1024,1024]{1,0:T(8,128)}, u32[]{:S(2)}, u32[]{:S(2)}) collective-permute-start(f32[1024,1024]{1,0:T(8,128)} %get-tuple-element.334), channel_id=1, source_target_pairs={{0,1},{1,0},{2,3},{3,2},{4,5},{5,4},{6,7},{7,6},{8,9},{9,8},{10,11... | collective-permute-start | bytes 12582920 | tf_op jit(solution)/shard_map/ppermute | solution.py:1489
  131.8 94.8 %collective-permute-start.4 = (f32[8,1024,256]{2,1,0:T(8,128)}, f32[8,1024,256]{2,1,0:T(8,128)}, u32[]{:S(2)}, u32[]{:S(2)}) collective-permute-start(f32[8,1024,256]{2,1,0:T(8,128)} %get-tuple-element.345), channel_id=1, source_target_pairs={{0,8},{2,10},{4,12},{6,14},{8,0},{10,2},{12,4},{14,6},{16,24},{18,... | collective-permute-start | bytes 25165832 | tf_op jit(solution)/shard_map/ppermute | solution.py:1381
  134.8 91.7 %collective-permute-start.5 = (f32[8,1024,256]{2,1,0:T(8,128)}, f32[8,1024,256]{2,1,0:T(8,128)}, u32[]{:S(2)}, u32[]{:S(2)}) collective-permute-start(f32[8,1024,256]{2,1,0:T(8,128)} %bitcast.41), channel_id=1, source_target_pairs={{1,5},{3,7},{5,1},{7,3},{9,13},{11,15},{13,9},{15,11},{17,21},{19,... | collective-permute-start | bytes 25165832 | tf_op jit(solution)/shard_map/ppermute | solution.py:1382
  138.8 7.2 %copy-start.5 = (bf16[1,4,256,256]{3,2,1,0:T(8,128)(2,1)S(1)}, bf16[1,4,256,256]{3,2,1,0:T(8,128)(2,1)}, u32[]{:S(2)}) copy-start(bf16[1,4,256,256]{3,2,1,0:T(8,128)(2,1)} %copy-done.4) | copy-start | bytes 1572868
  207.8 7.4 %collective-permute-start.3 = (f32[1024,1024]{1,0:T(8,128)}, f32[1024,1024]{1,0:T(8,128)S(1)}, u32[]{:S(2)}, u32[]{:S(2)}) collective-permute-start(f32[1024,1024]{1,0:T(8,128)} %get-tuple-element.341.own_ref), channel_id=1, source_target_pairs={{0,1},{1,0},{2,3},{3,2},{4,5},{5,4},{6,7},{7,6},{8,9},{9,8},{10,11... | collective-permute-start | bytes 12582920 | tf_op jit(solution)/shard_map/ppermute | solution.py:1483
  215.2 2.0 copy-start.3
